TPU v7x, 32 devices: a whole 2x2x4 slice. The times are simulated.
32 devices in a mesh: dp: 2 (over y), fsdp: 16 (over z, x, core).
Axes of the slice: x: 2, y: 2, z: 4, core: 2. Of those that a mesh axis runs over, the one named last changes fastest.
Arguments:
- tokens: bfloat16 [65536, 512], P(('dp', 'fsdp')), may hold values from -6 to 6
- routes: int32 [65536, 2], P(('dp', 'fsdp')), may hold values from 0 to 7, all different within a row
- lengths: int32 [64, 4], P(('dp', 'fsdp')), may hold values from 1 to 512, 1024 in all within a row
- ln1_gain: bfloat16 [512], P(('dp', 'fsdp')), may hold values from 0.5 to 1.5
- ln1_bias: bfloat16 [512], P(('dp', 'fsdp')), may hold values from -3 to 3
- w_query: bfloat16 [512, 512], P(('dp', 'fsdp')), may hold values from -0.25 to 0.25
- w_key: bfloat16 [512, 64], P(('dp', 'fsdp')), may hold values from -0.25 to 0.25
- w_value: bfloat16 [512, 64], P(('dp', 'fsdp')), may hold values from -0.25 to 0.25
- w_out: bfloat16 [512, 512], P(('dp', 'fsdp')), may hold values from -6 to 6
- w_router: bfloat16 [512, 8], P(('dp', 'fsdp')), may hold values from -0.1875 to 0.1875
- ln2_gain: bfloat16 [512], P(('dp', 'fsdp')), may hold values from 0.5 to 1.5
- ln2_bias: bfloat16 [512], P(('dp', 'fsdp')), may hold values from -3 to 3
- w_up: bfloat16 [512, 2048], P(('dp', 'fsdp')), may hold values from -0.25 to 0.25
- b_up: bfloat16 [2048], P(('dp', 'fsdp')), may hold values from -3 to 3
- w_down: bfloat16 [2048, 512], P(('dp', 'fsdp')), may hold values from -0.25 to 0.25
- b_down: bfloat16 [512], P(('dp', 'fsdp')), may hold values from -3 to 3
- cotangent: bfloat16 [65536, 512], P(('dp', 'fsdp')), may hold values from -6 to 6
Outputs:
- result: bfloat16 [65536, 512], P(('dp', 'fsdp'))
- grad_tokens: bfloat16 [65536, 512], P(('dp', 'fsdp'))
- grad_ln1_gain: float32 [512], P(('dp', 'fsdp'))
- grad_ln1_bias: float32 [512], P(('dp', 'fsdp'))
- grad_query: float32 [512, 512], P(('dp', 'fsdp'))
- grad_key: float32 [512, 64], P(('dp', 'fsdp'))
- grad_value: float32 [512, 64], P(('dp', 'fsdp'))
- grad_out: float32 [512, 512], P(('dp', 'fsdp'))
- grad_router: float32 [512, 8], P(('dp', 'fsdp'))
- grad_ln2_gain: float32 [512], P(('dp', 'fsdp'))
- grad_ln2_bias: float32 [512], P(('dp', 'fsdp'))
- grad_up: float32 [512, 2048], P(('dp', 'fsdp'))
- grad_up_bias: float32 [2048], P(('dp', 'fsdp'))
- grad_down: float32 [2048, 512], P(('dp', 'fsdp'))
- grad_down_bias: float32 [512], P(('dp', 'fsdp'))
- expert_load: float32 [8], replicated
Inputs may be any that keep to these rules, and one draw needn't show every extreme that they name: `routes`: the two experts of a token differ; every expert is named by some token. Each row's lengths sum to 1024; in every row one document has exactly 512 tokens.
All inputs are finite; a program needn't handle non-finite values.
Results may differ from a plain program's by a relative error of at most 0.014.
Values may be sent and summed in bfloat16 or wider, within the bound.
No kernel may reach another device: no remote copies, remote signals or barrier semaphores. Data moves between devices by JAX's collectives and lax.ppermute only.
A program may use at most 192 MiB of HBM per device.

v0:
```python
import jax
import jax.numpy as jnp
from jax import lax
from jax.sharding import PartitionSpec as P


def collect(shards):
    return (
        lax.all_gather(shards[0], ("dp", "fsdp"), axis=0, tiled=True),
        lax.all_gather(shards[1], ("dp", "fsdp"), axis=0, tiled=True),
        lax.all_gather(shards[2], ("dp", "fsdp"), axis=0, tiled=True),
        lax.all_gather(shards[3], ("dp", "fsdp"), axis=0, tiled=True),
        lax.all_gather(shards[4], ("dp", "fsdp"), axis=0, tiled=True),
        lax.all_gather(shards[5], ("dp", "fsdp"), axis=0, tiled=True),
        lax.all_gather(shards[6], ("dp", "fsdp"), axis=0, tiled=True),
        lax.all_gather(shards[7], ("dp", "fsdp"), axis=0, tiled=True),
        lax.all_gather(shards[8], ("dp", "fsdp"), axis=0, tiled=True),
        lax.all_gather(shards[9], ("dp", "fsdp"), axis=0, tiled=True),
        lax.all_gather(shards[10], ("dp", "fsdp"), axis=0, tiled=True),
        lax.all_gather(shards[11], ("dp", "fsdp"), axis=0, tiled=True),
        lax.all_gather(shards[12], ("dp", "fsdp"), axis=0, tiled=True),
    )


def spread_sums(grads):
    return (
        lax.psum_scatter(grads[0], ("dp", "fsdp"), scatter_dimension=0, tiled=True),
        lax.psum_scatter(grads[1], ("dp", "fsdp"), scatter_dimension=0, tiled=True),
        lax.psum_scatter(grads[2], ("dp", "fsdp"), scatter_dimension=0, tiled=True),
        lax.psum_scatter(grads[3], ("dp", "fsdp"), scatter_dimension=0, tiled=True),
        lax.psum_scatter(grads[4], ("dp", "fsdp"), scatter_dimension=0, tiled=True),
        lax.psum_scatter(grads[5], ("dp", "fsdp"), scatter_dimension=0, tiled=True),
        lax.psum_scatter(grads[6], ("dp", "fsdp"), scatter_dimension=0, tiled=True),
        lax.psum_scatter(grads[7], ("dp", "fsdp"), scatter_dimension=0, tiled=True),
        lax.psum_scatter(grads[8], ("dp", "fsdp"), scatter_dimension=0, tiled=True),
        lax.psum_scatter(grads[9], ("dp", "fsdp"), scatter_dimension=0, tiled=True),
        lax.psum_scatter(grads[10], ("dp", "fsdp"), scatter_dimension=0, tiled=True),
        lax.psum_scatter(grads[11], ("dp", "fsdp"), scatter_dimension=0, tiled=True),
        lax.psum_scatter(grads[12], ("dp", "fsdp"), scatter_dimension=0, tiled=True),
    )


def norm_forward(value, gain, bias):
    center = value - jnp.mean(value, -1, keepdims=True)
    scale_inv = lax.rsqrt(jnp.mean(center * center, -1, keepdims=True) + 1e-05)
    unit = center * scale_inv
    return (unit * gain + bias, unit, scale_inv)


def norm_backward(grad, unit, scale_inv, gain):
    scaled = grad * gain
    first = jnp.mean(scaled, -1, keepdims=True)
    second = jnp.mean(scaled * unit, -1, keepdims=True)
    back = scale_inv * (scaled - first - unit * second)
    return (back, jnp.sum(grad * unit, 0), jnp.sum(grad, 0))


def outer(left, right):
    return lax.dot_general(
        left, right, (((0,), (0,)), ((), ())), preferred_element_type=jnp.float32
    )


def matmul(left, right):
    return jnp.dot(left, right, preferred_element_type=jnp.float32)


def segment_ids(lengths, length):
    ends = jnp.cumsum(lengths, -1)
    places = jnp.arange(length, dtype=jnp.int32)
    return jnp.sum((places[None, :, None] >= ends[:, None, :]).astype(jnp.int32), -1)


def block_scores(query_block, key_row, seg_row, start, block, scale):
    scores = (
        jnp.einsum("beh,lh->ebl", query_block, key_row, preferred_element_type=jnp.float32) * scale
    )
    same = lax.dynamic_slice_in_dim(seg_row, start, block, 0)[:, None] == seg_row[None, :]
    return jnp.where(same[None], scores, -1e30)


def forward_row(items, experts, head, block):
    query_row, key_row, value_row, seg_row = items
    length = key_row.shape[0]
    scale = head ** (-0.5)
    outputs = []
    totals = []
    for start in range(0, length, block):
        query_block = query_row[start : start + block].reshape(block, experts, head)
        scores = block_scores(query_block, key_row, seg_row, start, block, scale)
        top = jnp.max(scores, -1, keepdims=True)
        raised = jnp.exp(scores - top)
        mass = jnp.sum(raised, -1, keepdims=True)
        probs = (raised / mass).astype(jnp.bfloat16)
        mixed = jnp.einsum("ebl,lh->beh", probs, value_row, preferred_element_type=jnp.float32)
        outputs.append(mixed.reshape(block, experts * head))
        totals.append((top + jnp.log(mass))[..., 0])
    return (jnp.concatenate(outputs, 0), jnp.concatenate(totals, 1))


def backward_row(items, experts, head, block):
    query_row, key_row, value_row, seg_row, lse_row, grad_row = items
    length = key_row.shape[0]
    scale = head ** (-0.5)
    grad_queries = []
    grad_keys = jnp.zeros((length, head), jnp.float32)
    grad_values = jnp.zeros((length, head), jnp.float32)
    for start in range(0, length, block):
        query_block = query_row[start : start + block].reshape(block, experts, head)
        grad_block = grad_row[start : start + block].reshape(block, experts, head)
        scores = block_scores(query_block, key_row, seg_row, start, block, scale)
        probs = jnp.exp(scores - lse_row[:, start : start + block, None])
        grad_probs = jnp.einsum(
            "beh,lh->ebl", grad_block, value_row, preferred_element_type=jnp.float32
        )
        center = jnp.sum(grad_probs * probs, -1, keepdims=True)
        grad_scores = (probs * (grad_probs - center)).astype(jnp.bfloat16)
        part = (
            jnp.einsum("ebl,lh->beh", grad_scores, key_row, preferred_element_type=jnp.float32)
            * scale
        )
        grad_queries.append(part.reshape(block, experts * head))
        grad_keys = (
            grad_keys
            + jnp.einsum(
                "ebl,beh->lh", grad_scores, query_block, preferred_element_type=jnp.float32
            )
            * scale
        )
        grad_values = grad_values + jnp.einsum(
            "ebl,beh->lh",
            probs.astype(jnp.bfloat16),
            grad_block,
            preferred_element_type=jnp.float32,
        )
    return (jnp.concatenate(grad_queries, 0), grad_keys, grad_values)


def on_device(
    tokens,
    routes,
    lengths,
    ln1_gain,
    ln1_bias,
    w_query,
    w_key,
    w_value,
    w_out,
    w_router,
    ln2_gain,
    ln2_bias,
    w_up,
    b_up,
    w_down,
    b_down,
    cotangent,
):
    shards = (
        ln1_gain,
        ln1_bias,
        w_query,
        w_key,
        w_value,
        w_out,
        w_router,
        ln2_gain,
        ln2_bias,
        w_up,
        b_up,
        w_down,
        b_down,
    )
    count_rows = lengths.shape[0]
    total = tokens.shape[0]
    length = total // count_rows
    experts = w_router.shape[1]
    head = w_key.shape[1]
    block = min(512, length)
    picked = jnp.sum(
        (routes[:, :, None] == jnp.arange(experts, dtype=jnp.int32)[None, None, :]).astype(
            jnp.float32
        ),
        1,
    )
    loads_sum = lax.psum(jnp.sum(picked, 0).astype(jnp.int32), ("dp", "fsdp"))
    expert_load = loads_sum.astype(jnp.float32) / (total * lax.axis_size(("dp", "fsdp")))
    weights = collect(shards)
    g_one, b_one, wq, wk, wv, wo, wr, g_two, b_two, wu, bu, wd, bd = weights
    seg = segment_ids(lengths, length)
    inputs = tokens.astype(jnp.float32)
    hidden, unit_one, inv_one = norm_forward(
        inputs, g_one.astype(jnp.float32), b_one.astype(jnp.float32)
    )
    hidden = hidden.astype(jnp.bfloat16)
    query = matmul(hidden, wq).astype(jnp.bfloat16)
    keys = matmul(hidden, wk).astype(jnp.bfloat16)
    values = matmul(hidden, wv).astype(jnp.bfloat16)
    logits = matmul(hidden, wr)
    probs = jax.nn.softmax(logits, axis=-1)
    gates = probs * picked
    query_rows = query.reshape(count_rows, length, experts * head)
    key_rows = keys.reshape(count_rows, length, head)
    value_rows = values.reshape(count_rows, length, head)
    heads, lse = lax.map(
        lambda items: forward_row(items, experts, head, block),
        (query_rows, key_rows, value_rows, seg),
    )
    heads = heads.reshape(total, experts, head)
    mixed = (heads * gates[:, :, None]).reshape(total, experts * head).astype(jnp.bfloat16)
    after = inputs + matmul(mixed, wo)
    second, unit_two, inv_two = norm_forward(
        after, g_two.astype(jnp.float32), b_two.astype(jnp.float32)
    )
    second = second.astype(jnp.bfloat16)
    inner = matmul(second, wu) + bu.astype(jnp.float32)
    active = jax.nn.gelu(inner).astype(jnp.bfloat16)
    result = (after + matmul(active, wd) + bd.astype(jnp.float32)).astype(jnp.bfloat16)
    weights = collect(shards)
    g_one, b_one, wq, wk, wv, wo, wr, g_two, b_two, wu, bu, wd, bd = weights
    grad_out_f = cotangent.astype(jnp.float32)
    grad_down = outer(active, cotangent)
    grad_down_bias = jnp.sum(grad_out_f, 0)
    grad_active = matmul(cotangent, wd.T)
    _, gelu_pull = jax.vjp(jax.nn.gelu, inner)
    grad_inner = gelu_pull(grad_active)[0].astype(jnp.bfloat16)
    grad_up = outer(second, grad_inner)
    grad_up_bias = jnp.sum(grad_inner.astype(jnp.float32), 0)
    grad_second = matmul(grad_inner, wu.T)
    back_two, grad_g_two, grad_b_two = norm_backward(
        grad_second, unit_two, inv_two, g_two.astype(jnp.float32)
    )
    grad_after = grad_out_f + back_two
    grad_after_low = grad_after.astype(jnp.bfloat16)
    grad_wo = outer(mixed, grad_after_low)
    grad_mixed = (
        matmul(grad_after_low, wo.T)
        .astype(jnp.bfloat16)
        .astype(jnp.float32)
        .reshape(total, experts, head)
    )
    grad_gates = jnp.sum(grad_mixed * heads, -1)
    grad_heads = (
        (grad_mixed * gates[:, :, None]).reshape(total, experts * head).astype(jnp.bfloat16)
    )
    grad_q, grad_k, grad_v = lax.map(
        lambda items: backward_row(items, experts, head, block),
        (
            query_rows,
            key_rows,
            value_rows,
            seg,
            lse,
            grad_heads.reshape(count_rows, length, experts * head),
        ),
    )
    grad_q = grad_q.reshape(total, experts * head).astype(jnp.bfloat16)
    grad_k = grad_k.reshape(total, head).astype(jnp.bfloat16)
    grad_v = grad_v.reshape(total, head).astype(jnp.bfloat16)
    grad_probs = grad_gates * picked
    grad_logits = (probs * (grad_probs - jnp.sum(grad_probs * probs, -1, keepdims=True))).astype(
        jnp.bfloat16
    )
    grad_wq = outer(hidden, grad_q)
    grad_wk = outer(hidden, grad_k)
    grad_wv = outer(hidden, grad_v)
    grad_wr = outer(hidden, grad_logits)
    grad_hidden = (
        matmul(grad_q, wq.T)
        + matmul(grad_k, wk.T)
        + matmul(grad_v, wv.T)
        + matmul(grad_logits, wr.T)
    )
    back_one, grad_g_one, grad_b_one = norm_backward(
        grad_hidden, unit_one, inv_one, g_one.astype(jnp.float32)
    )
    grad_tokens = (grad_after + back_one).astype(jnp.bfloat16)
    owned = spread_sums(
        (
            grad_g_one,
            grad_b_one,
            grad_wq,
            grad_wk,
            grad_wv,
            grad_wo,
            grad_wr,
            grad_g_two,
            grad_b_two,
            grad_up,
            grad_up_bias,
            grad_down,
            grad_down_bias,
        )
    )
    return (
        result,
        grad_tokens,
        owned[0],
        owned[1],
        owned[2],
        owned[3],
        owned[4],
        owned[5],
        owned[6],
        owned[7],
        owned[8],
        owned[9],
        owned[10],
        owned[11],
        owned[12],
        expert_load,
    )


def solution(mesh):
    placed = (
        P(("dp", "fsdp"), None),
        P(("dp", "fsdp"), None),
        P(("dp", "fsdp"), None),
        P(("dp", "fsdp")),
        P(("dp", "fsdp")),
        P(("dp", "fsdp"), None),
        P(("dp", "fsdp"), None),
        P(("dp", "fsdp"), None),
        P(("dp", "fsdp"), None),
        P(("dp", "fsdp"), None),
        P(("dp", "fsdp")),
        P(("dp", "fsdp")),
        P(("dp", "fsdp"), None),
        P(("dp", "fsdp")),
        P(("dp", "fsdp"), None),
        P(("dp", "fsdp")),
        P(("dp", "fsdp"), None),
    )
    return jax.shard_map(
        on_device,
        mesh=mesh,
        in_specs=placed,
        out_specs=(
            P(("dp", "fsdp"), None),
            P(("dp", "fsdp"), None),
            P(("dp", "fsdp")),
            P(("dp", "fsdp")),
            P(("dp", "fsdp"), None),
            P(("dp", "fsdp"), None),
            P(("dp", "fsdp"), None),
            P(("dp", "fsdp"), None),
            P(("dp", "fsdp"), None),
            P(("dp", "fsdp")),
            P(("dp", "fsdp")),
            P(("dp", "fsdp"), None),
            P(("dp", "fsdp")),
            P(("dp", "fsdp"), None),
            P(("dp", "fsdp")),
            P(),
        ),
        check_vma=False,
    )
```

profile of v0, /device:TPU:0, one launch (start us, length us, event | category | flops | bytes accessed | tf_op | source)
XLA Modules:
  0.0 1625.6 jit_solution(1144890637451724854)
XLA Ops:
  14.7 42.2 %all-reduce.13 = (bf16[512]{0:T(512)(128)(2,1)S(1)}, bf16[512]{0:T(512)(128)(2,1)S(1)}, bf16[512]{0:T(512)(128)(2,1)}, bf16[512]{0:T(512)(128)(2,1)}, bf16[2048]{0:T(1024)(128)(2,1)}, /*index=5*/bf16[512]{0:T(512)(128)(2,1)}) all-reduce(bf16[512]{0:T(512)(128)(2,1)S(1)} %dynamic-update-slice.1, ...), channel_id=1, replica_groups=mesh['dp'=2,'fsdp'=16] {'dp','fsdp'}, use_global_device_ids=true, to_apply=%add.1 | all-reduce | flops 4608 | bytes 18432
  57.0 41.2 %all-gather = bf16[32,16,8]{1,2,0:T(8,128)(2,1)S(1)} all-gather(bf16[1,16,8]{1,2,0:T(8,128)(2,1)} %bitcast.388), channel_id=1, replica_groups=mesh['dp'=2,'fsdp'=16] {'dp','fsdp'}, dimensions={0}, use_global_device_ids=true | all-gather | bytes 8448 | tf_op jit(solution)/shard_map/all_gather | solution.py:15
  99.9 37.5 %all_gather.51 = bf16[512,64]{1,0:T(8,128)(2,1)S(1)} all-gather(bf16[16,64]{1,0:T(8,128)(2,1)} %param.27), channel_id=1, replica_groups=mesh['dp'=2,'fsdp'=16] {'dp','fsdp'}, dimensions={0}, use_global_device_ids=true | all-gather | bytes 67584 | tf_op jit(solution)/shard_map/all_gather | solution.py:12
  137.4 38.3 %all_gather.50 = bf16[512,64]{1,0:T(8,128)(2,1)S(1)} all-gather(bf16[16,64]{1,0:T(8,128)(2,1)} %param.28), channel_id=1, replica_groups=mesh['dp'=2,'fsdp'=16] {'dp','fsdp'}, dimensions={0}, use_global_device_ids=true | all-gather | bytes 67584 | tf_op jit(solution)/shard_map/all_gather | solution.py:13
  175.7 38.5 %all_gather.52 = bf16[512,512]{1,0:T(8,128)(2,1)S(1)} all-gather(bf16[16,512]{1,0:T(8,128)(2,1)} %param.26), channel_id=1, replica_groups=mesh['dp'=2,'fsdp'=16] {'dp','fsdp'}, dimensions={0}, use_global_device_ids=true | all-gather | bytes 540672 | tf_op jit(solution)/shard_map/all_gather | solution.py:11
  214.2 42.3 %all_gather.54 = bf16[512,512]{1,0:T(8,128)(2,1)} all-gather(bf16[16,512]{1,0:T(8,128)(2,1)} %param.29), channel_id=1, replica_groups=mesh['dp'=2,'fsdp'=16] {'dp','fsdp'}, dimensions={0}, use_global_device_ids=true | all-gather | bytes 540672 | tf_op jit(solution)/shard_map/all_gather | solution.py:14
  268.7 148.0 %while.26 = (s32[]{:T(128)}, f32[2,1024,512]{1,0,2:T(2,128)}, f32[2,8,1024]{2,1,0:T(8,128)S(1)}, bf16[2,1024,64]{1,2,0:T(8,128)(2,1)S(1)}, s32[2,1024]{1,0:T(2,1...) while((s32[]{:T(128)}, f32[2,1024,512]{1,0,2:T(2,128)}, ...), condition=%wide.region_9.10_spmd, body=%wide.region_4.9_spmd.sunk | while | flops 2249719808 | bytes 123560088 | solution.py:204
  280.9 9.8 fusion.217
  306.2 36.4 %dynamic_update_slice.28 = f32[2,1024,512]{1,0,2:T(2,128)} dynamic-update-slice(f32[2,1024,512]{1,0,2:T(2,128)} %get-tuple-element.512, f32[1,1024,512]{1,0,2:T(1,128)S(1)} %copy.218, s32[]{:T(128)S(6)} %copy.236, s32[]{:T(128)} %constant.76.clone.1..sunk, s32[]{:T(128)} %constant.76.clone.1..sunk) | dynamic-update-slice | bytes 4194308 | tf_op jit(solution)/shard_map/while/body/jit(dynamic_update_index_in_dim)/dynamic_update_slice | solution.py:204
  354.6 9.8 fusion.217
  379.9 36.4 %dynamic_update_slice.28 = f32[2,1024,512]{1,0,2:T(2,128)} dynamic-update-slice(f32[2,1024,512]{1,0,2:T(2,128)} %get-tuple-element.512, f32[1,1024,512]{1,0,2:T(1,128)S(1)} %copy.218, s32[]{:T(128)S(6)} %copy.236, s32[]{:T(128)} %constant.76.clone.1..sunk, s32[]{:T(128)} %constant.76.clone.1..sunk) | dynamic-update-slice | bytes 4194308 | tf_op jit(solution)/shard_map/while/body/jit(dynamic_update_index_in_dim)/dynamic_update_slice | solution.py:204
  446.5 16.1 multiply_convert_fusion
  462.6 18.8 %convert_reduce_fusion = (f32[2048]{0:T(1024)}, bf16[2048,2048]{1,0:T(8,128)(2,1)S(1)}) fusion(f32[2048,2048]{1,0:T(8,128)} %get-tuple-element.335, f32[2048]{0:T(1024)S(1)} %convert_element_type.135, bf16[2048,512]{1,0:T(8,128)(2,1)} %param.37, bf16[2048,512]{1,0:T(8,128)(2,1)} %all-gather.6.cloned.1.call-done), kind=kOutput, calls=%fused_computation.114 | convolution fusion | flops 4391434240 | bytes 29376512 | tf_op jit(solution)/shard_map/dot_general | solution.py:65
  506.0 154.8 %while.27 = (s32[]{:T(128)}, bf16[2,1024,512]{2,1,0:T(8,128)(2,1)}, bf16[2,1024,64]{1,2,0:T(8,128)(2,1)}, bf16[2,1024,64]{1,2,0:T(8,128)(2,1)}, bf16[2,1024,64]{...) while((s32[]{:T(128)}, bf16[2,1024,512]{2,1,0:T(8,128)(2,1)}, ...), condition=%wide.region_20.21_spmd, body=%wide.region_17.20_spmd.sunk | while | flops 5448589312 | bytes 362275264 | solution.py:245
  512.6 9.0 fusion.244
  543.2 9.0 fusion.241
  552.2 8.6 fusion.248
  560.8 10.5 fusion.242
  589.7 9.0 fusion.244
  620.3 9.0 fusion.241
  638.0 10.5 fusion.242
  685.3 10.5 fusion.118
  696.5 11.2 fusion.107
  708.4 37.1 %psum.7 = s32[8]{0:T(128)S(1)} all-reduce(s32[8]{0:T(128)S(1)} %convert_element_type.154), channel_id=1, replica_groups=mesh['dp'=2,'fsdp'=16] {'dp','fsdp'}, use_global_device_ids=true, to_apply=%region_45.46 | all-reduce | flops 8 | bytes 64 | tf_op jit(solution)/shard_map/psum | solution.py:185
  746.0 9.9 add_convert_fusion
  765.7 42.0 %all-reduce.12 = (f32[512]{0:T(512)S(1)}, f32[512]{0:T(512)S(1)}, f32[512]{0:T(512)S(1)}, f32[512]{0:T(512)S(1)}, f32[2048]{0:T(1024)S(1)}, /*index=5*/f32[512]{0:T(512)S(1)}) all-reduce(f32[512]{0:T(512)S(1)} %get-tuple-element.247, f32[512]{0:T(512)S(1)} %get-tuple-element.251, ...), channel_id=2, replica_groups=mesh['dp'=2,'fsdp'=16] {'dp','fsdp'}, use_global_device_ids=true, to_apply=%region_26.27.clone | all-reduce | flops 4608 | bytes 36864
  822.7 113.6 %reduce-scatter.14.cloned.1.call-done = f32[16,64]{1,0:T(8,128)} async-done(((f32[512,64]{1,0:T(8,128)}), f32[16,64]{1,0:T(8,128)}) %reduce-scatter.14.cloned.1.call-update) | async-done | bytes 4112 | tf_op jit(solution)/shard_map/reduce_scatter | solution.py:31
  936.3 132.8 %reduce-scatter.12.cloned.1.call-done = f32[16,64]{1,0:T(8,128)} async-done(((f32[512,64]{1,0:T(8,128)}), f32[16,64]{1,0:T(8,128)}) %reduce-scatter.12.cloned.1.call-update) | async-done | bytes 4112 | tf_op jit(solution)/shard_map/reduce_scatter | solution.py:30
  1069.2 134.3 %reduce-scatter.16.cloned.1.call-done = f32[16,512]{1,0:T(8,128)} async-done(((f32[512,512]{1,0:T(8,128)}), f32[16,512]{1,0:T(8,128)}) %reduce-scatter.16.cloned.1.call-update) | async-done | bytes 32784 | tf_op jit(solution)/shard_map/reduce_scatter | solution.py:32
  1203.5 134.0 %reduce-scatter.10.cloned.1.call-done = f32[16,512]{1,0:T(8,128)} async-done(((f32[512,512]{1,0:T(8,128)}), f32[16,512]{1,0:T(8,128)}) %reduce-scatter.10.cloned.1.call-update) | async-done | bytes 32784 | tf_op jit(solution)/shard_map/reduce_scatter | solution.py:29
  1337.4 140.4 %reduce-scatter.20.cloned.1.call-done = f32[64,512]{1,0:T(8,128)} async-done(((f32[2048,512]{1,0:T(8,128)}), f32[64,512]{1,0:T(8,128)}) %reduce-scatter.20.cloned.1.call-update) | async-done | bytes 131088 | tf_op jit(solution)/shard_map/reduce_scatter | solution.py:38
  1477.8 141.1 %reduce-scatter.18.cloned.1.call-done = f32[16,2048]{1,0:T(8,128)} async-done(((f32[512,2048]{1,0:T(8,128)}), f32[16,2048]{1,0:T(8,128)}) %reduce-scatter.18.cloned.1.call-update) | async-done | bytes 131088 | tf_op jit(solution)/shard_map/reduce_scatter | solution.py:36
  (326 shorter events, 269.3 us)
Async XLA Ops:
  7.2 439.3 %all-gather.4.cloned.1.call-start = ((), (), s32[]{:S(2)}) async-start(), calls=%async_computation.7 | async-start | bytes 2162688 | tf_op jit(solution)/shard_map/all_gather | solution.py:18
  7.9 454.7 %all-gather.6.cloned.1.call-start = ((), (), s32[]{:S(2)}) async-start(), calls=%async_computation.8 | async-start | bytes 2162688 | tf_op jit(solution)/shard_map/all_gather | solution.py:20
  8.7 812.7 %reduce-scatter.22.cloned.1.call-start = ((), (), s32[]{:S(2)}) async-start(), calls=%async_computation.15 | async-start | bytes 270336
  56.9 203.4 %copy-start.43 = (f32[512]{0:T(512)}, f32[512]{0:T(512)S(1)}, u32[]{:S(2)}) copy-start(f32[512]{0:T(512)S(1)} %convert_element_type.123) | copy-start | bytes 6148
  98.4 162.8 %copy-start.39 = (bf16[512,8]{0,1:T(8,128)(2,1)}, bf16[512,8]{0,1:T(8,128)(2,1)S(1)}, u32[]{:S(2)}) copy-start(bf16[512,8]{0,1:T(8,128)(2,1)S(1)} %reshape.323) | copy-start | bytes 24580
  137.4 125.8 %copy-start.19 = (bf16[512,64]{1,0:T(8,128)(2,1)}, bf16[512,64]{1,0:T(8,128)(2,1)S(1)}, u32[]{:S(2)}) copy-start(bf16[512,64]{1,0:T(8,128)(2,1)S(1)} %all_gather.51) | copy-start | bytes 196612
  175.7 88.0 %copy-start.17 = (bf16[512,64]{1,0:T(8,128)(2,1)}, bf16[512,64]{1,0:T(8,128)(2,1)S(1)}, u32[]{:S(2)}) copy-start(bf16[512,64]{1,0:T(8,128)(2,1)S(1)} %all_gather.50) | copy-start | bytes 196612
  214.2 50.7 %copy-start.13 = (bf16[512,512]{1,0:T(8,128)(2,1)}, bf16[512,512]{1,0:T(8,128)(2,1)S(1)}, u32[]{:S(2)}) copy-start(bf16[512,512]{1,0:T(8,128)(2,1)S(1)} %all_gather.52) | copy-start | bytes 1572868
  426.3 6.7 copy-start.50
  433.0 66.5 %copy-start.45 = (f32[512]{0:T(512)}, f32[512]{0:T(512)S(1)}, u32[]{:S(2)}) copy-start(f32[512]{0:T(512)S(1)} %convert_element_type.132) | copy-start | bytes 6148
  433.0 13.5 copy-start.52
  443.8 55.6 %copy-start.37 = (f32[2048]{0:T(1024)}, f32[2048]{0:T(1024)S(1)}, u32[]{:S(2)}) copy-start(f32[2048]{0:T(1024)S(1)} %broadcast_multiply_fusion.4) | copy-start | bytes 24580
  446.5 52.9 %copy-start.41 = (f32[2048]{0:T(1024)}, f32[2048]{0:T(1024)S(1)}, u32[]{:S(2)}) copy-start(f32[2048]{0:T(1024)S(1)} %add_rsqrt_fusion) | copy-start | bytes 24580
  462.6 18.8 %copy-start.58 = (bf16[512,2048]{1,0:T(8,128)(2,1)S(1)}, bf16[512,2048]{1,0:T(8,128)(2,1)}, u32[]{:S(2)}) copy-start(bf16[512,2048]{1,0:T(8,128)(2,1)} %all-gather.4.cloned.1.call-done) | copy-start | bytes 6291460
  481.4 7.0 copy-start.59
  543.2 9.0 copy-start.24
  552.2 25.3 %slice-start = ((s8[8388608]{0:T(1024)(128)(4,1)}), s8[4194304]{0:T(1024)(128)(4,1)S(1)}, s32[]{:S(2)}) async-start(s8[8388608]{0:T(1024)(128)(4,1)} %bitcast.349), calls=%async_computation.16 | async-start | bytes 8388608 | tf_op jit(solution)/shard_map/while
  560.8 10.5 copy-start.25
  560.8 16.7 %slice-start.1 = ((s8[8388608]{0:T(1024)(128)(4,1)}), s8[4194304]{0:T(1024)(128)(4,1)S(1)}, s32[]{:S(2)}) async-start(s8[8388608]{0:T(1024)(128)(4,1)} %bitcast.349), calls=%async_computation.17 | async-start | bytes 8388608 | tf_op jit(solution)/shard_map/while
  571.3 8.8 slice-start.2
  620.3 9.0 copy-start.24
  629.4 25.3 %slice-start = ((s8[8388608]{0:T(1024)(128)(4,1)}), s8[4194304]{0:T(1024)(128)(4,1)S(1)}, s32[]{:S(2)}) async-start(s8[8388608]{0:T(1024)(128)(4,1)} %bitcast.349), calls=%async_computation.16 | async-start | bytes 8388608 | tf_op jit(solution)/shard_map/while
  637.9 10.5 copy-start.25
  638.0 16.7 %slice-start.1 = ((s8[8388608]{0:T(1024)(128)(4,1)}), s8[4194304]{0:T(1024)(128)(4,1)S(1)}, s32[]{:S(2)}) async-start(s8[8388608]{0:T(1024)(128)(4,1)} %bitcast.349), calls=%async_computation.17 | async-start | bytes 8388608 | tf_op jit(solution)/shard_map/while
  648.5 8.8 slice-start.2
  673.2 263.1 %reduce-scatter.14.cloned.1.call-start = ((), (), s32[]{:S(2)}) async-start(), calls=%async_computation.11 | async-start | bytes 270336 | tf_op jit(solution)/shard_map/reduce_scatter | solution.py:31
  674.7 394.4 %reduce-scatter.12.cloned.1.call-start = ((), (), s32[]{:S(2)}) async-start(), calls=%async_computation.10 | async-start | bytes 270336 | tf_op jit(solution)/shard_map/reduce_scatter | solution.py:30
  676.2 527.3 %reduce-scatter.16.cloned.1.call-start = ((), (), s32[]{:S(2)}) async-start(), calls=%async_computation.12 | async-start | bytes 1081344 | tf_op jit(solution)/shard_map/reduce_scatter | solution.py:32
  681.4 656.1 %reduce-scatter.10.cloned.1.call-start = ((), (), s32[]{:S(2)}) async-start(), calls=%async_computation.9 | async-start | bytes 1081344 | tf_op jit(solution)/shard_map/reduce_scatter | solution.py:29
  685.2 792.5 %reduce-scatter.20.cloned.1.call-start = ((), (), s32[]{:S(2)}) async-start(), calls=%async_computation.14 | async-start | bytes 4325376 | tf_op jit(solution)/shard_map/reduce_scatter | solution.py:38
  695.8 923.1 %reduce-scatter.18.cloned.1.call-start = ((), (), s32[]{:S(2)}) async-start(), calls=%async_computation.13 | async-start | bytes 4325376 | tf_op jit(solution)/shard_map/reduce_scatter | solution.py:36
  707.7 37.8 %copy-start.54 = (bf16[512]{0:T(512)(128)(2,1)S(1)}, bf16[512]{0:T(512)(128)(2,1)}, u32[]{:S(2)}) copy-start(bf16[512]{0:T(512)(128)(2,1)} %get-tuple-element.299) | copy-start | bytes 3076
  (50 other events, 159.6 us)
Sparse Core Ops, SparseCore 0:
  10.8 59.1 all-gather.3
  72.8 55.5 all-gather.5
  673.3 130.0 reduce-scatter.21
  806.2 130.0 reduce-scatter.13
  939.0 130.1 reduce-scatter.11
  1071.9 131.4 reduce-scatter.15
  1206.3 131.0 reduce-scatter.9
  1340.4 137.3 reduce-scatter.19
  1480.7 138.0 reduce-scatter.17
where the time goes:
time: 1640 us; the launch traced here: 1630 us
  waiting for transfers between devices  798 us (49%)
  blocking collectives  319 us (19%)
  matrix products  255 us (16%)
  local copies, waits for them, and re-layouts  152 us (9%)
  other arithmetic  85.8 us (5%)
    reduce_scatter x1, waiting for transfers between devices, spread_sums(): lax.psum_scatter(grads[9], ('dp', 'fsdp'), scatter_dimension=0, tiled=True)  141 us
    reduce_scatter x1, waiting for transfers between devices, spread_sums(): lax.psum_scatter(grads[11], ('dp', 'fsdp'), scatter_dimension=0, tiled=True)  140 us
    reduce_scatter x1, waiting for transfers between devices, spread_sums(): lax.psum_scatter(grads[5], ('dp', 'fsdp'), scatter_dimension=0, tiled=True)  134 us
    reduce_scatter x1, waiting for transfers between devices, spread_sums(): lax.psum_scatter(grads[2], ('dp', 'fsdp'), scatter_dimension=0, tiled=True)  134 us
    reduce_scatter x1, waiting for transfers between devices, spread_sums(): lax.psum_scatter(grads[3], ('dp', 'fsdp'), scatter_dimension=0, tiled=True)  133 us
    reduce_scatter x1, waiting for transfers between devices, spread_sums(): lax.psum_scatter(grads[4], ('dp', 'fsdp'), scatter_dimension=0, tiled=True)  114 us
    unnamed x2, blocking collectives  84.2 us
    dynamic_update_slice x8, local copies, waits for them, and re-layouts, on_device(): lax.map(lambda items: forward_row(items, experts, head, block), (query_ro...  80.4 us
  transfers between devices with their start and end apart: 9, of which 6 were waited for; matrix products, arithmetic and copies ran while one was open for 17% of the time, Pallas kernels for 0%

commit v1 on v0

v1 whole, which is shorter than its diff:
```python
import functools

import jax
import jax.numpy as jnp
from jax import lax
from jax.experimental import pallas as pl
from jax.experimental.pallas import tpu as pltpu
from jax.sharding import PartitionSpec as P

AXES = ("dp", "fsdp")
F32 = jnp.float32
BF = jnp.bfloat16
FAR = -1e30
LANES = 128
G1, B1, G2, B2, BD, BU, LOAD = 8, 9, 10, 11, 12, 13, 17
TILE = 256
VMEM = 56 * 1024 * 1024


def nn(left, right):
    return jnp.dot(left, right, preferred_element_type=F32)


def nt(left, right):
    return lax.dot_general(left, right, (((1,), (1,)), ((), ())), preferred_element_type=F32)


def iota(shape, dim):
    return lax.broadcasted_iota(jnp.int32, shape, dim)


def normed(value):
    center = value - jnp.mean(value, -1, keepdims=True)
    inv = lax.rsqrt(jnp.mean(center * center, -1, keepdims=True) + 1e-05)
    return center * inv, inv


def fetch(me, pieces, codes, block, dst, sem):
    for piece, own in zip(pieces, codes):
        for place, code in enumerate(own):
            at = pl.multiple_of(jnp.bitwise_xor(me, code) * block, block)
            pltpu.make_async_copy(piece.at[place], dst.at[pl.ds(at, block), :], sem).start()


def arrive(dst, sem):
    pltpu.make_async_copy(dst, dst, sem).wait()


def scatter(me, pieces, codes, block, src, sem):
    for piece, own in zip(pieces, codes):
        for place, code in enumerate(own):
            at = pl.multiple_of(jnp.bitwise_xor(me, code) * block, block)
            pltpu.make_async_copy(src.at[pl.ds(at, block), :], piece.at[place], sem).start()


def split3(value):
    high = value.astype(BF).astype(F32)
    rest = value - high
    mid = rest.astype(BF).astype(F32)
    return high, mid, rest - mid


def segment_of(lens, row, start, rows):
    place = iota((rows, LANES), 0) + start
    end = lens[row, 0]
    seg = (place >= end).astype(jnp.int32)
    for j in range(1, lens.shape[1]):
        end = end + lens[row, j]
        seg = seg + (place >= end).astype(jnp.int32)
    return seg


def pick(routes, rows, slot):
    return jnp.broadcast_to(routes[rows, slot : slot + 1], (TILE, LANES))


def chosen(wide, expert, half):
    out = jnp.zeros(expert.shape, F32)
    for j in range(wide.shape[1] // LANES):
        out = jnp.where(expert == 2 * j + half, wide[:, j * LANES : (j + 1) * LANES], out)
    return out


def forward_kernel(n_pieces, codes, block, experts, me, lens, tok, routes, *refs):
    pieces = refs[:n_pieces]
    hid_o, qx_o, kv_o, pr_o, o_o, u_o, x1_o, h2_o, vec_o, w, kx, vx, vec, sem = refs[n_pieces:]
    length, depth = tok.shape
    segs = lens.shape[1]
    row = pl.program_id(0)

    @pl.when(row == 0)
    def _():
        fetch(me[0], pieces, codes, block, w, sem)
        arrive(w, sem)
        vec[...] = w[:, 2 * depth + LANES :].astype(F32).T
        vec_o[...] = vec[0:32, :]

    lane = iota((TILE, LANES), 1)
    half = lane // 64
    low = lane < 64

    def first(c, _):
        rows = pl.ds(pl.multiple_of(c * TILE, TILE), TILE)
        unit, _ = normed(tok[rows, :].astype(F32))
        hid = (unit * vec[G1 : G1 + 1, :] + vec[B1 : B1 + 1, :]).astype(BF)
        hid_o[rows, :] = hid
        query = nn(hid, w[:, 0:depth])
        small = nn(hid, w[:, 2 * depth :])
        kv = small[:, :LANES].astype(BF)
        kv_o[rows, :] = kv
        kv = kv.astype(F32)
        swap = pltpu.roll(kv, 64, 1)
        seg = segment_of(lens, row, c * TILE, TILE)
        same = jnp.where(lane == seg, 1.0, 0.0)
        kx[rows, 0:LANES] = jnp.where(low, kv, swap).astype(BF)
        kx[rows, LANES:] = jnp.where(lane < segs, same, jnp.where(lane < 8, 1.0, 0.0)).astype(BF)
        vx[rows, 0:LANES] = jnp.where(low, swap, kv).astype(BF)
        vx[rows, LANES:] = jnp.ones((TILE, LANES), BF)
        logits = jnp.where(lane < experts, small[:, LANES:], FAR)
        raised = jnp.exp(logits - jnp.max(logits, -1, keepdims=True))
        pr_o[rows, :] = raised / jnp.sum(raised, -1, keepdims=True)
        apart = jnp.where(lane < segs, (1.0 - same) * FAR, 0.0)
        for slot in range(2):
            mine = chosen(query, pick(routes, rows, slot), half)
            qx_o[slot, rows, 0:LANES] = (mine * 0.125).astype(BF)
            qx_o[slot, rows, LANES:] = apart.astype(BF)
        return 0

    lax.fori_loop(0, length // TILE, first, 0)

    def second(c, _):
        rows = pl.ds(pl.multiple_of(c * TILE, TILE), TILE)
        probs = pr_o[rows, :]
        seen, gated, experts_of = [], [], []
        for slot in range(2):
            expert = pick(routes, rows, slot)
            scores = nt(qx_o[slot, rows, :], kx[...])
            top = jnp.max(scores, -1, keepdims=True)
            raised = jnp.exp(scores - top).astype(BF)
            both = nn(raised, vx[...])
            mass = both[:, LANES:]
            out = both[:, :LANES] / mass
            high, mid, rest = split3(top + jnp.log(mass))
            feats = qx_o[slot, rows, LANES:].astype(F32)
            feats = jnp.where(lane == 4, -high, jnp.where(lane == 5, -mid, jnp.where(lane == 6, -rest, feats)))
            qx_o[slot, rows, LANES:] = feats.astype(BF)
            gate = jnp.sum(jnp.where(lane == expert, probs, 0.0), -1, keepdims=True)
            seen.append(out)
            gated.append(out * gate)
            experts_of.append(expert)
        o_o[rows, :] = jnp.where(low, seen[0], seen[1])
        for j in range(depth // LANES):
            part = jnp.where(experts_of[0] == 2 * j + half, gated[0], jnp.where(experts_of[1] == 2 * j + half, gated[1], 0.0))
            u_o[rows, j * LANES : (j + 1) * LANES] = part.astype(BF)
        after = tok[rows, :].astype(F32) + nn(u_o[rows, :], w[:, depth : 2 * depth])
        x1_o[rows, :] = after
        unit, _ = normed(after)
        h2_o[rows, :] = (unit * vec[G2 : G2 + 1, :] + vec[B2 : B2 + 1, :]).astype(BF)
        return 0

    lax.fori_loop(0, length // TILE, second, 0)


def ffn_kernel(n_pieces, n_out, codes, out_codes, block, me, h2, dy, vec, *refs):
    pieces = refs[:n_pieces]
    act_o, dz_o, bias_o = refs[n_pieces : n_pieces + 3]
    grads = refs[n_pieces + 3 : n_pieces + 3 + n_out]
    w, ht, yt, up_acc, down_acc, out, sem, out_sem = refs[n_pieces + 3 + n_out :]
    sub, t = pl.program_id(0), pl.program_id(1)
    subs, tiles = pl.num_programs(0), pl.num_programs(1)
    span, depth = act_o.shape[0], h2.shape[1]
    width = act_o.shape[1]

    @pl.when((sub == 0) & (t == 0))
    def _():
        fetch(me[0], pieces, codes, block, w, sem)
        ht[depth:, :] = jnp.ones((16, ht.shape[1]), BF)
        arrive(w, sem)

    start = pl.multiple_of(t * span, span)

    @pl.when(sub == 0)
    def _():
        ht[0:depth, pl.ds(start, span)] = h2[pl.ds(start, span), :].T
        yt[:, pl.ds(start, span)] = dy[pl.ds(start, span), :].T

    here = pl.ds(pl.multiple_of(sub * width, width), width)
    there = pl.ds(pl.multiple_of((subs + sub) * width, width), width)
    bias = vec[pl.ds(BU + sub, 1), :]
    one = 0.7978845608028654
    two = one * 0.044715
    for c in range(span // TILE):
        rows = pl.ds(pl.multiple_of(start + c * TILE, TILE), TILE)
        own = slice(c * TILE, (c + 1) * TILE)
        z = nn(h2[rows, :], w[:, here]) + bias
        dact = nt(dy[rows, :], w[:, there])
        square = z * z
        tanh = jnp.tanh(z * (one + two * square))
        part = 0.5 * tanh + 0.5
        act = z * part
        slope = part + act * (1.0 - tanh) * (one + 3.0 * two * square)
        act_o[own, :] = act.astype(BF)
        dz_o[own, :] = (dact * slope).astype(BF)
    up = nn(ht[:, pl.ds(start, span)], dz_o[...])
    down = nn(yt[:, pl.ds(start, span)], act_o[...])

    @pl.when(t == 0)
    def _():
        up_acc[...] = up
        down_acc[...] = down

    @pl.when(t > 0)
    def _():
        up_acc[...] += up
        down_acc[...] += down

    @pl.when(t == tiles - 1)
    def _():
        out[:, here] = up_acc[0:depth, :].astype(BF)
        out[:, there] = down_acc[...].T.astype(BF)
        bias_o[pl.ds(sub, 1), :] = up_acc[depth : depth + 1, :]

    @pl.when((t == tiles - 1) & (sub == subs - 1))
    def _():
        scatter(me[0], grads, out_codes, block, out, out_sem)
        arrive(out, out_sem)


def backward_kernel(
    n_w, n_f, n_out, codes, f_codes, out_codes, block, experts,
    me, lens, dz, dy, x1, routes, hid, qx, kv, pr, o, u, vec, bias, *refs
):
    w_pieces = refs[:n_w]
    f_pieces = refs[n_w : n_w + n_f]
    dx1_o, dq_o, ds_o = refs[n_w + n_f : n_w + n_f + 3]
    grads = refs[n_w + n_f + 3 : n_w + n_f + 3 + n_out]
    (w, wu, kx, vx, dax, dk, dv, gq, gs, go, sums, loads, out, sem, f_sem, out_sem) = refs[n_w + n_f + 3 + n_out :]
    length, depth = dy.shape
    segs = lens.shape[1]
    row = pl.program_id(0)

    @pl.when(row == 0)
    def _():
        fetch(me[0], w_pieces, codes, block, w, sem)
        fetch(me[0], [piece.at[:, :, 0 : wu.shape[1]] for piece in f_pieces], f_codes, block, wu, f_sem)
        gq[...] = jnp.zeros_like(gq)
        gs[...] = jnp.zeros_like(gs)
        go[...] = jnp.zeros_like(go)
        sums[...] = jnp.zeros_like(sums)
        loads[...] = jnp.zeros_like(loads)
        arrive(w, sem)
        arrive(wu, f_sem)

    lane = iota((TILE, LANES), 1)
    half = lane // 64
    low = lane < 64
    dk[...] = jnp.zeros_like(dk)
    dv[...] = jnp.zeros_like(dv)

    def first(c, _):
        rows = pl.ds(pl.multiple_of(c * TILE, TILE), TILE)
        dh2 = nt(dz[rows, :], wu[...])
        unit, inv = normed(x1[rows, :])
        grad = dy[rows, :].astype(F32)
        sums[G2 : G2 + 1, :] += jnp.sum(dh2 * unit, 0, keepdims=True)
        sums[B2 : B2 + 1, :] += jnp.sum(dh2, 0, keepdims=True)
        sums[BD : BD + 1, :] += jnp.sum(grad, 0, keepdims=True)
        scaled = dh2 * vec[G2 : G2 + 1, :]
        one = jnp.mean(scaled, -1, keepdims=True)
        two = jnp.mean(scaled * unit, -1, keepdims=True)
        dx1 = grad + inv * (scaled - one - unit * two)
        dx1_o[rows, :] = dx1
        dx1 = dx1.astype(BF)
        go[...] += nn(u[rows, :].T, dx1)
        du = nt(dx1, w[:, depth : 2 * depth]).astype(BF).astype(F32)
        probs = pr[rows, :]
        heads = o[rows, :]
        swap = pltpu.roll(heads, 64, 1)
        dprobs = jnp.zeros((TILE, LANES), F32)
        for slot in range(2):
            expert = pick(routes, rows, slot)
            own = chosen(du, expert, half)
            here = lane == expert
            gate = jnp.sum(jnp.where(here, probs, 0.0), -1, keepdims=True)
            seen = jnp.where(low, heads, swap) if slot == 0 else jnp.where(low, swap, heads)
            dgate = jnp.sum(own * seen, -1, keepdims=True)
            da = (own * gate).astype(BF)
            high, mid, rest = split3(jnp.sum(da.astype(F32) * seen, -1, keepdims=True))
            dax[slot, rows, 0:LANES] = da
            feats = jnp.where(lane == 4, -high, jnp.where(lane == 5, -mid, jnp.where(lane == 6, -rest, 0.0)))
            dax[slot, rows, LANES:] = feats.astype(BF)
            dprobs = jnp.where(here, dgate, dprobs)
            loads[0:1, :] += jnp.sum(jnp.where(here, 1.0, 0.0), 0, keepdims=True)
        inner = jnp.sum(dprobs * probs, -1, keepdims=True)
        ds_o[rows, LANES:] = (probs * (dprobs - inner)).astype(BF)
        both = kv[rows, :].astype(F32)
        swap = pltpu.roll(both, 64, 1)
        seg = segment_of(lens, row, c * TILE, TILE)
        feats = jnp.where(lane < segs, jnp.where(lane == seg, 1.0, 0.0), jnp.where(lane < 8, 1.0, 0.0)).astype(BF)
        kx[rows, 0:LANES] = jnp.where(low, both, swap).astype(BF)
        kx[rows, LANES:] = feats
        vx[rows, 0:LANES] = jnp.where(low, swap, both).astype(BF)
        vx[rows, LANES:] = feats
        return 0

    lax.fori_loop(0, length // TILE, first, 0)

    def second(c, _):
        rows = pl.ds(pl.multiple_of(c * TILE, TILE), TILE)
        found = []
        for slot in range(2):
            probs = jnp.exp(nt(qx[slot, rows, :], kx[...]))
            away = nt(dax[slot, rows, :], vx[...])
            ds = (probs * away).astype(BF)
            found.append(nn(ds, kx[:, 0:LANES]) * 0.125)
            dk[...] += nn(qx[slot, rows, 0:LANES].T, ds)
            dv[...] += nn(dax[slot, rows, 0:LANES].T, probs.astype(BF))
        one, two = pick(routes, rows, 0), pick(routes, rows, 1)
        for j in range(depth // LANES):
            part = jnp.where(one == 2 * j + half, found[0], jnp.where(two == 2 * j + half, found[1], 0.0))
            dq_o[rows, j * LANES : (j + 1) * LANES] = part.astype(BF)
        return 0

    lax.fori_loop(0, length // TILE, second, 0)

    def third(c, _):
        rows = pl.ds(pl.multiple_of(c * TILE, TILE), TILE)
        both = jnp.concatenate([dk[0:64, rows] + dk[64:, rows], dv[0:64, rows] + dv[64:, rows]], 0)
        ds_o[rows, 0:LANES] = both.T.astype(BF)
        turned = jnp.concatenate([hid[rows, :].T, jnp.ones((16, TILE), BF)], 0)
        gq[...] += nn(turned, dq_o[rows, :])
        gs[...] += nn(turned, ds_o[rows, :])
        return 0

    lax.fori_loop(0, length // TILE, third, 0)

    @pl.when(row == pl.num_programs(0) - 1)
    def _():
        sums[BU : BU + 4, :] = bias[0:4, :]
        wq = w[:, 0:depth].astype(F32)
        ws = w[:, 2 * depth :].astype(F32)
        wide = iota((depth, LANES), 1)
        ws_own = jnp.where(wide < experts, ws[:, LANES:], 0.0)
        around = jnp.sum(gq[0:depth, :] * wq, -1, keepdims=True)
        around += jnp.sum(gs[0:depth, 0:LANES] * ws[:, 0:LANES] + gs[0:depth, LANES:] * ws_own, -1, keepdims=True)
        shift = jnp.sum(gq[depth : depth + 1, :] * wq, -1, keepdims=True)
        shift += jnp.sum(
            gs[depth : depth + 1, 0:LANES] * ws[:, 0:LANES] + gs[depth : depth + 1, LANES:] * ws_own, -1, keepdims=True
        )
        gain = ws[:, LANES + G1 : LANES + G1 + 1]
        lift = ws[:, LANES + B1 : LANES + B1 + 1]
        stretch = (around - lift * shift) / gain
        place = lax.rem(iota((depth, LANES), 0), block)
        load = jnp.sum(jnp.where(wide == place, loads[0:1, :], 0.0), -1, keepdims=True)
        columns = jnp.where(wide < experts, gs[0:depth, LANES:], sums[...].T)
        columns = jnp.where(wide == G1, stretch, columns)
        columns = jnp.where(wide == B1, shift, columns)
        columns = jnp.where(wide == LOAD, load, columns)
        out[:, 0:depth] = gq[0:depth, :].astype(BF)
        out[:, depth : 2 * depth] = go[...].astype(BF)
        out[:, 2 * depth : 2 * depth + LANES] = gs[0:depth, 0:LANES].astype(BF)
        out[:, 2 * depth + LANES :] = columns.astype(BF)
        scatter(me[0], grads, out_codes, block, out, out_sem)
        arrive(out, out_sem)


def last_kernel(
    n_w, n_f, codes, f_codes, block, me, act, x1, dx1, dq, ds, tok, vec, *refs
):
    w_pieces = refs[:n_w]
    f_pieces = refs[n_w : n_w + n_f]
    res_o, grad_o, w, wd, sem, f_sem = refs[n_w + n_f :]
    depth = tok.shape[1]

    @pl.when(pl.program_id(0) == 0)
    def _():
        fetch(me[0], w_pieces, codes, block, w, sem)
        fetch(me[0], [piece.at[:, :, wd.shape[1] :] for piece in f_pieces], f_codes, block, wd, f_sem)
        arrive(w, sem)
        lane = iota((depth, LANES), 1)
        own = w[:, 2 * depth + LANES :].astype(F32)
        w[:, 2 * depth + LANES :] = jnp.where(lane < G1, own, 0.0).astype(BF)
        arrive(wd, f_sem)

    out = x1[...] + vec[BD : BD + 1, :]
    for at in range(0, wd.shape[1], depth):
        out = out + nn(act[:, at : at + depth], wd[:, at : at + depth])
    res_o[...] = out.astype(BF)
    dh = nt(dq[...], w[:, 0:depth]) + nt(ds[...], w[:, 2 * depth :])
    unit, inv = normed(tok[...].astype(F32))
    scaled = dh * vec[G1 : G1 + 1, :]
    one = jnp.mean(scaled, -1, keepdims=True)
    two = jnp.mean(scaled * unit, -1, keepdims=True)
    grad_o[...] = (dx1[...] + inv * (scaled - one - unit * two)).astype(BF)


def xor_pairs(count, mask):
    return [(i, i ^ mask) for i in range(count)]


def hops(dp, fsdp):
    inner = fsdp.bit_length() - 1
    masks = [1 << bit for bit in range(inner - 1, 0, -1)]
    masks += [1 << (inner + bit) for bit in range(dp.bit_length() - 1)]
    if fsdp > 1:
        masks.append(1)
    return masks


def layout(masks):
    own = [0]
    for mask in masks[:-1]:
        own = own + [code ^ mask for code in own]
    if not masks:
        return [own]
    return [own, [code ^ masks[-1] for code in own]]


def gather(share, masks, count):
    held = share[None]
    for mask in masks[:-1]:
        held = jnp.concatenate([held, lax.ppermute(held, AXES, xor_pairs(count, mask))], 0)
    if not masks:
        return [held]
    return [held, lax.ppermute(held, AXES, xor_pairs(count, masks[-1]))]


def reduce(pieces, masks, count):
    if not masks:
        return pieces[0][0].astype(F32)
    keep, send = pieces
    for step, mask in enumerate(reversed(masks)):
        got = lax.ppermute(send, AXES, xor_pairs(count, mask))
        total = keep.astype(F32) + got.astype(F32)
        if step == len(masks) - 1:
            return total[0]
        half = total.shape[0] // 2
        keep, send = total[:half].astype(BF), total[half:].astype(BF)


def on_device(
    sizes, tokens, routes, lengths, ln1_gain, ln1_bias, w_query, w_key, w_value, w_out, w_router,
    ln2_gain, ln2_bias, w_up, b_up, w_down, b_down, cotangent
):
    dp, fsdp = sizes
    count = dp * fsdp
    total, depth = tokens.shape
    rows = lengths.shape[0]
    length = total // rows
    experts, head = w_router.shape[1], w_key.shape[1]
    share = w_query.shape[0]
    inner = w_up.shape[1]
    subs = inner // depth
    width = depth
    fast = share % 16 == 0
    me = (lax.axis_index(AXES) if fast else jnp.int32(0)).astype(jnp.int32).reshape(1)
    small = jnp.concatenate(
        [w_query, w_out, w_key, w_value, w_router]
        + [v[:, None] for v in (ln1_gain, ln1_bias, ln2_gain, ln2_bias, b_down)]
        + [b_up.reshape(subs, share).T],
        1,
    )
    first_width = 2 * depth + 2 * LANES
    small = jnp.pad(small, ((0, 0), (0, first_width - small.shape[1])))
    large = jnp.concatenate(
        [
            w_up.reshape(share, count, subs, share).transpose(0, 2, 1, 3).reshape(share, inner),
            w_down.reshape(subs, share, depth).transpose(1, 0, 2).reshape(share, inner),
        ],
        1,
    )
    if fast:
        masks = hops(dp, fsdp)
        block = share
        codes = layout(masks)
        w_pieces = gather(small, masks, count)
        f_pieces = gather(large, masks, count)
    else:
        masks = []
        block = depth
        codes = [[0]]
        w_pieces = [lax.all_gather(small, AXES, axis=0, tiled=True)[None]]
        f_pieces = [lax.all_gather(large, AXES, axis=0, tiled=True)[None]]
    n = len(w_pieces)
    blocks = len(codes[0])

    smem = pl.BlockSpec(memory_space=pltpu.SMEM)
    hbm = pl.BlockSpec(memory_space=pl.ANY)

    def whole(shape):
        return pl.BlockSpec(shape, lambda *_: (0,) * len(shape))

    def by_row(wide):
        return pl.BlockSpec((length, wide), lambda r: (r, 0))

    def shape(dims, dtype):
        return jax.ShapeDtypeStruct(dims, dtype)

    params = pltpu.CompilerParams(vmem_limit_bytes=VMEM)
    twice = pl.BlockSpec((2, length, 2 * LANES), lambda r: (0, r, 0))
    hid, qx, kv, pr, o, u, x1, h2, vec = pl.pallas_call(
        functools.partial(forward_kernel, n, codes, block, experts),
        grid=(rows,),
        in_specs=[smem, smem, by_row(depth), by_row(2)] + [hbm] * n,
        out_specs=[
            by_row(depth), twice, by_row(LANES), by_row(LANES), by_row(LANES), by_row(depth), by_row(depth), by_row(depth),
            whole((32, depth)),
        ],
        out_shape=[
            shape((total, depth), BF),
            shape((2, total, 2 * LANES), BF),
            shape((total, LANES), BF),
            shape((total, LANES), F32),
            shape((total, LANES), F32),
            shape((total, depth), BF),
            shape((total, depth), F32),
            shape((total, depth), BF),
            shape((32, depth), F32),
        ],
        scratch_shapes=[
            pltpu.VMEM((depth, first_width), BF),
            pltpu.VMEM((length, 2 * LANES), BF),
            pltpu.VMEM((length, 2 * LANES), BF),
            pltpu.VMEM((LANES, depth), F32),
            pltpu.SemaphoreType.DMA,
        ],
        compiler_params=params,
        name="attend",
    )(me, lengths, tokens, routes, *w_pieces)

    span = min(1024, total)
    act, dz, bias, *f_grads = pl.pallas_call(
        functools.partial(ffn_kernel, n, n, codes, codes, block),
        grid=(subs, total // span),
        in_specs=[smem, whole((total, depth)), whole((total, depth)), whole((32, depth))] + [hbm] * n,
        out_specs=[
            pl.BlockSpec((span, width), lambda s, t: (t, s)),
            pl.BlockSpec((span, width), lambda s, t: (t, s)),
            whole((8, depth)),
        ]
        + [hbm] * n,
        out_shape=[
            shape((total, inner), BF),
            shape((total, inner), BF),
            shape((8, depth), F32),
        ]
        + [shape((blocks, block, 2 * inner), BF)] * n,
        scratch_shapes=[
            pltpu.VMEM((depth, 2 * inner), BF),
            pltpu.VMEM((depth + 16, total), BF),
            pltpu.VMEM((depth, total), BF),
            pltpu.VMEM((depth + 16, width), F32),
            pltpu.VMEM((depth, width), F32),
            pltpu.VMEM((depth, 2 * inner), BF),
            pltpu.SemaphoreType.DMA,
            pltpu.SemaphoreType.DMA,
        ],
        compiler_params=params,
        name="feed",
    )(me, h2, cotangent, vec, *f_pieces)

    dx1, dq, ds, *w_grads = pl.pallas_call(
        functools.partial(backward_kernel, n, n, n, codes, codes, codes, block, experts),
        grid=(rows,),
        in_specs=[
            smem, smem, by_row(inner), by_row(depth), by_row(depth), by_row(2), by_row(depth), twice,
            by_row(LANES), by_row(LANES), by_row(LANES), by_row(depth), whole((32, depth)), whole((8, depth)),
        ]
        + [hbm] * (2 * n),
        out_specs=[by_row(depth), by_row(depth), by_row(2 * LANES)] + [hbm] * n,
        out_shape=[shape((total, depth), F32), shape((total, depth), BF), shape((total, 2 * LANES), BF)]
        + [shape((blocks, block, first_width), BF)] * n,
        scratch_shapes=[
            pltpu.VMEM((depth, first_width), BF),
            pltpu.VMEM((depth, inner), BF),
            pltpu.VMEM((length, 2 * LANES), BF),
            pltpu.VMEM((length, 2 * LANES), BF),
            pltpu.VMEM((2, length, 2 * LANES), BF),
            pltpu.VMEM((LANES, length), F32),
            pltpu.VMEM((LANES, length), F32),
            pltpu.VMEM((depth + 16, depth), F32),
            pltpu.VMEM((depth + 16, 2 * LANES), F32),
            pltpu.VMEM((depth, depth), F32),
            pltpu.VMEM((LANES, depth), F32),
            pltpu.VMEM((8, LANES), F32),
            pltpu.VMEM((depth, first_width), BF),
            pltpu.SemaphoreType.DMA,
            pltpu.SemaphoreType.DMA,
            pltpu.SemaphoreType.DMA,
        ],
        compiler_params=params,
        name="back",
    )(me, lengths, dz, cotangent, x1, routes, hid, qx, kv, pr, o, u, vec, bias, *w_pieces, *f_pieces)

    part = min(512, total)

    def by_part(wide):
        return pl.BlockSpec((part, wide), lambda t: (t, 0))

    result, grad_tokens = pl.pallas_call(
        functools.partial(last_kernel, n, n, codes, codes, block),
        grid=(total // part,),
        in_specs=[
            smem,
            by_part(inner), by_part(depth), by_part(depth), by_part(depth), by_part(2 * LANES), by_part(depth), whole((32, depth)),
        ]
        + [hbm] * (2 * n),
        out_specs=[by_part(depth), by_part(depth)],
        out_shape=[shape((total, depth), BF), shape((total, depth), BF)],
        scratch_shapes=[
            pltpu.VMEM((depth, first_width), BF),
            pltpu.VMEM((depth, inner), BF),
            pltpu.SemaphoreType.DMA,
            pltpu.SemaphoreType.DMA,
        ],
        compiler_params=params,
        name="close",
    )(me, act, x1, dx1, dq, ds, tokens, vec, *w_pieces, *f_pieces)

    if fast:
        own_f = reduce(f_grads, masks, count)
        own_w = reduce(w_grads, masks, count)
    else:
        own_f = lax.psum_scatter(f_grads[0][0].astype(F32), AXES, scatter_dimension=0, tiled=True)
        own_w = lax.psum_scatter(w_grads[0][0].astype(F32), AXES, scatter_dimension=0, tiled=True)
        load = lax.psum(w_grads[0][0][:experts, 2 * depth + LANES + LOAD].astype(F32), AXES)
    extra = own_w[:, 2 * depth + LANES :]
    if fast:
        load = extra[:experts, LOAD]
    grad_up = own_f[:, :inner].reshape(share, subs, count, share).transpose(0, 2, 1, 3).reshape(share, inner)
    grad_down = own_f[:, inner:].reshape(share, subs, depth).transpose(1, 0, 2).reshape(subs * share, depth)
    return (
        result,
        grad_tokens,
        extra[:, G1],
        extra[:, B1],
        own_w[:, 0:depth],
        own_w[:, 2 * depth : 2 * depth + head],
        own_w[:, 2 * depth + head : 2 * depth + 2 * head],
        own_w[:, depth : 2 * depth],
        extra[:, 0:experts],
        extra[:, G2],
        extra[:, B2],
        grad_up,
        extra[:, BU : BU + subs].T.reshape(subs * share),
        grad_down,
        extra[:, BD],
        load / (total * count),
    )


def solution(mesh):
    over = P(AXES)
    flat = P(AXES, None)
    sizes = (mesh.shape["dp"], mesh.shape["fsdp"])
    return jax.shard_map(
        functools.partial(on_device, sizes),
        mesh=mesh,
        in_specs=(
            flat, flat, flat, over, over, flat, flat, flat, flat, flat, over, over, flat, over, flat, over, flat,
        ),
        out_specs=(
            flat, flat, over, over, flat, flat, flat, flat, flat, over, over, flat, over, flat, over, P(),
        ),
        check_vma=False,
    )
```

time: 1640 us -> 257 us (0.16)
  waiting for transfers between devices: 798 us -> 80.7 us
  blocking collectives: 319 us -> 0 us
  matrix products: 255 us -> 0 us
  local copies, waits for them, and re-layouts: 152 us -> 12.8 us
  Pallas kernels: 0 us -> 122 us
  other arithmetic: 85.8 us -> 3.6 us
  starting transfers between devices: 0.36 us -> 35.8 us
    reduce_scatter x6 -> x0, waiting for transfers between devices: 796 us -> none  [the longest x1 141 us: spread_sums(): lax.psum_scatter(grads[9], ('dp', 'fsdp'), scatter_dimension=0, tiled=True)]
    dot_general x48 -> x0, matrix products: 253 us -> none  [the longest x14 70.7 us: matmul(): return jnp.dot(left, right, preferred_element_type=jnp.float32)]
    all_gather x5 -> x0, blocking collectives: 198 us -> none  [the longest x1 42.3 us: collect(): lax.all_gather(shards[5], ('dp', 'fsdp'), axis=0, tiled=True)]
    pallas_call x0 -> x4, Pallas kernels: none -> 122 us  [the longest x1 43.7 us: on_device(): pl.pallas_call(functools.partial(backward_kernel, n, n, n, codes, codes,...]
    unnamed x2 -> x0, blocking collectives: 84.2 us -> none
    ppermute x0 -> x20, waiting for transfers between devices: none -> 80.7 us  [the longest x8 51.4 us: gather(): lax.ppermute(held, AXES, xor_pairs(count, mask))]
    dynamic_update_slice x8 -> x0, local copies, waits for them, and re-layouts: 80.4 us -> none  [on_device(): lax.map(lambda items: forward_row(items, experts, head, block), (query_ro...]
    convert_element_type x15 -> x0, other arithmetic: 43.8 us -> none  [the longest x4 36.1 us: backward_row(): grad_scores = (probs * (grad_probs - center)).astype(jnp.bfloat16)]
  transfers between devices with their start and end apart: 9 -> 20, of which waited for: 6 -> 14; matrix products, arithmetic and copies ran while one was open for 17% -> 4% of each run, Pallas kernels for 0% -> 34%
where the time goes in v1:
time: 257 us; the launch traced here: 256 us
  Pallas kernels  122 us (47%)
  waiting for transfers between devices  80.7 us (31%)
  starting transfers between devices  35.8 us (14%)
  local copies, waits for them, and re-layouts  12.8 us (5%)
  other arithmetic  3.6 us (1%)
    ppermute x8, waiting for transfers between devices, gather(): lax.ppermute(held, AXES, xor_pairs(count, mask))  51.4 us
    pallas_call x1, Pallas kernels, on_device(): pl.pallas_call(functools.partial(backward_kernel, n, n, n, codes, codes,...  43.7 us
    pallas_call x1, Pallas kernels, on_device(): pl.pallas_call(functools.partial(ffn_kernel, n, n, codes, codes, block),...  34.4 us
    pallas_call x1, Pallas kernels, on_device(): pl.pallas_call(functools.partial(forward_kernel, n, codes, block, experts...  28.6 us
    ppermute x10, waiting for transfers between devices, reduce(): got = lax.ppermute(send, AXES, xor_pairs(count, mask))  28.5 us
    ppermute x10, starting transfers between devices, reduce(): got = lax.ppermute(send, AXES, xor_pairs(count, mask))  20.1 us
    ppermute x8, starting transfers between devices, gather(): lax.ppermute(held, AXES, xor_pairs(count, mask))  15.5 us
    pallas_call x1, Pallas kernels, on_device(): pl.pallas_call(functools.partial(last_kernel, n, n, codes, codes, block),...  15.5 us
  transfers between devices with their start and end apart: 20, of which 14 were waited for; matrix products, arithmetic and copies ran while one was open for 4% of the time, Pallas kernels for 34%

profile of v1, /device:TPU:0, one launch (start us, length us, event | category | flops | bytes accessed | tf_op | source)
XLA Modules:
  0.0 256.2 jit_solution(12335057423497165782)
XLA Ops:
  0.8 1.3 reshape.69
  3.1 4.1 %collective-permute-start.5 = (bf16[1,16,4096]{2,1,0:T(8,128)(2,1)S(1)}, bf16[1,16,4096]{2,1,0:T(8,128)(2,1)S(1)}, u32[]{:S(2)}, u32[]{:S(2)}) collective-permute-start(bf16[1,16,4096]{2,1,0:T(8,128)(2,1)S(1)} %maximum_bitcast_fusion), channel_id=1, source_target_pairs={{0,8},{1,9},{2,10},{3,11},{4,12},{5,13},{6,14},{7,15},{8,0},{9,1},... | collective-permute-start | bytes 393224 | tf_op jit(solution)/shard_map/ppermute | solution.py:422
  7.2 6.3 %collective-permute-done.5 = bf16[1,16,4096]{2,1,0:T(8,128)(2,1)S(1)} collective-permute-done((bf16[1,16,4096]{2,1,0:T(8,128)(2,1)S(1)}, bf16[1,16,4096]{2,1,0:T(8,128)(2,1)S(1)}, u32[]{:S(2)}, u32[]{:S(2)}) %collective-permute-start.5) | collective-permute-done | bytes 131104 | tf_op jit(solution)/shard_map/ppermute | solution.py:422
  15.2 3.4 %collective-permute-start = (bf16[1,16,1280]{2,1,0:T(8,128)(2,1)S(1)}, bf16[1,16,1280]{2,1,0:T(8,128)(2,1)S(1)}, u32[]{:S(2)}, u32[]{:S(2)}) collective-permute-start(bf16[1,16,1280]{2,1,0:T(8,128)(2,1)S(1)} %pad_bitcast_fusion), channel_id=1, source_target_pairs={{0,8},{1,9},{2,10},{3,11},{4,12},{5,13},{6,14},{7,15},{8,0},{9,1},... | collective-permute-start | bytes 122888 | tf_op jit(solution)/shard_map/ppermute | solution.py:422
  18.7 3.3 %collective-permute-done.6 = bf16[2,16,4096]{2,1,0:T(8,128)(2,1)S(1)} collective-permute-done((bf16[2,16,4096]{2,1,0:T(8,128)(2,1)S(1)}, bf16[2,16,4096]{2,1,0:T(8,128)(2,1)S(1)}, u32[]{:S(2)}, u32[]{:S(2)}) %collective-permute-start.6) | collective-permute-done | bytes 262176 | tf_op jit(solution)/shard_map/ppermute | solution.py:422
  23.4 1.8 collective-permute-start.1
  25.1 8.3 %collective-permute-done.7 = bf16[4,16,4096]{2,1,0:T(8,128)(2,1)S(1)} collective-permute-done((bf16[4,16,4096]{2,1,0:T(8,128)(2,1)S(1)}, bf16[4,16,4096]{2,1,0:T(8,128)(2,1)S(1)}, u32[]{:S(2)}, u32[]{:S(2)}) %collective-permute-start.7) | collective-permute-done | bytes 524320 | tf_op jit(solution)/shard_map/ppermute | solution.py:422
  33.5 1.4 collective-permute-start.8
  35.0 20.2 %collective-permute-done.8 = bf16[8,16,4096]{2,1,0:T(8,128)(2,1)S(1)} collective-permute-done((bf16[8,16,4096]{2,1,0:T(8,128)(2,1)S(1)}, bf16[8,16,4096]{2,1,0:T(8,128)(2,1)S(1)}, u32[]{:S(2)}, u32[]{:S(2)}) %collective-permute-start.8) | collective-permute-done | bytes 1048608 | tf_op jit(solution)/shard_map/ppermute | solution.py:422
  55.5 1.4 collective-permute-start.2
  56.8 5.3 %collective-permute-done.2 = bf16[4,16,1280]{2,1,0:T(8,128)(2,1)S(1)} collective-permute-done((bf16[4,16,1280]{2,1,0:T(8,128)(2,1)S(1)}, bf16[4,16,1280]{2,1,0:T(8,128)(2,1)S(1)}, u32[]{:S(2)}, u32[]{:S(2)}) %collective-permute-start.2) | collective-permute-done | bytes 163872 | tf_op jit(solution)/shard_map/ppermute | solution.py:422
  62.2 1.4 collective-permute-start.3
  63.6 8.0 %collective-permute-done.3 = bf16[8,16,1280]{2,1,0:T(8,128)(2,1)S(1)} collective-permute-done((bf16[8,16,1280]{2,1,0:T(8,128)(2,1)S(1)}, bf16[8,16,1280]{2,1,0:T(8,128)(2,1)S(1)}, u32[]{:S(2)}, u32[]{:S(2)}) %collective-permute-start.3) | collective-permute-done | bytes 327712 | tf_op jit(solution)/shard_map/ppermute | solution.py:422
  71.7 1.3 copy.55.routes
  74.6 28.6 %attend.1 = (bf16[2048,512]{1,0:T(8,128)(2,1)}, bf16[2,2048,256]{2,1,0:T(8,128)(2,1)}, bf16[2048,128]{1,0:T(8,128)(2,1)}, f32[2048,128]{1,0:T(8,128)}, f32[2048,...) custom-call(s32[1]{0:T(128)} %bitcast.me, ...), custom_call_target="tpu_custom_call" | custom-call | tf_op jit(solution)/shard_map/attend/pallas_call | solution.py:501
  103.3 34.4 %feed.1 = (bf16[2048,2048]{1,0:T(8,128)(2,1)}, bf16[2048,2048]{1,0:T(8,128)(2,1)}, f32[8,512]{1,0:T(8,128)}, bf16[16,16,4096]{2,1,0:T(8,128)(2,1)}, bf16[16,16,4096]{2,1,0:T(8,128)(2,1)}) custom-call(s32[1]{0:T(128)} %bitcast.me, bf16[2048,512]{1,0:T(8,128)(2,1)} %get-tuple-element.37.h2, bf16[2048,512]{1,0:T(8,128)(2,1)} %dy.3, ...), custom_call_target="tpu_custom_call" | custom-call | tf_op jit(solution)/shard_map/feed/pallas_call | solution.py:532
  137.9 43.7 %back.1 = (f32[2048,512]{1,0:T(8,128)}, bf16[2048,512]{1,0:T(8,128)(2,1)}, bf16[2048,256]{1,0:T(8,128)(2,1)}, bf16[16,16,1280]{2,1,0:T(8,128)(2,1)}, bf16[16,16,1280]{2,1,0:T(8,128)(2,1)}) custom-call(s32[1]{0:T(128)} %bitcast.me, s32[2,4]{1,0:T(2,128)} %lens.3, bf16[2048,2048]{1,0:T(8,128)(2,1)} %get-tuple-element.41.dz, bf16[2048,512]{1,0:T(8,128)(2,1)} %dy.3, ...), custom_call_target="tpu_custom_call" | custom-call | tf_op jit(solution)/shard_map/back/pallas_call | solution.py:562
  182.1 1.9 collective-permute-done.10
  185.3 1.4 collective-permute-start.11
  186.7 8.7 %collective-permute-done.11 = bf16[8,16,1280]{2,1,0:T(8,128)(2,1)S(1)} collective-permute-done((bf16[8,16,1280]{2,1,0:T(8,128)(2,1)S(1)}, bf16[8,16,1280]{2,1,0:T(8,128)(2,1)S(1)}, u32[]{:S(2)}, u32[]{:S(2)}) %collective-permute-start.11) | collective-permute-done | bytes 327712 | tf_op jit(solution)/shard_map/ppermute | solution.py:433
  195.4 1.4 collective-permute-start.12
  197.7 1.6 collective-permute-start.16
  199.3 1.9 collective-permute-done.12
  201.2 3.6 %collective-permute-start.13 = (bf16[2,16,1280]{2,1,0:T(8,128)(2,1)S(1)}, bf16[2,16,1280]{2,1,0:T(8,128)(2,1)S(1)}, u32[]{:S(2)}, u32[]{:S(2)}) collective-permute-start(bf16[2,16,1280]{2,1,0:T(8,128)(2,1)S(1)} %slice.150), channel_id=1, source_target_pairs={{0,4},{1,5},{2,6},{3,7},{4,0},{5,1},{6,2},{7,3},{8,12},{9,13},{10,... | collective-permute-start | bytes 245768 | tf_op jit(solution)/shard_map/ppermute | solution.py:433
  204.8 15.5 %close.1 = (bf16[2048,512]{1,0:T(8,128)(2,1)}, bf16[2048,512]{1,0:T(8,128)(2,1)}) custom-call(s32[1]{0:T(128)} %bitcast.me, bf16[2048,2048]{1,0:T(8,128)(2,1)} %get-tuple-element.39.act, f32[2048,512]{1,0:T(8,128)} %get-tuple-element.40.x1, f32[2048,512]{1,0:T(8,128)} %get-tuple-element.49.dx1, bf16[2048,512]{1,0:T(8,128)(2,1)} %get-tuple-element.50.dq, ...), custom_call_target="tpu_custom_call" | custom-call | tf_op jit(solution)/shard_map/close/pallas_call | solution.py:600
  220.3 4.8 %collective-permute-start.14 = (bf16[1,16,1280]{2,1,0:T(8,128)(2,1)S(1)}, bf16[1,16,1280]{2,1,0:T(8,128)(2,1)S(1)}, u32[]{:S(2)}, u32[]{:S(2)}) collective-permute-start(bf16[1,16,1280]{2,1,0:T(8,128)(2,1)S(1)} %slice.152), channel_id=1, source_target_pairs={{0,8},{1,9},{2,10},{3,11},{4,12},{5,13},{6,14},{7,15},{8,0},{9,1},... | collective-permute-start | bytes 122888 | tf_op jit(solution)/shard_map/ppermute | solution.py:433
  225.4 1.5 collective-permute-start.17
  227.7 9.6 %collective-permute-done.17 = bf16[4,16,4096]{2,1,0:T(8,128)(2,1)S(1)} collective-permute-done((bf16[4,16,4096]{2,1,0:T(8,128)(2,1)S(1)}, bf16[4,16,4096]{2,1,0:T(8,128)(2,1)S(1)}, u32[]{:S(2)}, u32[]{:S(2)}) %collective-permute-start.17) | collective-permute-done | bytes 524320 | tf_op jit(solution)/shard_map/ppermute | solution.py:433
  239.2 4.7 %collective-permute-done.18 = bf16[2,16,4096]{2,1,0:T(8,128)(2,1)S(1)} collective-permute-done((bf16[2,16,4096]{2,1,0:T(8,128)(2,1)S(1)}, bf16[2,16,4096]{2,1,0:T(8,128)(2,1)S(1)}, u32[]{:S(2)}, u32[]{:S(2)}) %collective-permute-start.18) | collective-permute-done | bytes 262176 | tf_op jit(solution)/shard_map/ppermute | solution.py:433
  244.0 4.3 %collective-permute-start.19 = (bf16[1,16,4096]{2,1,0:T(8,128)(2,1)S(1)}, bf16[1,16,4096]{2,1,0:T(8,128)(2,1)S(1)}, u32[]{:S(2)}, u32[]{:S(2)}) collective-permute-start(bf16[1,16,4096]{2,1,0:T(8,128)(2,1)S(1)} %slice.169), channel_id=1, source_target_pairs={{0,8},{1,9},{2,10},{3,11},{4,12},{5,13},{6,14},{7,15},{8,0},{9,1},... | collective-permute-start | bytes 393224 | tf_op jit(solution)/shard_map/ppermute | solution.py:433
  251.2 1.5 collective-permute-done.19
  253.8 1.6 reshape.74
  (112 shorter events, 16.8 us)
Async XLA Ops:
  0.7 13.9 %copy-start.11 = (bf16[16]{0:T(256)(128)(2,1)S(1)}, bf16[16]{0:T(256)(128)(2,1)}, u32[]{:S(2)}) copy-start(bf16[16]{0:T(256)(128)(2,1)} %param.20) | copy-start | bytes 100
  0.7 14.0 %copy-start.12 = (bf16[16]{0:T(256)(128)(2,1)S(1)}, bf16[16]{0:T(256)(128)(2,1)}, u32[]{:S(2)}) copy-start(bf16[16]{0:T(256)(128)(2,1)} %param.21) | copy-start | bytes 100
  0.7 14.1 %copy-start.13 = (bf16[16]{0:T(256)(128)(2,1)S(1)}, bf16[16]{0:T(256)(128)(2,1)}, u32[]{:S(2)}) copy-start(bf16[16]{0:T(256)(128)(2,1)} %param.27) | copy-start | bytes 100
  0.7 14.2 %copy-start.14 = (bf16[16]{0:T(256)(128)(2,1)S(1)}, bf16[16]{0:T(256)(128)(2,1)}, u32[]{:S(2)}) copy-start(bf16[16]{0:T(256)(128)(2,1)} %param.28) | copy-start | bytes 100
  0.7 14.3 %copy-start.15 = (bf16[16]{0:T(256)(128)(2,1)S(1)}, bf16[16]{0:T(256)(128)(2,1)}, u32[]{:S(2)}) copy-start(bf16[16]{0:T(256)(128)(2,1)} %param.32) | copy-start | bytes 100
  0.7 14.3 %copy-start.6 = (bf16[16,512]{1,0:T(8,128)(2,1)S(1)}, bf16[16,512]{1,0:T(8,128)(2,1)}, u32[]{:S(2)}) copy-start(bf16[16,512]{1,0:T(8,128)(2,1)} %param.22) | copy-start | bytes 49156
  0.7 14.3 %copy-start.8 = (bf16[16,64]{1,0:T(8,128)(2,1)S(1)}, bf16[16,64]{1,0:T(8,128)(2,1)}, u32[]{:S(2)}) copy-start(bf16[16,64]{1,0:T(8,128)(2,1)} %param.23) | copy-start | bytes 6148
  0.8 14.3 %copy-start.9 = (bf16[16,64]{1,0:T(8,128)(2,1)S(1)}, bf16[16,64]{1,0:T(8,128)(2,1)}, u32[]{:S(2)}) copy-start(bf16[16,64]{1,0:T(8,128)(2,1)} %param.24) | copy-start | bytes 6148
  0.8 14.3 %copy-start.7 = (bf16[16,512]{1,0:T(8,128)(2,1)S(1)}, bf16[16,512]{1,0:T(8,128)(2,1)}, u32[]{:S(2)}) copy-start(bf16[16,512]{1,0:T(8,128)(2,1)} %param.25) | copy-start | bytes 49156
  3.1 10.4 %collective-permute-start.5 = (bf16[1,16,4096]{2,1,0:T(8,128)(2,1)S(1)}, bf16[1,16,4096]{2,1,0:T(8,128)(2,1)S(1)}, u32[]{:S(2)}, u32[]{:S(2)}) collective-permute-start(bf16[1,16,4096]{2,1,0:T(8,128)(2,1)S(1)} %maximum_bitcast_fusion), channel_id=1, source_target_pairs={{0,8},{1,9},{2,10},{3,11},{4,12},{5,13},{6,14},{7,15},{8,0},{9,1},... | collective-permute-start | bytes 393224 | tf_op jit(solution)/shard_map/ppermute | solution.py:422
  13.5 8.4 %collective-permute-start.6 = (bf16[2,16,4096]{2,1,0:T(8,128)(2,1)S(1)}, bf16[2,16,4096]{2,1,0:T(8,128)(2,1)S(1)}, u32[]{:S(2)}, u32[]{:S(2)}) collective-permute-start(bf16[2,16,4096]{2,1,0:T(8,128)(2,1)S(1)} %pad_maximum_fusion.3), channel_id=1, source_target_pairs={{0,4},{1,5},{2,6},{3,7},{4,0},{5,1},{6,2},{7,3},{8,12},{9,13},{10,... | collective-permute-start | bytes 786440 | tf_op jit(solution)/shard_map/ppermute | solution.py:422
  15.2 8.1 %collective-permute-start = (bf16[1,16,1280]{2,1,0:T(8,128)(2,1)S(1)}, bf16[1,16,1280]{2,1,0:T(8,128)(2,1)S(1)}, u32[]{:S(2)}, u32[]{:S(2)}) collective-permute-start(bf16[1,16,1280]{2,1,0:T(8,128)(2,1)S(1)} %pad_bitcast_fusion), channel_id=1, source_target_pairs={{0,8},{1,9},{2,10},{3,11},{4,12},{5,13},{6,14},{7,15},{8,0},{9,1},... | collective-permute-start | bytes 122888 | tf_op jit(solution)/shard_map/ppermute | solution.py:422
  22.0 11.4 %collective-permute-start.7 = (bf16[4,16,4096]{2,1,0:T(8,128)(2,1)S(1)}, bf16[4,16,4096]{2,1,0:T(8,128)(2,1)S(1)}, u32[]{:S(2)}, u32[]{:S(2)}) collective-permute-start(bf16[4,16,4096]{2,1,0:T(8,128)(2,1)S(1)} %pad_maximum_fusion.1), channel_id=1, source_target_pairs={{0,2},{1,3},{2,0},{3,1},{4,6},{5,7},{6,4},{7,5},{8,10},{9,11},{10,... | collective-permute-start | bytes 1572872 | tf_op jit(solution)/shard_map/ppermute | solution.py:422
  23.4 32.1 %collective-permute-start.1 = (bf16[2,16,1280]{2,1,0:T(8,128)(2,1)S(1)}, bf16[2,16,1280]{2,1,0:T(8,128)(2,1)S(1)}, u32[]{:S(2)}, u32[]{:S(2)}) collective-permute-start(bf16[2,16,1280]{2,1,0:T(8,128)(2,1)S(1)} %pad_maximum_fusion.5), channel_id=1, source_target_pairs={{0,4},{1,5},{2,6},{3,7},{4,0},{5,1},{6,2},{7,3},{8,12},{9,13},{10,... | collective-permute-start | bytes 245768 | tf_op jit(solution)/shard_map/ppermute | solution.py:422
  33.5 21.7 %collective-permute-start.8 = (bf16[8,16,4096]{2,1,0:T(8,128)(2,1)S(1)}, bf16[8,16,4096]{2,1,0:T(8,128)(2,1)S(1)}, u32[]{:S(2)}, u32[]{:S(2)}) collective-permute-start(bf16[8,16,4096]{2,1,0:T(8,128)(2,1)S(1)} %pad_maximum_fusion), channel_id=1, source_target_pairs={{0,16},{1,17},{2,18},{3,19},{4,20},{5,21},{6,22},{7,23},{8,24},{9,... | collective-permute-start | bytes 3145736 | tf_op jit(solution)/shard_map/ppermute | solution.py:422
  35.0 36.7 %copy-start.5 = (s32[2048,2]{0,1:T(2,128)S(1)}, s32[2048,2]{0,1:T(2,128)}, u32[]{:S(2)}) copy-start(s32[2048,2]{0,1:T(2,128)} %param.18) | copy-start | bytes 49156
  55.3 47.9 %copy-start = (bf16[16,16,4096]{2,1,0:T(8,128)(2,1)}, bf16[16,16,4096]{2,1,0:T(8,128)(2,1)S(1)}, u32[]{:S(2)}) copy-start(bf16[16,16,4096]{2,1,0:T(8,128)(2,1)S(1)} %constant_dynamic-update-slice_fusion.5.refs_0_.refs_2_) | copy-start | bytes 6291460
  55.3 47.9 %collective-permute-start.9 = (bf16[16,16,4096]{2,1,0:T(8,128)(2,1)S(1)}, bf16[16,16,4096]{2,1,0:T(8,128)(2,1)}, u32[]{:S(2)}, u32[]{:S(2)}) collective-permute-start(bf16[16,16,4096]{2,1,0:T(8,128)(2,1)S(1)} %constant_dynamic-update-slice_fusion.5.refs_0_.refs_2_), channel_id=1, source_target_pairs={{0,1},{1,0},{2,3},{3,2},{4,5},{5,4},{6,7},{7,6},{8,9},{9,8},{10,11... | collective-permute-start | bytes 6291464 | tf_op jit(solution)/shard_map/ppermute | solution.py:425
  55.5 6.7 %collective-permute-start.2 = (bf16[4,16,1280]{2,1,0:T(8,128)(2,1)S(1)}, bf16[4,16,1280]{2,1,0:T(8,128)(2,1)S(1)}, u32[]{:S(2)}, u32[]{:S(2)}) collective-permute-start(bf16[4,16,1280]{2,1,0:T(8,128)(2,1)S(1)} %pad_maximum_fusion.4), channel_id=1, source_target_pairs={{0,2},{1,3},{2,0},{3,1},{4,6},{5,7},{6,4},{7,5},{8,10},{9,11},{10,... | collective-permute-start | bytes 491528 | tf_op jit(solution)/shard_map/ppermute | solution.py:422
  62.2 9.4 %collective-permute-start.3 = (bf16[8,16,1280]{2,1,0:T(8,128)(2,1)S(1)}, bf16[8,16,1280]{2,1,0:T(8,128)(2,1)S(1)}, u32[]{:S(2)}, u32[]{:S(2)}) collective-permute-start(bf16[8,16,1280]{2,1,0:T(8,128)(2,1)S(1)} %pad_maximum_fusion.2), channel_id=1, source_target_pairs={{0,16},{1,17},{2,18},{3,19},{4,20},{5,21},{6,22},{7,23},{8,24},{9,... | collective-permute-start | bytes 983048 | tf_op jit(solution)/shard_map/ppermute | solution.py:422
  71.6 2.2 collective-permute-start.4
  137.7 59.1 %collective-permute-start.15 = (bf16[16,16,4096]{2,1,0:T(8,128)(2,1)}, bf16[16,16,4096]{2,1,0:T(8,128)(2,1)S(1)}, u32[]{:S(2)}, u32[]{:S(2)}) collective-permute-start(bf16[16,16,4096]{2,1,0:T(8,128)(2,1)} %get-tuple-element.57), channel_id=1, source_target_pairs={{0,1},{1,0},{2,3},{3,2},{4,5},{5,4},{6,7},{7,6},{8,9},{9,8},{10,11... | collective-permute-start | bytes 6291464 | tf_op jit(solution)/shard_map/ppermute | solution.py:433
  181.6 15.2 %copy-start.3 = (bf16[16,16,4096]{2,1,0:T(8,128)(2,1)S(1)}, bf16[16,16,4096]{2,1,0:T(8,128)(2,1)}, u32[]{:S(2)}) copy-start(bf16[16,16,4096]{2,1,0:T(8,128)(2,1)} %get-tuple-element.56) | copy-start | bytes 6291460
  181.6 2.4 collective-permute-start.10
  185.3 10.0 %collective-permute-start.11 = (bf16[8,16,1280]{2,1,0:T(8,128)(2,1)S(1)}, bf16[8,16,1280]{2,1,0:T(8,128)(2,1)S(1)}, u32[]{:S(2)}, u32[]{:S(2)}) collective-permute-start(bf16[8,16,1280]{2,1,0:T(8,128)(2,1)S(1)} %slice.146), channel_id=1, source_target_pairs={{0,16},{1,17},{2,18},{3,19},{4,20},{5,21},{6,22},{7,23},{8,24},{9,... | collective-permute-start | bytes 983048 | tf_op jit(solution)/shard_map/ppermute | solution.py:433
  195.4 5.7 %collective-permute-start.12 = (bf16[4,16,1280]{2,1,0:T(8,128)(2,1)S(1)}, bf16[4,16,1280]{2,1,0:T(8,128)(2,1)S(1)}, u32[]{:S(2)}, u32[]{:S(2)}) collective-permute-start(bf16[4,16,1280]{2,1,0:T(8,128)(2,1)S(1)} %slice.148), channel_id=1, source_target_pairs={{0,2},{1,3},{2,0},{3,1},{4,6},{5,7},{6,4},{7,5},{8,10},{9,11},{10,... | collective-permute-start | bytes 491528 | tf_op jit(solution)/shard_map/ppermute | solution.py:433
  197.7 27.4 %collective-permute-start.16 = (bf16[8,16,4096]{2,1,0:T(8,128)(2,1)S(1)}, bf16[8,16,4096]{2,1,0:T(8,128)(2,1)S(1)}, u32[]{:S(2)}, u32[]{:S(2)}) collective-permute-start(bf16[8,16,4096]{2,1,0:T(8,128)(2,1)S(1)} %slice.163), channel_id=1, source_target_pairs={{0,16},{1,17},{2,18},{3,19},{4,20},{5,21},{6,22},{7,23},{8,24},{9,... | collective-permute-start | bytes 3145736 | tf_op jit(solution)/shard_map/ppermute | solution.py:433
  201.2 19.0 %collective-permute-start.13 = (bf16[2,16,1280]{2,1,0:T(8,128)(2,1)S(1)}, bf16[2,16,1280]{2,1,0:T(8,128)(2,1)S(1)}, u32[]{:S(2)}, u32[]{:S(2)}) collective-permute-start(bf16[2,16,1280]{2,1,0:T(8,128)(2,1)S(1)} %slice.150), channel_id=1, source_target_pairs={{0,4},{1,5},{2,6},{3,7},{4,0},{5,1},{6,2},{7,3},{8,12},{9,13},{10,... | collective-permute-start | bytes 245768 | tf_op jit(solution)/shard_map/ppermute | solution.py:433
  220.3 6.7 %collective-permute-start.14 = (bf16[1,16,1280]{2,1,0:T(8,128)(2,1)S(1)}, bf16[1,16,1280]{2,1,0:T(8,128)(2,1)S(1)}, u32[]{:S(2)}, u32[]{:S(2)}) collective-permute-start(bf16[1,16,1280]{2,1,0:T(8,128)(2,1)S(1)} %slice.152), channel_id=1, source_target_pairs={{0,8},{1,9},{2,10},{3,11},{4,12},{5,13},{6,14},{7,15},{8,0},{9,1},... | collective-permute-start | bytes 122888 | tf_op jit(solution)/shard_map/ppermute | solution.py:433
  225.4 12.0 %collective-permute-start.17 = (bf16[4,16,4096]{2,1,0:T(8,128)(2,1)S(1)}, bf16[4,16,4096]{2,1,0:T(8,128)(2,1)S(1)}, u32[]{:S(2)}, u32[]{:S(2)}) collective-permute-start(bf16[4,16,4096]{2,1,0:T(8,128)(2,1)S(1)} %slice.165), channel_id=1, source_target_pairs={{0,2},{1,3},{2,0},{3,1},{4,6},{5,7},{6,4},{7,5},{8,10},{9,11},{10,... | collective-permute-start | bytes 1572872 | tf_op jit(solution)/shard_map/ppermute | solution.py:433
  237.5 6.4 %collective-permute-start.18 = (bf16[2,16,4096]{2,1,0:T(8,128)(2,1)S(1)}, bf16[2,16,4096]{2,1,0:T(8,128)(2,1)S(1)}, u32[]{:S(2)}, u32[]{:S(2)}) collective-permute-start(bf16[2,16,4096]{2,1,0:T(8,128)(2,1)S(1)} %slice.167), channel_id=1, source_target_pairs={{0,4},{1,5},{2,6},{3,7},{4,0},{5,1},{6,2},{7,3},{8,12},{9,13},{10,... | collective-permute-start | bytes 786440 | tf_op jit(solution)/shard_map/ppermute | solution.py:433
  244.0 8.7 %collective-permute-start.19 = (bf16[1,16,4096]{2,1,0:T(8,128)(2,1)S(1)}, bf16[1,16,4096]{2,1,0:T(8,128)(2,1)S(1)}, u32[]{:S(2)}, u32[]{:S(2)}) collective-permute-start(bf16[1,16,4096]{2,1,0:T(8,128)(2,1)S(1)} %slice.169), channel_id=1, source_target_pairs={{0,8},{1,9},{2,10},{3,11},{4,12},{5,13},{6,14},{7,15},{8,0},{9,1},... | collective-permute-start | bytes 393224 | tf_op jit(solution)/shard_map/ppermute | solution.py:433
  (5 other events, 32.9 us)

commit v2 on v1

v2 whole, which is shorter than its diff:
```python
import functools

import jax
import jax.numpy as jnp
from jax import lax
from jax.experimental import pallas as pl
from jax.experimental.pallas import tpu as pltpu
from jax.sharding import PartitionSpec as P

AXES = ("dp", "fsdp")
F32 = jnp.float32
BF = jnp.bfloat16
FAR = -1e30
LANES = 128
G1, B1, G2, B2, BD, BU, LOAD = 8, 9, 10, 11, 12, 13, 17
TILE = 256
STEP = 512
VMEM = 56 * 1024 * 1024


def nn(left, right):
    return jnp.dot(left, right, preferred_element_type=F32)


def nt(left, right):
    return lax.dot_general(left, right, (((1,), (1,)), ((), ())), preferred_element_type=F32)


def iota(shape, dim):
    return lax.broadcasted_iota(jnp.int32, shape, dim)


def normed(value):
    center = value - jnp.mean(value, -1, keepdims=True)
    inv = lax.rsqrt(jnp.mean(center * center, -1, keepdims=True) + 1e-05)
    return center * inv, inv


def fetch(me, pieces, block, parts, sem):
    for piece, codes in pieces:
        for place, code in enumerate(codes):
            own = jnp.bitwise_xor(me, code) * block
            for start, wide, dst, row, column in parts:
                at = pl.multiple_of(own + row, 16)
                pltpu.make_async_copy(
                    piece.at[place, :, start : start + wide], dst.at[pl.ds(at, block), column : column + wide], sem
                ).start()


def arrive(dst, sem):
    pltpu.make_async_copy(dst, dst, sem).wait()


def scatter(me, pieces, block, src, start, sem):
    for piece, codes in pieces:
        wide = piece.shape[2]
        for place, code in enumerate(codes):
            at = pl.multiple_of(jnp.bitwise_xor(me, code) * block, 16)
            pltpu.make_async_copy(src.at[pl.ds(at, block), start : start + wide], piece.at[place], sem).start()


def ffn_parts(wu, wd, half, depth, up, down):
    parts = []
    if up:
        parts.append((0, 2 * depth, wu, 0, half * 2 * depth))
    if down:
        parts += [((2 + j) * depth, depth, wd, (2 * half + j) * depth, 0) for j in range(2)]
    return parts


def split3(value):
    high = value.astype(BF).astype(F32)
    rest = value - high
    mid = rest.astype(BF).astype(F32)
    return high, mid, rest - mid


def three(lane, value):
    high, mid, rest = split3(value)
    return jnp.where(lane == 4, -high, jnp.where(lane == 5, -mid, jnp.where(lane == 6, -rest, 0.0)))


def segment_of(lens, row, start, rows):
    place = iota((rows, LANES), 0) + start
    end = lens[row, 0]
    seg = (place >= end).astype(jnp.int32)
    for j in range(1, lens.shape[1]):
        end = end + lens[row, j]
        seg = seg + (place >= end).astype(jnp.int32)
    return seg


def pick(routes, rows, slot):
    return jnp.broadcast_to(routes[rows, slot : slot + 1], (TILE, LANES))


def chosen(wide, expert, half):
    out = jnp.zeros(expert.shape, F32)
    for j in range(wide.shape[1] // LANES):
        out = jnp.where(expert == 2 * j + half, wide[:, j * LANES : (j + 1) * LANES], out)
    return out


def project_kernel(codes, block, length, segs, experts, me, lens, tok, routes, *refs):
    n = len(codes)
    pieces = list(zip(refs[:n], codes))
    hid_o, qa_o, kx_o, vx_o, pr_o, vec_o, w, vec, sem = refs[n:]
    span, depth = tok.shape
    step = pl.program_id(0)
    row = lax.div(step * span, length)
    begin = lax.rem(step * span, length)

    @pl.when(step == 0)
    def _():
        fetch(me[0], pieces, block, [(0, depth, w, 0, 0), (2 * depth, 2 * LANES, w, 0, depth)], sem)
        arrive(w, sem)
        vec[...] = w[:, depth + LANES :].astype(F32).T
        vec_o[...] = vec[0:32, :]

    lane = iota((TILE, LANES), 1)
    half = lane // 64
    low = lane < 64
    for c in range(span // TILE):
        rows = slice(c * TILE, (c + 1) * TILE)
        unit, _ = normed(tok[rows, :].astype(F32))
        hid = (unit * vec[G1 : G1 + 1, :] + vec[B1 : B1 + 1, :]).astype(BF)
        hid_o[rows, :] = hid
        query = nn(hid, w[:, 0:depth])
        small = nn(hid, w[:, depth:])
        kv = small[:, :LANES].astype(BF).astype(F32)
        swap = pltpu.roll(kv, 64, 1)
        seg = segment_of(lens, row, begin + c * TILE, TILE)
        same = jnp.where(lane == seg, 1.0, 0.0)
        kx_o[rows, 0:LANES] = jnp.where(low, kv, swap).astype(BF)
        kx_o[rows, LANES:] = jnp.where(lane < segs, same, jnp.where(lane < 8, 1.0, 0.0)).astype(BF)
        vx_o[rows, 0:LANES] = jnp.where(low, swap, kv).astype(BF)
        vx_o[rows, LANES:] = jnp.ones((TILE, LANES), BF)
        logits = jnp.where(lane < experts, small[:, LANES:], FAR)
        raised = jnp.exp(logits - jnp.max(logits, -1, keepdims=True))
        pr_o[rows, :] = raised / jnp.sum(raised, -1, keepdims=True)
        for slot in range(2):
            qa_o[slot, rows, :] = (chosen(query, pick(routes, rows, slot), half) * 0.125).astype(BF)


def attend_kernel(segs, lens, routes, qa, kx, vx, pr, o_o, u_o, qf_o):
    span, depth = u_o.shape
    row, step = pl.program_id(0), pl.program_id(1)
    lane = iota((TILE, LANES), 1)
    half = lane // 64
    low = lane < 64
    for c in range(span // TILE):
        rows = slice(c * TILE, (c + 1) * TILE)
        seg = segment_of(lens, row, step * span + c * TILE, TILE)
        apart = jnp.where((lane < segs) & (lane != seg), FAR, 0.0)
        probs = pr[rows, :]
        seen, gated, experts_of = [], [], []
        for slot in range(2):
            expert = pick(routes, rows, slot)
            scores = nt(jnp.concatenate([qa[slot, rows, :], apart.astype(BF)], 1), kx[...])
            top = jnp.max(scores, -1, keepdims=True)
            raised = jnp.exp(scores - top).astype(BF)
            both = nn(raised, vx[...])
            mass = both[:, LANES:]
            out = both[:, :LANES] / mass
            qf_o[slot, rows, :] = (apart + three(lane, top + jnp.log(mass))).astype(BF)
            gate = jnp.sum(jnp.where(lane == expert, probs, 0.0), -1, keepdims=True)
            seen.append(out)
            gated.append(out * gate)
            experts_of.append(expert)
        o_o[rows, :] = jnp.where(low, seen[0], seen[1])
        for j in range(depth // LANES):
            part = jnp.where(experts_of[0] == 2 * j + half, gated[0], jnp.where(experts_of[1] == 2 * j + half, gated[1], 0.0))
            u_o[rows, j * LANES : (j + 1) * LANES] = part.astype(BF)


def mix_kernel(codes, block, me, tok, u, vec, *refs):
    n = len(codes)
    x1_o, h2_o, w, sem = refs[n:]
    span, depth = tok.shape

    @pl.when(pl.program_id(0) == 0)
    def _():
        fetch(me[0], list(zip(refs[:n], codes)), block, [(depth, depth, w, 0, 0)], sem)
        arrive(w, sem)

    for c in range(span // TILE):
        rows = slice(c * TILE, (c + 1) * TILE)
        after = tok[rows, :].astype(F32) + nn(u[rows, :], w[...])
        x1_o[rows, :] = after
        unit, _ = normed(after)
        h2_o[rows, :] = (unit * vec[G2 : G2 + 1, :] + vec[B2 : B2 + 1, :]).astype(BF)


def ffn_kernel(codes, block, me, h2, dy, vec, *refs):
    n = [len(own) for own in codes]
    total_pieces = sum(n)
    pieces = [list(zip(refs[: n[0]], codes[0])), list(zip(refs[n[0] : total_pieces], codes[1]))]
    act_o, dz_o, bias_o = refs[total_pieces : total_pieces + 3]
    at = total_pieces + 3
    grads = [list(zip(refs[at : at + n[0]], codes[0])), list(zip(refs[at + n[0] : at + total_pieces], codes[1]))]
    wu, wd, ht, yt, out, sem, out_sem = refs[at + total_pieces :]
    sub = pl.program_id(0)
    total, width = act_o.shape
    depth = h2.shape[1]
    wide = 256

    @pl.when(sub == 0)
    def _():
        for half in range(2):
            fetch(me[0], pieces[half], block, ffn_parts(wu, wd, half, depth, True, True), sem)
        for t in range(0, total, STEP):
            ht[0:depth, t : t + STEP] = h2[t : t + STEP, :].T
            yt[:, t : t + STEP] = dy[t : t + STEP, :].T
        ht[depth:, :] = jnp.ones((16, total), BF)
        arrive(wu, sem)
        arrive(wd, sem)

    one = 0.7978845608028654
    two = one * 0.044715
    up_at = lax.div(sub, 2) * 4 * depth + lax.rem(sub, 2) * depth
    for k in range(width // wide):
        here = pl.ds(pl.multiple_of(sub * width + k * wide, wide), wide)
        own = slice(k * wide, (k + 1) * wide)
        z = nn(h2[...], wu[:, here]) + vec[pl.ds(BU + sub, 1), own]
        dact = nt(dy[...], wd[here, :])
        square = z * z
        tanh = jnp.tanh(z * (one + two * square))
        part = 0.5 * tanh + 0.5
        act = z * part
        slope = part + act * (1.0 - tanh) * (one + 3.0 * two * square)
        act_o[:, own] = act.astype(BF)
        dz_o[:, own] = (dact * slope).astype(BF)
    for k in range(width // wide):
        own = slice(k * wide, (k + 1) * wide)
        up = nn(ht[...], dz_o[:, own])
        out[:, pl.ds(pl.multiple_of(up_at + k * wide, wide), wide)] = up[0:depth, :].astype(BF)
        bias_o[pl.ds(sub, 1), own] = up[depth : depth + 1, :]
    down = nn(yt[...], act_o[...])
    out[:, pl.ds(pl.multiple_of(up_at + 2 * depth, width), width)] = down.T.astype(BF)

    @pl.when(sub == 1)
    def _():
        scatter(me[0], grads[0], block, out, 0, out_sem)

    @pl.when(sub == 3)
    def _():
        scatter(me[0], grads[1], block, out, 4 * depth, out_sem)
        arrive(out, out_sem)


def turn_kernel(codes, f_codes, go_codes, block, me, dz, dy, x1, routes, pr, o, u, vec, *refs):
    n, n_f, n_go = len(codes), [len(own) for own in f_codes], len(go_codes)
    w_pieces = list(zip(refs[:n], codes))
    f_pieces = [list(zip(refs[n : n + n_f[0]], f_codes[0])), list(zip(refs[n + n_f[0] : n + sum(n_f)], f_codes[1]))]
    at = n + sum(n_f)
    dx1_o, da_o, df_o, ds_o, sums_o = refs[at : at + 5]
    go_pieces = list(zip(refs[at + 5 : at + 5 + n_go], go_codes))
    w, wu, go, sums, out, sem, f_sem, out_sem = refs[at + 5 + n_go :]
    span, depth = dy.shape
    step = pl.program_id(0)

    @pl.when(step == 0)
    def _():
        for half in range(2):
            fetch(me[0], f_pieces[half], block, ffn_parts(wu, None, half, depth, True, False), f_sem)
        fetch(me[0], w_pieces, block, [(depth, depth, w, 0, 0)], sem)
        go[...] = jnp.zeros_like(go)
        sums[...] = jnp.zeros_like(sums)
        arrive(wu, f_sem)
        arrive(w, sem)

    lane = iota((TILE, LANES), 1)
    half = lane // 64
    low = lane < 64
    for c in range(span // TILE):
        rows = slice(c * TILE, (c + 1) * TILE)
        dh2 = nt(dz[rows, :], wu[...])
        unit, inv = normed(x1[rows, :])
        grad = dy[rows, :].astype(F32)
        sums[G2 : G2 + 1, :] += jnp.sum(dh2 * unit, 0, keepdims=True)
        sums[B2 : B2 + 1, :] += jnp.sum(dh2, 0, keepdims=True)
        sums[BD : BD + 1, :] += jnp.sum(grad, 0, keepdims=True)
        scaled = dh2 * vec[G2 : G2 + 1, :]
        one = jnp.mean(scaled, -1, keepdims=True)
        two = jnp.mean(scaled * unit, -1, keepdims=True)
        dx1 = grad + inv * (scaled - one - unit * two)
        dx1_o[rows, :] = dx1
        dx1 = dx1.astype(BF)
        go[...] += nn(u[rows, :].T, dx1)
        du = nt(dx1, w[...]).astype(BF).astype(F32)
        probs = pr[rows, :]
        heads = o[rows, :]
        swap = pltpu.roll(heads, 64, 1)
        dprobs = jnp.zeros((TILE, LANES), F32)
        for slot in range(2):
            expert = pick(routes, rows, slot)
            own = chosen(du, expert, half)
            here = lane == expert
            gate = jnp.sum(jnp.where(here, probs, 0.0), -1, keepdims=True)
            seen = jnp.where(low, heads, swap) if slot == 0 else jnp.where(low, swap, heads)
            dgate = jnp.sum(own * seen, -1, keepdims=True)
            da = (own * gate).astype(BF)
            da_o[slot, rows, :] = da
            df_o[slot, rows, :] = three(lane, jnp.sum(da.astype(F32) * seen, -1, keepdims=True)).astype(BF)
            dprobs = jnp.where(here, dgate, dprobs)
            sums[LOAD : LOAD + 1, 0:LANES] += jnp.sum(jnp.where(here, 1.0, 0.0), 0, keepdims=True)
        inner = jnp.sum(dprobs * probs, -1, keepdims=True)
        ds_o[rows, :] = (probs * (dprobs - inner)).astype(BF)

    @pl.when(step == pl.num_programs(0) - 1)
    def _():
        sums_o[...] = sums[...]
        out[...] = go[...].astype(BF)
        scatter(me[0], go_pieces, block, out, 0, out_sem)
        arrive(out, out_sem)


def attend_back_kernel(routes, qa, qf, kx, vx, da, df, dq_o, kv_o, dk, dv, ds, ps):
    span, depth = dq_o.shape
    step = pl.program_id(1)
    lane = iota((TILE, LANES), 1)
    half = lane // 64

    for slot in range(2):
        own = slice(slot * span, (slot + 1) * span)
        probs = jnp.exp(nt(jnp.concatenate([qa[slot], qf[slot]], 1), kx[...]))
        ps[own, :] = probs.astype(BF)
        away = nt(jnp.concatenate([da[slot], df[slot]], 1), vx[...])
        ds[own, :] = (probs * away).astype(BF)
    dk_part = nn(jnp.concatenate([qa[0].T, qa[1].T], 1), ds[...])
    dv_part = nn(jnp.concatenate([da[0].T, da[1].T], 1), ps[...])
    found = nn(ds[...], kx[:, 0:LANES]) * 0.125
    for c in range(span // TILE):
        rows = slice(c * TILE, (c + 1) * TILE)
        others = slice(span + c * TILE, span + (c + 1) * TILE)
        one, two = pick(routes, rows, 0), pick(routes, rows, 1)
        for j in range(depth // LANES):
            part = jnp.where(one == 2 * j + half, found[rows, :], jnp.where(two == 2 * j + half, found[others, :], 0.0))
            dq_o[rows, j * LANES : (j + 1) * LANES] = part.astype(BF)

    @pl.when(step == 0)
    def _():
        dk[...] = dk_part
        dv[...] = dv_part

    @pl.when(step > 0)
    def _():
        dk[...] += dk_part
        dv[...] += dv_part

    @pl.when(step == pl.num_programs(1) - 1)
    def _():
        for c in range(kv_o.shape[0] // TILE):
            rows = slice(c * TILE, (c + 1) * TILE)
            both = jnp.concatenate([dk[0:64, rows] + dk[64:, rows], dv[0:64, rows] + dv[64:, rows]], 0)
            kv_o[rows, :] = both.T.astype(BF)


def sum_kernel(codes, out_codes, block, experts, me, hid, dq, kv, ds, sums, bias, *refs):
    n, n_out = len(codes), len(out_codes)
    pieces = list(zip(refs[:n], codes))
    grads = list(zip(refs[n : n + n_out], out_codes))
    w, gq, gs, all_sums, out, sem, out_sem = refs[n + n_out :]
    span, depth = hid.shape
    step = pl.program_id(0)

    @pl.when(step == 0)
    def _():
        fetch(me[0], pieces, block, [(0, depth, w, 0, 0), (2 * depth, 2 * LANES, w, 0, depth)], sem)
        gq[...] = jnp.zeros_like(gq)
        gs[...] = jnp.zeros_like(gs)

    turned = jnp.concatenate([hid[...].T, jnp.ones((16, span), BF)], 0)
    gq[...] += nn(turned, dq[...])
    gs[...] += nn(turned, jnp.concatenate([kv[...], ds[...]], 1))

    @pl.when(step == pl.num_programs(0) - 1)
    def _():
        arrive(w, sem)
        all_sums[...] = jnp.zeros_like(all_sums)
        all_sums[0:32, :] = sums[...]
        all_sums[BU : BU + 4, :] = bias[0:4, :]
        wq = w[:, 0:depth].astype(F32)
        ws = w[:, depth:].astype(F32)
        wide = iota((depth, LANES), 1)
        ws_own = jnp.where(wide < experts, ws[:, LANES:], 0.0)
        around = jnp.sum(gq[0:depth, :] * wq, -1, keepdims=True)
        around += jnp.sum(gs[0:depth, 0:LANES] * ws[:, 0:LANES] + gs[0:depth, LANES:] * ws_own, -1, keepdims=True)
        shift = jnp.sum(gq[depth : depth + 1, :] * wq, -1, keepdims=True)
        shift += jnp.sum(
            gs[depth : depth + 1, 0:LANES] * ws[:, 0:LANES] + gs[depth : depth + 1, LANES:] * ws_own, -1, keepdims=True
        )
        gain = ws[:, LANES + G1 : LANES + G1 + 1]
        lift = ws[:, LANES + B1 : LANES + B1 + 1]
        stretch = (around - lift * shift) / gain
        place = lax.rem(iota((depth, LANES), 0), block)
        load = jnp.sum(jnp.where(wide == place, sums[LOAD : LOAD + 1, 0:LANES], 0.0), -1, keepdims=True)
        columns = jnp.where(wide < experts, gs[0:depth, LANES:], all_sums[...].T)
        columns = jnp.where(wide == G1, stretch, columns)
        columns = jnp.where(wide == B1, shift, columns)
        columns = jnp.where(wide == LOAD, load, columns)
        out[:, 0:depth] = gq[0:depth, :].astype(BF)
        out[:, depth : depth + LANES] = gs[0:depth, 0:LANES].astype(BF)
        out[:, depth + LANES :] = columns.astype(BF)
        scatter(me[0], grads, block, out, 0, out_sem)
        arrive(out, out_sem)


def result_kernel(f_codes, block, me, act, x1, vec, *refs):
    n = [len(own) for own in f_codes]
    f_pieces = [list(zip(refs[: n[0]], f_codes[0])), list(zip(refs[n[0] : sum(n)], f_codes[1]))]
    res_o, wd, sem = refs[sum(n) :]
    depth = x1.shape[1]

    @pl.when(pl.program_id(0) == 0)
    def _():
        for half in range(2):
            fetch(me[0], f_pieces[half], block, ffn_parts(None, wd, half, depth, False, True), sem)
        arrive(wd, sem)

    res_o[...] = (x1[...] + vec[BD : BD + 1, :] + nn(act[...], wd[...])).astype(BF)


def close_kernel(codes, block, me, dx1, dq, kv, ds, tok, vec, *refs):
    n = len(codes)
    grad_o, w, sem = refs[n:]
    span, depth = tok.shape

    @pl.when(pl.program_id(0) == 0)
    def _():
        fetch(me[0], list(zip(refs[:n], codes)), block, [(0, depth, w, 0, 0), (2 * depth, 2 * LANES, w, 0, depth)], sem)
        arrive(w, sem)

    for c in range(span // TILE):
        rows = slice(c * TILE, (c + 1) * TILE)
        dh = nt(dq[rows, :], w[:, 0:depth]) + nt(jnp.concatenate([kv[rows, :], ds[rows, :]], 1), w[:, depth:])
        unit, inv = normed(tok[rows, :].astype(F32))
        scaled = dh * vec[G1 : G1 + 1, :]
        one = jnp.mean(scaled, -1, keepdims=True)
        two = jnp.mean(scaled * unit, -1, keepdims=True)
        grad_o[rows, :] = (dx1[rows, :] + inv * (scaled - one - unit * two)).astype(BF)


def xor_pairs(count, mask):
    return [(i, i ^ mask) for i in range(count)]


def hops(dp, fsdp):
    inner = fsdp.bit_length() - 1
    along = [1 << bit for bit in range(inner - 1, 1, -1)]
    across = [2] if inner > 1 else []
    rows = [1 << (inner + bit) for bit in range(dp.bit_length() - 1)]
    core = [1] if inner > 0 else []
    return along + across + rows + core, along + rows + across + core


def layout(masks):
    own = [0]
    for mask in masks[:-1]:
        own = own + [code ^ mask for code in own]
    if not masks:
        return [own]
    return [own, [code ^ masks[-1] for code in own]]


def after(value, *others):
    return lax.optimization_barrier((value, *others))[0]


def move(value, mask, count):
    return lax.ppermute(value, AXES, xor_pairs(count, mask))


def spread(held, mask, count):
    return jnp.concatenate([held, move(held, mask, count)], 0)


def joined(keep, got, dtype=BF):
    return (keep.astype(F32) + got.astype(F32)).astype(dtype)


def halves(value):
    half = value.shape[0] // 2
    return value[:half], value[half:]


def cost(micros):
    return pl.CostEstimate(flops=int(micros * 1.0e9), bytes_accessed=1024, transcendentals=0)


def on_device(
    sizes, tokens, routes, lengths, ln1_gain, ln1_bias, w_query, w_key, w_value, w_out, w_router,
    ln2_gain, ln2_bias, w_up, b_up, w_down, b_down, cotangent
):
    dp, fsdp = sizes
    count = dp * fsdp
    total, depth = tokens.shape
    rows = lengths.shape[0]
    length = total // rows
    experts, head = w_router.shape[1], w_key.shape[1]
    segs = lengths.shape[1]
    share = w_query.shape[0]
    inner = w_up.shape[1]
    subs = inner // depth
    fast = share % 16 == 0 and fsdp >= 8 and dp >= 2
    me = (lax.axis_index(AXES) if fast else jnp.int32(0)).astype(jnp.int32).reshape(1)
    small = jnp.concatenate(
        [w_query, w_out, w_key, w_value, w_router]
        + [v[:, None] for v in (ln1_gain, ln1_bias, ln2_gain, ln2_bias, b_down)]
        + [b_up.reshape(subs, share).T],
        1,
    )
    first_width = 2 * depth + 2 * LANES
    small = jnp.pad(small, ((0, 0), (0, first_width - small.shape[1])))
    ups = w_up.reshape(share, count, subs, share).transpose(0, 2, 1, 3).reshape(share, subs, depth)
    downs = w_down.reshape(subs, share, depth).transpose(1, 0, 2)
    large = [
        jnp.concatenate([ups[:, 2 * i : 2 * i + 2], downs[:, 2 * i : 2 * i + 2]], 1).reshape(share, 4 * depth)
        for i in range(2)
    ]
    stage = [lambda value: value] * 8
    if fast:
        orders = hops(dp, fsdp)
        block = share
        codes = layout(orders[0])
        f_codes = [layout(order) for order in orders]
        steps = len(orders[0])
        held = spread(small[None], orders[0][0], count)
        big = [after(half[None], held) for half in large]
        big_all = spread(jnp.concatenate(big, 2), orders[0][0], count)
        early = len([m for m in orders[0][:-1] if orders[0].index(m) == orders[1].index(m)])
        for mask in orders[0][1 : -2]:
            held = spread(held, mask, count)
        held = after(held, big_all)
        for mask in orders[0][1:early]:
            big_all = spread(big_all, mask, count)
        held = spread(held, orders[0][-2], count)
        w_pieces = [held, move(held, orders[0][-1], count)]
        big = [big_all[:, :, : 4 * depth], big_all[:, :, 4 * depth :]]
        w_pieces[0] = after(w_pieces[0], *big)
        pending = list(range(early, steps - 1))
    else:
        block = depth
        codes = [[0]]
        f_codes = [[[0]], [[0]]]
        w_pieces = [lax.all_gather(small, AXES, axis=0, tiled=True)[None]]
        f_pieces = [[lax.all_gather(half, AXES, axis=0, tiled=True)[None]] for half in large]
    n, n_f = len(codes), [len(own) for own in f_codes]
    blocks = len(codes[0])

    smem = pl.BlockSpec(memory_space=pltpu.SMEM)
    hbm = pl.BlockSpec(memory_space=pl.ANY)
    dma = pltpu.SemaphoreType.DMA

    def whole(dims):
        return pl.BlockSpec(dims, lambda *_: (0,) * len(dims))

    def shape(dims, dtype):
        return jax.ShapeDtypeStruct(dims, dtype)

    def call(kernel, name, micros, grid, ins, in_specs, outs, out_specs, scratch):
        return pl.pallas_call(
            kernel, grid=grid, in_specs=in_specs, out_specs=out_specs, out_shape=outs, scratch_shapes=scratch,
            compiler_params=pltpu.CompilerParams(vmem_limit_bytes=VMEM), cost_estimate=cost(micros), name=name,
        )(*ins)

    span = min(STEP, length)
    tiles = total // span
    per_row = length // span

    def tile(wide):
        return pl.BlockSpec((span, wide), lambda t: (t, 0))

    def pair(wide):
        return pl.BlockSpec((2, span, wide), lambda t: (0, t, 0))

    def row_tile(wide):
        return pl.BlockSpec((span, wide), lambda r, t: (r * per_row + t, 0))

    def row_pair(wide):
        return pl.BlockSpec((2, span, wide), lambda r, t: (0, r * per_row + t, 0))

    def by_row(wide):
        return pl.BlockSpec((length, wide), lambda r, t: (r, 0))

    hid, qa, kx, vx, pr, vec = call(
        functools.partial(project_kernel, codes, block, length, segs, experts), "project", 9.0, (tiles,),
        (me, lengths, tokens, routes, *w_pieces),
        [smem, smem, tile(depth), tile(2)] + [hbm] * n,
        [
            shape((total, depth), BF), shape((2, total, LANES), BF), shape((total, 2 * LANES), BF),
            shape((total, 2 * LANES), BF), shape((total, LANES), F32), shape((32, depth), F32),
        ],
        [tile(depth), pair(LANES), tile(2 * LANES), tile(2 * LANES), tile(LANES), whole((32, depth))],
        [pltpu.VMEM((depth, depth + 2 * LANES), BF), pltpu.VMEM((LANES, depth), F32), dma],
    )
    if fast:
        big = [spread(half, order[pending[0]], count) for half, order in zip(big, orders)]
        qa = after(qa, *big)
        big = [after(half, kx) for half in big]
    o, u, qf = call(
        functools.partial(attend_kernel, segs), "attend", 13.0, (rows, per_row),
        (lengths, routes, qa, kx, vx, pr),
        [smem, row_tile(2), row_pair(LANES), by_row(2 * LANES), by_row(2 * LANES), row_tile(LANES)],
        [shape((total, LANES), F32), shape((total, depth), BF), shape((2, total, LANES), BF)],
        [row_tile(LANES), row_tile(depth), row_pair(LANES)],
        [],
    )
    if fast:
        for at in pending[1:]:
            big = [spread(half, order[at], count) for half, order in zip(big, orders)]
        u = after(u, *big)
        big = [after(half, o) for half in big]
        f_pieces = [[half, move(half, orders[0][-1], count)] for half in big]
    x1, h2 = call(
        functools.partial(mix_kernel, codes, block), "mix", 5.0, (tiles,),
        (me, tokens, u, vec, *w_pieces),
        [smem, tile(depth), tile(depth), whole((32, depth))] + [hbm] * n,
        [shape((total, depth), F32), shape((total, depth), BF)],
        [tile(depth), tile(depth)],
        [pltpu.VMEM((depth, depth), BF), dma],
    )
    flat_f = [piece for half in f_pieces for piece in half]

    act, dz, bias, *f_grads = call(
        functools.partial(ffn_kernel, f_codes, block), "feed", 25.0, (subs,),
        (me, h2, cotangent, vec, *flat_f),
        [smem, whole((total, depth)), whole((total, depth)), whole((32, depth))] + [hbm] * sum(n_f),
        [shape((total, inner), BF), shape((total, inner), BF), shape((8, depth), F32)]
        + [shape((blocks, block, 4 * depth), BF)] * sum(n_f),
        [pl.BlockSpec((total, depth), lambda s: (0, s)), pl.BlockSpec((total, depth), lambda s: (0, s)), whole((8, depth))]
        + [hbm] * sum(n_f),
        [
            pltpu.VMEM((depth, inner), BF), pltpu.VMEM((inner, depth), BF), pltpu.VMEM((depth + 16, total), BF),
            pltpu.VMEM((depth, total), BF), pltpu.VMEM((depth, 2 * inner), BF), dma, dma,
        ],
    )
    f_grads = [f_grads[: n_f[0]], f_grads[n_f[0] :]]
    if fast:
        sent = [move(half[1], orders[0][-1], count) for half in f_grads]

    dx1, da, df, ds, sums, *go = call(
        functools.partial(turn_kernel, codes, f_codes, f_codes[0], block), "turn", 20.0, (tiles,),
        (me, dz, cotangent, x1, routes, pr, o, u, vec, *w_pieces, *flat_f),
        [smem, tile(inner), tile(depth), tile(depth), tile(2), tile(LANES), tile(LANES), tile(depth), whole((32, depth))]
        + [hbm] * (n + sum(n_f)),
        [
            shape((total, depth), F32), shape((2, total, LANES), BF), shape((2, total, LANES), BF),
            shape((total, LANES), BF), shape((32, depth), F32),
        ]
        + [shape((blocks, block, depth), BF)] * n_f[0],
        [tile(depth), pair(LANES), pair(LANES), tile(LANES), whole((32, depth))] + [hbm] * n_f[0],
        [
            pltpu.VMEM((depth, depth), BF), pltpu.VMEM((depth, inner), BF), pltpu.VMEM((depth, depth), F32),
            pltpu.VMEM((32, depth), F32), pltpu.VMEM((depth, depth), BF), dma, dma, dma,
        ],
    )
    if fast:
        got = move(go[1], orders[0][-1], count)
        acc = [joined(half[0], s) for half, s in zip(f_grads, sent)]
        acc[0] = jnp.concatenate([acc[0], joined(go[0], got)], 2)
        acc = [after(a, dx1) for a in acc]
        back_orders = [list(reversed(order[:-1])) for order in orders]
        split = [halves(a) for a in acc]
        acc = [joined(keep, move(send, order[0], count)) for (keep, send), order in zip(split, back_orders)]

    dq, kv = call(
        attend_back_kernel, "attend_back", 18.0, (rows, per_row),
        (routes, qa, qf, kx, vx, da, df),
        [row_tile(2), row_pair(LANES), row_pair(LANES), by_row(2 * LANES), by_row(2 * LANES), row_pair(LANES), row_pair(LANES)],
        [shape((total, depth), BF), shape((total, LANES), BF)],
        [row_tile(depth), by_row(LANES)],
        [
            pltpu.VMEM((LANES, length), F32), pltpu.VMEM((LANES, length), F32), pltpu.VMEM((2 * span, length), BF),
            pltpu.VMEM((2 * span, length), BF),
        ],
    )
    if fast:
        kv = after(kv, *acc)
        acc = [after(a, kv) for a in acc]
        split = [halves(a) for a in acc]
        acc = [joined(keep, move(send, order[1], count)) for (keep, send), order in zip(split, back_orders)]
    w_grads = call(
        functools.partial(sum_kernel, codes, codes, block, experts), "sums", 6.0, (tiles,),
        (me, hid, dq, kv, ds, sums, bias, *w_pieces),
        [smem, tile(depth), tile(depth), tile(LANES), tile(LANES), whole((32, depth)), whole((8, depth))] + [hbm] * n,
        [shape((blocks, block, depth + 2 * LANES), BF)] * n,
        [hbm] * n,
        [
            pltpu.VMEM((depth, depth + 2 * LANES), BF), pltpu.VMEM((depth + 16, depth), F32),
            pltpu.VMEM((depth + 16, 2 * LANES), F32), pltpu.VMEM((LANES, depth), F32),
            pltpu.VMEM((depth, depth + 2 * LANES), BF), dma, dma,
        ],
    )
    if fast:
        tail = joined(w_grads[0], move(w_grads[1], orders[0][-1], count))
        late = back_orders[0]
        tail_keep, tail_send = halves(tail)
        tail = joined(tail_keep, move(tail_send, late[0], count))
        tail_keep, tail_send = halves(tail)
    grad_tokens = call(
        functools.partial(close_kernel, codes, block), "close", 6.0, (tiles,),
        (me, dx1, dq, kv, ds, tokens, vec, *w_pieces),
        [smem, tile(depth), tile(depth), tile(LANES), tile(LANES), tile(depth), whole((32, depth))] + [hbm] * n,
        [shape((total, depth), BF)],
        [tile(depth)],
        [pltpu.VMEM((depth, depth + 2 * LANES), BF), dma],
    )[0]
    result = call(
        functools.partial(result_kernel, f_codes, block), "result", 6.0, (tiles,),
        (me, act, x1, vec, *flat_f),
        [smem, tile(inner), tile(depth), whole((32, depth))] + [hbm] * sum(n_f),
        [shape((total, depth), BF)],
        [tile(depth)],
        [pltpu.VMEM((inner, depth), BF), dma],
    )[0]

    if fast:
        for step in range(2, len(back_orders[0])):
            split = [halves(a) for a in acc]
            acc = [
                joined(keep, move(send, order[step], count), F32 if step == len(back_orders[0]) - 1 else BF)
                for (keep, send), order in zip(split, back_orders)
            ]
        for step in range(1, len(late)):
            tail = joined(tail_keep, move(tail_send, late[step], count), F32 if step == len(late) - 1 else BF)
            if step < len(late) - 1:
                tail_keep, tail_send = halves(tail)
        own_f = [acc[0][0, :, : 4 * depth], acc[1][0]]
        grad_out = acc[0][0, :, 4 * depth :]
        own_w = tail[0]
        load = own_w[:experts, depth + LANES + LOAD]
    else:
        def scattered(value):
            return lax.psum_scatter(value[0].astype(F32), AXES, scatter_dimension=0, tiled=True)

        own_f = [scattered(half[0]) for half in f_grads]
        grad_out = scattered(go[0])
        own_w = scattered(w_grads[0])
        load = lax.psum(w_grads[0][0][:experts, depth + LANES + LOAD].astype(F32), AXES)
    extra = own_w[:, depth + LANES :]
    grad_up = jnp.concatenate([half[:, : 2 * depth] for half in own_f], 1)
    grad_up = grad_up.reshape(share, subs, count, share).transpose(0, 2, 1, 3).reshape(share, inner)
    grad_down = jnp.concatenate([half[:, 2 * depth :] for half in own_f], 1)
    grad_down = grad_down.reshape(share, subs, depth).transpose(1, 0, 2).reshape(subs * share, depth)
    return (
        result,
        grad_tokens,
        extra[:, G1],
        extra[:, B1],
        own_w[:, 0:depth],
        own_w[:, depth : depth + head],
        own_w[:, depth + head : depth + 2 * head],
        grad_out,
        extra[:, 0:experts],
        extra[:, G2],
        extra[:, B2],
        grad_up,
        extra[:, BU : BU + subs].T.reshape(subs * share),
        grad_down,
        extra[:, BD],
        load / (total * count),
    )


def solution(mesh):
    over = P(AXES)
    flat = P(AXES, None)
    sizes = (mesh.shape["dp"], mesh.shape["fsdp"])
    return jax.shard_map(
        functools.partial(on_device, sizes),
        mesh=mesh,
        in_specs=(
            flat, flat, flat, over, over, flat, flat, flat, flat, flat, over, over, flat, over, flat, over, flat,
        ),
        out_specs=(
            flat, flat, over, over, flat, flat, flat, flat, flat, over, over, flat, over, flat, over, P(),
        ),
        check_vma=False,
    )
```

time: 257 us -> 218 us (0.85)
  waiting for transfers between devices: 80.7 us -> 37.2 us
  local copies, waits for them, and re-layouts: 12.8 us -> 21.2 us
    ppermute x20 -> x29, waiting for transfers between devices: 80.7 us -> 37.2 us  [move(): return lax.ppermute(value, AXES, xor_pairs(count, mask))]
    broadcast_in_dim x5, local copies, waits for them, and re-layouts: 0.47 us -> 3.73 us  [on_device(): v[:, None]]
    pallas_call x4 -> x9, Pallas kernels: 122 us -> 120 us  [call(): pl.pallas_call(kernel, grid=grid, in_specs=in_specs, out_specs=out_specs,...]
    another operation x8 -> x0, other arithmetic: 2.6 us -> none
    unnamed x45 -> x33, local copies, waits for them, and re-layouts: 3.15 us -> 5.55 us
    ppermute x20 -> x29, starting transfers between devices: 35.8 us -> 35.1 us  [move(): return lax.ppermute(value, AXES, xor_pairs(count, mask))]
  transfers between devices with their start and end apart: 20 -> 29, of which waited for: 14 -> 14; matrix products, arithmetic and copies ran while one was open for 4% -> 5% of each run, Pallas kernels for 34% -> 26%
where the time goes in v2:
time: 218 us; the launch traced here: 217 us
  Pallas kernels  120 us (55%)
  waiting for transfers between devices  37.2 us (17%)
  starting transfers between devices  35.1 us (16%)
  local copies, waits for them, and re-layouts  21.2 us (10%)
  other arithmetic  2.63 us (1%)
    pallas_call x9, Pallas kernels, call(): pl.pallas_call(kernel, grid=grid, in_specs=in_specs, out_specs=out_specs,...  120 us
    ppermute x29, waiting for transfers between devices, move(): return lax.ppermute(value, AXES, xor_pairs(count, mask))  37.2 us
    ppermute x29, starting transfers between devices, move(): return lax.ppermute(value, AXES, xor_pairs(count, mask))  35.1 us
    unnamed x33, local copies, waits for them, and re-layouts  5.55 us
  transfers between devices with their start and end apart: 29, of which 14 were waited for; matrix products, arithmetic and copies ran while one was open for 5% of the time, Pallas kernels for 26%

profile of v2, /device:TPU:0, one launch (start us, length us, event | category | flops | bytes accessed | tf_op | source)
XLA Modules:
  0.0 217.0 jit_solution(9470597201251413417)
XLA Ops:
  6.8 4.1 %collective-permute-start = (bf16[1,16,1280]{2,1,0:T(8,128)(2,1)S(1)}, bf16[1,16,1280]{2,1,0:T(8,128)(2,1)S(1)}, u32[]{:S(2)}, u32[]{:S(2)}) collective-permute-start(bf16[1,16,1280]{2,1,0:T(8,128)(2,1)S(1)} %pad_bitcast_fusion), channel_id=1, source_target_pairs={{0,8},{1,9},{2,10},{3,11},{4,12},{5,13},{6,14},{7,15},{8,0},{9,1},... | collective-permute-start | bytes 122888 | tf_op jit(solution)/shard_map/ppermute | solution.py:471
  14.1 1.6 collective-permute-start.1
  15.7 2.2 collective-permute-start.3
  18.6 1.6 collective-permute-start.2
  20.1 3.9 %collective-permute-done.3 = bf16[1,16,4096]{2,1,0:T(8,128)(2,1)S(1)} collective-permute-done((bf16[1,16,4096]{2,1,0:T(8,128)(2,1)S(1)}, bf16[1,16,4096]{2,1,0:T(8,128)(2,1)S(1)}, u32[]{:S(2)}, u32[]{:S(2)}) %collective-permute-start.3) | collective-permute-done | bytes 131104 | tf_op jit(solution)/shard_map/ppermute | solution.py:471
  24.2 1.6 collective-permute-start.4
  25.8 5.9 %collective-permute-done.5 = bf16[2,16,4096]{2,1,0:T(8,128)(2,1)S(1)} collective-permute-done((bf16[2,16,4096]{2,1,0:T(8,128)(2,1)S(1)}, bf16[2,16,4096]{2,1,0:T(8,128)(2,1)S(1)}, u32[]{:S(2)}, u32[]{:S(2)}) %collective-permute-start.5) | collective-permute-done | bytes 262176 | tf_op jit(solution)/shard_map/ppermute | solution.py:471
  31.8 1.6 collective-permute-start.8
  36.5 2.3 %collective-permute-done.8 = bf16[4,16,2048]{2,1,0:T(8,128)(2,1)S(1)} collective-permute-done((bf16[4,16,2048]{2,1,0:T(8,128)(2,1)S(1)}, bf16[4,16,2048]{2,1,0:T(8,128)(2,1)S(1)}, u32[]{:S(2)}, u32[]{:S(2)}) %collective-permute-start.8) | collective-permute-done | bytes 262176 | tf_op jit(solution)/shard_map/ppermute | solution.py:471
  38.9 3.4 %collective-permute-done.7 = bf16[4,16,2048]{2,1,0:T(8,128)(2,1)S(1)} collective-permute-done((bf16[4,16,2048]{2,1,0:T(8,128)(2,1)S(1)}, bf16[4,16,2048]{2,1,0:T(8,128)(2,1)S(1)}, u32[]{:S(2)}, u32[]{:S(2)}) %collective-permute-start.7) | collective-permute-done | bytes 262176 | tf_op jit(solution)/shard_map/ppermute | solution.py:471
  43.3 9.7 %project.1 = (bf16[2048,512]{1,0:T(8,128)(2,1)}, bf16[2,2048,128]{2,1,0:T(8,128)(2,1)}, bf16[2048,256]{1,0:T(8,128)(2,1)}, bf16[2048,256]{1,0:T(8,128)(2,1)}, f32[2048,128]{1,0:T(8,128)}, /*index=5*/f32[32,512]{1,0:T(8,128)}) custom-call(s32[1]{0:T(128)} %bitcast.me, s32[2,4]{1,0:T(2,128)} %lens.3, bf16[2048,512]{1,0:T(8,128)(2,1)} %tok.5, ...), custom_call_target="tpu_custom_call" | custom-call | flops 8999999488 | bytes 1024 | tf_op jit(solution)/shard_map/project/pallas_call | solution.py:562
  53.0 1.6 collective-permute-start.9
  56.1 11.2 %attend.1 = (f32[2048,128]{1,0:T(8,128)}, bf16[2048,512]{1,0:T(8,128)(2,1)}, bf16[2,2048,128]{2,1,0:T(8,128)(2,1)}) custom-call(s32[2,4]{1,0:T(2,128)} %lens.3, s32[2048,2]{1,0:T(8,128)} %copy.61.routes, bf16[2,2048,128]{2,1,0:T(8,128)(2,1)} %get-tuple-element.65.qa, bf16[2048,256]{1,0:T(8,128)(2,1)} %get-tuple-element.66.kx, ...), custom_call_target="tpu_custom_call" | custom-call | flops 12999999488 | bytes 1024 | tf_op jit(solution)/shard_map/attend/pallas_call | solution.py:562
  68.5 7.4 %mix.1 = (f32[2048,512]{1,0:T(8,128)}, bf16[2048,512]{1,0:T(8,128)(2,1)}) custom-call(s32[1]{0:T(128)} %bitcast.me, bf16[2048,512]{1,0:T(8,128)(2,1)} %tok.5, bf16[2048,512]{1,0:T(8,128)(2,1)} %get-tuple-element.72.u, f32[32,512]{1,0:T(8,128)} %get-tuple-element.73.vec, bf16[16,16,1280]{2,1,0:T(8,128)(2,1)} %copy-done.6, bf16[16,16,1280]{2,1,0:T(8,128)(2,1)} %copy-done.12), custom_call_target="tpu_custom_call" | custom-call | flops 5000000000 | bytes 1024 | tf_op jit(solution)/shard_map/mix/pallas_call | solution.py:562
  77.3 32.5 %feed.1 = (bf16[2048,2048]{1,0:T(8,128)(2,1)}, bf16[2048,2048]{1,0:T(8,128)(2,1)}, f32[8,512]{1,0:T(8,128)}, bf16[16,16,2048]{2,1,0:T(8,128)(2,1)}, bf16[16,16,2...) custom-call(s32[1]{0:T(128)} %bitcast.me, ...), custom_call_target="tpu_custom_call" | custom-call | flops 24999999488 | bytes 1024 | tf_op jit(solution)/shard_map/feed/pallas_call | solution.py:562
  109.8 19.8 %turn.1 = (f32[2048,512]{1,0:T(8,128)}, bf16[2,2048,128]{2,1,0:T(8,128)(2,1)}, bf16[2,2048,128]{2,1,0:T(8,128)(2,1)}, bf16[2048,128]{1,0:T(8,128)(2,1)}, f32[32,...) custom-call(s32[1]{0:T(128)} %bitcast.me, bf16[2048,2048]{1,0:T(8,128)(2,1)} %get-tuple-element.80.dz, ...), custom_call_target="tpu_custom_call" | custom-call | flops 20000000000 | bytes 1024 | tf_op jit(solution)/shard_map/turn/pallas_call | solution.py:562
  130.3 13.7 %attend_back.1 = (bf16[2048,512]{1,0:T(8,128)(2,1)}, bf16[2048,128]{1,0:T(8,128)(2,1)}) custom-call(s32[2048,2]{1,0:T(8,128)} %copy.61.routes, bf16[2,2048,128]{2,1,0:T(8,128)(2,1)} %get-tuple-element.65.qa, bf16[2,2048,128]{2,1,0:T(8,128)(2,1)} %get-tuple-element.82.qf, bf16[2048,256]{1,0:T(8,128)(2,1)} %get-tuple-element.66.kx, ...), custom_call_target="tpu_custom_call" | custom-call | flops 17999998976 | bytes 1024 | tf_op jit(solution)/shard_map/attend_back/pallas_call | solution.py:562
  147.7 10.5 %result.1 = bf16[2048,512]{1,0:T(8,128)(2,1)} custom-call(s32[1]{0:T(128)} %bitcast.me, bf16[2048,2048]{1,0:T(8,128)(2,1)} %get-tuple-element.78.act, f32[2048,512]{1,0:T(8,128)} %get-tuple-element.79.x1, f32[32,512]{1,0:T(8,128)} %get-tuple-element.73.vec, bf16[16,16,2048]{2,1,0:T(8,128)(2,1)} %copy-done.4, bf16[16,16,2048]{2,1,0:T(8,128)(2,1)} %copy-done.8, ...), custom_call_target="tpu_custom_call" | custom-call | flops 6000000000 | bytes 1024 | tf_op jit(solution)/shard_map/result/pallas_call | solution.py:562
  158.2 2.3 %collective-permute-done.17 = bf16[8,16,2048]{2,1,0:T(8,128)(2,1)S(1)} collective-permute-done((bf16[8,16,2048]{2,1,0:T(8,128)(2,1)S(1)}, bf16[8,16,2048]{2,1,0:T(8,128)(2,1)S(1)}, u32[]{:S(2)}, u32[]{:S(2)}) %collective-permute-start.17) | collective-permute-done | bytes 524320 | tf_op jit(solution)/shard_map/ppermute | solution.py:471
  164.1 6.3 %sums.1 = (bf16[16,16,768]{2,1,0:T(8,128)(2,1)}, bf16[16,16,768]{2,1,0:T(8,128)(2,1)}) custom-call(s32[1]{0:T(128)} %bitcast.me, bf16[2048,512]{1,0:T(8,128)(2,1)} %get-tuple-element.97.hid, bf16[2048,512]{1,0:T(8,128)(2,1)} %get-tuple-element.85.dq, bf16[2048,128]{1,0:T(8,128)(2,1)} %get-tuple-element.95.kv, bf16[2048,128]{1,0:T(8,128)(2,1)} %get-tuple-element.96.ds, ...), custom_call_target="tpu_custom_call" | custom-call | flops 6000000000 | bytes 1024 | tf_op jit(solution)/shard_map/sums/pallas_call | solution.py:562
  170.6 8.4 %close.1 = bf16[2048,512]{1,0:T(8,128)(2,1)} custom-call(s32[1]{0:T(128)} %bitcast.me, f32[2048,512]{1,0:T(8,128)} %get-tuple-element.81.dx1, bf16[2048,512]{1,0:T(8,128)(2,1)} %get-tuple-element.85.dq, bf16[2048,128]{1,0:T(8,128)(2,1)} %get-tuple-element.95.kv, bf16[2048,128]{1,0:T(8,128)(2,1)} %get-tuple-element.96.ds, bf16[2048,512]{1,0:T(8,128)(2,1)} %tok.5, ...), custom_call_target="tpu_custom_call" | custom-call | flops 6000000000 | bytes 1024 | tf_op jit(solution)/shard_map/close/pallas_call | solution.py:562
  179.1 2.9 %collective-permute-start.27 = (bf16[2,16,2048]{2,1,0:T(8,128)(2,1)S(1)}, bf16[2,16,2048]{2,1,0:T(8,128)(2,1)S(1)}, u32[]{:S(2)}, u32[]{:S(2)}) collective-permute-start(bf16[2,16,2048]{2,1,0:T(8,128)(2,1)S(1)} %slice.226), channel_id=1, source_target_pairs={{0,4},{1,5},{2,6},{3,7},{4,0},{5,1},{6,2},{7,3},{8,12},{9,13},{10,... | collective-permute-start | bytes 393224 | tf_op jit(solution)/shard_map/ppermute | solution.py:471
  182.2 4.1 %collective-permute-done.27 = bf16[2,16,2048]{2,1,0:T(8,128)(2,1)S(1)} collective-permute-done((bf16[2,16,2048]{2,1,0:T(8,128)(2,1)S(1)}, bf16[2,16,2048]{2,1,0:T(8,128)(2,1)S(1)}, u32[]{:S(2)}, u32[]{:S(2)}) %collective-permute-start.27) | collective-permute-done | bytes 131104 | tf_op jit(solution)/shard_map/ppermute | solution.py:471
  188.0 1.6 collective-permute-start.19
  189.6 2.5 %collective-permute-done.28 = bf16[1,16,2048]{2,1,0:T(8,128)(2,1)S(1)} collective-permute-done((bf16[1,16,2048]{2,1,0:T(8,128)(2,1)S(1)}, bf16[1,16,2048]{2,1,0:T(8,128)(2,1)S(1)}, u32[]{:S(2)}, u32[]{:S(2)}) %collective-permute-start.28) | collective-permute-done | bytes 65568 | tf_op jit(solution)/shard_map/ppermute | solution.py:471
  192.1 1.8 collective-permute-start.25
  194.0 3.6 %collective-permute-done.25 = bf16[1,16,2560]{2,1,0:T(8,128)(2,1)S(1)} collective-permute-done((bf16[1,16,2560]{2,1,0:T(8,128)(2,1)S(1)}, bf16[1,16,2560]{2,1,0:T(8,128)(2,1)S(1)}, u32[]{:S(2)}, u32[]{:S(2)}) %collective-permute-start.25) | collective-permute-done | bytes 81952 | tf_op jit(solution)/shard_map/ppermute | solution.py:471
  198.3 4.1 %collective-permute-done.20 = bf16[4,16,768]{2,1,0:T(8,128)(2,1)S(1)} collective-permute-done((bf16[4,16,768]{2,1,0:T(8,128)(2,1)S(1)}, bf16[4,16,768]{2,1,0:T(8,128)(2,1)S(1)}, u32[]{:S(2)}, u32[]{:S(2)}) %collective-permute-start.20) | collective-permute-done | bytes 98336 | tf_op jit(solution)/shard_map/ppermute | solution.py:471
  202.4 1.6 collective-permute-start.21
  204.0 2.6 %collective-permute-done.21 = bf16[2,16,768]{2,1,0:T(8,128)(2,1)S(1)} collective-permute-done((bf16[2,16,768]{2,1,0:T(8,128)(2,1)S(1)}, bf16[2,16,768]{2,1,0:T(8,128)(2,1)S(1)}, u32[]{:S(2)}, u32[]{:S(2)}) %collective-permute-start.21) | collective-permute-done | bytes 49184 | tf_op jit(solution)/shard_map/ppermute | solution.py:471
  206.7 2.0 collective-permute-start.22
  211.2 1.6 reshape.70
  (147 shorter events, 35.6 us)
Async XLA Ops:
  6.8 7.2 %collective-permute-start = (bf16[1,16,1280]{2,1,0:T(8,128)(2,1)S(1)}, bf16[1,16,1280]{2,1,0:T(8,128)(2,1)S(1)}, u32[]{:S(2)}, u32[]{:S(2)}) collective-permute-start(bf16[1,16,1280]{2,1,0:T(8,128)(2,1)S(1)} %pad_bitcast_fusion), channel_id=1, source_target_pairs={{0,8},{1,9},{2,10},{3,11},{4,12},{5,13},{6,14},{7,15},{8,0},{9,1},... | collective-permute-start | bytes 122888 | tf_op jit(solution)/shard_map/ppermute | solution.py:471
  14.1 4.5 %collective-permute-start.1 = (bf16[2,16,1280]{2,1,0:T(8,128)(2,1)S(1)}, bf16[2,16,1280]{2,1,0:T(8,128)(2,1)S(1)}, u32[]{:S(2)}, u32[]{:S(2)}) collective-permute-start(bf16[2,16,1280]{2,1,0:T(8,128)(2,1)S(1)} %pad_maximum_fusion.9), channel_id=1, source_target_pairs={{0,4},{1,5},{2,6},{3,7},{4,0},{5,1},{6,2},{7,3},{8,12},{9,13},{10,... | collective-permute-start | bytes 245768 | tf_op jit(solution)/shard_map/ppermute | solution.py:471
  15.7 8.3 %collective-permute-start.3 = (bf16[1,16,4096]{2,1,0:T(8,128)(2,1)S(1)}, bf16[1,16,4096]{2,1,0:T(8,128)(2,1)S(1)}, u32[]{:S(2)}, u32[]{:S(2)}) collective-permute-start(bf16[1,16,4096]{2,1,0:T(8,128)(2,1)S(1)} %constant_dynamic-update-slice_fusion), channel_id=1, source_target_pairs={{0,8},{1,9},{2,10},{3,11},{4,12},{5,13},{6,14},{7,15},{8,0},{9,1},... | collective-permute-start | bytes 393224 | tf_op jit(solution)/shard_map/ppermute | solution.py:471
  18.6 5.6 %collective-permute-start.2 = (bf16[4,16,1280]{2,1,0:T(8,128)(2,1)S(1)}, bf16[4,16,1280]{2,1,0:T(8,128)(2,1)S(1)}, u32[]{:S(2)}, u32[]{:S(2)}) collective-permute-start(bf16[4,16,1280]{2,1,0:T(8,128)(2,1)S(1)} %pad_maximum_fusion.6), channel_id=1, source_target_pairs={{0,2},{1,3},{2,0},{3,1},{4,6},{5,7},{6,4},{7,5},{8,10},{9,11},{10,... | collective-permute-start | bytes 491528 | tf_op jit(solution)/shard_map/ppermute | solution.py:471
  24.1 7.6 %collective-permute-start.5 = (bf16[2,16,4096]{2,1,0:T(8,128)(2,1)S(1)}, bf16[2,16,4096]{2,1,0:T(8,128)(2,1)S(1)}, u32[]{:S(2)}, u32[]{:S(2)}) collective-permute-start(bf16[2,16,4096]{2,1,0:T(8,128)(2,1)S(1)} %pad_maximum_fusion.5), channel_id=1, source_target_pairs={{0,4},{1,5},{2,6},{3,7},{4,0},{5,1},{6,2},{7,3},{8,12},{9,13},{10,... | collective-permute-start | bytes 786440 | tf_op jit(solution)/shard_map/ppermute | solution.py:471
  24.2 9.3 %collective-permute-start.4 = (bf16[8,16,1280]{2,1,0:T(8,128)(2,1)S(1)}, bf16[8,16,1280]{2,1,0:T(8,128)(2,1)S(1)}, u32[]{:S(2)}, u32[]{:S(2)}) collective-permute-start(bf16[8,16,1280]{2,1,0:T(8,128)(2,1)S(1)} %pad_maximum_fusion.4), channel_id=1, source_target_pairs={{0,16},{1,17},{2,18},{3,19},{4,20},{5,21},{6,22},{7,23},{8,24},{9,... | collective-permute-start | bytes 983048 | tf_op jit(solution)/shard_map/ppermute | solution.py:471
  31.8 7.1 %collective-permute-start.8 = (bf16[4,16,2048]{2,1,0:T(8,128)(2,1)S(1)}, bf16[4,16,2048]{2,1,0:T(8,128)(2,1)S(1)}, u32[]{:S(2)}, u32[]{:S(2)}) collective-permute-start(bf16[4,16,2048]{2,1,0:T(8,128)(2,1)S(1)} %get-tuple-element.141), channel_id=1, source_target_pairs={{0,16},{1,17},{2,18},{3,19},{4,20},{5,21},{6,22},{7,23},{8,24},{9,... | collective-permute-start | bytes 786440 | tf_op jit(solution)/shard_map/ppermute | solution.py:471
  33.6 8.9 %collective-permute-start.6 = (bf16[16,16,1280]{2,1,0:T(8,128)(2,1)S(1)}, bf16[16,16,1280]{2,1,0:T(8,128)(2,1)S(1)}, u32[]{:S(2)}, u32[]{:S(2)}) collective-permute-start(bf16[16,16,1280]{2,1,0:T(8,128)(2,1)S(1)} %constant_dynamic-update-slice_fusion.2.refs_0_), channel_id=1, source_target_pairs={{0,1},{1,0},{2,3},{3,2},{4,5},{5,4},{6,7},{7,6},{8,9},{9,8},{10,11... | collective-permute-start | bytes 1966088 | tf_op jit(solution)/shard_map/ppermute | solution.py:471
  33.7 8.7 %collective-permute-start.7 = (bf16[4,16,2048]{2,1,0:T(8,128)(2,1)S(1)}, bf16[4,16,2048]{2,1,0:T(8,128)(2,1)S(1)}, u32[]{:S(2)}, u32[]{:S(2)}) collective-permute-start(bf16[4,16,2048]{2,1,0:T(8,128)(2,1)S(1)} %get-tuple-element.142), channel_id=1, source_target_pairs={{0,2},{1,3},{2,0},{3,1},{4,6},{5,7},{6,4},{7,5},{8,10},{9,11},{10,... | collective-permute-start | bytes 786440 | tf_op jit(solution)/shard_map/ppermute | solution.py:471
  53.0 14.9 %collective-permute-start.9 = (bf16[8,16,2048]{2,1,0:T(8,128)(2,1)S(1)}, bf16[8,16,2048]{2,1,0:T(8,128)(2,1)S(1)}, u32[]{:S(2)}, u32[]{:S(2)}) collective-permute-start(bf16[8,16,2048]{2,1,0:T(8,128)(2,1)S(1)} %pad_maximum_fusion.2), channel_id=1, source_target_pairs={{0,16},{1,17},{2,18},{3,19},{4,20},{5,21},{6,22},{7,23},{8,24},{9,... | collective-permute-start | bytes 1572872 | tf_op jit(solution)/shard_map/ppermute | solution.py:471
  54.6 13.2 %collective-permute-start.10 = (bf16[8,16,2048]{2,1,0:T(8,128)(2,1)S(1)}, bf16[8,16,2048]{2,1,0:T(8,128)(2,1)S(1)}, u32[]{:S(2)}, u32[]{:S(2)}) collective-permute-start(bf16[8,16,2048]{2,1,0:T(8,128)(2,1)S(1)} %pad_maximum_fusion.3), channel_id=1, source_target_pairs={{0,2},{1,3},{2,0},{3,1},{4,6},{5,7},{6,4},{7,5},{8,10},{9,11},{10,... | collective-permute-start | bytes 1572872 | tf_op jit(solution)/shard_map/ppermute | solution.py:471
  67.9 8.0 %collective-permute-start.11 = (bf16[16,16,2048]{2,1,0:T(8,128)(2,1)S(1)}, bf16[16,16,2048]{2,1,0:T(8,128)(2,1)S(1)}, u32[]{:S(2)}, u32[]{:S(2)}) collective-permute-start(bf16[16,16,2048]{2,1,0:T(8,128)(2,1)S(1)} %constant_dynamic-update-slice_fusion.4.refs_0_.refs_2_), channel_id=1, source_target_pairs={{0,1},{1,0},{2,3},{3,2},{4,5},{5,4},{6,7},{7,6},{8,9},{9,8},{10,11... | collective-permute-start | bytes 3145736 | tf_op jit(solution)/shard_map/ppermute | solution.py:471
  68.0 7.9 %collective-permute-start.12 = (bf16[16,16,2048]{2,1,0:T(8,128)(2,1)S(1)}, bf16[16,16,2048]{2,1,0:T(8,128)(2,1)S(1)}, u32[]{:S(2)}, u32[]{:S(2)}) collective-permute-start(bf16[16,16,2048]{2,1,0:T(8,128)(2,1)S(1)} %constant_dynamic-update-slice_fusion.6.refs_2_.refs_4_), channel_id=1, source_target_pairs={{0,1},{1,0},{2,3},{3,2},{4,5},{5,4},{6,7},{7,6},{8,9},{9,8},{10,11... | collective-permute-start | bytes 3145736 | tf_op jit(solution)/shard_map/ppermute | solution.py:471
  109.8 19.9 %copy-start.11 = (bf16[16,16,2048]{2,1,0:T(8,128)(2,1)S(1)}, bf16[16,16,2048]{2,1,0:T(8,128)(2,1)}, u32[]{:S(2)}) copy-start(bf16[16,16,2048]{2,1,0:T(8,128)(2,1)} %get-tuple-element.88) | copy-start | bytes 3145732
  109.8 20.4 %copy-start.10 = (bf16[16,16,2048]{2,1,0:T(8,128)(2,1)S(1)}, bf16[16,16,2048]{2,1,0:T(8,128)(2,1)}, u32[]{:S(2)}) copy-start(bf16[16,16,2048]{2,1,0:T(8,128)(2,1)} %get-tuple-element.93) | copy-start | bytes 3145732
  129.6 14.4 %collective-permute-start.14 = (bf16[16,16,512]{2,1,0:T(8,128)(2,1)}, bf16[16,16,512]{2,1,0:T(8,128)(2,1)S(1)}, u32[]{:S(2)}, u32[]{:S(2)}) collective-permute-start(bf16[16,16,512]{2,1,0:T(8,128)(2,1)} %get-tuple-element.90), channel_id=1, source_target_pairs={{0,1},{1,0},{2,3},{3,2},{4,5},{5,4},{6,7},{7,6},{8,9},{9,8},{10,11... | collective-permute-start | bytes 786440 | tf_op jit(solution)/shard_map/ppermute | solution.py:471
  129.7 14.4 %collective-permute-start.13 = (bf16[16,16,2048]{2,1,0:T(8,128)(2,1)S(1)}, bf16[16,16,2048]{2,1,0:T(8,128)(2,1)S(1)}, u32[]{:S(2)}, u32[]{:S(2)}) collective-permute-start(bf16[16,16,2048]{2,1,0:T(8,128)(2,1)S(1)} %copy-done.11), channel_id=1, source_target_pairs={{0,1},{1,0},{2,3},{3,2},{4,5},{5,4},{6,7},{7,6},{8,9},{9,8},{10,11... | collective-permute-start | bytes 3145736 | tf_op jit(solution)/shard_map/ppermute | solution.py:471
  130.2 15.1 %collective-permute-start.16 = (bf16[16,16,2048]{2,1,0:T(8,128)(2,1)S(1)}, bf16[16,16,2048]{2,1,0:T(8,128)(2,1)S(1)}, u32[]{:S(2)}, u32[]{:S(2)}) collective-permute-start(bf16[16,16,2048]{2,1,0:T(8,128)(2,1)S(1)} %copy-done.10), channel_id=1, source_target_pairs={{0,1},{1,0},{2,3},{3,2},{4,5},{5,4},{6,7},{7,6},{8,9},{9,8},{10,11... | collective-permute-start | bytes 3145736 | tf_op jit(solution)/shard_map/ppermute | solution.py:471
  130.3 13.8 %copy-start.1 = (bf16[16,16,2048]{2,1,0:T(8,128)(2,1)S(1)}, bf16[16,16,2048]{2,1,0:T(8,128)(2,1)}, u32[]{:S(2)}) copy-start(bf16[16,16,2048]{2,1,0:T(8,128)(2,1)} %get-tuple-element.87) | copy-start | bytes 3145732
  144.7 17.1 %collective-permute-start.15 = (bf16[8,16,2560]{2,1,0:T(8,128)(2,1)S(1)}, bf16[8,16,2560]{2,1,0:T(8,128)(2,1)S(1)}, u32[]{:S(2)}, u32[]{:S(2)}) collective-permute-start(bf16[8,16,2560]{2,1,0:T(8,128)(2,1)S(1)} %slice.156), channel_id=1, source_target_pairs={{0,16},{1,17},{2,18},{3,19},{4,20},{5,21},{6,22},{7,23},{8,24},{9,... | collective-permute-start | bytes 1966088 | tf_op jit(solution)/shard_map/ppermute | solution.py:471
  146.2 14.3 %collective-permute-start.17 = (bf16[8,16,2048]{2,1,0:T(8,128)(2,1)S(1)}, bf16[8,16,2048]{2,1,0:T(8,128)(2,1)S(1)}, u32[]{:S(2)}, u32[]{:S(2)}) collective-permute-start(bf16[8,16,2048]{2,1,0:T(8,128)(2,1)S(1)} %slice.158), channel_id=1, source_target_pairs={{0,2},{1,3},{2,0},{3,1},{4,6},{5,7},{6,4},{7,5},{8,10},{9,11},{10,... | collective-permute-start | bytes 1572872 | tf_op jit(solution)/shard_map/ppermute | solution.py:471
  162.0 17.0 %collective-permute-start.26 = (bf16[4,16,2048]{2,1,0:T(8,128)(2,1)S(1)}, bf16[4,16,2048]{2,1,0:T(8,128)(2,1)S(1)}, u32[]{:S(2)}, u32[]{:S(2)}) collective-permute-start(bf16[4,16,2048]{2,1,0:T(8,128)(2,1)S(1)} %slice.185), channel_id=1, source_target_pairs={{0,16},{1,17},{2,18},{3,19},{4,20},{5,21},{6,22},{7,23},{8,24},{9,... | collective-permute-start | bytes 786440 | tf_op jit(solution)/shard_map/ppermute | solution.py:471
  162.6 19.4 %collective-permute-start.23 = (bf16[4,16,2560]{2,1,0:T(8,128)(2,1)S(1)}, bf16[4,16,2560]{2,1,0:T(8,128)(2,1)S(1)}, u32[]{:S(2)}, u32[]{:S(2)}) collective-permute-start(bf16[4,16,2560]{2,1,0:T(8,128)(2,1)S(1)} %slice.173), channel_id=1, source_target_pairs={{0,2},{1,3},{2,0},{3,1},{4,6},{5,7},{6,4},{7,5},{8,10},{9,11},{10,... | collective-permute-start | bytes 983048 | tf_op jit(solution)/shard_map/ppermute | solution.py:471
  170.5 17.4 %collective-permute-start.18 = (bf16[16,16,768]{2,1,0:T(8,128)(2,1)}, bf16[16,16,768]{2,1,0:T(8,128)(2,1)S(1)}, u32[]{:S(2)}, u32[]{:S(2)}) collective-permute-start(bf16[16,16,768]{2,1,0:T(8,128)(2,1)} %get-tuple-element.101), channel_id=1, source_target_pairs={{0,1},{1,0},{2,3},{3,2},{4,5},{5,4},{6,7},{7,6},{8,9},{9,8},{10,11... | collective-permute-start | bytes 1179656 | tf_op jit(solution)/shard_map/ppermute | solution.py:471
  179.1 7.3 %collective-permute-start.27 = (bf16[2,16,2048]{2,1,0:T(8,128)(2,1)S(1)}, bf16[2,16,2048]{2,1,0:T(8,128)(2,1)S(1)}, u32[]{:S(2)}, u32[]{:S(2)}) collective-permute-start(bf16[2,16,2048]{2,1,0:T(8,128)(2,1)S(1)} %slice.226), channel_id=1, source_target_pairs={{0,4},{1,5},{2,6},{3,7},{4,0},{5,1},{6,2},{7,3},{8,12},{9,13},{10,... | collective-permute-start | bytes 393224 | tf_op jit(solution)/shard_map/ppermute | solution.py:471
  182.1 9.9 %collective-permute-start.24 = (bf16[2,16,2560]{2,1,0:T(8,128)(2,1)S(1)}, bf16[2,16,2560]{2,1,0:T(8,128)(2,1)S(1)}, u32[]{:S(2)}, u32[]{:S(2)}) collective-permute-start(bf16[2,16,2560]{2,1,0:T(8,128)(2,1)S(1)} %slice.216), channel_id=1, source_target_pairs={{0,4},{1,5},{2,6},{3,7},{4,0},{5,1},{6,2},{7,3},{8,12},{9,13},{10,... | collective-permute-start | bytes 491528 | tf_op jit(solution)/shard_map/ppermute | solution.py:471
  186.4 5.6 %collective-permute-start.28 = (bf16[1,16,2048]{2,1,0:T(8,128)(2,1)S(1)}, bf16[1,16,2048]{2,1,0:T(8,128)(2,1)S(1)}, u32[]{:S(2)}, u32[]{:S(2)}) collective-permute-start(bf16[1,16,2048]{2,1,0:T(8,128)(2,1)S(1)} %slice.228), channel_id=1, source_target_pairs={{0,8},{1,9},{2,10},{3,11},{4,12},{5,13},{6,14},{7,15},{8,0},{9,1},... | collective-permute-start | bytes 196616 | tf_op jit(solution)/shard_map/ppermute | solution.py:471
  188.0 9.6 %collective-permute-start.19 = (bf16[8,16,768]{2,1,0:T(8,128)(2,1)S(1)}, bf16[8,16,768]{2,1,0:T(8,128)(2,1)S(1)}, u32[]{:S(2)}, u32[]{:S(2)}) collective-permute-start(bf16[8,16,768]{2,1,0:T(8,128)(2,1)S(1)} %slice.203), channel_id=1, source_target_pairs={{0,16},{1,17},{2,18},{3,19},{4,20},{5,21},{6,22},{7,23},{8,24},{9,... | collective-permute-start | bytes 589832 | tf_op jit(solution)/shard_map/ppermute | solution.py:471
  192.1 5.4 %collective-permute-start.25 = (bf16[1,16,2560]{2,1,0:T(8,128)(2,1)S(1)}, bf16[1,16,2560]{2,1,0:T(8,128)(2,1)S(1)}, u32[]{:S(2)}, u32[]{:S(2)}) collective-permute-start(bf16[1,16,2560]{2,1,0:T(8,128)(2,1)S(1)} %slice.218), channel_id=1, source_target_pairs={{0,8},{1,9},{2,10},{3,11},{4,12},{5,13},{6,14},{7,15},{8,0},{9,1},... | collective-permute-start | bytes 245768 | tf_op jit(solution)/shard_map/ppermute | solution.py:471
  197.7 4.7 %collective-permute-start.20 = (bf16[4,16,768]{2,1,0:T(8,128)(2,1)S(1)}, bf16[4,16,768]{2,1,0:T(8,128)(2,1)S(1)}, u32[]{:S(2)}, u32[]{:S(2)}) collective-permute-start(bf16[4,16,768]{2,1,0:T(8,128)(2,1)S(1)} %slice.205), channel_id=1, source_target_pairs={{0,2},{1,3},{2,0},{3,1},{4,6},{5,7},{6,4},{7,5},{8,10},{9,11},{10,... | collective-permute-start | bytes 294920 | tf_op jit(solution)/shard_map/ppermute | solution.py:471
  202.4 4.3 %collective-permute-start.21 = (bf16[2,16,768]{2,1,0:T(8,128)(2,1)S(1)}, bf16[2,16,768]{2,1,0:T(8,128)(2,1)S(1)}, u32[]{:S(2)}, u32[]{:S(2)}) collective-permute-start(bf16[2,16,768]{2,1,0:T(8,128)(2,1)S(1)} %slice.207), channel_id=1, source_target_pairs={{0,4},{1,5},{2,6},{3,7},{4,0},{5,1},{6,2},{7,3},{8,12},{9,13},{10,... | collective-permute-start | bytes 147464 | tf_op jit(solution)/shard_map/ppermute | solution.py:471
  206.7 6.1 %collective-permute-start.22 = (bf16[1,16,768]{2,1,0:T(8,128)(2,1)S(1)}, bf16[1,16,768]{2,1,0:T(8,128)(2,1)S(1)}, u32[]{:S(2)}, u32[]{:S(2)}) collective-permute-start(bf16[1,16,768]{2,1,0:T(8,128)(2,1)S(1)} %slice.209), channel_id=1, source_target_pairs={{0,8},{1,9},{2,10},{3,11},{4,12},{5,13},{6,14},{7,15},{8,0},{9,1},... | collective-permute-start | bytes 73736 | tf_op jit(solution)/shard_map/ppermute | solution.py:471
  (10 other events, 63.0 us)

commit v3 on v2

v3 whole, which is shorter than its diff:
```python
import functools

import jax
import jax.numpy as jnp
from jax import lax
from jax.experimental import pallas as pl
from jax.experimental.pallas import tpu as pltpu
from jax.sharding import PartitionSpec as P

AXES = ("dp", "fsdp")
F32 = jnp.float32
BF = jnp.bfloat16
FAR = -1e30
LANES = 128
G1, B1, G2, B2, BD, BU, LOAD = 8, 9, 10, 11, 12, 13, 17
TILE = 256
STEP = 512
ROOM = {
    "project": 16, "attend": 20, "mix": 14, "feed": 32, "turn": 28, "gates": 16, "attend_back": 32, "sums": 18, "close": 18,
    "result": 22,
}


def nn(left, right):
    return jnp.dot(left, right, preferred_element_type=F32)


def nt(left, right):
    return lax.dot_general(left, right, (((1,), (1,)), ((), ())), preferred_element_type=F32)


def iota(shape, dim):
    return lax.broadcasted_iota(jnp.int32, shape, dim)


def normed(value):
    center = value - jnp.mean(value, -1, keepdims=True)
    inv = lax.rsqrt(jnp.mean(center * center, -1, keepdims=True) + 1e-05)
    return center * inv, inv


def fetch(core, pieces, parts, sem):
    for other, piece in enumerate(pieces):
        own = jnp.bitwise_xor(core, other)
        for start, wide, dst in parts:
            blocks, block, _ = piece.shape
            view = dst.reshape(blocks, len(pieces), block, wide)
            pltpu.make_async_copy(piece.at[:, :, start : start + wide], view.at[:, own], sem).start()


def arrive(dst, sem):
    pltpu.make_async_copy(dst, dst, sem).wait()


def scatter(core, pieces, src, sem):
    for other, piece in enumerate(pieces):
        own = jnp.bitwise_xor(core, other)
        blocks, block, wide = piece.shape
        view = src.reshape(blocks, len(pieces), block, wide)
        pltpu.make_async_copy(view.at[:, own], piece, sem).start()


def ffn_parts(wu, wd, half, depth, up, down):
    parts = []
    if up:
        parts.append((0, 2 * depth, wu.at[half]))
    if down:
        parts += [((2 + j) * depth, depth, wd.at[pl.ds((2 * half + j) * depth, depth), :]) for j in range(2)]
    return parts


def pack_kernel(wq, wo, wk, wv, wr, g1, b1, g2, b2, bd, bu, o):
    share, depth = wq.shape
    head, experts = wk.shape[1], wr.shape[1]
    same = iota((share, share), 0) == iota((share, share), 1)
    lane = iota((share, LANES), 1)

    def column(v):
        return jnp.sum(jnp.where(same, jnp.broadcast_to(v.astype(F32), (share, share)), 0.0), 1, keepdims=True)

    out = jnp.zeros((share, LANES), F32)
    for at, v in zip((G1, B1, G2, B2, BD), (g1, b1, g2, b2, bd)):
        out = jnp.where(lane == at, column(v[...].reshape(1, share)), out)
    flat = bu[...].reshape(1, bu.shape[0])
    for j in range(bu.shape[0] // share):
        out = jnp.where(lane == BU + j, column(flat[:, j * share : (j + 1) * share]), out)
    o[:, 0:depth] = wq[...]
    o[:, depth : depth + head] = wk[...]
    o[:, depth + head : depth + LANES] = wv[...]
    o[:, depth + LANES : depth + 2 * LANES] = out.astype(BF)
    o[:, depth + LANES : depth + LANES + experts] = wr[...]
    o[:, depth + 2 * LANES :] = wo[...]


def split3(value):
    high = value.astype(BF).astype(F32)
    rest = value - high
    mid = rest.astype(BF).astype(F32)
    return high, mid, rest - mid


def three(lane, value):
    high, mid, rest = split3(value)
    return jnp.where(lane == 4, -high, jnp.where(lane == 5, -mid, jnp.where(lane == 6, -rest, 0.0)))


def segment_of(lens, row, start, rows):
    place = iota((rows, LANES), 0) + start
    end = lens[row, 0]
    seg = (place >= end).astype(jnp.int32)
    for j in range(1, lens.shape[1]):
        end = end + lens[row, j]
        seg = seg + (place >= end).astype(jnp.int32)
    return seg


def pick(routes, rows, slot):
    return jnp.broadcast_to(routes[rows, slot : slot + 1], (TILE, LANES))


def chosen(wide, expert, half):
    out = jnp.zeros(expert.shape, F32)
    for j in range(wide.shape[1] // LANES):
        out = jnp.where(expert == 2 * j + half, wide[:, j * LANES : (j + 1) * LANES], out)
    return out


def project_kernel(n, length, segs, experts, me, lens, tok, routes, *refs):
    hid_o, qa_o, kx_o, vx_o, pr_o, vec_o, w, vec, sem = refs[n:]
    span, depth = tok.shape
    step = pl.program_id(0)
    row = lax.div(step * span, length)
    begin = lax.rem(step * span, length)

    @pl.when(step == 0)
    def _():
        fetch(me[0], refs[:n], [(0, depth + 2 * LANES, w)], sem)
        arrive(w, sem)
        vec[...] = w[:, depth + LANES :].astype(F32).T
        vec_o[...] = vec[0:32, :]

    lane = iota((TILE, LANES), 1)
    half = lane // 64
    low = lane < 64
    for c in range(span // TILE):
        rows = slice(c * TILE, (c + 1) * TILE)
        unit, _ = normed(tok[rows, :].astype(F32))
        hid = (unit * vec[G1 : G1 + 1, :] + vec[B1 : B1 + 1, :]).astype(BF)
        hid_o[rows, :] = hid
        query = nn(hid, w[:, 0:depth])
        small = nn(hid, w[:, depth:])
        kv = small[:, :LANES].astype(BF).astype(F32)
        swap = pltpu.roll(kv, 64, 1)
        seg = segment_of(lens, row, begin + c * TILE, TILE)
        same = jnp.where(lane == seg, 1.0, 0.0)
        kx_o[rows, 0:LANES] = jnp.where(low, kv, swap).astype(BF)
        kx_o[rows, LANES:] = jnp.where(lane < segs, same, jnp.where(lane < 8, 1.0, 0.0)).astype(BF)
        vx_o[rows, 0:LANES] = jnp.where(low, swap, kv).astype(BF)
        vx_o[rows, LANES:] = jnp.ones((TILE, LANES), BF)
        logits = jnp.where(lane < experts, small[:, LANES:], FAR)
        raised = jnp.exp(logits - jnp.max(logits, -1, keepdims=True))
        pr_o[rows, :] = raised / jnp.sum(raised, -1, keepdims=True)
        for slot in range(2):
            qa_o[slot, rows, :] = (chosen(query, pick(routes, rows, slot), half) * 0.125).astype(BF)


def attend_kernel(segs, lens, routes, qa, kx, vx, pr, o_o, u_o, qf_o):
    span, depth = u_o.shape
    row, step = pl.program_id(0), pl.program_id(1)
    lane = iota((TILE, LANES), 1)
    half = lane // 64
    low = lane < 64
    for c in range(span // TILE):
        rows = slice(c * TILE, (c + 1) * TILE)
        seg = segment_of(lens, row, step * span + c * TILE, TILE)
        apart = jnp.where((lane < segs) & (lane != seg), FAR, 0.0)
        probs = pr[rows, :]
        seen, gated, experts_of = [], [], []
        for slot in range(2):
            expert = pick(routes, rows, slot)
            scores = nt(jnp.concatenate([qa[slot, rows, :], apart.astype(BF)], 1), kx[...])
            top = jnp.max(scores, -1, keepdims=True)
            raised = jnp.exp(scores - top).astype(BF)
            both = nn(raised, vx[...])
            mass = both[:, LANES:]
            out = both[:, :LANES] / mass
            qf_o[slot, rows, :] = (apart + three(lane, top + jnp.log(mass))).astype(BF)
            gate = jnp.sum(jnp.where(lane == expert, probs, 0.0), -1, keepdims=True)
            seen.append(out)
            gated.append(out * gate)
            experts_of.append(expert)
        o_o[rows, :] = jnp.where(low, seen[0], seen[1])
        for j in range(depth // LANES):
            part = jnp.where(experts_of[0] == 2 * j + half, gated[0], jnp.where(experts_of[1] == 2 * j + half, gated[1], 0.0))
            u_o[rows, j * LANES : (j + 1) * LANES] = part.astype(BF)


def mix_kernel(n, me, tok, u, vec, *refs):
    x1_o, h2_o, w, sem = refs[n:]
    span, depth = tok.shape

    @pl.when(pl.program_id(0) == 0)
    def _():
        fetch(me[0], refs[:n], [(depth + 2 * LANES, depth, w)], sem)
        arrive(w, sem)

    for c in range(span // TILE):
        rows = slice(c * TILE, (c + 1) * TILE)
        after = tok[rows, :].astype(F32) + nn(u[rows, :], w[...])
        x1_o[rows, :] = after
        unit, _ = normed(after)
        h2_o[rows, :] = (unit * vec[G2 : G2 + 1, :] + vec[B2 : B2 + 1, :]).astype(BF)


def ffn_kernel(n, me, h2, dy, vec, *refs):
    pieces = [refs[:n], refs[n : 2 * n]]
    act_o, dz_o, bias_o = refs[2 * n : 2 * n + 3]
    grads = [refs[2 * n + 3 : 3 * n + 3], refs[3 * n + 3 : 4 * n + 3]]
    wu, wd, ht, yt, acts, dzs, out, sem, out_sem = refs[4 * n + 3 :]
    step = pl.program_id(0)
    steps = pl.num_programs(0) - 1
    total, wide = act_o.shape
    depth = h2.shape[1]
    per = depth // wide
    some = wu.shape[2]

    @pl.when(step == 0)
    def _():
        for half in range(2):
            fetch(me[0], pieces[half], ffn_parts(wu, wd, half, depth, True, True), sem.at[half])
        for t in range(0, total, STEP):
            ht[0:depth, t : t + STEP] = h2[t : t + STEP, :].T
            yt[:, t : t + STEP] = dy[t : t + STEP, :].T
        ht[depth:, :] = jnp.ones((16, total), BF)

    for half in range(2):
        @pl.when(step == half * steps // 2)
        def _():
            arrive(wu.at[half], sem.at[half])
            arrive(wd.at[pl.ds(half * some, some), :], sem.at[half])

    one = 0.7978845608028654
    two = one * 0.044715
    cur = lax.rem(step, 2)

    def place(t):
        sub = lax.div(t, per)
        return sub, lax.rem(t, per), lax.rem(sub, 2) * depth, lax.div(sub, 2)

    def grad_up(t, slot):
        sub, part, column, half = place(t)
        up = nn(ht[...], dzs[slot])
        out[half, :, pl.ds(pl.multiple_of(column + part * wide, wide), wide)] = up[0:depth, :].astype(BF)
        bias_o[pl.ds(sub, 1), pl.ds(pl.multiple_of(part * wide, wide), wide)] = up[depth : depth + 1, :]

    def grad_down(t, slot):
        _, part, column, half = place(t)
        rows = pl.ds(pl.multiple_of(part * wide, wide), wide)
        out[half, rows, pl.ds(pl.multiple_of(column + 2 * depth, depth), depth)] = nn(yt[...], acts[slot]).T.astype(BF)

    @pl.when(step < steps)
    def _():
        before = jnp.maximum(step - 1, 0)
        sub, part, column, which = place(step)
        here = pl.ds(pl.multiple_of(step * wide, wide), wide)
        across = pl.ds(pl.multiple_of(column + part * wide, wide), wide)
        bias = vec[pl.ds(BU + sub, 1), pl.ds(pl.multiple_of(part * wide, wide), wide)]
        count = total // TILE
        for c in range(count):
            rows = slice(c * TILE, (c + 1) * TILE)
            z = nn(h2[rows, :], wu[which, :, across]) + bias
            dact = nt(dy[rows, :], wd[here, :])
            if c == 0:
                grad_up(before, 1 - cur)
            if c == count // 2:
                grad_down(before, 1 - cur)
            square = z * z
            tanh = jnp.tanh(z * (one + two * square))
            half = 0.5 * tanh + 0.5
            act = z * half
            slope = half + act * (1.0 - tanh) * (one + 3.0 * two * square)
            act = act.astype(BF)
            dz = (dact * slope).astype(BF)
            act_o[rows, :] = act
            dz_o[rows, :] = dz
            acts[cur, rows, :] = act
            dzs[cur, rows, :] = dz

    @pl.when(step == steps // 2)
    def _():
        scatter(me[0], grads[0], out.at[0], out_sem)

    @pl.when(step == steps)
    def _():
        grad_up(steps - 1, 1 - cur)
        grad_down(steps - 1, 1 - cur)
        scatter(me[0], grads[1], out.at[1], out_sem)
        arrive(out, out_sem)


def turn_kernel(n, me, dz, dy, x1, vec, *refs):
    dx1_o, low_o, sums_o, wu, f_sem = refs[2 * n :]
    span, depth = dy.shape
    step = pl.program_id(0)

    @pl.when(step == 0)
    def _():
        for half in range(2):
            fetch(me[0], refs[half * n : half * n + n], ffn_parts(wu, None, half, depth, True, False), f_sem)
        sums_o[...] = jnp.zeros_like(sums_o)
        arrive(wu, f_sem)

    for c in range(span // TILE):
        rows = slice(c * TILE, (c + 1) * TILE)
        dh2 = nt(dz[rows, 0 : 2 * depth], wu[0]) + nt(dz[rows, 2 * depth :], wu[1])
        unit, inv = normed(x1[rows, :])
        grad = dy[rows, :].astype(F32)
        sums_o[G2 : G2 + 1, :] += jnp.sum(dh2 * unit, 0, keepdims=True)
        sums_o[B2 : B2 + 1, :] += jnp.sum(dh2, 0, keepdims=True)
        sums_o[BD : BD + 1, :] += jnp.sum(grad, 0, keepdims=True)
        scaled = dh2 * vec[G2 : G2 + 1, :]
        one = jnp.mean(scaled, -1, keepdims=True)
        two = jnp.mean(scaled * unit, -1, keepdims=True)
        dx1 = grad + inv * (scaled - one - unit * two)
        dx1_o[rows, :] = dx1
        low_o[rows, :] = dx1.astype(BF)


def gates_kernel(n, me, dx1, routes, pr, o, u, *refs):
    da_o, df_o, ds_o, load_o, go_o, w, go, sem = refs[n:]
    span, depth = dx1.shape
    step = pl.program_id(0)

    @pl.when(step == 0)
    def _():
        fetch(me[0], refs[:n], [(depth + 2 * LANES, depth, w)], sem)
        go[...] = jnp.zeros_like(go)
        load_o[...] = jnp.zeros_like(load_o)
        arrive(w, sem)

    lane = iota((TILE, LANES), 1)
    half = lane // 64
    low = lane < 64
    go[...] += nn(u[...].T, dx1[...])
    for c in range(span // TILE):
        rows = slice(c * TILE, (c + 1) * TILE)
        du = nt(dx1[rows, :], w[...]).astype(BF).astype(F32)
        probs = pr[rows, :]
        heads = o[rows, :]
        swap = pltpu.roll(heads, 64, 1)
        dprobs = jnp.zeros((TILE, LANES), F32)
        loads = jnp.zeros((TILE, LANES), F32)
        for slot in range(2):
            expert = pick(routes, rows, slot)
            own = chosen(du, expert, half)
            here = lane == expert
            gate = jnp.sum(jnp.where(here, probs, 0.0), -1, keepdims=True)
            seen = jnp.where(low, heads, swap) if slot == 0 else jnp.where(low, swap, heads)
            dgate = jnp.sum(own * seen, -1, keepdims=True)
            da = (own * gate).astype(BF)
            da_o[slot, rows, :] = da
            df_o[slot, rows, :] = three(lane, jnp.sum(da.astype(F32) * seen, -1, keepdims=True)).astype(BF)
            dprobs = jnp.where(here, dgate, dprobs)
            loads = jnp.where(here, 1.0, loads)
        load_o[0:1, :] += jnp.sum(loads, 0, keepdims=True)
        inner = jnp.sum(dprobs * probs, -1, keepdims=True)
        ds_o[rows, :] = (probs * (dprobs - inner)).astype(BF)

    @pl.when(step == pl.num_programs(0) - 1)
    def _():
        go_o[...] = go[...].astype(BF)


def attend_back_kernel(routes, qa, qf, kx, vx, da, df, dq_o, kv_o, dk, dv, ds, ps):
    span, depth = dq_o.shape
    step = pl.program_id(1)
    lane = iota((TILE, LANES), 1)
    half = lane // 64

    for slot in range(2):
        own = slice(slot * span, (slot + 1) * span)
        probs = jnp.exp(nt(jnp.concatenate([qa[slot], qf[slot]], 1), kx[...]))
        ps[own, :] = probs.astype(BF)
        away = nt(jnp.concatenate([da[slot], df[slot]], 1), vx[...])
        ds[own, :] = (probs * away).astype(BF)
    dk_part = nn(jnp.concatenate([qa[0].T, qa[1].T], 1), ds[...])
    dv_part = nn(jnp.concatenate([da[0].T, da[1].T], 1), ps[...])
    found = nn(ds[...], kx[:, 0:LANES]) * 0.125
    for c in range(span // TILE):
        rows = slice(c * TILE, (c + 1) * TILE)
        others = slice(span + c * TILE, span + (c + 1) * TILE)
        one, two = pick(routes, rows, 0), pick(routes, rows, 1)
        for j in range(depth // LANES):
            part = jnp.where(one == 2 * j + half, found[rows, :], jnp.where(two == 2 * j + half, found[others, :], 0.0))
            dq_o[rows, j * LANES : (j + 1) * LANES] = part.astype(BF)

    @pl.when(step == 0)
    def _():
        dk[...] = dk_part
        dv[...] = dv_part

    @pl.when(step > 0)
    def _():
        dk[...] += dk_part
        dv[...] += dv_part

    @pl.when(step == pl.num_programs(1) - 1)
    def _():
        for c in range(kv_o.shape[0] // TILE):
            rows = slice(c * TILE, (c + 1) * TILE)
            both = jnp.concatenate([dk[0:64, rows] + dk[64:, rows], dv[0:64, rows] + dv[64:, rows]], 0)
            kv_o[rows, :] = both.T.astype(BF)


def sum_kernel(n, block, experts, me, hid, dq, kv, ds, sums, bias, loads, go, *refs):
    w, gq, gs, all_sums, out, sem, out_sem = refs[2 * n :]
    span, depth = hid.shape
    step = pl.program_id(0)

    @pl.when(step == 0)
    def _():
        fetch(me[0], refs[:n], [(0, depth + 2 * LANES, w)], sem)
        gq[...] = jnp.zeros_like(gq)
        gs[...] = jnp.zeros_like(gs)

    turned = jnp.concatenate([hid[...].T, jnp.ones((16, span), BF)], 0)
    gq[...] += nn(turned, dq[...])
    gs[...] += nn(turned, jnp.concatenate([kv[...], ds[...]], 1))

    @pl.when(step == pl.num_programs(0) - 1)
    def _():
        arrive(w, sem)
        all_sums[...] = jnp.zeros_like(all_sums)
        all_sums[0:32, :] = sums[...]
        all_sums[BU : BU + 4, :] = bias[0:4, :]
        wq = w[:, 0:depth].astype(F32)
        ws = w[:, depth:].astype(F32)
        wide = iota((depth, LANES), 1)
        ws_own = jnp.where(wide < experts, ws[:, LANES:], 0.0)
        around = jnp.sum(gq[0:depth, :] * wq, -1, keepdims=True)
        around += jnp.sum(gs[0:depth, 0:LANES] * ws[:, 0:LANES] + gs[0:depth, LANES:] * ws_own, -1, keepdims=True)
        shift = jnp.sum(gq[depth : depth + 1, :] * wq, -1, keepdims=True)
        shift += jnp.sum(
            gs[depth : depth + 1, 0:LANES] * ws[:, 0:LANES] + gs[depth : depth + 1, LANES:] * ws_own, -1, keepdims=True
        )
        gain = ws[:, LANES + G1 : LANES + G1 + 1]
        lift = ws[:, LANES + B1 : LANES + B1 + 1]
        stretch = (around - lift * shift) / gain
        place = lax.rem(iota((depth, LANES), 0), block)
        load = jnp.sum(jnp.where(wide == place, loads[0:1, :], 0.0), -1, keepdims=True)
        columns = jnp.where(wide < experts, gs[0:depth, LANES:], all_sums[...].T)
        columns = jnp.where(wide == G1, stretch, columns)
        columns = jnp.where(wide == B1, shift, columns)
        columns = jnp.where(wide == LOAD, load, columns)
        out[:, 0:depth] = gq[0:depth, :].astype(BF)
        out[:, depth : 2 * depth] = go[...]
        out[:, 2 * depth : 2 * depth + LANES] = gs[0:depth, 0:LANES].astype(BF)
        out[:, 2 * depth + LANES :] = columns.astype(BF)
        scatter(me[0], refs[n : 2 * n], out, out_sem)
        arrive(out, out_sem)


def result_kernel(n, me, act, x1, vec, *refs):
    res_o, wd, sem = refs[2 * n :]
    depth = x1.shape[1]

    @pl.when(pl.program_id(0) == 0)
    def _():
        for half in range(2):
            fetch(me[0], refs[half * n : half * n + n], ffn_parts(None, wd, half, depth, False, True), sem)
        arrive(wd, sem)

    res_o[...] = (x1[...] + vec[BD : BD + 1, :] + nn(act[...], wd[...])).astype(BF)


def close_kernel(n, me, dx1, dq, kv, ds, tok, vec, *refs):
    grad_o, w, sem = refs[n:]
    span, depth = tok.shape

    @pl.when(pl.program_id(0) == 0)
    def _():
        fetch(me[0], refs[:n], [(0, depth + 2 * LANES, w)], sem)
        arrive(w, sem)

    for c in range(span // TILE):
        rows = slice(c * TILE, (c + 1) * TILE)
        dh = nt(dq[rows, :], w[:, 0:depth]) + nt(jnp.concatenate([kv[rows, :], ds[rows, :]], 1), w[:, depth:])
        unit, inv = normed(tok[rows, :].astype(F32))
        scaled = dh * vec[G1 : G1 + 1, :]
        one = jnp.mean(scaled, -1, keepdims=True)
        two = jnp.mean(scaled * unit, -1, keepdims=True)
        grad_o[rows, :] = (dx1[rows, :] + inv * (scaled - one - unit * two)).astype(BF)


def xor_pairs(count, mask):
    return [(i, i ^ mask) for i in range(count)]


def hops(dp, fsdp):
    inner = fsdp.bit_length() - 1
    along = [1 << bit for bit in range(inner - 1, 1, -1)]
    across = [2] if inner > 1 else []
    rows = [1 << (inner + bit) for bit in range(dp.bit_length() - 1)]
    core = [1] if inner > 0 else []
    return along + across + rows + core, along + rows + across + core


def after(value, *others):
    return lax.optimization_barrier((value, *others))[0]


def move(value, mask, count):
    return lax.ppermute(value, AXES, xor_pairs(count, mask))


def spread(held, have, mask, me, count):
    axis = len([other for other in have if other > mask])
    own = jnp.expand_dims(held, axis)
    got = jnp.expand_dims(move(held, mask, count), axis)
    high = jnp.bitwise_and(me, mask) != 0
    return jnp.where(high, jnp.concatenate([got, own], axis), jnp.concatenate([own, got], axis))


def parted(value, have, mask, me):
    axis = len([other for other in have if other > mask])
    bit = (jnp.bitwise_and(me, mask) != 0).astype(jnp.int32)
    return (
        lax.dynamic_index_in_dim(value, bit, axis, keepdims=False),
        lax.dynamic_index_in_dim(value, 1 - bit, axis, keepdims=False),
    )


def joined(keep, got, dtype=BF):
    return (keep.astype(F32) + got.astype(F32)).astype(dtype)


def shrink(value, have, mask, me, count, dtype=BF):
    keep, send = parted(value, have, mask, me)
    return joined(keep, move(send, mask, count), dtype)


def cost(micros):
    return pl.CostEstimate(flops=int(micros * 1.0e9), bytes_accessed=1024, transcendentals=0)


def on_device(
    sizes, tokens, routes, lengths, ln1_gain, ln1_bias, w_query, w_key, w_value, w_out, w_router,
    ln2_gain, ln2_bias, w_up, b_up, w_down, b_down, cotangent
):
    dp, fsdp = sizes
    count = dp * fsdp
    total, depth = tokens.shape
    rows = lengths.shape[0]
    length = total // rows
    experts, head = w_router.shape[1], w_key.shape[1]
    segs = lengths.shape[1]
    share = w_query.shape[0]
    inner = w_up.shape[1]
    subs = inner // depth
    fast = share % 16 == 0 and fsdp >= 8 and dp >= 2
    first_width = 2 * depth + 2 * LANES
    me = lax.axis_index(AXES).astype(jnp.int32)
    core = (jnp.bitwise_and(me, 1) if fast else jnp.int32(0)).reshape(1)
    packed = (w_query, w_out, w_key, w_value, w_router, ln1_gain, ln1_bias, ln2_gain, ln2_bias, b_down, b_up)
    small = pl.pallas_call(pack_kernel, out_shape=jax.ShapeDtypeStruct((share, first_width), BF), name="pack")(*packed)
    ups = w_up.reshape(share, count, subs, share).transpose(0, 2, 1, 3).reshape(share, subs, depth)
    downs = w_down.reshape(subs, share, depth).transpose(1, 0, 2)
    large = [
        jnp.concatenate([ups[:, 2 * i : 2 * i + 2], downs[:, 2 * i : 2 * i + 2]], 1).reshape(share, 4 * depth)
        for i in range(2)
    ]
    if fast:
        orders = hops(dp, fsdp)
        steps = len(orders[0])
        early = len([m for m in orders[0][:-1] if orders[0].index(m) == orders[1].index(m)])
        blocks, block, n = count // 2, share, 2
        dims = (2,) * (steps - 1)

        def grow(held, order, at):
            return spread(held, order[:at], order[at], me, count)

        def flat(value):
            return value.reshape(blocks, block, value.shape[-1])

        held = grow(small, orders[0], 0)
        big = after(jnp.concatenate(large, 1), held)
        for at in range(1, early):
            held = grow(held, orders[0], at)
        big = grow(big, orders[0], 0)
        for at in range(early, steps - 2):
            held = grow(held, orders[0], at)
        held = after(held, big)
        for at in range(1, early):
            big = grow(big, orders[0], at)
        held = flat(grow(held, orders[0], steps - 2))
        held = after(held, big)
        w_pieces = [held, move(held, orders[0][-1], count)]
        big = [after(half, w_pieces[1]) for half in (big[..., : 4 * depth], big[..., 4 * depth :])]
        pending = list(range(early, steps - 1))
    else:
        blocks, block, n = 1, depth, 1
        w_pieces = [lax.all_gather(small, AXES, axis=0, tiled=True)[None]]
        f_pieces = [[lax.all_gather(half, AXES, axis=0, tiled=True)[None]] for half in large]

    smem = pl.BlockSpec(memory_space=pltpu.SMEM)
    hbm = pl.BlockSpec(memory_space=pl.ANY)
    dma = pltpu.SemaphoreType.DMA

    def whole(dims):
        return pl.BlockSpec(dims, lambda *_: (0,) * len(dims))

    def shape(dims, dtype):
        return jax.ShapeDtypeStruct(dims, dtype)

    def keep_far(value):
        return pltpu.with_memory_space_constraint(value, pltpu.HBM)

    def far(dims, dtype):
        return pltpu.HBM(dims, dtype)

    def call(kernel, name, micros, grid, ins, in_specs, outs, out_specs, scratch):
        return pl.pallas_call(
            kernel, grid=grid, in_specs=in_specs, out_specs=out_specs, out_shape=outs, scratch_shapes=scratch,
            compiler_params=pltpu.CompilerParams(vmem_limit_bytes=ROOM[name] << 20), cost_estimate=cost(micros), name=name,
        )(*ins)

    span = min(STEP, length)
    tiles = total // span
    per_row = length // span

    def tile(wide):
        return pl.BlockSpec((span, wide), lambda t: (t, 0))

    def pair(wide):
        return pl.BlockSpec((2, span, wide), lambda t: (0, t, 0))

    def row_tile(wide):
        return pl.BlockSpec((span, wide), lambda r, t: (r * per_row + t, 0))

    def row_pair(wide):
        return pl.BlockSpec((2, span, wide), lambda r, t: (0, r * per_row + t, 0))

    def by_row(wide):
        return pl.BlockSpec((length, wide), lambda r, t: (r, 0))

    hid, qa, kx, vx, pr, vec = call(
        functools.partial(project_kernel, n, length, segs, experts), "project", 9.0, (tiles,),
        (core, lengths, tokens, routes, *w_pieces),
        [smem, smem, tile(depth), tile(2)] + [hbm] * n,
        [
            shape((total, depth), BF), shape((2, total, LANES), BF), shape((total, 2 * LANES), BF),
            shape((total, 2 * LANES), BF), shape((total, LANES), F32), shape((32, depth), F32),
        ],
        [tile(depth), pair(LANES), tile(2 * LANES), tile(2 * LANES), tile(LANES), whole((32, depth))],
        [pltpu.VMEM((depth, depth + 2 * LANES), BF), pltpu.VMEM((LANES, depth), F32), dma],
    )
    if fast:
        big = [grow(half, order, pending[0]) for half, order in zip(big, orders)]
        qa = after(qa, *big)
        big = [after(half, kx) for half in big]
    o, u, qf = call(
        functools.partial(attend_kernel, segs), "attend", 13.0, (rows, per_row),
        (lengths, routes, qa, kx, vx, pr),
        [smem, row_tile(2), row_pair(LANES), by_row(2 * LANES), by_row(2 * LANES), row_tile(LANES)],
        [shape((total, LANES), F32), shape((total, depth), BF), shape((2, total, LANES), BF)],
        [row_tile(LANES), row_tile(depth), row_pair(LANES)],
        [],
    )
    if fast:
        for at in pending[1:]:
            big = [grow(half, order, at) for half, order in zip(big, orders)]
        big = [flat(half) for half in big]
        u = after(u, *big)
        big = [after(half, o) for half in big]
        f_pieces = [[half, move(half, orders[0][-1], count)] for half in big]
    x1, h2 = call(
        functools.partial(mix_kernel, n), "mix", 5.0, (tiles,),
        (core, tokens, u, vec, *w_pieces),
        [smem, tile(depth), tile(depth), whole((32, depth))] + [hbm] * n,
        [far((total, depth), F32), shape((total, depth), BF)],
        [tile(depth), tile(depth)],
        [pltpu.VMEM((depth, depth), BF), dma],
    )
    flat_f = [piece for half in f_pieces for piece in half]

    wide = 256

    def once(dims):
        return pl.BlockSpec(dims, lambda *_: (0,) * len(dims), pipeline_mode=pl.Buffered(1))

    column = pl.BlockSpec((total, wide), lambda s: (0, jnp.minimum(s, inner // wide - 1)))
    act, dz, bias, *f_grads = call(
        functools.partial(ffn_kernel, n), "feed", 25.0, (inner // wide + 1,),
        (core, h2, cotangent, vec, *flat_f),
        [smem, once((total, depth)), once((total, depth)), whole((32, depth))] + [hbm] * 2 * n,
        [far((total, inner), BF), far((total, inner), BF), shape((8, depth), F32)]
        + [shape((blocks, block, 4 * depth), BF)] * 2 * n,
        [column, column, whole((8, depth))] + [hbm] * 2 * n,
        [
            pltpu.VMEM((2, depth, inner // 2), BF), pltpu.VMEM((inner, depth), BF), pltpu.VMEM((depth + 16, total), BF),
            pltpu.VMEM((depth, total), BF), pltpu.VMEM((2, total, wide), BF), pltpu.VMEM((2, total, wide), BF),
            pltpu.VMEM((2, depth, inner), BF), pltpu.SemaphoreType.DMA((2,)), dma,
        ],
    )
    f_grads = [f_grads[:n], f_grads[n:]]
    dx1, low, sums = call(
        functools.partial(turn_kernel, n), "turn", 12.0, (tiles,),
        (core, keep_far(dz), cotangent, keep_far(x1), vec, *flat_f),
        [smem, tile(inner), tile(depth), tile(depth), whole((32, depth))] + [hbm] * 2 * n,
        [shape((total, depth), F32), shape((total, depth), BF), shape((32, depth), F32)],
        [tile(depth), tile(depth), whole((32, depth))],
        [pltpu.VMEM((2, depth, inner // 2), BF), dma],
    )
    if fast:
        back_orders = [list(reversed(order[:-1])) for order in orders]

        def fall(value, order, at, dtype=BF):
            return shrink(value, order[at:], order[at], me, count, dtype)

        acc = [joined(half[0], move(half[1], orders[0][-1], count)).reshape(*dims, block, 4 * depth) for half in f_grads]
        low = after(low, *acc)
        acc = [after(a, dx1) for a in acc]
        acc = [fall(a, order, 0) for a, order in zip(acc, back_orders)]
    da, df, ds, loads, go = call(
        functools.partial(gates_kernel, n), "gates", 9.0, (tiles,),
        (core, low, routes, pr, o, u, *w_pieces),
        [smem, tile(depth), tile(2), tile(LANES), tile(LANES), tile(depth)] + [hbm] * n,
        [
            shape((2, total, LANES), BF), shape((2, total, LANES), BF), shape((total, LANES), BF), shape((8, LANES), F32),
            shape((depth, depth), BF),
        ],
        [pair(LANES), pair(LANES), tile(LANES), whole((8, LANES)), whole((depth, depth))],
        [pltpu.VMEM((depth, depth), BF), pltpu.VMEM((depth, depth), F32), dma],
    )
    if fast:
        da = after(da, *acc)
        acc = [after(a, ds) for a in acc]
        acc = [fall(a, order, 1) for a, order in zip(acc, back_orders)]

    dq, kv = call(
        attend_back_kernel, "attend_back", 18.0, (rows, per_row),
        (routes, qa, qf, kx, vx, da, df),
        [row_tile(2), row_pair(LANES), row_pair(LANES), by_row(2 * LANES), by_row(2 * LANES), row_pair(LANES), row_pair(LANES)],
        [shape((total, depth), BF), shape((total, LANES), BF)],
        [row_tile(depth), by_row(LANES)],
        [
            pltpu.VMEM((LANES, length), F32), pltpu.VMEM((LANES, length), F32), pltpu.VMEM((2 * span, length), BF),
            pltpu.VMEM((2 * span, length), BF),
        ],
    )
    if fast:
        kv = after(kv, *acc)
        late = back_orders[0]
        acc = jnp.concatenate([after(a, dq) for a in acc], -1)
        acc = fall(acc, late, 2, F32 if len(late) == 3 else BF)
    w_grads = call(
        functools.partial(sum_kernel, n, block, experts), "sums", 6.0, (tiles,),
        (core, hid, dq, kv, ds, sums, bias, loads, go, *w_pieces),
        [
            smem, tile(depth), tile(depth), tile(LANES), tile(LANES), whole((32, depth)), whole((8, depth)),
            whole((8, LANES)), whole((depth, depth)),
        ]
        + [hbm] * n,
        [shape((blocks, block, first_width), BF)] * n,
        [hbm] * n,
        [
            pltpu.VMEM((depth, depth + 2 * LANES), BF), pltpu.VMEM((depth + 16, depth), F32),
            pltpu.VMEM((depth + 16, 2 * LANES), F32), pltpu.VMEM((LANES, depth), F32),
            pltpu.VMEM((depth, first_width), BF), dma, dma,
        ],
    )
    closing = dx1
    if fast:
        tail = joined(w_grads[0], move(w_grads[1], orders[0][-1], count)).reshape(*dims, block, first_width)
        closing = after(dx1, tail, acc)
        for at in range(3, len(late)):
            acc = fall(after(acc, tail), late, at, F32 if at == len(late) - 1 else BF)
        tail = fall(tail, late, 0)
    grad_tokens = call(
        functools.partial(close_kernel, n), "close", 6.0, (tiles,),
        (core, closing, dq, kv, ds, tokens, vec, *w_pieces),
        [smem, tile(depth), tile(depth), tile(LANES), tile(LANES), tile(depth), whole((32, depth))] + [hbm] * n,
        [shape((total, depth), BF)],
        [tile(depth)],
        [pltpu.VMEM((depth, depth + 2 * LANES), BF), dma],
    )[0]
    closing = x1
    if fast:
        closing = after(x1, tail, acc)
        tail = after(tail, grad_tokens)
        tail = fall(tail, late, 1)
    result = call(
        functools.partial(result_kernel, n), "result", 6.0, (tiles,),
        (core, act, closing, vec, *flat_f),
        [smem, tile(inner), tile(depth), whole((32, depth))] + [hbm] * 2 * n,
        [shape((total, depth), BF)],
        [tile(depth)],
        [pltpu.VMEM((inner, depth), BF), dma],
    )[0]

    if fast:
        tail = after(tail, result)
        for at in range(2, len(late)):
            tail = fall(tail, late, at, F32 if at == len(late) - 1 else BF)
        own_f = [acc[:, : 4 * depth], acc[:, 4 * depth :]]
        grad_out = tail[:, depth : 2 * depth]
        own_w = tail
        load = own_w[:experts, 2 * depth + LANES + LOAD]
    else:
        def scattered(value):
            return lax.psum_scatter(value[0].astype(F32), AXES, scatter_dimension=0, tiled=True)

        own_f = [scattered(half[0]) for half in f_grads]
        own_w = scattered(w_grads[0])
        grad_out = own_w[:, depth : 2 * depth]
        load = lax.psum(w_grads[0][0][:experts, 2 * depth + LANES + LOAD].astype(F32), AXES)
    extra = own_w[:, 2 * depth + LANES :]
    grad_up = jnp.concatenate([half[:, : 2 * depth] for half in own_f], 1)
    grad_up = grad_up.reshape(share, subs, count, share).transpose(0, 2, 1, 3).reshape(share, inner)
    grad_down = jnp.concatenate([half[:, 2 * depth :] for half in own_f], 1)
    grad_down = grad_down.reshape(share, subs, depth).transpose(1, 0, 2).reshape(subs * share, depth)
    return (
        result,
        grad_tokens,
        extra[:, G1],
        extra[:, B1],
        own_w[:, 0:depth],
        own_w[:, 2 * depth : 2 * depth + head],
        own_w[:, 2 * depth + head : 2 * depth + 2 * head],
        grad_out,
        extra[:, 0:experts],
        extra[:, G2],
        extra[:, B2],
        grad_up,
        extra[:, BU : BU + subs].T.reshape(subs * share),
        grad_down,
        extra[:, BD],
        load / (total * count),
    )


def solution(mesh):
    over = P(AXES)
    flat = P(AXES, None)
    sizes = (mesh.shape["dp"], mesh.shape["fsdp"])
    return jax.shard_map(
        functools.partial(on_device, sizes),
        mesh=mesh,
        in_specs=(
            flat, flat, flat, over, over, flat, flat, flat, flat, flat, over, over, flat, over, flat, over, flat,
        ),
        out_specs=(
            flat, flat, over, over, flat, flat, flat, flat, flat, over, over, flat, over, flat, over, P(),
        ),
        check_vma=False,
    )
```

time: 218 us -> 177 us (0.81)
  Pallas kernels: 120 us -> 92 us
  waiting for transfers between devices: 37.2 us -> 31.3 us
  starting transfers between devices: 35.1 us -> 29.6 us
    pallas_call x9 -> x10, Pallas kernels: 120 us -> 90.5 us  [call(): pl.pallas_call(kernel, grid=grid, in_specs=in_specs, out_specs=out_specs,...]
    ppermute x29 -> x26, waiting for transfers between devices: 37.2 us -> 31.3 us  [move(): return lax.ppermute(value, AXES, xor_pairs(count, mask))]
    ppermute x29 -> x26, starting transfers between devices: 35.1 us -> 29.6 us  [move(): return lax.ppermute(value, AXES, xor_pairs(count, mask))]
    unnamed x33 -> x70, local copies, waits for them, and re-layouts: 5.55 us -> 9.47 us
    broadcast_in_dim x6 -> x0, local copies, waits for them, and re-layouts: 3.73 us -> none  [the longest x5 3.73 us: on_device(): v[:, None]]
  transfers between devices with their start and end apart: 29 -> 26, of which waited for: 14 -> 12; matrix products, arithmetic and copies ran while one was open for 5% -> 5% of each run, Pallas kernels for 26% -> 36%
where the time goes in v3:
time: 177 us
  Pallas kernels  92 us (52%)
  waiting for transfers between devices  31.3 us (18%)
  starting transfers between devices  29.6 us (17%)
  local copies, waits for them, and re-layouts  19.1 us (11%)
  other arithmetic  3.13 us (2%)
    pallas_call x10, Pallas kernels, call(): pl.pallas_call(kernel, grid=grid, in_specs=in_specs, out_specs=out_specs,...  90.5 us
    ppermute x26, waiting for transfers between devices, move(): return lax.ppermute(value, AXES, xor_pairs(count, mask))  31.3 us
    ppermute x26, starting transfers between devices, move(): return lax.ppermute(value, AXES, xor_pairs(count, mask))  29.6 us
    unnamed x70, local copies, waits for them, and re-layouts  9.47 us
  transfers between devices with their start and end apart: 26, of which 12 were waited for; matrix products, arithmetic and copies ran while one was open for 5% of the time, Pallas kernels for 36%

profile of v3, /device:TPU:0, one launch (start us, length us, event | category | flops | bytes accessed | tf_op | source)
XLA Modules:
  0.0 176.7 jit_solution(12277993909690657751)
XLA Ops:
  2.0 1.6 pack.1
  3.6 4.0 %collective-permute-start = (bf16[16,1280]{1,0:T(8,128)(2,1)}, bf16[16,1280]{1,0:T(8,128)(2,1)S(1)}, u32[]{:S(2)}, u32[]{:S(2)}) collective-permute-start(bf16[16,1280]{1,0:T(8,128)(2,1)} %pack.1), channel_id=1, source_target_pairs={{0,8},{1,9},{2,10},{3,11},{4,12},{5,13},{6,14},{7,15},{8,0},{9,1},... | collective-permute-start | bytes 122888 | tf_op jit(solution)/shard_map/ppermute | solution.py:513
  10.6 1.6 collective-permute-start.1
  12.3 2.4 %collective-permute-start.3 = (bf16[16,4096]{1,0:T(8,128)(2,1)S(1)}, bf16[16,4096]{1,0:T(8,128)(2,1)S(1)}, u32[]{:S(2)}, u32[]{:S(2)}) collective-permute-start(bf16[16,4096]{1,0:T(8,128)(2,1)S(1)} %pad_maximum_fusion), channel_id=1, source_target_pairs={{0,8},{1,9},{2,10},{3,11},{4,12},{5,13},{6,14},{7,15},{8,0},{9,1},... | collective-permute-start | bytes 393224 | tf_op jit(solution)/shard_map/ppermute | solution.py:513
  15.2 1.6 collective-permute-start.2
  16.7 3.8 %collective-permute-done.3 = bf16[16,4096]{1,0:T(8,128)(2,1)S(1)} collective-permute-done((bf16[16,4096]{1,0:T(8,128)(2,1)S(1)}, bf16[16,4096]{1,0:T(8,128)(2,1)S(1)}, u32[]{:S(2)}, u32[]{:S(2)}) %collective-permute-start.3) | collective-permute-done | bytes 131104 | tf_op jit(solution)/shard_map/ppermute | solution.py:513
  20.8 1.6 collective-permute-start.4
  22.3 6.1 %collective-permute-done.5 = bf16[2,16,4096]{2,1,0:T(8,128)(2,1)S(1)} collective-permute-done((bf16[2,16,4096]{2,1,0:T(8,128)(2,1)S(1)}, bf16[2,16,4096]{2,1,0:T(8,128)(2,1)S(1)}, u32[]{:S(2)}, u32[]{:S(2)}) %collective-permute-start.5) | collective-permute-done | bytes 262176 | tf_op jit(solution)/shard_map/ppermute | solution.py:513
  28.5 1.5 collective-permute-done.4
  30.7 1.6 collective-permute-done.6.refs_1_
  33.9 1.5 collective-permute-start.8
  35.4 1.6 copy-done.4
  37.0 7.0 %project.1 = (bf16[2048,512]{1,0:T(8,128)(2,1)S(1)}, bf16[2,2048,128]{2,1,0:T(8,128)(2,1)S(1)}, bf16[2048,256]{1,0:T(8,128)(2,1)S(1)}, bf16[2048,256]{1,0:T(8,12...) custom-call(s32[1]{0:T(128)} %bitcast.me, s32[2,4]{1,0:T(2,128)S(1)} %copy-done.10, ...), custom_call_target="tpu_custom_call" | custom-call | flops 8999999488 | bytes 1024 | tf_op jit(solution)/shard_map/project/pallas_call | solution.py:622
  45.4 9.5 %attend.1 = (f32[2048,128]{1,0:T(8,128)S(1)}, bf16[2048,512]{1,0:T(8,128)(2,1)S(1)}, bf16[2,2048,128]{2,1,0:T(8,128)(2,1)S(1)}) custom-call(s32[2,4]{1,0:T(2,128)S(1)} %copy-done.10, s32[2048,2]{1,0:T(8,128)S(1)} %copy.131.routes, bf16[2,2048,128]{2,1,0:T(8,128)(2,1)S(1)} %get-tuple-element.77.qa, bf16[2048,256]{1,0:T(8,128)(2,1)S(1)} %get-tuple-element.78.kx, ...), custom_call_target="tpu_custom_call" | custom-call | flops 12999999488 | bytes 1024 | tf_op jit(solution)/shard_map/attend/pallas_call | solution.py:622
  55.0 2.7 %collective-permute-done.9 = bf16[2,2,2,16,2048]{4,3,1,0,2:T(8,128)(2,1)S(1)} collective-permute-done((bf16[2,2,2,16,2048]{4,3,1,0,2:T(8,128)(2,1)S(1)}, bf16[2,2,2,16,2048]{4,3,1,0,2:T(8,128)(2,1)S(1)}, u32[]{:S(2)}, u32[]{:S(2)}) %collective-permute-start.9) | collective-permute-done | bytes 524320 | tf_op jit(solution)/shard_map/ppermute | solution.py:513
  60.0 1.6 copy-done.5
  62.7 1.6 copy-done.13
  64.3 3.8 %mix.1 = (f32[2048,512]{1,0:T(8,128)}, bf16[2048,512]{1,0:T(8,128)(2,1)S(1)}) custom-call(s32[1]{0:T(128)} %bitcast.me, bf16[2048,512]{1,0:T(8,128)(2,1)S(1)} %copy-done.5, bf16[2048,512]{1,0:T(8,128)(2,1)S(1)} %copy-done.13, f32[32,512]{1,0:T(8,128)S(1)} %get-tuple-element.85.vec, bf16[16,16,1280]{2,1,0:T(8,128)(2,1)S(1)} %bitcast.117, ...), custom_call_target="tpu_custom_call" | custom-call | flops 5000000000 | bytes 1024 | tf_op jit(solution)/shard_map/mix/pallas_call | solution.py:622
  68.1 27.1 %feed.1 = (bf16[2048,2048]{1,0:T(8,128)(2,1)}, bf16[2048,2048]{1,0:T(8,128)(2,1)}, f32[8,512]{1,0:T(8,128)S(1)}, bf16[16,16,2048]{2,1,0:T(8,128)(2,1)S(1)}, bf16...) custom-call(s32[1]{0:T(128)} %bitcast.me, ...), custom_call_target="tpu_custom_call" | custom-call | flops 24999999488 | bytes 1024 | tf_op jit(solution)/shard_map/feed/pallas_call | solution.py:622
  95.8 10.7 %turn.1 = (f32[2048,512]{1,0:T(8,128)S(1)}, bf16[2048,512]{1,0:T(8,128)(2,1)S(1)}, f32[32,512]{1,0:T(8,128)S(1)}) custom-call(s32[1]{0:T(128)} %bitcast.me, bf16[2048,2048]{1,0:T(8,128)(2,1)} %get-tuple-element.94.dz, bf16[2048,512]{1,0:T(8,128)(2,1)S(1)} %copy-done.3, f32[2048,512]{1,0:T(8,128)} %get-tuple-element.122.x1, ...), custom_call_target="tpu_custom_call" | custom-call | flops 12000000000 | bytes 1024 | tf_op jit(solution)/shard_map/turn/pallas_call | solution.py:622
  109.5 6.1 %gates.1 = (bf16[2,2048,128]{2,1,0:T(8,128)(2,1)S(1)}, bf16[2,2048,128]{2,1,0:T(8,128)(2,1)S(1)}, bf16[2048,128]{1,0:T(8,128)(2,1)S(1)}, f32[8,128]{1,0:T(8,128)S(1)}, bf16[512,512]{1,0:T(8,128)(2,1)S(1)}) custom-call(s32[1]{0:T(128)} %bitcast.me, bf16[2048,512]{1,0:T(8,128)(2,1)S(1)} %get-tuple-element.100.dx1, s32[2048,2]{1,0:T(8,128)S(1)} %copy.131.routes, ...), custom_call_target="tpu_custom_call" | custom-call | flops 8999999488 | bytes 1024 | tf_op jit(solution)/shard_map/gates/pallas_call | solution.py:622
  115.7 5.6 %collective-permute-done.16 = bf16[2,2,2,16,2048]{4,3,1,2,0:T(8,128)(2,1)S(1)} collective-permute-done((bf16[2,2,2,16,2048]{4,3,1,2,0:T(8,128)(2,1)S(1)}, bf16[2,2,2,16,2048]{4,3,1,2,0:T(8,128)(2,1)S(1)}, u32[]{:S(2)}, u32[]{:S(2)}) %collective-permute-start.16) | collective-permute-done | bytes 524320 | tf_op jit(solution)/shard_map/ppermute | solution.py:513
  123.8 11.3 %attend_back.1 = (bf16[2048,512]{1,0:T(8,128)(2,1)S(1)}, bf16[2048,128]{1,0:T(8,128)(2,1)S(1)}) custom-call(s32[2048,2]{1,0:T(8,128)S(1)} %copy.131.routes, bf16[2,2048,128]{2,1,0:T(8,128)(2,1)S(1)} %copy-done.22, bf16[2,2048,128]{2,1,0:T(8,128)(2,1)S(1)} %copy-done.28, bf16[2048,256]{1,0:T(8,128)(2,1)S(1)} %copy-done.24, bf16[2048,256]{1,0:T(8,128)(2,1)S(1)} %copy-done.26, ...), custom_call_target="tpu_custom_call" | custom-call | flops 17999998976 | bytes 1024 | tf_op jit(solution)/shard_map/attend_back/pallas_call | solution.py:622
  135.4 1.8 %collective-permute-start.21 = (bf16[2,16,4096]{2,1,0:T(8,128)(2,1)S(1)}, bf16[2,16,4096]{2,1,0:T(8,128)(2,1)S(1)}, u32[]{:S(2)}, u32[]{:S(2)}) collective-permute-start(bf16[2,16,4096]{2,1,0:T(8,128)(2,1)S(1)} %dynamic-slice_bitcast_fusion.1), channel_id=1, source_target_pairs={{0,4},{1,5},{2,6},{3,7},{4,0},{5,1},{6,2},{7,3},{8,12},{9,13},{10,... | collective-permute-start | bytes 786440 | tf_op jit(solution)/shard_map/ppermute | solution.py:513
  137.1 3.6 %sums.1 = (bf16[16,16,1280]{2,1,0:T(8,128)(2,1)S(1)}, bf16[16,16,1280]{2,1,0:T(8,128)(2,1)S(1)}) custom-call(s32[1]{0:T(128)} %bitcast.me, bf16[2048,512]{1,0:T(8,128)(2,1)S(1)} %copy-done.16, bf16[2048,512]{1,0:T(8,128)(2,1)S(1)} %get-tuple-element.107.dq, bf16[2048,128]{1,0:T(8,128)(2,1)S(1)} %get-tuple-element.112.kv, ...), custom_call_target="tpu_custom_call" | custom-call | flops 6000000000 | bytes 1024 | tf_op jit(solution)/shard_map/sums/pallas_call | solution.py:622
  144.5 4.3 %close.1 = bf16[2048,512]{1,0:T(8,128)(2,1)} custom-call(s32[1]{0:T(128)} %bitcast.me, f32[2048,512]{1,0:T(8,128)S(1)} %get-tuple-element.123.dx1, bf16[2048,512]{1,0:T(8,128)(2,1)S(1)} %get-tuple-element.107.dq, bf16[2048,128]{1,0:T(8,128)(2,1)S(1)} %get-tuple-element.112.kv, bf16[2048,128]{1,0:T(8,128)(2,1)S(1)} %get-tuple-element.109.ds, ...), custom_call_target="tpu_custom_call" | custom-call | flops 6000000000 | bytes 1024 | tf_op jit(solution)/shard_map/close/pallas_call | solution.py:622
  148.8 3.7 %collective-permute-done.22 = bf16[16,4096]{1,0:T(8,128)(2,1)S(1)} collective-permute-done((bf16[16,4096]{1,0:T(8,128)(2,1)S(1)}, bf16[16,4096]{1,0:T(8,128)(2,1)S(1)}, u32[]{:S(2)}, u32[]{:S(2)}) %collective-permute-start.22) | collective-permute-done | bytes 131104 | tf_op jit(solution)/shard_map/ppermute | solution.py:513
  153.1 1.6 collective-permute-start.23
  154.7 7.1 %result.1 = bf16[2048,512]{1,0:T(8,128)(2,1)} custom-call(s32[1]{0:T(128)} %bitcast.me, bf16[2048,2048]{1,0:T(8,128)(2,1)S(1)} %bitcast.122, f32[2048,512]{1,0:T(8,128)S(1)} %copy-done.11, f32[32,512]{1,0:T(8,128)S(1)} %get-tuple-element.85.vec, bf16[16,16,2048]{2,1,0:T(8,128)(2,1)S(1)} %bitcast.110, bf16[16,16,2048]{2,1,0:T(8,128)(2,1)} %collective-permute-done.11.refs_1_, ...), custom_call_target="tpu_custom_call" | custom-call | flops 6000000000 | bytes 1024 | tf_op jit(solution)/shard_map/result/pallas_call | solution.py:622
  163.3 3.2 %collective-permute-done.24 = bf16[2,16,1280]{2,1,0:T(8,128)(2,1)S(1)} collective-permute-done((bf16[2,16,1280]{2,1,0:T(8,128)(2,1)S(1)}, bf16[2,16,1280]{2,1,0:T(8,128)(2,1)S(1)}, u32[]{:S(2)}, u32[]{:S(2)}) %collective-permute-start.24) | collective-permute-done | bytes 81952 | tf_op jit(solution)/shard_map/ppermute | solution.py:513
  166.5 2.6 %collective-permute-start.25 = (bf16[16,1280]{1,0:T(8,128)(2,1)S(1)}, bf16[16,1280]{1,0:T(8,128)(2,1)S(1)}, u32[]{:S(2)}, u32[]{:S(2)}) collective-permute-start(bf16[16,1280]{1,0:T(8,128)(2,1)S(1)} %dynamic-slice_bitcast_fusion.7), channel_id=1, source_target_pairs={{0,8},{1,9},{2,10},{3,11},{4,12},{5,13},{6,14},{7,15},{8,0},{9,1},... | collective-permute-start | bytes 122888 | tf_op jit(solution)/shard_map/ppermute | solution.py:513
  170.9 1.6 reshape.356
  (167 shorter events, 29.7 us)
Async XLA Ops:
  3.6 7.0 %collective-permute-start = (bf16[16,1280]{1,0:T(8,128)(2,1)}, bf16[16,1280]{1,0:T(8,128)(2,1)S(1)}, u32[]{:S(2)}, u32[]{:S(2)}) collective-permute-start(bf16[16,1280]{1,0:T(8,128)(2,1)} %pack.1), channel_id=1, source_target_pairs={{0,8},{1,9},{2,10},{3,11},{4,12},{5,13},{6,14},{7,15},{8,0},{9,1},... | collective-permute-start | bytes 122888 | tf_op jit(solution)/shard_map/ppermute | solution.py:513
  10.6 4.5 %collective-permute-start.1 = (bf16[2,16,1280]{2,1,0:T(8,128)(2,1)S(1)}, bf16[2,16,1280]{2,1,0:T(8,128)(2,1)S(1)}, u32[]{:S(2)}, u32[]{:S(2)}) collective-permute-start(bf16[2,16,1280]{2,1,0:T(8,128)(2,1)S(1)} %maximum_select_fusion.11), channel_id=1, source_target_pairs={{0,4},{1,5},{2,6},{3,7},{4,0},{5,1},{6,2},{7,3},{8,12},{9,13},{10,... | collective-permute-start | bytes 245768 | tf_op jit(solution)/shard_map/ppermute | solution.py:513
  12.3 8.3 %collective-permute-start.3 = (bf16[16,4096]{1,0:T(8,128)(2,1)S(1)}, bf16[16,4096]{1,0:T(8,128)(2,1)S(1)}, u32[]{:S(2)}, u32[]{:S(2)}) collective-permute-start(bf16[16,4096]{1,0:T(8,128)(2,1)S(1)} %pad_maximum_fusion), channel_id=1, source_target_pairs={{0,8},{1,9},{2,10},{3,11},{4,12},{5,13},{6,14},{7,15},{8,0},{9,1},... | collective-permute-start | bytes 393224 | tf_op jit(solution)/shard_map/ppermute | solution.py:513
  15.2 5.5 %collective-permute-start.2 = (bf16[2,2,16,1280]{3,2,0,1:T(8,128)(2,1)S(1)}, bf16[2,2,16,1280]{3,2,0,1:T(8,128)(2,1)S(1)}, u32[]{:S(2)}, u32[]{:S(2)}) collective-permute-start(bf16[2,2,16,1280]{3,2,0,1:T(8,128)(2,1)S(1)} %maximum_select_fusion.9), channel_id=1, source_target_pairs={{0,2},{1,3},{2,0},{3,1},{4,6},{5,7},{6,4},{7,5},{8,10},{9,11},{10,... | collective-permute-start | bytes 491528 | tf_op jit(solution)/shard_map/ppermute | solution.py:513
  20.6 7.9 %collective-permute-start.5 = (bf16[2,16,4096]{2,1,0:T(8,128)(2,1)S(1)}, bf16[2,16,4096]{2,1,0:T(8,128)(2,1)S(1)}, u32[]{:S(2)}, u32[]{:S(2)}) collective-permute-start(bf16[2,16,4096]{2,1,0:T(8,128)(2,1)S(1)} %maximum_select_fusion.7), channel_id=1, source_target_pairs={{0,4},{1,5},{2,6},{3,7},{4,0},{5,1},{6,2},{7,3},{8,12},{9,13},{10,... | collective-permute-start | bytes 786440 | tf_op jit(solution)/shard_map/ppermute | solution.py:513
  20.8 9.3 %collective-permute-start.4 = (bf16[2,2,2,16,1280]{4,3,0,2,1:T(8,128)(2,1)S(1)}, bf16[2,2,2,16,1280]{4,3,0,2,1:T(8,128)(2,1)S(1)}, u32[]{:S(2)}, u32[]{:S(2)}) collective-permute-start(bf16[2,2,2,16,1280]{4,3,0,2,1:T(8,128)(2,1)S(1)} %maximum_select_fusion.6), channel_id=1, source_target_pairs={{0,16},{1,17},{2,18},{3,19},{4,20},{5,21},{6,22},{7,23},{8,24},{9,... | collective-permute-start | bytes 983048 | tf_op jit(solution)/shard_map/ppermute | solution.py:513
  30.2 13.8 %copy-start = (bf16[2,2,2,2,16,1280]{5,4,3,2,1,0:T(8,128)(2,1)}, bf16[2,2,2,2,16,1280]{5,4,3,2,1,0:T(8,128)(2,1)S(1)}, u32[]{:S(2)}) copy-start(bf16[2,2,2,2,16,1280]{5,4,3,2,1,0:T(8,128)(2,1)S(1)} %copy.129) | copy-start | bytes 1966084
  30.2 2.2 %collective-permute-start.6 = (bf16[16,16,1280]{2,1,0:T(8,128)(2,1)S(1)}, bf16[16,16,1280]{2,1,0:T(8,128)(2,1)S(1)}, u32[]{:S(2)}, u32[]{:S(2)}) collective-permute-start(bf16[16,16,1280]{2,1,0:T(8,128)(2,1)S(1)} %bitcast.115), channel_id=1, source_target_pairs={{0,1},{1,0},{2,3},{3,2},{4,5},{5,4},{6,7},{7,6},{8,9},{9,8},{10,11... | collective-permute-start | bytes 1966088 | tf_op jit(solution)/shard_map/ppermute | solution.py:513
  32.4 11.6 %copy-start.7 = (bf16[16,16,1280]{2,1,0:T(8,128)(2,1)}, bf16[16,16,1280]{2,1,0:T(8,128)(2,1)S(1)}, u32[]{:S(2)}) copy-start(bf16[16,16,1280]{2,1,0:T(8,128)(2,1)S(1)} %collective-permute-done.6.refs_1_) | copy-start | bytes 1966084
  32.4 11.7 %collective-permute-start.7 = (bf16[2,2,16,2048]{3,2,1,0:T(8,128)(2,1)S(1)}, bf16[2,2,16,2048]{3,2,1,0:T(8,128)(2,1)S(1)}, u32[]{:S(2)}, u32[]{:S(2)}) collective-permute-start(bf16[2,2,16,2048]{3,2,1,0:T(8,128)(2,1)S(1)} %get-tuple-element.75), channel_id=1, source_target_pairs={{0,2},{1,3},{2,0},{3,1},{4,6},{5,7},{6,4},{7,5},{8,10},{9,11},{10,... | collective-permute-start | bytes 786440 | tf_op jit(solution)/shard_map/ppermute | solution.py:513
  33.9 10.3 %collective-permute-start.8 = (bf16[2,2,16,2048]{3,2,1,0:T(8,128)(2,1)S(1)}, bf16[2,2,16,2048]{3,2,1,0:T(8,128)(2,1)S(1)}, u32[]{:S(2)}, u32[]{:S(2)}) collective-permute-start(bf16[2,2,16,2048]{3,2,1,0:T(8,128)(2,1)S(1)} %get-tuple-element.76), channel_id=1, source_target_pairs={{0,16},{1,17},{2,18},{3,19},{4,20},{5,21},{6,22},{7,23},{8,24},{9,... | collective-permute-start | bytes 786440 | tf_op jit(solution)/shard_map/ppermute | solution.py:513
  44.0 10.9 %copy-start.17 = (f32[2048,128]{1,0:T(8,128)}, f32[2048,128]{1,0:T(8,128)S(1)}, u32[]{:S(2)}) copy-start(f32[2048,128]{1,0:T(8,128)S(1)} %get-tuple-element.80.pr) | copy-start | bytes 3145732
  44.0 10.9 %copy-start.21 = (bf16[2,2048,128]{2,1,0:T(8,128)(2,1)}, bf16[2,2048,128]{2,1,0:T(8,128)(2,1)S(1)}, u32[]{:S(2)}) copy-start(bf16[2,2048,128]{2,1,0:T(8,128)(2,1)S(1)} %get-tuple-element.77.qa) | copy-start | bytes 3145732
  44.2 13.5 %collective-permute-start.9 = (bf16[2,2,2,16,2048]{4,3,1,0,2:T(8,128)(2,1)S(1)}, bf16[2,2,2,16,2048]{4,3,1,0,2:T(8,128)(2,1)S(1)}, u32[]{:S(2)}, u32[]{:S(2)}) collective-permute-start(bf16[2,2,2,16,2048]{4,3,1,0,2:T(8,128)(2,1)S(1)} %maximum_select_fusion.4), channel_id=1, source_target_pairs={{0,16},{1,17},{2,18},{3,19},{4,20},{5,21},{6,22},{7,23},{8,24},{9,... | collective-permute-start | bytes 1572872 | tf_op jit(solution)/shard_map/ppermute | solution.py:513
  44.8 13.2 %collective-permute-start.10 = (bf16[2,2,2,16,2048]{4,3,2,1,0:T(8,128)(2,1)S(1)}, bf16[2,2,2,16,2048]{4,3,2,1,0:T(8,128)(2,1)S(1)}, u32[]{:S(2)}, u32[]{:S(2)}) collective-permute-start(bf16[2,2,2,16,2048]{4,3,2,1,0:T(8,128)(2,1)S(1)} %maximum_select_fusion.5), channel_id=1, source_target_pairs={{0,2},{1,3},{2,0},{3,1},{4,6},{5,7},{6,4},{7,5},{8,10},{9,11},{10,... | collective-permute-start | bytes 1572872 | tf_op jit(solution)/shard_map/ppermute | solution.py:513
  58.3 9.8 %collective-permute-start.11 = (bf16[16,16,2048]{2,1,0:T(8,128)(2,1)S(1)}, bf16[16,16,2048]{2,1,0:T(8,128)(2,1)}, u32[]{:S(2)}, u32[]{:S(2)}) collective-permute-start(bf16[16,16,2048]{2,1,0:T(8,128)(2,1)S(1)} %bitcast.107), channel_id=1, source_target_pairs={{0,1},{1,0},{2,3},{3,2},{4,5},{5,4},{6,7},{7,6},{8,9},{9,8},{10,11... | collective-permute-start | bytes 3145736 | tf_op jit(solution)/shard_map/ppermute | solution.py:513
  58.4 9.7 %collective-permute-start.12 = (bf16[16,16,2048]{2,1,0:T(8,128)(2,1)S(1)}, bf16[16,16,2048]{2,1,0:T(8,128)(2,1)}, u32[]{:S(2)}, u32[]{:S(2)}) collective-permute-start(bf16[16,16,2048]{2,1,0:T(8,128)(2,1)S(1)} %bitcast.111), channel_id=1, source_target_pairs={{0,1},{1,0},{2,3},{3,2},{4,5},{5,4},{6,7},{7,6},{8,9},{9,8},{10,11... | collective-permute-start | bytes 3145736 | tf_op jit(solution)/shard_map/ppermute | solution.py:513
  95.2 11.7 %collective-permute-start.13 = (bf16[16,16,2048]{2,1,0:T(8,128)(2,1)S(1)}, bf16[16,16,2048]{2,1,0:T(8,128)(2,1)S(1)}, u32[]{:S(2)}, u32[]{:S(2)}) collective-permute-start(bf16[16,16,2048]{2,1,0:T(8,128)(2,1)S(1)} %get-tuple-element.97), channel_id=1, source_target_pairs={{0,1},{1,0},{2,3},{3,2},{4,5},{5,4},{6,7},{7,6},{8,9},{9,8},{10,11... | collective-permute-start | bytes 3145736 | tf_op jit(solution)/shard_map/ppermute | solution.py:513
  95.4 11.1 %collective-permute-start.14 = (bf16[16,16,2048]{2,1,0:T(8,128)(2,1)S(1)}, bf16[16,16,2048]{2,1,0:T(8,128)(2,1)S(1)}, u32[]{:S(2)}, u32[]{:S(2)}) collective-permute-start(bf16[16,16,2048]{2,1,0:T(8,128)(2,1)S(1)} %get-tuple-element.99), channel_id=1, source_target_pairs={{0,1},{1,0},{2,3},{3,2},{4,5},{5,4},{6,7},{7,6},{8,9},{9,8},{10,11... | collective-permute-start | bytes 3145736 | tf_op jit(solution)/shard_map/ppermute | solution.py:513
  107.4 14.0 %collective-permute-start.16 = (bf16[2,2,2,16,2048]{4,3,1,2,0:T(8,128)(2,1)S(1)}, bf16[2,2,2,16,2048]{4,3,1,2,0:T(8,128)(2,1)S(1)}, u32[]{:S(2)}, u32[]{:S(2)}) collective-permute-start(bf16[2,2,2,16,2048]{4,3,1,2,0:T(8,128)(2,1)S(1)} %copy_bitcast_fusion), channel_id=1, source_target_pairs={{0,2},{1,3},{2,0},{3,1},{4,6},{5,7},{6,4},{7,5},{8,10},{9,11},{10,... | collective-permute-start | bytes 1572872 | tf_op jit(solution)/shard_map/ppermute | solution.py:513
  108.0 15.0 %collective-permute-start.15 = (bf16[2,2,2,16,2048]{4,3,0,1,2:T(8,128)(2,1)S(1)}, bf16[2,2,2,16,2048]{4,3,0,1,2:T(8,128)(2,1)S(1)}, u32[]{:S(2)}, u32[]{:S(2)}) collective-permute-start(bf16[2,2,2,16,2048]{4,3,0,1,2:T(8,128)(2,1)S(1)} %copy_bitcast_fusion.1), channel_id=1, source_target_pairs={{0,16},{1,17},{2,18},{3,19},{4,20},{5,21},{6,22},{7,23},{8,24},{9,... | collective-permute-start | bytes 1572872 | tf_op jit(solution)/shard_map/ppermute | solution.py:513
  121.5 13.6 %collective-permute-start.18 = (bf16[2,2,16,2048]{3,2,0,1:T(8,128)(2,1)S(1)}, bf16[2,2,16,2048]{3,2,0,1:T(8,128)(2,1)S(1)}, u32[]{:S(2)}, u32[]{:S(2)}) collective-permute-start(bf16[2,2,16,2048]{3,2,0,1:T(8,128)(2,1)S(1)} %dynamic-slice_bitcast_fusion.2), channel_id=1, source_target_pairs={{0,16},{1,17},{2,18},{3,19},{4,20},{5,21},{6,22},{7,23},{8,24},{9,... | collective-permute-start | bytes 786440 | tf_op jit(solution)/shard_map/ppermute | solution.py:513
  123.2 12.0 %collective-permute-start.17 = (bf16[2,2,16,2048]{3,2,0,1:T(8,128)(2,1)S(1)}, bf16[2,2,16,2048]{3,2,0,1:T(8,128)(2,1)S(1)}, u32[]{:S(2)}, u32[]{:S(2)}) collective-permute-start(bf16[2,2,16,2048]{3,2,0,1:T(8,128)(2,1)S(1)} %dynamic-slice_bitcast_fusion.3), channel_id=1, source_target_pairs={{0,2},{1,3},{2,0},{3,1},{4,6},{5,7},{6,4},{7,5},{8,10},{9,11},{10,... | collective-permute-start | bytes 786440 | tf_op jit(solution)/shard_map/ppermute | solution.py:513
  135.4 7.0 %collective-permute-start.21 = (bf16[2,16,4096]{2,1,0:T(8,128)(2,1)S(1)}, bf16[2,16,4096]{2,1,0:T(8,128)(2,1)S(1)}, u32[]{:S(2)}, u32[]{:S(2)}) collective-permute-start(bf16[2,16,4096]{2,1,0:T(8,128)(2,1)S(1)} %dynamic-slice_bitcast_fusion.1), channel_id=1, source_target_pairs={{0,4},{1,5},{2,6},{3,7},{4,0},{5,1},{6,2},{7,3},{8,12},{9,13},{10,... | collective-permute-start | bytes 786440 | tf_op jit(solution)/shard_map/ppermute | solution.py:513
  140.7 2.2 %collective-permute-start.19 = (bf16[16,16,1280]{2,1,0:T(8,128)(2,1)S(1)}, bf16[16,16,1280]{2,1,0:T(8,128)(2,1)S(1)}, u32[]{:S(2)}, u32[]{:S(2)}) collective-permute-start(bf16[16,16,1280]{2,1,0:T(8,128)(2,1)S(1)} %get-tuple-element.118), channel_id=1, source_target_pairs={{0,1},{1,0},{2,3},{3,2},{4,5},{5,4},{6,7},{7,6},{8,9},{9,8},{10,11... | collective-permute-start | bytes 1966088 | tf_op jit(solution)/shard_map/ppermute | solution.py:513
  142.9 11.8 %slice-start = ((s8[8388608]{0:T(1024)(128)(4,1)}), s8[4194304]{0:T(1024)(128)(4,1)S(1)}, s32[]{:S(2)}) async-start(s8[8388608]{0:T(1024)(128)(4,1)} %bitcast.121), calls=%async_computation | async-start | bytes 8388608
  143.1 11.6 %slice-start.1 = ((s8[8388608]{0:T(1024)(128)(4,1)}), s8[4194304]{0:T(1024)(128)(4,1)S(1)}, s32[]{:S(2)}) async-start(s8[8388608]{0:T(1024)(128)(4,1)} %bitcast.121), calls=%async_computation.1 | async-start | bytes 8388608
  143.1 9.3 %collective-permute-start.22 = (bf16[16,4096]{1,0:T(8,128)(2,1)S(1)}, bf16[16,4096]{1,0:T(8,128)(2,1)S(1)}, u32[]{:S(2)}, u32[]{:S(2)}) collective-permute-start(bf16[16,4096]{1,0:T(8,128)(2,1)S(1)} %dynamic-slice_bitcast_fusion.5), channel_id=1, source_target_pairs={{0,8},{1,9},{2,10},{3,11},{4,12},{5,13},{6,14},{7,15},{8,0},{9,1},... | collective-permute-start | bytes 393224 | tf_op jit(solution)/shard_map/ppermute | solution.py:513
  143.4 9.6 %collective-permute-start.20 = (bf16[2,2,2,16,1280]{4,3,2,1,0:T(8,128)(2,1)S(1)}, bf16[2,2,2,16,1280]{4,3,2,1,0:T(8,128)(2,1)S(1)}, u32[]{:S(2)}, u32[]{:S(2)}) collective-permute-start(bf16[2,2,2,16,1280]{4,3,2,1,0:T(8,128)(2,1)S(1)} %dynamic-slice_bitcast_fusion), channel_id=1, source_target_pairs={{0,16},{1,17},{2,18},{3,19},{4,20},{5,21},{6,22},{7,23},{8,24},{9,... | collective-permute-start | bytes 983048 | tf_op jit(solution)/shard_map/ppermute | solution.py:513
  153.1 8.7 %collective-permute-start.23 = (bf16[2,2,16,1280]{3,2,1,0:T(8,128)(2,1)S(1)}, bf16[2,2,16,1280]{3,2,1,0:T(8,128)(2,1)S(1)}, u32[]{:S(2)}, u32[]{:S(2)}) collective-permute-start(bf16[2,2,16,1280]{3,2,1,0:T(8,128)(2,1)S(1)} %dynamic-slice_bitcast_fusion.4), channel_id=1, source_target_pairs={{0,2},{1,3},{2,0},{3,1},{4,6},{5,7},{6,4},{7,5},{8,10},{9,11},{10,... | collective-permute-start | bytes 491528 | tf_op jit(solution)/shard_map/ppermute | solution.py:513
  162.0 4.5 %collective-permute-start.24 = (bf16[2,16,1280]{2,1,0:T(8,128)(2,1)S(1)}, bf16[2,16,1280]{2,1,0:T(8,128)(2,1)S(1)}, u32[]{:S(2)}, u32[]{:S(2)}) collective-permute-start(bf16[2,16,1280]{2,1,0:T(8,128)(2,1)S(1)} %dynamic-slice_bitcast_fusion.6), channel_id=1, source_target_pairs={{0,4},{1,5},{2,6},{3,7},{4,0},{5,1},{6,2},{7,3},{8,12},{9,13},{10,... | collective-permute-start | bytes 245768 | tf_op jit(solution)/shard_map/ppermute | solution.py:513
  166.5 6.0 %collective-permute-start.25 = (bf16[16,1280]{1,0:T(8,128)(2,1)S(1)}, bf16[16,1280]{1,0:T(8,128)(2,1)S(1)}, u32[]{:S(2)}, u32[]{:S(2)}) collective-permute-start(bf16[16,1280]{1,0:T(8,128)(2,1)S(1)} %dynamic-slice_bitcast_fusion.7), channel_id=1, source_target_pairs={{0,8},{1,9},{2,10},{3,11},{4,12},{5,13},{6,14},{7,15},{8,0},{9,1},... | collective-permute-start | bytes 122888 | tf_op jit(solution)/shard_map/ppermute | solution.py:513
  (27 other events, 127.1 us)

commit v4 on v3

--- a/solution.py
+++ b/solution.py
@@ -16,8 +16,8 @@
 TILE = 256
 STEP = 512
 ROOM = {
-    "project": 16, "attend": 20, "mix": 14, "feed": 32, "turn": 28, "gates": 16, "attend_back": 32, "sums": 18, "close": 18,
-    "result": 22,
+    "project": 12, "attend": 14, "mix": 10, "feed": 29, "turn": 18, "gates": 12, "attend_back": 28, "sums": 14, "close": 14,
+    "result": 18,
 }
 
 
@@ -69,9 +69,9 @@
     return parts
 
 
-def pack_kernel(wq, wo, wk, wv, wr, g1, b1, g2, b2, bd, bu, o):
+def pack_kernel(wq, wo, wk, wv, wr, g1, b1, g2, b2, bd, bu, up, down, o, big_o):
     share, depth = wq.shape
-    head, experts = wk.shape[1], wr.shape[1]
+    head, experts = wk.shape[1], wr.shape[0]
     same = iota((share, share), 0) == iota((share, share), 1)
     lane = iota((share, LANES), 1)
 
@@ -88,8 +88,21 @@
     o[:, depth : depth + head] = wk[...]
     o[:, depth + head : depth + LANES] = wv[...]
     o[:, depth + LANES : depth + 2 * LANES] = out.astype(BF)
-    o[:, depth + LANES : depth + LANES + experts] = wr[...]
+    o[:, depth + LANES : depth + LANES + experts] = nt(jnp.where(same, 1.0, 0.0).astype(BF), wr[...]).astype(BF)
     o[:, depth + 2 * LANES :] = wo[...]
+    subs = bu.shape[0] // share
+    wide = subs * LANES
+    row, col = iota((wide, wide), 0), iota((wide, wide), 1)
+    at = lax.div(lax.rem(row, subs * share), share) * LANES + lax.div(row, subs * share) * share + lax.rem(row, share)
+    turn = jnp.where(at == col, 1.0, 0.0).astype(BF)
+    for part in range(up.shape[1] // wide):
+        moved = nn(up[:, part * wide : (part + 1) * wide], turn).astype(BF)
+        for j in range(subs):
+            place = (j // 2) * 4 * depth + (j % 2) * depth + part * LANES
+            big_o[:, place : place + LANES] = moved[:, j * LANES : (j + 1) * LANES]
+    for j in range(subs):
+        place = (j // 2) * 4 * depth + (2 + j % 2) * depth
+        big_o[:, place : place + depth] = down[j * share : (j + 1) * share, :]
 
 
 def split3(value):
@@ -142,13 +155,13 @@
     lane = iota((TILE, LANES), 1)
     half = lane // 64
     low = lane < 64
-    for c in range(span // TILE):
-        rows = slice(c * TILE, (c + 1) * TILE)
+    parts = [slice(c * TILE, (c + 1) * TILE) for c in range(span // TILE)]
+    for rows in parts:
         unit, _ = normed(tok[rows, :].astype(F32))
-        hid = (unit * vec[G1 : G1 + 1, :] + vec[B1 : B1 + 1, :]).astype(BF)
-        hid_o[rows, :] = hid
-        query = nn(hid, w[:, 0:depth])
-        small = nn(hid, w[:, depth:])
+        hid_o[rows, :] = (unit * vec[G1 : G1 + 1, :] + vec[B1 : B1 + 1, :]).astype(BF)
+    products = [(nn(hid_o[rows, :], w[:, 0:depth]), nn(hid_o[rows, :], w[:, depth:])) for rows in parts]
+    for c, rows in enumerate(parts):
+        query, small = products[c]
         kv = small[:, :LANES].astype(BF).astype(F32)
         swap = pltpu.roll(kv, 64, 1)
         seg = segment_of(lens, row, begin + c * TILE, TILE)
@@ -204,9 +217,10 @@
         fetch(me[0], refs[:n], [(depth + 2 * LANES, depth, w)], sem)
         arrive(w, sem)
 
-    for c in range(span // TILE):
-        rows = slice(c * TILE, (c + 1) * TILE)
-        after = tok[rows, :].astype(F32) + nn(u[rows, :], w[...])
+    parts = [slice(c * TILE, (c + 1) * TILE) for c in range(span // TILE)]
+    products = [nn(u[rows, :], w[...]) for rows in parts]
+    for rows, product in zip(parts, products):
+        after = tok[rows, :].astype(F32) + product
         x1_o[rows, :] = after
         unit, _ = normed(after)
         h2_o[rows, :] = (unit * vec[G2 : G2 + 1, :] + vec[B2 : B2 + 1, :]).astype(BF)
@@ -298,7 +312,9 @@
         arrive(out, out_sem)
 
 
-def turn_kernel(n, me, dz, dy, x1, vec, *refs):
+def turn_kernel(n, again, me, dz, dy, x1, vec, *refs):
+    if again:
+        before, refs = refs[0], refs[3:]
     dx1_o, low_o, sums_o, wu, f_sem = refs[2 * n :]
     span, depth = dy.shape
     step = pl.program_id(0)
@@ -307,12 +323,12 @@
     def _():
         for half in range(2):
             fetch(me[0], refs[half * n : half * n + n], ffn_parts(wu, None, half, depth, True, False), f_sem)
-        sums_o[...] = jnp.zeros_like(sums_o)
+        sums_o[...] = before[...] if again else jnp.zeros_like(sums_o)
         arrive(wu, f_sem)
 
-    for c in range(span // TILE):
-        rows = slice(c * TILE, (c + 1) * TILE)
-        dh2 = nt(dz[rows, 0 : 2 * depth], wu[0]) + nt(dz[rows, 2 * depth :], wu[1])
+    parts = [slice(c * TILE, (c + 1) * TILE) for c in range(span // TILE)]
+    products = [nt(dz[rows, 0 : 2 * depth], wu[0]) + nt(dz[rows, 2 * depth :], wu[1]) for rows in parts]
+    for rows, dh2 in zip(parts, products):
         unit, inv = normed(x1[rows, :])
         grad = dy[rows, :].astype(F32)
         sums_o[G2 : G2 + 1, :] += jnp.sum(dh2 * unit, 0, keepdims=True)
@@ -342,9 +358,10 @@
     half = lane // 64
     low = lane < 64
     go[...] += nn(u[...].T, dx1[...])
-    for c in range(span // TILE):
-        rows = slice(c * TILE, (c + 1) * TILE)
-        du = nt(dx1[rows, :], w[...]).astype(BF).astype(F32)
+    parts = [slice(c * TILE, (c + 1) * TILE) for c in range(span // TILE)]
+    products = [nt(dx1[rows, :], w[...]) for rows in parts]
+    for rows, product in zip(parts, products):
+        du = product.astype(BF).astype(F32)
         probs = pr[rows, :]
         heads = o[rows, :]
         swap = pltpu.roll(heads, 64, 1)
@@ -371,9 +388,10 @@
         go_o[...] = go[...].astype(BF)
 
 
-def attend_back_kernel(routes, qa, qf, kx, vx, da, df, dq_o, kv_o, dk, dv, ds, ps):
+def attend_back_kernel(routes, qa, qf, kx, vx, da, df, *refs):
+    dq_o, kv_o, dk, dv, ds, ps = refs[-6:]
     span, depth = dq_o.shape
-    step = pl.program_id(1)
+    step = pl.program_id(0)
     lane = iota((TILE, LANES), 1)
     half = lane // 64
 
@@ -404,7 +422,7 @@
         dk[...] += dk_part
         dv[...] += dv_part
 
-    @pl.when(step == pl.num_programs(1) - 1)
+    @pl.when(step == pl.num_programs(0) - 1)
     def _():
         for c in range(kv_o.shape[0] // TILE):
             rows = slice(c * TILE, (c + 1) * TILE)
@@ -482,14 +500,33 @@
         fetch(me[0], refs[:n], [(0, depth + 2 * LANES, w)], sem)
         arrive(w, sem)
 
-    for c in range(span // TILE):
-        rows = slice(c * TILE, (c + 1) * TILE)
-        dh = nt(dq[rows, :], w[:, 0:depth]) + nt(jnp.concatenate([kv[rows, :], ds[rows, :]], 1), w[:, depth:])
+    parts = [slice(c * TILE, (c + 1) * TILE) for c in range(span // TILE)]
+    products = [
+        nt(dq[rows, :], w[:, 0:depth]) + nt(jnp.concatenate([kv[rows, :], ds[rows, :]], 1), w[:, depth:]) for rows in parts
+    ]
+    for rows, dh in zip(parts, products):
         unit, inv = normed(tok[rows, :].astype(F32))
         scaled = dh * vec[G1 : G1 + 1, :]
         one = jnp.mean(scaled, -1, keepdims=True)
         two = jnp.mean(scaled * unit, -1, keepdims=True)
         grad_o[rows, :] = (dx1[rows, :] + inv * (scaled - one - unit * two)).astype(BF)
+
+
+def finish_kernel(share_of, keep, got, gq, gk, gv, go, gr, g1, b1, g2, b2, bd, bu, load):
+    share, depth = gq.shape
+    head, experts = gk.shape[1], gr.shape[0]
+    total = keep[...].astype(F32) + got[...].astype(F32)
+    gq[...] = total[:, 0:depth]
+    go[...] = total[:, depth : 2 * depth]
+    gk[...] = total[:, 2 * depth : 2 * depth + head]
+    gv[...] = total[:, 2 * depth + head : 2 * depth + 2 * head]
+    turned = jnp.concatenate([total[:, 2 * depth + LANES :], jnp.zeros((LANES - share, LANES), F32)], 0).T
+    gr[...] = turned[0:experts, 0:share]
+    for at, out in zip((G1, B1, G2, B2, BD), (g1, b1, g2, b2, bd)):
+        out[...] = turned[at : at + 1, 0:share].reshape(share)
+    lines = [turned[BU + j : BU + j + 1, 0:share] for j in range(bu.shape[0] // share)]
+    bu[...] = jnp.concatenate(lines, 1).reshape(bu.shape[0])
+    load[...] = (turned[LOAD : LOAD + 1, 0:experts] * share_of).reshape(experts)
 
 
 def xor_pairs(count, mask):
@@ -561,14 +598,14 @@
     first_width = 2 * depth + 2 * LANES
     me = lax.axis_index(AXES).astype(jnp.int32)
     core = (jnp.bitwise_and(me, 1) if fast else jnp.int32(0)).reshape(1)
-    packed = (w_query, w_out, w_key, w_value, w_router, ln1_gain, ln1_bias, ln2_gain, ln2_bias, b_down, b_up)
-    small = pl.pallas_call(pack_kernel, out_shape=jax.ShapeDtypeStruct((share, first_width), BF), name="pack")(*packed)
-    ups = w_up.reshape(share, count, subs, share).transpose(0, 2, 1, 3).reshape(share, subs, depth)
-    downs = w_down.reshape(subs, share, depth).transpose(1, 0, 2)
-    large = [
-        jnp.concatenate([ups[:, 2 * i : 2 * i + 2], downs[:, 2 * i : 2 * i + 2]], 1).reshape(share, 4 * depth)
-        for i in range(2)
-    ]
+    packed = (w_query, w_out, w_key, w_value, w_router.T, ln1_gain, ln1_bias, ln2_gain, ln2_bias, b_down, b_up, w_up, w_down)
+    small, large = pl.pallas_call(
+        pack_kernel,
+        out_shape=[
+            pltpu.VMEM((share, first_width), BF), pltpu.VMEM((share, 2 * inner), BF),
+        ],
+        name="pack",
+    )(*packed)
     if fast:
         orders = hops(dp, fsdp)
         steps = len(orders[0])
@@ -582,25 +619,25 @@
         def flat(value):
             return value.reshape(blocks, block, value.shape[-1])
 
-        held = grow(small, orders[0], 0)
-        big = after(jnp.concatenate(large, 1), held)
-        for at in range(1, early):
+        held = small
+        for at in range(early):
             held = grow(held, orders[0], at)
-        big = grow(big, orders[0], 0)
-        for at in range(early, steps - 2):
-            held = grow(held, orders[0], at)
-        held = after(held, big)
-        for at in range(1, early):
-            big = grow(big, orders[0], at)
-        held = flat(grow(held, orders[0], steps - 2))
-        held = after(held, big)
+        big = grow(large, orders[0], 0)
+        parts = [held[..., : first_width // 2], held[..., first_width // 2 :]]
+        for at in range(early, steps - 1):
+            parts = [grow(part, order, at) for part, order in zip(parts, orders)]
+            if at == early:
+                for other in range(1, early):
+                    big = grow(after(big, *parts), orders[0], other)
+        held = flat(jnp.concatenate(parts, -1))
         w_pieces = [held, move(held, orders[0][-1], count)]
         big = [after(half, w_pieces[1]) for half in (big[..., : 4 * depth], big[..., 4 * depth :])]
         pending = list(range(early, steps - 1))
     else:
         blocks, block, n = 1, depth, 1
         w_pieces = [lax.all_gather(small, AXES, axis=0, tiled=True)[None]]
-        f_pieces = [[lax.all_gather(half, AXES, axis=0, tiled=True)[None]] for half in large]
+        large = lax.all_gather(large, AXES, axis=0, tiled=True)[None]
+        f_pieces = [[large[..., : 4 * depth]], [large[..., 4 * depth :]]]
 
     smem = pl.BlockSpec(memory_space=pltpu.SMEM)
     hbm = pl.BlockSpec(memory_space=pl.ANY)
@@ -645,11 +682,11 @@
 
     hid, qa, kx, vx, pr, vec = call(
         functools.partial(project_kernel, n, length, segs, experts), "project", 9.0, (tiles,),
-        (core, lengths, tokens, routes, *w_pieces),
+        (core, lengths, keep_far(tokens), routes, *w_pieces),
         [smem, smem, tile(depth), tile(2)] + [hbm] * n,
         [
-            shape((total, depth), BF), shape((2, total, LANES), BF), shape((total, 2 * LANES), BF),
-            shape((total, 2 * LANES), BF), shape((total, LANES), F32), shape((32, depth), F32),
+            far((total, depth), BF), shape((2, total, LANES), BF), far((total, 2 * LANES), BF),
+            far((total, 2 * LANES), BF), shape((total, LANES), F32), shape((32, depth), F32),
         ],
         [tile(depth), pair(LANES), tile(2 * LANES), tile(2 * LANES), tile(LANES), whole((32, depth))],
         [pltpu.VMEM((depth, depth + 2 * LANES), BF), pltpu.VMEM((LANES, depth), F32), dma],
@@ -662,7 +699,7 @@
         functools.partial(attend_kernel, segs), "attend", 13.0, (rows, per_row),
         (lengths, routes, qa, kx, vx, pr),
         [smem, row_tile(2), row_pair(LANES), by_row(2 * LANES), by_row(2 * LANES), row_tile(LANES)],
-        [shape((total, LANES), F32), shape((total, depth), BF), shape((2, total, LANES), BF)],
+        [shape((total, LANES), F32), shape((total, depth), BF), far((2, total, LANES), BF)],
         [row_tile(LANES), row_tile(depth), row_pair(LANES)],
         [],
     )
@@ -694,7 +731,7 @@
         (core, h2, cotangent, vec, *flat_f),
         [smem, once((total, depth)), once((total, depth)), whole((32, depth))] + [hbm] * 2 * n,
         [far((total, inner), BF), far((total, inner), BF), shape((8, depth), F32)]
-        + [shape((blocks, block, 4 * depth), BF)] * 2 * n,
+        + [far((blocks, block, 4 * depth), BF)] * 2 * n,
         [column, column, whole((8, depth))] + [hbm] * 2 * n,
         [
             pltpu.VMEM((2, depth, inner // 2), BF), pltpu.VMEM((inner, depth), BF), pltpu.VMEM((depth + 16, total), BF),
@@ -703,24 +740,34 @@
         ],
     )
     f_grads = [f_grads[:n], f_grads[n:]]
-    dx1, low, sums = call(
-        functools.partial(turn_kernel, n), "turn", 12.0, (tiles,),
-        (core, keep_far(dz), cotangent, keep_far(x1), vec, *flat_f),
-        [smem, tile(inner), tile(depth), tile(depth), whole((32, depth))] + [hbm] * 2 * n,
-        [shape((total, depth), F32), shape((total, depth), BF), shape((32, depth), F32)],
-        [tile(depth), tile(depth), whole((32, depth))],
-        [pltpu.VMEM((2, depth, inner // 2), BF), dma],
-    )
+    def turn(begin, again):
+        def part(wide):
+            return pl.BlockSpec((span, wide), lambda t: (t + begin, 0))
+
+        return pl.pallas_call(
+            functools.partial(turn_kernel, n, len(again) > 0), grid=(tiles // 2,),
+            in_specs=[smem, part(inner), part(depth), part(depth), whole((32, depth))]
+            + ([whole((32, depth)), hbm, hbm] if again else []) + [hbm] * 2 * n,
+            out_specs=[part(depth), part(depth), whole((32, depth))],
+            out_shape=[shape((total, depth), F32), shape((total, depth), BF), shape((32, depth), F32)],
+            scratch_shapes=[pltpu.VMEM((2, depth, inner // 2), BF), dma],
+            input_output_aliases={6: 0, 7: 1} if again else {},
+            compiler_params=pltpu.CompilerParams(vmem_limit_bytes=ROOM["turn"] << 20), cost_estimate=cost(6.0), name="turn",
+        )(core, keep_far(dz), cotangent, keep_far(x1), vec, *again, *flat_f)
+
+    dx1, low, sums = turn(0, ())
     if fast:
         back_orders = [list(reversed(order[:-1])) for order in orders]
+        late = back_orders[0]
 
         def fall(value, order, at, dtype=BF):
             return shrink(value, order[at:], order[at], me, count, dtype)
 
         acc = [joined(half[0], move(half[1], orders[0][-1], count)).reshape(*dims, block, 4 * depth) for half in f_grads]
-        low = after(low, *acc)
+        sums = after(sums, *acc)
         acc = [after(a, dx1) for a in acc]
         acc = [fall(a, order, 0) for a, order in zip(acc, back_orders)]
+    dx1, low, sums = turn(tiles // 2, (sums, dx1, low))
     da, df, ds, loads, go = call(
         functools.partial(gates_kernel, n), "gates", 9.0, (tiles,),
         (core, low, routes, pr, o, u, *w_pieces),
@@ -737,22 +784,42 @@
         acc = [after(a, ds) for a in acc]
         acc = [fall(a, order, 1) for a, order in zip(acc, back_orders)]
 
-    dq, kv = call(
-        attend_back_kernel, "attend_back", 18.0, (rows, per_row),
-        (routes, qa, qf, kx, vx, da, df),
-        [row_tile(2), row_pair(LANES), row_pair(LANES), by_row(2 * LANES), by_row(2 * LANES), row_pair(LANES), row_pair(LANES)],
-        [shape((total, depth), BF), shape((total, LANES), BF)],
-        [row_tile(depth), by_row(LANES)],
-        [
-            pltpu.VMEM((LANES, length), F32), pltpu.VMEM((LANES, length), F32), pltpu.VMEM((2 * span, length), BF),
-            pltpu.VMEM((2 * span, length), BF),
-        ],
-    )
+    def back(row, again):
+        def part(wide):
+            return pl.BlockSpec((span, wide), lambda t: (row * per_row + t, 0))
+
+        def both(wide):
+            return pl.BlockSpec((2, span, wide), lambda t: (0, row * per_row + t, 0))
+
+        def full(wide):
+            return pl.BlockSpec((length, wide), lambda t: (row, 0))
+
+        return pl.pallas_call(
+            attend_back_kernel, grid=(per_row,),
+            in_specs=[part(2), both(LANES), both(LANES), full(2 * LANES), full(2 * LANES), both(LANES), both(LANES)]
+            + [hbm] * len(again),
+            out_specs=[part(depth), full(LANES)],
+            out_shape=[shape((total, depth), BF), shape((total, LANES), BF)],
+            scratch_shapes=[
+                pltpu.VMEM((LANES, length), F32), pltpu.VMEM((LANES, length), F32), pltpu.VMEM((2 * span, length), BF),
+                pltpu.VMEM((2 * span, length), BF),
+            ],
+            input_output_aliases={7: 0, 8: 1} if again else {},
+            compiler_params=pltpu.CompilerParams(vmem_limit_bytes=ROOM["attend_back"] << 20), cost_estimate=cost(8.0),
+            name="attend_back",
+        )(routes, qa, qf, kx, vx, da, df, *again)
+
+    dq, kv = back(0, ())
+    for row in range(1, rows):
+        if fast and row == 1:
+            dq = after(dq, *acc)
+            acc = jnp.concatenate([after(a, kv) for a in acc], -1)
+            acc = fall(acc, late, 2, F32 if len(late) == 3 else BF)
+        dq, kv = back(row, (dq, kv))
     if fast:
-        kv = after(kv, *acc)
-        late = back_orders[0]
-        acc = jnp.concatenate([after(a, dq) for a in acc], -1)
-        acc = fall(acc, late, 2, F32 if len(late) == 3 else BF)
+        kv = after(kv, acc)
+        for at in range(3, len(late)):
+            acc = fall(after(acc, dq), late, at, F32 if at == len(late) - 1 else BF)
     w_grads = call(
         functools.partial(sum_kernel, n, block, experts), "sums", 6.0, (tiles,),
         (core, hid, dq, kv, ds, sums, bias, loads, go, *w_pieces),
@@ -773,9 +840,8 @@
     if fast:
         tail = joined(w_grads[0], move(w_grads[1], orders[0][-1], count)).reshape(*dims, block, first_width)
         closing = after(dx1, tail, acc)
-        for at in range(3, len(late)):
-            acc = fall(after(acc, tail), late, at, F32 if at == len(late) - 1 else BF)
-        tail = fall(tail, late, 0)
+        tails = [tail[..., : first_width // 2], tail[..., first_width // 2 :]]
+        tails = [fall(part, order, 0) for part, order in zip(tails, back_orders)]
     grad_tokens = call(
         functools.partial(close_kernel, n), "close", 6.0, (tiles,),
         (core, closing, dq, kv, ds, tokens, vec, *w_pieces),
@@ -786,9 +852,8 @@
     )[0]
     closing = x1
     if fast:
-        closing = after(x1, tail, acc)
-        tail = after(tail, grad_tokens)
-        tail = fall(tail, late, 1)
+        closing = after(x1, *tails)
+        tails = [fall(after(part, grad_tokens), order, 1) for part, order in zip(tails, back_orders)]
     result = call(
         functools.partial(result_kernel, n), "result", 6.0, (tiles,),
         (core, act, closing, vec, *flat_f),
@@ -798,44 +863,43 @@
         [pltpu.VMEM((inner, depth), BF), dma],
     )[0]
 
+    def unpacked(halves):
+        up = jnp.concatenate([half[:, : 2 * depth] for half in halves], 1)
+        up = up.reshape(share, subs, count, share).transpose(0, 2, 1, 3).reshape(share, inner)
+        down = jnp.concatenate([half[:, 2 * depth :] for half in halves], 1)
+        return up, down.reshape(share, subs, depth).transpose(1, 0, 2).reshape(subs * share, depth)
+
     if fast:
-        tail = after(tail, result)
-        for at in range(2, len(late)):
-            tail = fall(tail, late, at, F32 if at == len(late) - 1 else BF)
-        own_f = [acc[:, : 4 * depth], acc[:, 4 * depth :]]
-        grad_out = tail[:, depth : 2 * depth]
-        own_w = tail
-        load = own_w[:experts, 2 * depth + LANES + LOAD]
+        tail = after(jnp.concatenate(tails, -1), result)
+        grad_up, grad_down = unpacked([acc[:, : 4 * depth], acc[:, 4 * depth :]])
+        for at in range(2, len(late) - 1):
+            tail = fall(tail, late, at)
+        keep, send = parted(after(tail, grad_up, grad_down), late[-1:], late[-1], me)
+        own = functools.partial(jax.ShapeDtypeStruct, dtype=F32)
+        grad_query, grad_key, grad_value, grad_out, grad_router, *lines = pl.pallas_call(
+            functools.partial(finish_kernel, 1.0 / (total * count)),
+            out_shape=[own((share, depth)), own((share, head)), own((share, head)), own((share, depth)), own((experts, share))]
+            + [own((share,))] * 5 + [own((subs * share,)), own((experts,))],
+            name="finish",
+        )(keep, move(send, late[-1], count))
+        grad_router = grad_router.T
+        grad_g1, grad_b1, grad_g2, grad_b2, grad_bd, grad_bu, load = lines
     else:
         def scattered(value):
             return lax.psum_scatter(value[0].astype(F32), AXES, scatter_dimension=0, tiled=True)
 
-        own_f = [scattered(half[0]) for half in f_grads]
+        grad_up, grad_down = unpacked([scattered(half[0]) for half in f_grads])
         own_w = scattered(w_grads[0])
-        grad_out = own_w[:, depth : 2 * depth]
-        load = lax.psum(w_grads[0][0][:experts, 2 * depth + LANES + LOAD].astype(F32), AXES)
-    extra = own_w[:, 2 * depth + LANES :]
-    grad_up = jnp.concatenate([half[:, : 2 * depth] for half in own_f], 1)
-    grad_up = grad_up.reshape(share, subs, count, share).transpose(0, 2, 1, 3).reshape(share, inner)
-    grad_down = jnp.concatenate([half[:, 2 * depth :] for half in own_f], 1)
-    grad_down = grad_down.reshape(share, subs, depth).transpose(1, 0, 2).reshape(subs * share, depth)
+        load = lax.psum(w_grads[0][0][:experts, 2 * depth + LANES + LOAD].astype(F32), AXES) / (total * count)
+        extra = own_w[:, 2 * depth + LANES :]
+        grad_query, grad_out = own_w[:, 0:depth], own_w[:, depth : 2 * depth]
+        grad_key, grad_value = own_w[:, 2 * depth : 2 * depth + head], own_w[:, 2 * depth + head : 2 * depth + 2 * head]
+        grad_router = extra[:, 0:experts]
+        grad_g1, grad_b1, grad_g2, grad_b2, grad_bd = [extra[:, at] for at in (G1, B1, G2, B2, BD)]
+        grad_bu = extra[:, BU : BU + subs].T.reshape(subs * share)
     return (
-        result,
-        grad_tokens,
-        extra[:, G1],
-        extra[:, B1],
-        own_w[:, 0:depth],
-        own_w[:, 2 * depth : 2 * depth + head],
-        own_w[:, 2 * depth + head : 2 * depth + 2 * head],
-        grad_out,
-        extra[:, 0:experts],
-        extra[:, G2],
-        extra[:, B2],
-        grad_up,
-        extra[:, BU : BU + subs].T.reshape(subs * share),
-        grad_down,
-        extra[:, BD],
-        load / (total * count),
+        result, grad_tokens, grad_g1, grad_b1, grad_query, grad_key, grad_value, grad_out, grad_router, grad_g2, grad_b2,
+        grad_up, grad_bu, grad_down, grad_bd, load,
     )
 
 

time: 177 us -> 168 us (0.949)
  waiting for transfers between devices: 31.3 us -> 22.2 us
  local copies, waits for them, and re-layouts: 19.1 us -> 10.7 us
  starting transfers between devices: 29.6 us -> 33.9 us
  Pallas kernels: 92 us -> 95.5 us
    pallas_call x1 -> x6, Pallas kernels: 1.59 us -> 25.9 us  [the longest x2 11.4 us: turn(): pl.pallas_call(functools.partial(turn_kernel, n, len(again) > 0), grid=(t...]
    pallas_call x10 -> x8, Pallas kernels: 90.5 us -> 69.7 us  [call(): pl.pallas_call(kernel, grid=grid, in_specs=in_specs, out_specs=out_specs,...]
    ppermute x26 -> x30, waiting for transfers between devices: 31.3 us -> 22.2 us  [move(): return lax.ppermute(value, AXES, xor_pairs(count, mask))]
    ppermute x26 -> x30, starting transfers between devices: 29.6 us -> 33.9 us  [move(): return lax.ppermute(value, AXES, xor_pairs(count, mask))]
    unnamed x70 -> x74, local copies, waits for them, and re-layouts: 9.47 us -> 6.04 us
    slice x7 -> x2, local copies, waits for them, and re-layouts: 2.88 us -> 0.09 us  [the longest x1 0.07 us: on_device(): tails = [tail[..., :first_width // 2], tail[..., first_width // 2:]]]
    reshape x8 -> x3, local copies, waits for them, and re-layouts: 5.22 us -> 2.61 us  [the longest x2 1.95 us: unpacked(): up.reshape(share, subs, count, share).transpose(0, 2, 1, 3)]
  transfers between devices with their start and end apart: 26 -> 30, of which waited for: 12 -> 15; matrix products, arithmetic and copies ran while one was open for 5% -> 5% of each run, Pallas kernels for 36% -> 39%
where the time goes in v4:
time: 168 us
  Pallas kernels  95.5 us (57%)
  starting transfers between devices  33.9 us (20%)
  waiting for transfers between devices  22.2 us (13%)
  local copies, waits for them, and re-layouts  10.7 us (6%)
  other arithmetic  3.82 us (2%)
  between operations  1.72 us (1%)
    pallas_call x8, Pallas kernels, call(): pl.pallas_call(kernel, grid=grid, in_specs=in_specs, out_specs=out_specs,...  69.7 us
    ppermute x30, starting transfers between devices, move(): return lax.ppermute(value, AXES, xor_pairs(count, mask))  33.9 us
    ppermute x30, waiting for transfers between devices, move(): return lax.ppermute(value, AXES, xor_pairs(count, mask))  22.2 us
    pallas_call x2, Pallas kernels, turn(): pl.pallas_call(functools.partial(turn_kernel, n, len(again) > 0), grid=(t...  11.4 us
    pallas_call x2, Pallas kernels, back(): pl.pallas_call(attend_back_kernel, grid=(per_row,), in_specs=[part(2), bo...  11.4 us
    unnamed x74, local copies, waits for them, and re-layouts  6.04 us
  transfers between devices with their start and end apart: 30, of which 15 were waited for; matrix products, arithmetic and copies ran while one was open for 5% of the time, Pallas kernels for 39%

profile of v4, /device:TPU:0, one launch (start us, length us, event | category | flops | bytes accessed | tf_op | source)
XLA Modules:
  0.0 167.9 jit_solution(9679780784360110548)
XLA Ops:
  0.7 1.5 pack.1
  2.1 4.1 %collective-permute-start = (bf16[16,1280]{1,0:T(8,128)(2,1)S(1)}, bf16[16,1280]{1,0:T(8,128)(2,1)S(1)}, u32[]{:S(2)}, u32[]{:S(2)}) collective-permute-start(bf16[16,1280]{1,0:T(8,128)(2,1)S(1)} %get-tuple-element.91), channel_id=1, source_target_pairs={{0,8},{1,9},{2,10},{3,11},{4,12},{5,13},{6,14},{7,15},{8,0},{9,1},... | collective-permute-start | bytes 122888 | tf_op jit(solution)/shard_map/ppermute | solution.py:550
  8.6 3.7 %collective-permute-start.1 = (bf16[2,16,1280]{2,1,0:T(8,128)(2,1)S(1)}, bf16[2,16,1280]{2,1,0:T(8,128)(2,1)S(1)}, u32[]{:S(2)}, u32[]{:S(2)}) collective-permute-start(bf16[2,16,1280]{2,1,0:T(8,128)(2,1)S(1)} %maximum_select_fusion.13), channel_id=1, source_target_pairs={{0,4},{1,5},{2,6},{3,7},{4,0},{5,1},{6,2},{7,3},{8,12},{9,13},{10,... | collective-permute-start | bytes 245768 | tf_op jit(solution)/shard_map/ppermute | solution.py:550
  12.4 4.3 %collective-permute-done.1 = bf16[2,16,1280]{2,1,0:T(8,128)(2,1)S(1)} collective-permute-done((bf16[2,16,1280]{2,1,0:T(8,128)(2,1)S(1)}, bf16[2,16,1280]{2,1,0:T(8,128)(2,1)S(1)}, u32[]{:S(2)}, u32[]{:S(2)}) %collective-permute-start.1) | collective-permute-done | bytes 81952 | tf_op jit(solution)/shard_map/ppermute | solution.py:550
  16.8 1.6 collective-permute-start.4
  18.4 1.5 collective-permute-start.2
  19.9 1.4 collective-permute-done.4
  21.3 1.6 collective-permute-start.5
  23.0 1.5 collective-permute-start.3
  24.6 2.1 %collective-permute-done.5 = bf16[2,2,2,16,640]{4,3,2,1,0:T(8,128)(2,1)S(1)} collective-permute-done((bf16[2,2,2,16,640]{4,3,2,1,0:T(8,128)(2,1)S(1)}, bf16[2,2,2,16,640]{4,3,2,1,0:T(8,128)(2,1)S(1)}, u32[]{:S(2)}, u32[]{:S(2)}) %collective-permute-start.5) | collective-permute-done | bytes 163872 | tf_op jit(solution)/shard_map/ppermute | solution.py:550
  26.8 1.7 collective-permute-done.3
  28.7 2.2 %collective-permute-done.8 = bf16[2,16,4096]{2,1,0:T(8,128)(2,1)S(1)} collective-permute-done((bf16[2,16,4096]{2,1,0:T(8,128)(2,1)S(1)}, bf16[2,16,4096]{2,1,0:T(8,128)(2,1)S(1)}, u32[]{:S(2)}, u32[]{:S(2)}) %collective-permute-start.8) | collective-permute-done | bytes 262176 | tf_op jit(solution)/shard_map/ppermute | solution.py:550
  33.2 8.1 %project.1 = (bf16[2048,512]{1,0:T(8,128)(2,1)}, bf16[2,2048,128]{2,1,0:T(8,128)(2,1)S(1)}, bf16[2048,256]{1,0:T(8,128)(2,1)}, bf16[2048,256]{1,0:T(8,128)(2,1)}...) custom-call(s32[1]{0:T(128)} %bitcast.me, s32[2,4]{1,0:T(2,128)S(1)} %copy-done.15, bf16[2048,512]{1,0:T(8,128)(2,1)} %tok.5, ...), custom_call_target="tpu_custom_call" | custom-call | flops 8999999488 | bytes 1024 | tf_op jit(solution)/shard_map/project/pallas_call | solution.py:659
  43.6 10.7 %attend.1 = (f32[2048,128]{1,0:T(8,128)S(1)}, bf16[2048,512]{1,0:T(8,128)(2,1)S(1)}, bf16[2,2048,128]{2,1,0:T(8,128)(2,1)}) custom-call(s32[2,4]{1,0:T(2,128)S(1)} %copy-done.15, s32[2048,2]{1,0:T(8,128)S(1)} %copy.55.routes, bf16[2,2048,128]{2,1,0:T(8,128)(2,1)S(1)} %get-tuple-element.97.qa, bf16[2048,256]{1,0:T(8,128)(2,1)S(1)} %copy-done.21, ...), custom_call_target="tpu_custom_call" | custom-call | flops 12999999488 | bytes 1024 | tf_op jit(solution)/shard_map/attend/pallas_call | solution.py:659
  57.4 3.8 %mix.1 = (f32[2048,512]{1,0:T(8,128)}, bf16[2048,512]{1,0:T(8,128)(2,1)S(1)}) custom-call(s32[1]{0:T(128)} %bitcast.me, bf16[2048,512]{1,0:T(8,128)(2,1)S(1)} %copy-done.11, bf16[2048,512]{1,0:T(8,128)(2,1)S(1)} %get-tuple-element.104.u, f32[32,512]{1,0:T(8,128)S(1)} %get-tuple-element.105.vec, bf16[16,16,1280]{2,1,0:T(8,128)(2,1)S(1)} %pad_maximum_fusion.refs_0_, ...), custom_call_target="tpu_custom_call" | custom-call | flops 5000000000 | bytes 1024 | tf_op jit(solution)/shard_map/mix/pallas_call | solution.py:659
  61.3 27.3 %feed.1 = (bf16[2048,2048]{1,0:T(8,128)(2,1)}, bf16[2048,2048]{1,0:T(8,128)(2,1)}, f32[8,512]{1,0:T(8,128)S(1)}, bf16[16,16,2048]{2,1,0:T(8,128)(2,1)}, bf16[16,...) custom-call(s32[1]{0:T(128)} %bitcast.me, ...), custom_call_target="tpu_custom_call" | custom-call | flops 24999999488 | bytes 1024 | tf_op jit(solution)/shard_map/feed/pallas_call | solution.py:659
  89.2 1.6 copy-done.2
  92.0 5.8 %turn.2 = (f32[2048,512]{1,0:T(8,128)S(1)}, bf16[2048,512]{1,0:T(8,128)(2,1)S(1)}, f32[32,512]{1,0:T(8,128)S(1)}) custom-call(s32[1]{0:T(128)} %bitcast.me, bf16[2048,2048]{1,0:T(8,128)(2,1)} %get-tuple-element.114.dz, bf16[2048,512]{1,0:T(8,128)(2,1)S(1)} %copy-done.2, f32[2048,512]{1,0:T(8,128)} %get-tuple-element.146.x1, ...), custom_call_target="tpu_custom_call" | custom-call | flops 6000000000 | bytes 1024 | tf_op jit(solution)/shard_map/turn/pallas_call | solution.py:747
  97.8 1.7 %add_convert_fusion = bf16[16,16,2048]{2,1,0:T(8,128)(2,1)S(1)} fusion(bf16[16,16,2048]{2,1,0:T(8,128)(2,1)} %collective-permute-done.16, bf16[16,16,2048]{2,1,0:T(8,128)(2,1)S(1)} %copy-done.31), kind=kLoop, calls=%fused_computation | loop fusion | flops 2097152 | bytes 3145728 | tf_op jit(solution)/shard_map/convert_element_type | solution.py:571
  102.2 5.7 %turn.3 = (f32[2048,512]{1,0:T(8,128)S(1)}, bf16[2048,512]{1,0:T(8,128)(2,1)S(1)}, f32[32,512]{1,0:T(8,128)S(1)}) custom-call(s32[1]{0:T(128)} %bitcast.me, bf16[2048,2048]{1,0:T(8,128)(2,1)} %get-tuple-element.114.dz, bf16[2048,512]{1,0:T(8,128)(2,1)S(1)} %copy-done.3, ...), custom_call_target="tpu_custom_call", output_to_operand_aliasing={{0}: (6, {}), {1}: (7, {})} | custom-call | flops 6000000000 | bytes 1024 | tf_op jit(solution)/shard_map/turn/pallas_call | solution.py:747
  108.0 6.1 %gates.1 = (bf16[2,2048,128]{2,1,0:T(8,128)(2,1)S(1)}, bf16[2,2048,128]{2,1,0:T(8,128)(2,1)S(1)}, bf16[2048,128]{1,0:T(8,128)(2,1)S(1)}, f32[8,128]{1,0:T(8,128)S(1)}, bf16[512,512]{1,0:T(8,128)(2,1)S(1)}) custom-call(s32[1]{0:T(128)} %bitcast.me, bf16[2048,512]{1,0:T(8,128)(2,1)S(1)} %get-tuple-element.123.dx1, s32[2048,2]{1,0:T(8,128)S(1)} %copy-done.8, ...), custom_call_target="tpu_custom_call" | custom-call | flops 8999999488 | bytes 1024 | tf_op jit(solution)/shard_map/gates/pallas_call | solution.py:659
  116.7 5.7 %attend_back.2 = (bf16[2048,512]{1,0:T(8,128)(2,1)S(1)}, bf16[2048,128]{1,0:T(8,128)(2,1)S(1)}) custom-call(s32[2048,2]{1,0:T(8,128)S(1)} %copy-done.8, bf16[2,2048,128]{2,1,0:T(8,128)(2,1)S(1)} %copy-done.20, bf16[2,2048,128]{2,1,0:T(8,128)(2,1)S(1)} %copy-done.25, bf16[2048,256]{1,0:T(8,128)(2,1)S(1)} %copy-done.22, bf16[2048,256]{1,0:T(8,128)(2,1)S(1)} %copy-done.24, ...), custom_call_target="tpu_custom_call" | custom-call | flops 8000000000 | bytes 1024 | tf_op jit(solution)/shard_map/attend_back/pallas_call | solution.py:797
  124.0 5.7 %attend_back.3 = (bf16[2048,512]{1,0:T(8,128)(2,1)S(1)}, bf16[2048,128]{1,0:T(8,128)(2,1)S(1)}) custom-call(s32[2048,2]{1,0:T(8,128)S(1)} %copy-done.8, bf16[2,2048,128]{2,1,0:T(8,128)(2,1)S(1)} %copy-done.20, bf16[2,2048,128]{2,1,0:T(8,128)(2,1)S(1)} %copy-done.25, bf16[2048,256]{1,0:T(8,128)(2,1)S(1)} %copy-done.22, ...), custom_call_target="tpu_custom_call", output_to_operand_aliasing={{0}: (7, {}), {1}: (8, {})} | custom-call | flops 8000000000 | bytes 1024 | tf_op jit(solution)/shard_map/attend_back/pallas_call | solution.py:797
  130.7 2.7 %collective-permute-start.25 = (bf16[16,4096]{1,0:T(8,128)(2,1)S(1)}, bf16[16,4096]{1,0:T(8,128)(2,1)S(1)}, u32[]{:S(2)}, u32[]{:S(2)}) collective-permute-start(bf16[16,4096]{1,0:T(8,128)(2,1)S(1)} %dynamic-slice_bitcast_fusion.3), channel_id=1, source_target_pairs={{0,8},{1,9},{2,10},{3,11},{4,12},{5,13},{6,14},{7,15},{8,0},{9,1},... | collective-permute-start | bytes 393224 | tf_op jit(solution)/shard_map/ppermute | solution.py:550
  133.5 3.6 %sums.1 = (bf16[16,16,1280]{2,1,0:T(8,128)(2,1)S(1)}, bf16[16,16,1280]{2,1,0:T(8,128)(2,1)S(1)}) custom-call(s32[1]{0:T(128)} %bitcast.me, bf16[2048,512]{1,0:T(8,128)(2,1)S(1)} %copy-done.18, bf16[2048,512]{1,0:T(8,128)(2,1)S(1)} %get-tuple-element.135.dq, bf16[2048,128]{1,0:T(8,128)(2,1)S(1)} %get-tuple-element.139.kv, ...), custom_call_target="tpu_custom_call" | custom-call | flops 6000000000 | bytes 1024 | tf_op jit(solution)/shard_map/sums/pallas_call | solution.py:659
  140.7 1.4 collective-permute-start.24
  142.2 4.1 %close.1 = bf16[2048,512]{1,0:T(8,128)(2,1)} custom-call(s32[1]{0:T(128)} %bitcast.me, f32[2048,512]{1,0:T(8,128)S(1)} %get-tuple-element.149.dx1, bf16[2048,512]{1,0:T(8,128)(2,1)S(1)} %get-tuple-element.135.dq, bf16[2048,128]{1,0:T(8,128)(2,1)S(1)} %get-tuple-element.139.kv, bf16[2048,128]{1,0:T(8,128)(2,1)S(1)} %get-tuple-element.130.ds, ...), custom_call_target="tpu_custom_call" | custom-call | flops 6000000000 | bytes 1024 | tf_op jit(solution)/shard_map/close/pallas_call | solution.py:659
  149.0 6.1 %result.1 = bf16[2048,512]{1,0:T(8,128)(2,1)} custom-call(s32[1]{0:T(128)} %bitcast.me, bf16[2048,2048]{1,0:T(8,128)(2,1)S(1)} %bitcast.128, f32[2048,512]{1,0:T(8,128)S(1)} %copy-done, f32[32,512]{1,0:T(8,128)S(1)} %get-tuple-element.105.vec, bf16[16,16,2048]{2,1,0:T(8,128)(2,1)S(1)} %bitcast.118, ...), custom_call_target="tpu_custom_call" | custom-call | flops 6000000000 | bytes 1024 | tf_op jit(solution)/shard_map/result/pallas_call | solution.py:659
  155.2 1.5 collective-permute-start.28
  157.8 1.6 reshape.281
  161.6 3.9 %collective-permute-done.29.got = bf16[16,1280]{1,0:T(8,128)(2,1)S(1)} collective-permute-done((bf16[16,1280]{1,0:T(8,128)(2,1)S(1)}, bf16[16,1280]{1,0:T(8,128)(2,1)S(1)}, u32[]{:S(2)}, u32[]{:S(2)}) %collective-permute-start.29) | collective-permute-done | bytes 40992 | tf_op jit(solution)/shard_map/ppermute | solution.py:550
  166.2 1.6 finish.1
  (174 shorter events, 30.8 us)
Async XLA Ops:
  2.1 6.5 %collective-permute-start = (bf16[16,1280]{1,0:T(8,128)(2,1)S(1)}, bf16[16,1280]{1,0:T(8,128)(2,1)S(1)}, u32[]{:S(2)}, u32[]{:S(2)}) collective-permute-start(bf16[16,1280]{1,0:T(8,128)(2,1)S(1)} %get-tuple-element.91), channel_id=1, source_target_pairs={{0,8},{1,9},{2,10},{3,11},{4,12},{5,13},{6,14},{7,15},{8,0},{9,1},... | collective-permute-start | bytes 122888 | tf_op jit(solution)/shard_map/ppermute | solution.py:550
  6.2 13.7 %collective-permute-start.7 = (bf16[16,4096]{1,0:T(8,128)(2,1)S(1)}, bf16[16,4096]{1,0:T(8,128)(2,1)S(1)}, u32[]{:S(2)}, u32[]{:S(2)}) collective-permute-start(bf16[16,4096]{1,0:T(8,128)(2,1)S(1)} %get-tuple-element.93), channel_id=1, source_target_pairs={{0,8},{1,9},{2,10},{3,11},{4,12},{5,13},{6,14},{7,15},{8,0},{9,1},... | collective-permute-start | bytes 393224 | tf_op jit(solution)/shard_map/ppermute | solution.py:550
  7.4 36.2 %copy-start.7 = (s32[2048,2]{1,0:T(8,128)}, s32[2048,2]{1,0:T(8,128)S(1)}, u32[]{:S(2)}) copy-start(s32[2048,2]{1,0:T(8,128)S(1)} %copy.55.routes) | copy-start | bytes 49156
  8.6 8.1 %collective-permute-start.1 = (bf16[2,16,1280]{2,1,0:T(8,128)(2,1)S(1)}, bf16[2,16,1280]{2,1,0:T(8,128)(2,1)S(1)}, u32[]{:S(2)}, u32[]{:S(2)}) collective-permute-start(bf16[2,16,1280]{2,1,0:T(8,128)(2,1)S(1)} %maximum_select_fusion.13), channel_id=1, source_target_pairs={{0,4},{1,5},{2,6},{3,7},{4,0},{5,1},{6,2},{7,3},{8,12},{9,13},{10,... | collective-permute-start | bytes 245768 | tf_op jit(solution)/shard_map/ppermute | solution.py:550
  16.8 4.5 %collective-permute-start.4 = (bf16[2,2,16,640]{3,2,1,0:T(8,128)(2,1)S(1)}, bf16[2,2,16,640]{3,2,1,0:T(8,128)(2,1)S(1)}, u32[]{:S(2)}, u32[]{:S(2)}) collective-permute-start(bf16[2,2,16,640]{3,2,1,0:T(8,128)(2,1)S(1)} %get-tuple-element.182), channel_id=1, source_target_pairs={{0,16},{1,17},{2,18},{3,19},{4,20},{5,21},{6,22},{7,23},{8,24},{9,... | collective-permute-start | bytes 245768 | tf_op jit(solution)/shard_map/ppermute | solution.py:550
  18.4 4.6 %collective-permute-start.2 = (bf16[2,2,16,640]{3,2,1,0:T(8,128)(2,1)S(1)}, bf16[2,2,16,640]{3,2,1,0:T(8,128)(2,1)S(1)}, u32[]{:S(2)}, u32[]{:S(2)}) collective-permute-start(bf16[2,2,16,640]{3,2,1,0:T(8,128)(2,1)S(1)} %get-tuple-element.183), channel_id=1, source_target_pairs={{0,2},{1,3},{2,0},{3,1},{4,6},{5,7},{6,4},{7,5},{8,10},{9,11},{10,... | collective-permute-start | bytes 245768 | tf_op jit(solution)/shard_map/ppermute | solution.py:550
  21.3 5.4 %collective-permute-start.5 = (bf16[2,2,2,16,640]{4,3,2,1,0:T(8,128)(2,1)S(1)}, bf16[2,2,2,16,640]{4,3,2,1,0:T(8,128)(2,1)S(1)}, u32[]{:S(2)}, u32[]{:S(2)}) collective-permute-start(bf16[2,2,2,16,640]{4,3,2,1,0:T(8,128)(2,1)S(1)} %maximum_select_fusion.11), channel_id=1, source_target_pairs={{0,2},{1,3},{2,0},{3,1},{4,6},{5,7},{6,4},{7,5},{8,10},{9,11},{10,... | collective-permute-start | bytes 491528 | tf_op jit(solution)/shard_map/ppermute | solution.py:550
  23.0 5.4 %collective-permute-start.3 = (bf16[2,2,2,16,640]{4,3,1,0,2:T(8,128)(2,1)S(1)}, bf16[2,2,2,16,640]{4,3,1,0,2:T(8,128)(2,1)S(1)}, u32[]{:S(2)}, u32[]{:S(2)}) collective-permute-start(bf16[2,2,2,16,640]{4,3,1,0,2:T(8,128)(2,1)S(1)} %maximum_select_fusion.9), channel_id=1, source_target_pairs={{0,16},{1,17},{2,18},{3,19},{4,20},{5,21},{6,22},{7,23},{8,24},{9,... | collective-permute-start | bytes 491528 | tf_op jit(solution)/shard_map/ppermute | solution.py:550
  24.5 6.4 %collective-permute-start.8 = (bf16[2,16,4096]{2,1,0:T(8,128)(2,1)S(1)}, bf16[2,16,4096]{2,1,0:T(8,128)(2,1)S(1)}, u32[]{:S(2)}, u32[]{:S(2)}) collective-permute-start(bf16[2,16,4096]{2,1,0:T(8,128)(2,1)S(1)} %maximum_select_fusion.7), channel_id=1, source_target_pairs={{0,4},{1,5},{2,6},{3,7},{4,0},{5,1},{6,2},{7,3},{8,12},{9,13},{10,... | collective-permute-start | bytes 786440 | tf_op jit(solution)/shard_map/ppermute | solution.py:550
  28.6 28.1 %copy-start.9 = (bf16[16,16,1280]{2,1,0:T(8,128)(2,1)}, bf16[16,16,1280]{2,1,0:T(8,128)(2,1)S(1)}, u32[]{:S(2)}) copy-start(bf16[16,16,1280]{2,1,0:T(8,128)(2,1)S(1)} %pad_maximum_fusion.refs_0_) | copy-start | bytes 1966084
  28.6 2.4 %collective-permute-start.6 = (bf16[16,16,1280]{2,1,0:T(8,128)(2,1)S(1)}, bf16[16,16,1280]{2,1,0:T(8,128)(2,1)S(1)}, u32[]{:S(2)}, u32[]{:S(2)}) collective-permute-start(bf16[16,16,1280]{2,1,0:T(8,128)(2,1)S(1)} %pad_maximum_fusion.refs_0_), channel_id=1, source_target_pairs={{0,1},{1,0},{2,3},{3,2},{4,5},{5,4},{6,7},{7,6},{8,9},{9,8},{10,11... | collective-permute-start | bytes 1966088 | tf_op jit(solution)/shard_map/ppermute | solution.py:550
  31.0 10.3 %collective-permute-start.9 = (bf16[2,2,16,2048]{3,2,0,1:T(8,128)(2,1)S(1)}, bf16[2,2,16,2048]{3,2,0,1:T(8,128)(2,1)S(1)}, u32[]{:S(2)}, u32[]{:S(2)}) collective-permute-start(bf16[2,2,16,2048]{3,2,0,1:T(8,128)(2,1)S(1)} %get-tuple-element.95), channel_id=1, source_target_pairs={{0,2},{1,3},{2,0},{3,1},{4,6},{5,7},{6,4},{7,5},{8,10},{9,11},{10,... | collective-permute-start | bytes 786440 | tf_op jit(solution)/shard_map/ppermute | solution.py:550
  32.3 9.2 %collective-permute-start.10 = (bf16[2,2,16,2048]{3,2,0,1:T(8,128)(2,1)S(1)}, bf16[2,2,16,2048]{3,2,0,1:T(8,128)(2,1)S(1)}, u32[]{:S(2)}, u32[]{:S(2)}) collective-permute-start(bf16[2,2,16,2048]{3,2,0,1:T(8,128)(2,1)S(1)} %get-tuple-element.96), channel_id=1, source_target_pairs={{0,16},{1,17},{2,18},{3,19},{4,20},{5,21},{6,22},{7,23},{8,24},{9,... | collective-permute-start | bytes 786440 | tf_op jit(solution)/shard_map/ppermute | solution.py:550
  41.6 13.0 %collective-permute-start.11 = (bf16[2,2,2,16,2048]{4,3,0,1,2:T(8,128)(2,1)S(1)}, bf16[2,2,2,16,2048]{4,3,0,1,2:T(8,128)(2,1)S(1)}, u32[]{:S(2)}, u32[]{:S(2)}) collective-permute-start(bf16[2,2,2,16,2048]{4,3,0,1,2:T(8,128)(2,1)S(1)} %maximum_select_fusion.3), channel_id=1, source_target_pairs={{0,16},{1,17},{2,18},{3,19},{4,20},{5,21},{6,22},{7,23},{8,24},{9,... | collective-permute-start | bytes 1572872 | tf_op jit(solution)/shard_map/ppermute | solution.py:550
  42.7 13.1 %collective-permute-start.12 = (bf16[2,2,2,16,2048]{4,3,1,2,0:T(8,128)(2,1)S(1)}, bf16[2,2,2,16,2048]{4,3,1,2,0:T(8,128)(2,1)S(1)}, u32[]{:S(2)}, u32[]{:S(2)}) collective-permute-start(bf16[2,2,2,16,2048]{4,3,1,2,0:T(8,128)(2,1)S(1)} %maximum_select_fusion.4), channel_id=1, source_target_pairs={{0,2},{1,3},{2,0},{3,1},{4,6},{5,7},{6,4},{7,5},{8,10},{9,11},{10,... | collective-permute-start | bytes 1572872 | tf_op jit(solution)/shard_map/ppermute | solution.py:550
  56.1 5.1 %collective-permute-start.13 = (bf16[16,16,2048]{2,1,0:T(8,128)(2,1)S(1)}, bf16[16,16,2048]{2,1,0:T(8,128)(2,1)S(1)}, u32[]{:S(2)}, u32[]{:S(2)}) collective-permute-start(bf16[16,16,2048]{2,1,0:T(8,128)(2,1)S(1)} %bitcast.114), channel_id=1, source_target_pairs={{0,1},{1,0},{2,3},{3,2},{4,5},{5,4},{6,7},{7,6},{8,9},{9,8},{10,11... | collective-permute-start | bytes 3145736 | tf_op jit(solution)/shard_map/ppermute | solution.py:550
  56.2 5.1 %collective-permute-start.14 = (bf16[16,16,2048]{2,1,0:T(8,128)(2,1)S(1)}, bf16[16,16,2048]{2,1,0:T(8,128)(2,1)S(1)}, u32[]{:S(2)}, u32[]{:S(2)}) collective-permute-start(bf16[16,16,2048]{2,1,0:T(8,128)(2,1)S(1)} %bitcast.119), channel_id=1, source_target_pairs={{0,1},{1,0},{2,3},{3,2},{4,5},{5,4},{6,7},{7,6},{8,9},{9,8},{10,11... | collective-permute-start | bytes 3145736 | tf_op jit(solution)/shard_map/ppermute | solution.py:550
  88.6 9.2 %collective-permute-start.16 = (bf16[16,16,2048]{2,1,0:T(8,128)(2,1)}, bf16[16,16,2048]{2,1,0:T(8,128)(2,1)}, u32[]{:S(2)}, u32[]{:S(2)}) collective-permute-start(bf16[16,16,2048]{2,1,0:T(8,128)(2,1)} %get-tuple-element.119), channel_id=1, source_target_pairs={{0,1},{1,0},{2,3},{3,2},{4,5},{5,4},{6,7},{7,6},{8,9},{9,8},{10,11... | collective-permute-start | bytes 3145736 | tf_op jit(solution)/shard_map/ppermute | solution.py:550
  88.7 11.6 %collective-permute-start.15 = (bf16[16,16,2048]{2,1,0:T(8,128)(2,1)}, bf16[16,16,2048]{2,1,0:T(8,128)(2,1)S(1)}, u32[]{:S(2)}, u32[]{:S(2)}) collective-permute-start(bf16[16,16,2048]{2,1,0:T(8,128)(2,1)} %get-tuple-element.117), channel_id=1, source_target_pairs={{0,1},{1,0},{2,3},{3,2},{4,5},{5,4},{6,7},{7,6},{8,9},{9,8},{10,11... | collective-permute-start | bytes 3145736 | tf_op jit(solution)/shard_map/ppermute | solution.py:550
  99.6 14.5 %collective-permute-start.18 = (bf16[2,2,2,16,2048]{4,3,1,2,0:T(8,128)(2,1)S(1)}, bf16[2,2,2,16,2048]{4,3,1,2,0:T(8,128)(2,1)S(1)}, u32[]{:S(2)}, u32[]{:S(2)}) collective-permute-start(bf16[2,2,2,16,2048]{4,3,1,2,0:T(8,128)(2,1)S(1)} %copy_bitcast_fusion), channel_id=1, source_target_pairs={{0,2},{1,3},{2,0},{3,1},{4,6},{5,7},{6,4},{7,5},{8,10},{9,11},{10,... | collective-permute-start | bytes 1572872 | tf_op jit(solution)/shard_map/ppermute | solution.py:550
  100.8 14.8 %collective-permute-start.17 = (bf16[2,2,2,16,2048]{4,3,0,1,2:T(8,128)(2,1)S(1)}, bf16[2,2,2,16,2048]{4,3,0,1,2:T(8,128)(2,1)S(1)}, u32[]{:S(2)}, u32[]{:S(2)}) collective-permute-start(bf16[2,2,2,16,2048]{4,3,0,1,2:T(8,128)(2,1)S(1)} %copy_bitcast_fusion.1), channel_id=1, source_target_pairs={{0,16},{1,17},{2,18},{3,19},{4,20},{5,21},{6,22},{7,23},{8,24},{9,... | collective-permute-start | bytes 1572872 | tf_op jit(solution)/shard_map/ppermute | solution.py:550
  114.3 8.1 %collective-permute-start.20 = (bf16[2,2,16,2048]{3,2,0,1:T(8,128)(2,1)S(1)}, bf16[2,2,16,2048]{3,2,0,1:T(8,128)(2,1)S(1)}, u32[]{:S(2)}, u32[]{:S(2)}) collective-permute-start(bf16[2,2,16,2048]{3,2,0,1:T(8,128)(2,1)S(1)} %dynamic-slice_bitcast_fusion.1), channel_id=1, source_target_pairs={{0,16},{1,17},{2,18},{3,19},{4,20},{5,21},{6,22},{7,23},{8,24},{9,... | collective-permute-start | bytes 786440 | tf_op jit(solution)/shard_map/ppermute | solution.py:550
  115.8 7.8 %collective-permute-start.19 = (bf16[2,2,16,2048]{3,2,0,1:T(8,128)(2,1)S(1)}, bf16[2,2,16,2048]{3,2,0,1:T(8,128)(2,1)S(1)}, u32[]{:S(2)}, u32[]{:S(2)}) collective-permute-start(bf16[2,2,16,2048]{3,2,0,1:T(8,128)(2,1)S(1)} %dynamic-slice_bitcast_fusion.2), channel_id=1, source_target_pairs={{0,2},{1,3},{2,0},{3,1},{4,6},{5,7},{6,4},{7,5},{8,10},{9,11},{10,... | collective-permute-start | bytes 786440 | tf_op jit(solution)/shard_map/ppermute | solution.py:550
  123.7 6.9 %collective-permute-start.21 = (bf16[2,16,4096]{2,1,0:T(8,128)(2,1)S(1)}, bf16[2,16,4096]{2,1,0:T(8,128)(2,1)S(1)}, u32[]{:S(2)}, u32[]{:S(2)}) collective-permute-start(bf16[2,16,4096]{2,1,0:T(8,128)(2,1)S(1)} %dynamic-slice_bitcast_fusion), channel_id=1, source_target_pairs={{0,4},{1,5},{2,6},{3,7},{4,0},{5,1},{6,2},{7,3},{8,12},{9,13},{10,... | collective-permute-start | bytes 786440 | tf_op jit(solution)/shard_map/ppermute | solution.py:550
  130.7 7.5 %collective-permute-start.25 = (bf16[16,4096]{1,0:T(8,128)(2,1)S(1)}, bf16[16,4096]{1,0:T(8,128)(2,1)S(1)}, u32[]{:S(2)}, u32[]{:S(2)}) collective-permute-start(bf16[16,4096]{1,0:T(8,128)(2,1)S(1)} %dynamic-slice_bitcast_fusion.3), channel_id=1, source_target_pairs={{0,8},{1,9},{2,10},{3,11},{4,12},{5,13},{6,14},{7,15},{8,0},{9,1},... | collective-permute-start | bytes 393224 | tf_op jit(solution)/shard_map/ppermute | solution.py:550
  137.0 2.2 %collective-permute-start.22 = (bf16[16,16,1280]{2,1,0:T(8,128)(2,1)S(1)}, bf16[16,16,1280]{2,1,0:T(8,128)(2,1)S(1)}, u32[]{:S(2)}, u32[]{:S(2)}) collective-permute-start(bf16[16,16,1280]{2,1,0:T(8,128)(2,1)S(1)} %get-tuple-element.145), channel_id=1, source_target_pairs={{0,1},{1,0},{2,3},{3,2},{4,5},{5,4},{6,7},{7,6},{8,9},{9,8},{10,11... | collective-permute-start | bytes 1966088 | tf_op jit(solution)/shard_map/ppermute | solution.py:550
  139.5 6.8 %collective-permute-start.23 = (bf16[2,2,2,16,640]{4,3,0,1,2:T(8,128)(2,1)S(1)}, bf16[2,2,2,16,640]{4,3,0,1,2:T(8,128)(2,1)S(1)}, u32[]{:S(2)}, u32[]{:S(2)}) collective-permute-start(bf16[2,2,2,16,640]{4,3,0,1,2:T(8,128)(2,1)S(1)} %bitcast.154), channel_id=1, source_target_pairs={{0,16},{1,17},{2,18},{3,19},{4,20},{5,21},{6,22},{7,23},{8,24},{9,... | collective-permute-start | bytes 491528 | tf_op jit(solution)/shard_map/ppermute | solution.py:550
  140.7 6.0 %collective-permute-start.24 = (bf16[2,2,2,16,640]{4,3,1,2,0:T(8,128)(2,1)S(1)}, bf16[2,2,2,16,640]{4,3,1,2,0:T(8,128)(2,1)S(1)}, u32[]{:S(2)}, u32[]{:S(2)}) collective-permute-start(bf16[2,2,2,16,640]{4,3,1,2,0:T(8,128)(2,1)S(1)} %bitcast.155), channel_id=1, source_target_pairs={{0,2},{1,3},{2,0},{3,1},{4,6},{5,7},{6,4},{7,5},{8,10},{9,11},{10,... | collective-permute-start | bytes 491528 | tf_op jit(solution)/shard_map/ppermute | solution.py:550
  146.8 8.2 %collective-permute-start.27 = (bf16[2,2,16,640]{3,2,0,1:T(8,128)(2,1)S(1)}, bf16[2,2,16,640]{3,2,0,1:T(8,128)(2,1)S(1)}, u32[]{:S(2)}, u32[]{:S(2)}) collective-permute-start(bf16[2,2,16,640]{3,2,0,1:T(8,128)(2,1)S(1)} %dynamic-slice_bitcast_fusion.5), channel_id=1, source_target_pairs={{0,16},{1,17},{2,18},{3,19},{4,20},{5,21},{6,22},{7,23},{8,24},{9,... | collective-permute-start | bytes 245768 | tf_op jit(solution)/shard_map/ppermute | solution.py:550
  147.8 7.3 %collective-permute-start.26 = (bf16[2,2,16,640]{3,2,0,1:T(8,128)(2,1)S(1)}, bf16[2,2,16,640]{3,2,0,1:T(8,128)(2,1)S(1)}, u32[]{:S(2)}, u32[]{:S(2)}) collective-permute-start(bf16[2,2,16,640]{3,2,0,1:T(8,128)(2,1)S(1)} %dynamic-slice_bitcast_fusion.6), channel_id=1, source_target_pairs={{0,2},{1,3},{2,0},{3,1},{4,6},{5,7},{6,4},{7,5},{8,10},{9,11},{10,... | collective-permute-start | bytes 245768 | tf_op jit(solution)/shard_map/ppermute | solution.py:550
  155.2 4.8 %collective-permute-start.28 = (bf16[2,16,1280]{2,1,0:T(8,128)(2,1)S(1)}, bf16[2,16,1280]{2,1,0:T(8,128)(2,1)S(1)}, u32[]{:S(2)}, u32[]{:S(2)}) collective-permute-start(bf16[2,16,1280]{2,1,0:T(8,128)(2,1)S(1)} %dynamic-slice_bitcast_fusion.4), channel_id=1, source_target_pairs={{0,4},{1,5},{2,6},{3,7},{4,0},{5,1},{6,2},{7,3},{8,12},{9,13},{10,... | collective-permute-start | bytes 245768 | tf_op jit(solution)/shard_map/ppermute | solution.py:550
  160.7 4.9 %collective-permute-start.29 = (bf16[16,1280]{1,0:T(8,128)(2,1)S(1)}, bf16[16,1280]{1,0:T(8,128)(2,1)S(1)}, u32[]{:S(2)}, u32[]{:S(2)}) collective-permute-start(bf16[16,1280]{1,0:T(8,128)(2,1)S(1)} %get-tuple-element.184), channel_id=1, source_target_pairs={{0,8},{1,9},{2,10},{3,11},{4,12},{5,13},{6,14},{7,15},{8,0},{9,1},... | collective-permute-start | bytes 122888 | tf_op jit(solution)/shard_map/ppermute | solution.py:550
  (33 other events, 193.1 us)

commit v5 on v4

--- a/solution.py
+++ b/solution.py
@@ -16,7 +16,7 @@
 TILE = 256
 STEP = 512
 ROOM = {
-    "project": 12, "attend": 14, "mix": 10, "feed": 29, "turn": 18, "gates": 12, "attend_back": 28, "sums": 14, "close": 14,
+    "project": 12, "attend": 14, "mix": 10, "feed": 25, "turn": 18, "gates": 12, "attend_back": 28, "sums": 14, "close": 14,
     "result": 18,
 }
 
@@ -479,7 +479,7 @@
 
 
 def result_kernel(n, me, act, x1, vec, *refs):
-    res_o, wd, sem = refs[2 * n :]
+    res_o, wd, sem = refs[-3:]
     depth = x1.shape[1]
 
     @pl.when(pl.program_id(0) == 0)
@@ -622,7 +622,9 @@
         held = small
         for at in range(early):
             held = grow(held, orders[0], at)
-        big = grow(large, orders[0], 0)
+            if at == 0:
+                big = after(large, held)
+        big = grow(big, orders[0], 0)
         parts = [held[..., : first_width // 2], held[..., first_width // 2 :]]
         for at in range(early, steps - 1):
             parts = [grow(part, order, at) for part, order in zip(parts, orders)]
@@ -641,6 +643,7 @@
 
     smem = pl.BlockSpec(memory_space=pltpu.SMEM)
     hbm = pl.BlockSpec(memory_space=pl.ANY)
+    vmem = pl.BlockSpec(memory_space=pltpu.VMEM)
     dma = pltpu.SemaphoreType.DMA
 
     def whole(dims):
@@ -722,14 +725,11 @@
 
     wide = 256
 
-    def once(dims):
-        return pl.BlockSpec(dims, lambda *_: (0,) * len(dims), pipeline_mode=pl.Buffered(1))
-
     column = pl.BlockSpec((total, wide), lambda s: (0, jnp.minimum(s, inner // wide - 1)))
     act, dz, bias, *f_grads = call(
         functools.partial(ffn_kernel, n), "feed", 25.0, (inner // wide + 1,),
         (core, h2, cotangent, vec, *flat_f),
-        [smem, once((total, depth)), once((total, depth)), whole((32, depth))] + [hbm] * 2 * n,
+        [smem, vmem, vmem, whole((32, depth))] + [hbm] * 2 * n,
         [far((total, inner), BF), far((total, inner), BF), shape((8, depth), F32)]
         + [far((blocks, block, 4 * depth), BF)] * 2 * n,
         [column, column, whole((8, depth))] + [hbm] * 2 * n,
@@ -753,7 +753,7 @@
             scratch_shapes=[pltpu.VMEM((2, depth, inner // 2), BF), dma],
             input_output_aliases={6: 0, 7: 1} if again else {},
             compiler_params=pltpu.CompilerParams(vmem_limit_bytes=ROOM["turn"] << 20), cost_estimate=cost(6.0), name="turn",
-        )(core, keep_far(dz), cotangent, keep_far(x1), vec, *again, *flat_f)
+        )(core, keep_far(dz), keep_far(cotangent), keep_far(x1), vec, *again, *flat_f)
 
     dx1, low, sums = turn(0, ())
     if fast:
@@ -854,14 +854,25 @@
     if fast:
         closing = after(x1, *tails)
         tails = [fall(after(part, grad_tokens), order, 1) for part, order in zip(tails, back_orders)]
-    result = call(
-        functools.partial(result_kernel, n), "result", 6.0, (tiles,),
-        (core, act, closing, vec, *flat_f),
-        [smem, tile(inner), tile(depth), whole((32, depth))] + [hbm] * 2 * n,
-        [shape((total, depth), BF)],
-        [tile(depth)],
-        [pltpu.VMEM((inner, depth), BF), dma],
-    )[0]
+    def results(begin, again, x1):
+        def part(wide):
+            return pl.BlockSpec((span, wide), lambda t: (t + begin, 0))
+
+        return pl.pallas_call(
+            functools.partial(result_kernel, n), grid=(tiles // 2,),
+            in_specs=[smem, part(inner), part(depth), whole((32, depth))] + [hbm] * 2 * n + [hbm] * len(again),
+            out_specs=[part(depth)],
+            out_shape=[shape((total, depth), BF)],
+            scratch_shapes=[pltpu.VMEM((inner, depth), BF), dma],
+            input_output_aliases={4 + 2 * n: 0} if again else {},
+            compiler_params=pltpu.CompilerParams(vmem_limit_bytes=ROOM["result"] << 20), cost_estimate=cost(3.5), name="result",
+        )(core, act, x1, vec, *flat_f, *again)
+
+    result = results(0, (), closing)
+    if fast:
+        tail = after(jnp.concatenate(tails, -1), *result)
+        tail = fall(tail, late, 2, F32 if len(late) == 3 else BF)
+    result = results(tiles // 2, result, closing)[0]
 
     def unpacked(halves):
         up = jnp.concatenate([half[:, : 2 * depth] for half in halves], 1)
@@ -870,11 +881,12 @@
         return up, down.reshape(share, subs, depth).transpose(1, 0, 2).reshape(subs * share, depth)
 
     if fast:
-        tail = after(jnp.concatenate(tails, -1), result)
+        tail = after(tail, result)
+        acc = after(acc, result)
         grad_up, grad_down = unpacked([acc[:, : 4 * depth], acc[:, 4 * depth :]])
-        for at in range(2, len(late) - 1):
+        for at in range(3, len(late) - 1):
             tail = fall(tail, late, at)
-        keep, send = parted(after(tail, grad_up, grad_down), late[-1:], late[-1], me)
+        keep, send = parted(tail, late[-1:], late[-1], me)
         own = functools.partial(jax.ShapeDtypeStruct, dtype=F32)
         grad_query, grad_key, grad_value, grad_out, grad_router, *lines = pl.pallas_call(
             functools.partial(finish_kernel, 1.0 / (total * count)),

time: 168 us -> 161 us (0.958)
  waiting for transfers between devices: 22.2 us -> 13 us
  starting transfers between devices: 33.9 us -> 37.5 us
  local copies, waits for them, and re-layouts: 10.7 us -> 8.6 us
    ppermute x30, waiting for transfers between devices: 22.2 us -> 13 us  [move(): return lax.ppermute(value, AXES, xor_pairs(count, mask))]
    pallas_call x0 -> x2, Pallas kernels: none -> 7 us  [results(): pl.pallas_call(functools.partial(result_kernel, n), grid=(tiles // 2,), i...]
    pallas_call x8 -> x7, Pallas kernels: 69.7 us -> 63.1 us  [call(): pl.pallas_call(kernel, grid=grid, in_specs=in_specs, out_specs=out_specs,...]
    ppermute x30, starting transfers between devices: 33.9 us -> 37.5 us  [move(): return lax.ppermute(value, AXES, xor_pairs(count, mask))]
    unnamed x74 -> x70, local copies, waits for them, and re-layouts: 6.04 us -> 3.96 us
  transfers between devices with their start and end apart: 30 -> 30, of which waited for: 15 -> 15; matrix products, arithmetic and copies ran while one was open for 5% -> 5% of each run, Pallas kernels for 39% -> 41%
where the time goes in v5:
time: 161 us
  Pallas kernels  96.2 us (60%)
  starting transfers between devices  37.5 us (23%)
  waiting for transfers between devices  13 us (8%)
  local copies, waits for them, and re-layouts  8.6 us (5%)
  other arithmetic  3.82 us (2%)
  between operations  1.76 us (1%)
    pallas_call x7, Pallas kernels, call(): pl.pallas_call(kernel, grid=grid, in_specs=in_specs, out_specs=out_specs,...  63.1 us
    ppermute x30, starting transfers between devices, move(): return lax.ppermute(value, AXES, xor_pairs(count, mask))  37.5 us
    ppermute x30, waiting for transfers between devices, move(): return lax.ppermute(value, AXES, xor_pairs(count, mask))  13 us
    pallas_call x2, Pallas kernels, turn(): pl.pallas_call(functools.partial(turn_kernel, n, len(again) > 0), grid=(t...  11.7 us
    pallas_call x2, Pallas kernels, back(): pl.pallas_call(attend_back_kernel, grid=(per_row,), in_specs=[part(2), bo...  11.4 us
    pallas_call x2, Pallas kernels, results(): pl.pallas_call(functools.partial(result_kernel, n), grid=(tiles // 2,), i...  7 us
    unnamed x70, local copies, waits for them, and re-layouts  3.96 us
  transfers between devices with their start and end apart: 30, of which 15 were waited for; matrix products, arithmetic and copies ran while one was open for 5% of the time, Pallas kernels for 41%

profile of v5, /device:TPU:0, one launch (start us, length us, event | category | flops | bytes accessed | tf_op | source)
XLA Modules:
  0.0 160.9 jit_solution(13681348597836618802)
XLA Ops:
  0.7 1.5 pack.1
  2.1 4.1 %collective-permute-start = (bf16[16,1280]{1,0:T(8,128)(2,1)S(1)}, bf16[16,1280]{1,0:T(8,128)(2,1)S(1)}, u32[]{:S(2)}, u32[]{:S(2)}) collective-permute-start(bf16[16,1280]{1,0:T(8,128)(2,1)S(1)} %get-tuple-element.93), channel_id=1, source_target_pairs={{0,8},{1,9},{2,10},{3,11},{4,12},{5,13},{6,14},{7,15},{8,0},{9,1},... | collective-permute-start | bytes 122888 | tf_op jit(solution)/shard_map/ppermute | solution.py:550
  8.6 1.5 collective-permute-start.1
  10.2 2.9 %collective-permute-start.7 = (bf16[16,4096]{1,0:T(8,128)(2,1)S(1)}, bf16[16,4096]{1,0:T(8,128)(2,1)S(1)}, u32[]{:S(2)}, u32[]{:S(2)}) collective-permute-start(bf16[16,4096]{1,0:T(8,128)(2,1)S(1)} %get-tuple-element.96), channel_id=1, source_target_pairs={{0,8},{1,9},{2,10},{3,11},{4,12},{5,13},{6,14},{7,15},{8,0},{9,1},... | collective-permute-start | bytes 393224 | tf_op jit(solution)/shard_map/ppermute | solution.py:550
  13.9 1.7 %collective-permute-start.4 = (bf16[2,2,16,640]{3,2,1,0:T(8,128)(2,1)S(1)}, bf16[2,2,16,640]{3,2,1,0:T(8,128)(2,1)S(1)}, u32[]{:S(2)}, u32[]{:S(2)}) collective-permute-start(bf16[2,2,16,640]{3,2,1,0:T(8,128)(2,1)S(1)} %get-tuple-element.186), channel_id=1, source_target_pairs={{0,16},{1,17},{2,18},{3,19},{4,20},{5,21},{6,22},{7,23},{8,24},{9,... | collective-permute-start | bytes 245768 | tf_op jit(solution)/shard_map/ppermute | solution.py:550
  15.6 1.5 collective-permute-start.2
  18.5 1.6 %collective-permute-start.5 = (bf16[2,2,2,16,640]{4,3,2,1,0:T(8,128)(2,1)S(1)}, bf16[2,2,2,16,640]{4,3,2,1,0:T(8,128)(2,1)S(1)}, u32[]{:S(2)}, u32[]{:S(2)}) collective-permute-start(bf16[2,2,2,16,640]{4,3,2,1,0:T(8,128)(2,1)S(1)} %maximum_select_fusion.11), channel_id=1, source_target_pairs={{0,2},{1,3},{2,0},{3,1},{4,6},{5,7},{6,4},{7,5},{8,10},{9,11},{10,... | collective-permute-start | bytes 491528 | tf_op jit(solution)/shard_map/ppermute | solution.py:550
  20.3 1.5 collective-permute-start.3
  21.7 2.2 %collective-permute-start.8 = (bf16[2,16,4096]{2,1,0:T(8,128)(2,1)S(1)}, bf16[2,16,4096]{2,1,0:T(8,128)(2,1)S(1)}, u32[]{:S(2)}, u32[]{:S(2)}) collective-permute-start(bf16[2,16,4096]{2,1,0:T(8,128)(2,1)S(1)} %maximum_select_fusion.7), channel_id=1, source_target_pairs={{0,4},{1,5},{2,6},{3,7},{4,0},{5,1},{6,2},{7,3},{8,12},{9,13},{10,... | collective-permute-start | bytes 786440 | tf_op jit(solution)/shard_map/ppermute | solution.py:550
  24.0 1.6 %collective-permute-done.3 = bf16[2,2,2,16,640]{4,3,1,0,2:T(8,128)(2,1)S(1)} collective-permute-done((bf16[2,2,2,16,640]{4,3,1,0,2:T(8,128)(2,1)S(1)}, bf16[2,2,2,16,640]{4,3,1,0,2:T(8,128)(2,1)S(1)}, u32[]{:S(2)}, u32[]{:S(2)}) %collective-permute-start.3) | collective-permute-done | bytes 163872 | tf_op jit(solution)/shard_map/ppermute | solution.py:550
  25.9 2.3 %collective-permute-done.8 = bf16[2,16,4096]{2,1,0:T(8,128)(2,1)S(1)} collective-permute-done((bf16[2,16,4096]{2,1,0:T(8,128)(2,1)S(1)}, bf16[2,16,4096]{2,1,0:T(8,128)(2,1)S(1)}, u32[]{:S(2)}, u32[]{:S(2)}) %collective-permute-start.8) | collective-permute-done | bytes 262176 | tf_op jit(solution)/shard_map/ppermute | solution.py:550
  30.4 8.1 %project.1 = (bf16[2048,512]{1,0:T(8,128)(2,1)}, bf16[2,2048,128]{2,1,0:T(8,128)(2,1)S(1)}, bf16[2048,256]{1,0:T(8,128)(2,1)}, bf16[2048,256]{1,0:T(8,128)(2,1)}...) custom-call(s32[1]{0:T(128)} %bitcast.me, s32[2,4]{1,0:T(2,128)S(1)} %copy-done.13, bf16[2048,512]{1,0:T(8,128)(2,1)} %tok.5, ...), custom_call_target="tpu_custom_call" | custom-call | flops 8999999488 | bytes 1024 | tf_op jit(solution)/shard_map/project/pallas_call | solution.py:662
  41.0 10.2 %attend.1 = (f32[2048,128]{1,0:T(8,128)S(1)}, bf16[2048,512]{1,0:T(8,128)(2,1)S(1)}, bf16[2,2048,128]{2,1,0:T(8,128)(2,1)}) custom-call(s32[2,4]{1,0:T(2,128)S(1)} %copy-done.13, s32[2048,2]{1,0:T(8,128)S(1)} %copy.56.routes, bf16[2,2048,128]{2,1,0:T(8,128)(2,1)S(1)} %get-tuple-element.100.qa, bf16[2048,256]{1,0:T(8,128)(2,1)S(1)} %copy-done.19, ...), custom_call_target="tpu_custom_call" | custom-call | flops 12999999488 | bytes 1024 | tf_op jit(solution)/shard_map/attend/pallas_call | solution.py:662
  54.7 3.8 %mix.1 = (f32[2048,512]{1,0:T(8,128)}, bf16[2048,512]{1,0:T(8,128)(2,1)S(1)}) custom-call(s32[1]{0:T(128)} %bitcast.me, bf16[2048,512]{1,0:T(8,128)(2,1)S(1)} %copy-done.9, bf16[2048,512]{1,0:T(8,128)(2,1)S(1)} %get-tuple-element.107.u, f32[32,512]{1,0:T(8,128)S(1)} %get-tuple-element.108.vec, bf16[16,16,1280]{2,1,0:T(8,128)(2,1)S(1)} %pad_maximum_fusion.refs_0_, ...), custom_call_target="tpu_custom_call" | custom-call | flops 5000000000 | bytes 1024 | tf_op jit(solution)/shard_map/mix/pallas_call | solution.py:662
  58.5 27.3 %feed.1 = (bf16[2048,2048]{1,0:T(8,128)(2,1)}, bf16[2048,2048]{1,0:T(8,128)(2,1)}, f32[8,512]{1,0:T(8,128)S(1)}, bf16[16,16,2048]{2,1,0:T(8,128)(2,1)}, bf16[16,...) custom-call(s32[1]{0:T(128)} %bitcast.me, ...), custom_call_target="tpu_custom_call" | custom-call | flops 24999999488 | bytes 1024 | tf_op jit(solution)/shard_map/feed/pallas_call | solution.py:662
  87.6 5.9 %turn.2 = (f32[2048,512]{1,0:T(8,128)S(1)}, bf16[2048,512]{1,0:T(8,128)(2,1)S(1)}, f32[32,512]{1,0:T(8,128)S(1)}) custom-call(s32[1]{0:T(128)} %bitcast.me, bf16[2048,2048]{1,0:T(8,128)(2,1)} %get-tuple-element.117.dz, bf16[2048,512]{1,0:T(8,128)(2,1)} %dy.5, f32[2048,512]{1,0:T(8,128)} %get-tuple-element.149.x1, f32[32,512]{1,0:T(8,128)S(1)} %get-tuple-element.108.vec, ...), custom_call_target="tpu_custom_call" | custom-call | flops 6000000000 | bytes 1024 | tf_op jit(solution)/shard_map/turn/pallas_call | solution.py:747
  93.6 1.7 %add_convert_fusion = bf16[16,16,2048]{2,1,0:T(8,128)(2,1)S(1)} fusion(bf16[16,16,2048]{2,1,0:T(8,128)(2,1)} %collective-permute-done.16, bf16[16,16,2048]{2,1,0:T(8,128)(2,1)S(1)} %copy-done.29), kind=kLoop, calls=%fused_computation | loop fusion | flops 2097152 | bytes 3145728 | tf_op jit(solution)/shard_map/convert_element_type | solution.py:571
  97.9 5.8 %turn.3 = (f32[2048,512]{1,0:T(8,128)S(1)}, bf16[2048,512]{1,0:T(8,128)(2,1)S(1)}, f32[32,512]{1,0:T(8,128)S(1)}) custom-call(s32[1]{0:T(128)} %bitcast.me, bf16[2048,2048]{1,0:T(8,128)(2,1)} %get-tuple-element.117.dz, bf16[2048,512]{1,0:T(8,128)(2,1)} %dy.5, f32[2048,512]{1,0:T(8,128)} %get-tuple-element.149.x1, ...), custom_call_target="tpu_custom_call", output_to_operand_aliasing={{0}: (6, {}), {1}: (7, {})} | custom-call | flops 6000000000 | bytes 1024 | tf_op jit(solution)/shard_map/turn/pallas_call | solution.py:747
  103.8 6.1 %gates.1 = (bf16[2,2048,128]{2,1,0:T(8,128)(2,1)S(1)}, bf16[2,2048,128]{2,1,0:T(8,128)(2,1)S(1)}, bf16[2048,128]{1,0:T(8,128)(2,1)S(1)}, f32[8,128]{1,0:T(8,128)S(1)}, bf16[512,512]{1,0:T(8,128)(2,1)S(1)}) custom-call(s32[1]{0:T(128)} %bitcast.me, bf16[2048,512]{1,0:T(8,128)(2,1)S(1)} %get-tuple-element.126.dx1, s32[2048,2]{1,0:T(8,128)S(1)} %copy-done.6, ...), custom_call_target="tpu_custom_call" | custom-call | flops 8999999488 | bytes 1024 | tf_op jit(solution)/shard_map/gates/pallas_call | solution.py:662
  111.0 1.5 collective-permute-start.19
  112.5 5.7 %attend_back.2 = (bf16[2048,512]{1,0:T(8,128)(2,1)S(1)}, bf16[2048,128]{1,0:T(8,128)(2,1)S(1)}) custom-call(s32[2048,2]{1,0:T(8,128)S(1)} %copy-done.6, bf16[2,2048,128]{2,1,0:T(8,128)(2,1)S(1)} %copy-done.18, bf16[2,2048,128]{2,1,0:T(8,128)(2,1)S(1)} %copy-done.23, bf16[2048,256]{1,0:T(8,128)(2,1)S(1)} %copy-done.20, bf16[2048,256]{1,0:T(8,128)(2,1)S(1)} %copy-done.22, ...), custom_call_target="tpu_custom_call" | custom-call | flops 8000000000 | bytes 1024 | tf_op jit(solution)/shard_map/attend_back/pallas_call | solution.py:797
  119.0 2.3 %collective-permute-start.21 = (bf16[2,16,4096]{2,1,0:T(8,128)(2,1)S(1)}, bf16[2,16,4096]{2,1,0:T(8,128)(2,1)S(1)}, u32[]{:S(2)}, u32[]{:S(2)}) collective-permute-start(bf16[2,16,4096]{2,1,0:T(8,128)(2,1)S(1)} %dynamic-slice_bitcast_fusion), channel_id=1, source_target_pairs={{0,4},{1,5},{2,6},{3,7},{4,0},{5,1},{6,2},{7,3},{8,12},{9,13},{10,... | collective-permute-start | bytes 786440 | tf_op jit(solution)/shard_map/ppermute | solution.py:550
  121.2 5.7 %attend_back.3 = (bf16[2048,512]{1,0:T(8,128)(2,1)S(1)}, bf16[2048,128]{1,0:T(8,128)(2,1)S(1)}) custom-call(s32[2048,2]{1,0:T(8,128)S(1)} %copy-done.6, bf16[2,2048,128]{2,1,0:T(8,128)(2,1)S(1)} %copy-done.18, bf16[2,2048,128]{2,1,0:T(8,128)(2,1)S(1)} %copy-done.23, bf16[2048,256]{1,0:T(8,128)(2,1)S(1)} %copy-done.20, ...), custom_call_target="tpu_custom_call", output_to_operand_aliasing={{0}: (7, {}), {1}: (8, {})} | custom-call | flops 8000000000 | bytes 1024 | tf_op jit(solution)/shard_map/attend_back/pallas_call | solution.py:797
  127.0 2.2 %collective-permute-start.25 = (bf16[16,4096]{1,0:T(8,128)(2,1)S(1)}, bf16[16,4096]{1,0:T(8,128)(2,1)S(1)}, u32[]{:S(2)}, u32[]{:S(2)}) collective-permute-start(bf16[16,4096]{1,0:T(8,128)(2,1)S(1)} %dynamic-slice_bitcast_fusion.3), channel_id=1, source_target_pairs={{0,8},{1,9},{2,10},{3,11},{4,12},{5,13},{6,14},{7,15},{8,0},{9,1},... | collective-permute-start | bytes 393224 | tf_op jit(solution)/shard_map/ppermute | solution.py:550
  129.3 3.6 %sums.1 = (bf16[16,16,1280]{2,1,0:T(8,128)(2,1)S(1)}, bf16[16,16,1280]{2,1,0:T(8,128)(2,1)S(1)}) custom-call(s32[1]{0:T(128)} %bitcast.me, bf16[2048,512]{1,0:T(8,128)(2,1)S(1)} %copy-done.16, bf16[2048,512]{1,0:T(8,128)(2,1)S(1)} %get-tuple-element.138.dq, bf16[2048,128]{1,0:T(8,128)(2,1)S(1)} %get-tuple-element.142.kv, ...), custom_call_target="tpu_custom_call" | custom-call | flops 6000000000 | bytes 1024 | tf_op jit(solution)/shard_map/sums/pallas_call | solution.py:662
  132.9 1.6 collective-permute-done.25
  137.2 4.1 %close.1 = bf16[2048,512]{1,0:T(8,128)(2,1)} custom-call(s32[1]{0:T(128)} %bitcast.me, f32[2048,512]{1,0:T(8,128)S(1)} %get-tuple-element.152.dx1, bf16[2048,512]{1,0:T(8,128)(2,1)S(1)} %get-tuple-element.138.dq, bf16[2048,128]{1,0:T(8,128)(2,1)S(1)} %get-tuple-element.142.kv, bf16[2048,128]{1,0:T(8,128)(2,1)S(1)} %get-tuple-element.133.ds, ...), custom_call_target="tpu_custom_call" | custom-call | flops 6000000000 | bytes 1024 | tf_op jit(solution)/shard_map/close/pallas_call | solution.py:662
  143.3 1.5 collective-permute-start.26
  144.8 3.5 %result.2.refs_4_ = bf16[2048,512]{1,0:T(8,128)(2,1)} custom-call(s32[1]{0:T(128)} %bitcast.me, bf16[2048,2048]{1,0:T(8,128)(2,1)S(1)} %bitcast.115, f32[2048,512]{1,0:T(8,128)S(1)} %copy-done, f32[32,512]{1,0:T(8,128)S(1)} %get-tuple-element.108.vec, bf16[16,16,2048]{2,1,0:T(8,128)(2,1)S(1)} %bitcast.120, ...), custom_call_target="tpu_custom_call" | custom-call | flops 3500000000 | bytes 1024 | tf_op jit(solution)/shard_map/result/pallas_call | solution.py:861
  149.5 3.5 %result.3 = bf16[2048,512]{1,0:T(8,128)(2,1)} custom-call(s32[1]{0:T(128)} %bitcast.me, bf16[2048,2048]{1,0:T(8,128)(2,1)S(1)} %bitcast.115, f32[2048,512]{1,0:T(8,128)S(1)} %copy-done, f32[32,512]{1,0:T(8,128)S(1)} %get-tuple-element.108.vec, bf16[16,16,2048]{2,1,0:T(8,128)(2,1)S(1)} %bitcast.121, ...), custom_call_target="tpu_custom_call", output_to_operand_aliasing={{}: (8, {})} | custom-call | flops 3500000000 | bytes 1024 | tf_op jit(solution)/shard_map/result/pallas_call | solution.py:861
  155.7 1.6 reshape.281
  159.2 1.6 finish.1
  (171 shorter events, 29.8 us)
Async XLA Ops:
  2.1 6.5 %collective-permute-start = (bf16[16,1280]{1,0:T(8,128)(2,1)S(1)}, bf16[16,1280]{1,0:T(8,128)(2,1)S(1)}, u32[]{:S(2)}, u32[]{:S(2)}) collective-permute-start(bf16[16,1280]{1,0:T(8,128)(2,1)S(1)} %get-tuple-element.93), channel_id=1, source_target_pairs={{0,8},{1,9},{2,10},{3,11},{4,12},{5,13},{6,14},{7,15},{8,0},{9,1},... | collective-permute-start | bytes 122888 | tf_op jit(solution)/shard_map/ppermute | solution.py:550
  7.3 33.7 %copy-start.5 = (s32[2048,2]{1,0:T(8,128)}, s32[2048,2]{1,0:T(8,128)S(1)}, u32[]{:S(2)}) copy-start(s32[2048,2]{1,0:T(8,128)S(1)} %copy.56.routes) | copy-start | bytes 49156
  8.6 5.2 %collective-permute-start.1 = (bf16[2,16,1280]{2,1,0:T(8,128)(2,1)S(1)}, bf16[2,16,1280]{2,1,0:T(8,128)(2,1)S(1)}, u32[]{:S(2)}, u32[]{:S(2)}) collective-permute-start(bf16[2,16,1280]{2,1,0:T(8,128)(2,1)S(1)} %maximum_select_fusion.13), channel_id=1, source_target_pairs={{0,4},{1,5},{2,6},{3,7},{4,0},{5,1},{6,2},{7,3},{8,12},{9,13},{10,... | collective-permute-start | bytes 245768 | tf_op jit(solution)/shard_map/ppermute | solution.py:550
  10.2 7.8 %collective-permute-start.7 = (bf16[16,4096]{1,0:T(8,128)(2,1)S(1)}, bf16[16,4096]{1,0:T(8,128)(2,1)S(1)}, u32[]{:S(2)}, u32[]{:S(2)}) collective-permute-start(bf16[16,4096]{1,0:T(8,128)(2,1)S(1)} %get-tuple-element.96), channel_id=1, source_target_pairs={{0,8},{1,9},{2,10},{3,11},{4,12},{5,13},{6,14},{7,15},{8,0},{9,1},... | collective-permute-start | bytes 393224 | tf_op jit(solution)/shard_map/ppermute | solution.py:550
  13.9 4.5 %collective-permute-start.4 = (bf16[2,2,16,640]{3,2,1,0:T(8,128)(2,1)S(1)}, bf16[2,2,16,640]{3,2,1,0:T(8,128)(2,1)S(1)}, u32[]{:S(2)}, u32[]{:S(2)}) collective-permute-start(bf16[2,2,16,640]{3,2,1,0:T(8,128)(2,1)S(1)} %get-tuple-element.186), channel_id=1, source_target_pairs={{0,16},{1,17},{2,18},{3,19},{4,20},{5,21},{6,22},{7,23},{8,24},{9,... | collective-permute-start | bytes 245768 | tf_op jit(solution)/shard_map/ppermute | solution.py:550
  15.6 4.6 %collective-permute-start.2 = (bf16[2,2,16,640]{3,2,1,0:T(8,128)(2,1)S(1)}, bf16[2,2,16,640]{3,2,1,0:T(8,128)(2,1)S(1)}, u32[]{:S(2)}, u32[]{:S(2)}) collective-permute-start(bf16[2,2,16,640]{3,2,1,0:T(8,128)(2,1)S(1)} %get-tuple-element.187), channel_id=1, source_target_pairs={{0,2},{1,3},{2,0},{3,1},{4,6},{5,7},{6,4},{7,5},{8,10},{9,11},{10,... | collective-permute-start | bytes 245768 | tf_op jit(solution)/shard_map/ppermute | solution.py:550
  18.5 5.5 %collective-permute-start.5 = (bf16[2,2,2,16,640]{4,3,2,1,0:T(8,128)(2,1)S(1)}, bf16[2,2,2,16,640]{4,3,2,1,0:T(8,128)(2,1)S(1)}, u32[]{:S(2)}, u32[]{:S(2)}) collective-permute-start(bf16[2,2,2,16,640]{4,3,2,1,0:T(8,128)(2,1)S(1)} %maximum_select_fusion.11), channel_id=1, source_target_pairs={{0,2},{1,3},{2,0},{3,1},{4,6},{5,7},{6,4},{7,5},{8,10},{9,11},{10,... | collective-permute-start | bytes 491528 | tf_op jit(solution)/shard_map/ppermute | solution.py:550
  20.3 5.4 %collective-permute-start.3 = (bf16[2,2,2,16,640]{4,3,1,0,2:T(8,128)(2,1)S(1)}, bf16[2,2,2,16,640]{4,3,1,0,2:T(8,128)(2,1)S(1)}, u32[]{:S(2)}, u32[]{:S(2)}) collective-permute-start(bf16[2,2,2,16,640]{4,3,1,0,2:T(8,128)(2,1)S(1)} %maximum_select_fusion.9), channel_id=1, source_target_pairs={{0,16},{1,17},{2,18},{3,19},{4,20},{5,21},{6,22},{7,23},{8,24},{9,... | collective-permute-start | bytes 491528 | tf_op jit(solution)/shard_map/ppermute | solution.py:550
  21.7 6.5 %collective-permute-start.8 = (bf16[2,16,4096]{2,1,0:T(8,128)(2,1)S(1)}, bf16[2,16,4096]{2,1,0:T(8,128)(2,1)S(1)}, u32[]{:S(2)}, u32[]{:S(2)}) collective-permute-start(bf16[2,16,4096]{2,1,0:T(8,128)(2,1)S(1)} %maximum_select_fusion.7), channel_id=1, source_target_pairs={{0,4},{1,5},{2,6},{3,7},{4,0},{5,1},{6,2},{7,3},{8,12},{9,13},{10,... | collective-permute-start | bytes 786440 | tf_op jit(solution)/shard_map/ppermute | solution.py:550
  25.8 28.1 %copy-start.7 = (bf16[16,16,1280]{2,1,0:T(8,128)(2,1)}, bf16[16,16,1280]{2,1,0:T(8,128)(2,1)S(1)}, u32[]{:S(2)}) copy-start(bf16[16,16,1280]{2,1,0:T(8,128)(2,1)S(1)} %pad_maximum_fusion.refs_0_) | copy-start | bytes 1966084
  25.8 2.5 %collective-permute-start.6 = (bf16[16,16,1280]{2,1,0:T(8,128)(2,1)S(1)}, bf16[16,16,1280]{2,1,0:T(8,128)(2,1)S(1)}, u32[]{:S(2)}, u32[]{:S(2)}) collective-permute-start(bf16[16,16,1280]{2,1,0:T(8,128)(2,1)S(1)} %pad_maximum_fusion.refs_0_), channel_id=1, source_target_pairs={{0,1},{1,0},{2,3},{3,2},{4,5},{5,4},{6,7},{7,6},{8,9},{9,8},{10,11... | collective-permute-start | bytes 1966088 | tf_op jit(solution)/shard_map/ppermute | solution.py:550
  28.4 10.2 %collective-permute-start.9 = (bf16[2,2,16,2048]{3,2,0,1:T(8,128)(2,1)S(1)}, bf16[2,2,16,2048]{3,2,0,1:T(8,128)(2,1)S(1)}, u32[]{:S(2)}, u32[]{:S(2)}) collective-permute-start(bf16[2,2,16,2048]{3,2,0,1:T(8,128)(2,1)S(1)} %get-tuple-element.98), channel_id=1, source_target_pairs={{0,2},{1,3},{2,0},{3,1},{4,6},{5,7},{6,4},{7,5},{8,10},{9,11},{10,... | collective-permute-start | bytes 786440 | tf_op jit(solution)/shard_map/ppermute | solution.py:550
  29.5 9.2 %collective-permute-start.10 = (bf16[2,2,16,2048]{3,2,0,1:T(8,128)(2,1)S(1)}, bf16[2,2,16,2048]{3,2,0,1:T(8,128)(2,1)S(1)}, u32[]{:S(2)}, u32[]{:S(2)}) collective-permute-start(bf16[2,2,16,2048]{3,2,0,1:T(8,128)(2,1)S(1)} %get-tuple-element.99), channel_id=1, source_target_pairs={{0,16},{1,17},{2,18},{3,19},{4,20},{5,21},{6,22},{7,23},{8,24},{9,... | collective-permute-start | bytes 786440 | tf_op jit(solution)/shard_map/ppermute | solution.py:550
  38.8 13.0 %collective-permute-start.11 = (bf16[2,2,2,16,2048]{4,3,0,1,2:T(8,128)(2,1)S(1)}, bf16[2,2,2,16,2048]{4,3,0,1,2:T(8,128)(2,1)S(1)}, u32[]{:S(2)}, u32[]{:S(2)}) collective-permute-start(bf16[2,2,2,16,2048]{4,3,0,1,2:T(8,128)(2,1)S(1)} %maximum_select_fusion.3), channel_id=1, source_target_pairs={{0,16},{1,17},{2,18},{3,19},{4,20},{5,21},{6,22},{7,23},{8,24},{9,... | collective-permute-start | bytes 1572872 | tf_op jit(solution)/shard_map/ppermute | solution.py:550
  40.0 13.1 %collective-permute-start.12 = (bf16[2,2,2,16,2048]{4,3,1,2,0:T(8,128)(2,1)S(1)}, bf16[2,2,2,16,2048]{4,3,1,2,0:T(8,128)(2,1)S(1)}, u32[]{:S(2)}, u32[]{:S(2)}) collective-permute-start(bf16[2,2,2,16,2048]{4,3,1,2,0:T(8,128)(2,1)S(1)} %maximum_select_fusion.4), channel_id=1, source_target_pairs={{0,2},{1,3},{2,0},{3,1},{4,6},{5,7},{6,4},{7,5},{8,10},{9,11},{10,... | collective-permute-start | bytes 1572872 | tf_op jit(solution)/shard_map/ppermute | solution.py:550
  53.3 5.1 %collective-permute-start.13 = (bf16[16,16,2048]{2,1,0:T(8,128)(2,1)S(1)}, bf16[16,16,2048]{2,1,0:T(8,128)(2,1)S(1)}, u32[]{:S(2)}, u32[]{:S(2)}) collective-permute-start(bf16[16,16,2048]{2,1,0:T(8,128)(2,1)S(1)} %bitcast.116), channel_id=1, source_target_pairs={{0,1},{1,0},{2,3},{3,2},{4,5},{5,4},{6,7},{7,6},{8,9},{9,8},{10,11... | collective-permute-start | bytes 3145736 | tf_op jit(solution)/shard_map/ppermute | solution.py:550
  53.4 5.1 %collective-permute-start.14 = (bf16[16,16,2048]{2,1,0:T(8,128)(2,1)S(1)}, bf16[16,16,2048]{2,1,0:T(8,128)(2,1)S(1)}, u32[]{:S(2)}, u32[]{:S(2)}) collective-permute-start(bf16[16,16,2048]{2,1,0:T(8,128)(2,1)S(1)} %bitcast.122), channel_id=1, source_target_pairs={{0,1},{1,0},{2,3},{3,2},{4,5},{5,4},{6,7},{7,6},{8,9},{9,8},{10,11... | collective-permute-start | bytes 3145736 | tf_op jit(solution)/shard_map/ppermute | solution.py:550
  85.8 7.7 %collective-permute-start.16 = (bf16[16,16,2048]{2,1,0:T(8,128)(2,1)}, bf16[16,16,2048]{2,1,0:T(8,128)(2,1)}, u32[]{:S(2)}, u32[]{:S(2)}) collective-permute-start(bf16[16,16,2048]{2,1,0:T(8,128)(2,1)} %get-tuple-element.122), channel_id=1, source_target_pairs={{0,1},{1,0},{2,3},{3,2},{4,5},{5,4},{6,7},{7,6},{8,9},{9,8},{10,11... | collective-permute-start | bytes 3145736 | tf_op jit(solution)/shard_map/ppermute | solution.py:550
  85.9 10.0 %collective-permute-start.15 = (bf16[16,16,2048]{2,1,0:T(8,128)(2,1)}, bf16[16,16,2048]{2,1,0:T(8,128)(2,1)S(1)}, u32[]{:S(2)}, u32[]{:S(2)}) collective-permute-start(bf16[16,16,2048]{2,1,0:T(8,128)(2,1)} %get-tuple-element.120), channel_id=1, source_target_pairs={{0,1},{1,0},{2,3},{3,2},{4,5},{5,4},{6,7},{7,6},{8,9},{9,8},{10,11... | collective-permute-start | bytes 3145736 | tf_op jit(solution)/shard_map/ppermute | solution.py:550
  95.3 14.5 %collective-permute-start.18 = (bf16[2,2,2,16,2048]{4,3,1,2,0:T(8,128)(2,1)S(1)}, bf16[2,2,2,16,2048]{4,3,1,2,0:T(8,128)(2,1)S(1)}, u32[]{:S(2)}, u32[]{:S(2)}) collective-permute-start(bf16[2,2,2,16,2048]{4,3,1,2,0:T(8,128)(2,1)S(1)} %copy_bitcast_fusion), channel_id=1, source_target_pairs={{0,2},{1,3},{2,0},{3,1},{4,6},{5,7},{6,4},{7,5},{8,10},{9,11},{10,... | collective-permute-start | bytes 1572872 | tf_op jit(solution)/shard_map/ppermute | solution.py:550
  96.4 14.4 %collective-permute-start.17 = (bf16[2,2,2,16,2048]{4,3,0,1,2:T(8,128)(2,1)S(1)}, bf16[2,2,2,16,2048]{4,3,0,1,2:T(8,128)(2,1)S(1)}, u32[]{:S(2)}, u32[]{:S(2)}) collective-permute-start(bf16[2,2,2,16,2048]{4,3,0,1,2:T(8,128)(2,1)S(1)} %copy_bitcast_fusion.1), channel_id=1, source_target_pairs={{0,16},{1,17},{2,18},{3,19},{4,20},{5,21},{6,22},{7,23},{8,24},{9,... | collective-permute-start | bytes 1572872 | tf_op jit(solution)/shard_map/ppermute | solution.py:550
  110.0 8.2 %collective-permute-start.20 = (bf16[2,2,16,2048]{3,2,0,1:T(8,128)(2,1)S(1)}, bf16[2,2,16,2048]{3,2,0,1:T(8,128)(2,1)S(1)}, u32[]{:S(2)}, u32[]{:S(2)}) collective-permute-start(bf16[2,2,16,2048]{3,2,0,1:T(8,128)(2,1)S(1)} %dynamic-slice_bitcast_fusion.1), channel_id=1, source_target_pairs={{0,16},{1,17},{2,18},{3,19},{4,20},{5,21},{6,22},{7,23},{8,24},{9,... | collective-permute-start | bytes 786440 | tf_op jit(solution)/shard_map/ppermute | solution.py:550
  111.0 7.8 %collective-permute-start.19 = (bf16[2,2,16,2048]{3,2,0,1:T(8,128)(2,1)S(1)}, bf16[2,2,16,2048]{3,2,0,1:T(8,128)(2,1)S(1)}, u32[]{:S(2)}, u32[]{:S(2)}) collective-permute-start(bf16[2,2,16,2048]{3,2,0,1:T(8,128)(2,1)S(1)} %dynamic-slice_bitcast_fusion.2), channel_id=1, source_target_pairs={{0,2},{1,3},{2,0},{3,1},{4,6},{5,7},{6,4},{7,5},{8,10},{9,11},{10,... | collective-permute-start | bytes 786440 | tf_op jit(solution)/shard_map/ppermute | solution.py:550
  119.0 7.9 %collective-permute-start.21 = (bf16[2,16,4096]{2,1,0:T(8,128)(2,1)S(1)}, bf16[2,16,4096]{2,1,0:T(8,128)(2,1)S(1)}, u32[]{:S(2)}, u32[]{:S(2)}) collective-permute-start(bf16[2,16,4096]{2,1,0:T(8,128)(2,1)S(1)} %dynamic-slice_bitcast_fusion), channel_id=1, source_target_pairs={{0,4},{1,5},{2,6},{3,7},{4,0},{5,1},{6,2},{7,3},{8,12},{9,13},{10,... | collective-permute-start | bytes 786440 | tf_op jit(solution)/shard_map/ppermute | solution.py:550
  127.0 7.4 %collective-permute-start.25 = (bf16[16,4096]{1,0:T(8,128)(2,1)S(1)}, bf16[16,4096]{1,0:T(8,128)(2,1)S(1)}, u32[]{:S(2)}, u32[]{:S(2)}) collective-permute-start(bf16[16,4096]{1,0:T(8,128)(2,1)S(1)} %dynamic-slice_bitcast_fusion.3), channel_id=1, source_target_pairs={{0,8},{1,9},{2,10},{3,11},{4,12},{5,13},{6,14},{7,15},{8,0},{9,1},... | collective-permute-start | bytes 393224 | tf_op jit(solution)/shard_map/ppermute | solution.py:550
  132.8 2.2 %collective-permute-start.22 = (bf16[16,16,1280]{2,1,0:T(8,128)(2,1)S(1)}, bf16[16,16,1280]{2,1,0:T(8,128)(2,1)S(1)}, u32[]{:S(2)}, u32[]{:S(2)}) collective-permute-start(bf16[16,16,1280]{2,1,0:T(8,128)(2,1)S(1)} %get-tuple-element.148), channel_id=1, source_target_pairs={{0,1},{1,0},{2,3},{3,2},{4,5},{5,4},{6,7},{7,6},{8,9},{9,8},{10,11... | collective-permute-start | bytes 1966088 | tf_op jit(solution)/shard_map/ppermute | solution.py:550
  135.3 6.3 %collective-permute-start.24 = (bf16[2,2,2,16,640]{4,3,1,2,0:T(8,128)(2,1)S(1)}, bf16[2,2,2,16,640]{4,3,1,2,0:T(8,128)(2,1)S(1)}, u32[]{:S(2)}, u32[]{:S(2)}) collective-permute-start(bf16[2,2,2,16,640]{4,3,1,2,0:T(8,128)(2,1)S(1)} %bitcast.156), channel_id=1, source_target_pairs={{0,2},{1,3},{2,0},{3,1},{4,6},{5,7},{6,4},{7,5},{8,10},{9,11},{10,... | collective-permute-start | bytes 491528 | tf_op jit(solution)/shard_map/ppermute | solution.py:550
  136.1 6.0 %collective-permute-start.23 = (bf16[2,2,2,16,640]{4,3,0,1,2:T(8,128)(2,1)S(1)}, bf16[2,2,2,16,640]{4,3,0,1,2:T(8,128)(2,1)S(1)}, u32[]{:S(2)}, u32[]{:S(2)}) collective-permute-start(bf16[2,2,2,16,640]{4,3,0,1,2:T(8,128)(2,1)S(1)} %bitcast.157), channel_id=1, source_target_pairs={{0,16},{1,17},{2,18},{3,19},{4,20},{5,21},{6,22},{7,23},{8,24},{9,... | collective-permute-start | bytes 491528 | tf_op jit(solution)/shard_map/ppermute | solution.py:550
  142.2 6.1 %collective-permute-start.27 = (bf16[2,2,16,640]{3,2,0,1:T(8,128)(2,1)S(1)}, bf16[2,2,16,640]{3,2,0,1:T(8,128)(2,1)S(1)}, u32[]{:S(2)}, u32[]{:S(2)}) collective-permute-start(bf16[2,2,16,640]{3,2,0,1:T(8,128)(2,1)S(1)} %dynamic-slice_bitcast_fusion.5), channel_id=1, source_target_pairs={{0,16},{1,17},{2,18},{3,19},{4,20},{5,21},{6,22},{7,23},{8,24},{9,... | collective-permute-start | bytes 245768 | tf_op jit(solution)/shard_map/ppermute | solution.py:550
  143.3 5.0 %collective-permute-start.26 = (bf16[2,2,16,640]{3,2,0,1:T(8,128)(2,1)S(1)}, bf16[2,2,16,640]{3,2,0,1:T(8,128)(2,1)S(1)}, u32[]{:S(2)}, u32[]{:S(2)}) collective-permute-start(bf16[2,2,16,640]{3,2,0,1:T(8,128)(2,1)S(1)} %dynamic-slice_bitcast_fusion.6), channel_id=1, source_target_pairs={{0,2},{1,3},{2,0},{3,1},{4,6},{5,7},{6,4},{7,5},{8,10},{9,11},{10,... | collective-permute-start | bytes 245768 | tf_op jit(solution)/shard_map/ppermute | solution.py:550
  148.4 4.5 %collective-permute-start.28 = (bf16[2,16,1280]{2,1,0:T(8,128)(2,1)S(1)}, bf16[2,16,1280]{2,1,0:T(8,128)(2,1)S(1)}, u32[]{:S(2)}, u32[]{:S(2)}) collective-permute-start(bf16[2,16,1280]{2,1,0:T(8,128)(2,1)S(1)} %dynamic-slice_bitcast_fusion.4), channel_id=1, source_target_pairs={{0,4},{1,5},{2,6},{3,7},{4,0},{5,1},{6,2},{7,3},{8,12},{9,13},{10,... | collective-permute-start | bytes 245768 | tf_op jit(solution)/shard_map/ppermute | solution.py:550
  153.7 4.9 %collective-permute-start.29 = (bf16[16,1280]{1,0:T(8,128)(2,1)S(1)}, bf16[16,1280]{1,0:T(8,128)(2,1)S(1)}, u32[]{:S(2)}, u32[]{:S(2)}) collective-permute-start(bf16[16,1280]{1,0:T(8,128)(2,1)S(1)} %get-tuple-element.188), channel_id=1, source_target_pairs={{0,8},{1,9},{2,10},{3,11},{4,12},{5,13},{6,14},{7,15},{8,0},{9,1},... | collective-permute-start | bytes 122888 | tf_op jit(solution)/shard_map/ppermute | solution.py:550
  (31 other events, 191.8 us)

commit v6 on v5

--- a/solution.py
+++ b/solution.py
@@ -892,6 +892,7 @@
             functools.partial(finish_kernel, 1.0 / (total * count)),
             out_shape=[own((share, depth)), own((share, head)), own((share, head)), own((share, depth)), own((experts, share))]
             + [own((share,))] * 5 + [own((subs * share,)), own((experts,))],
+            compiler_params=pltpu.CompilerParams(vmem_limit_bytes=8 << 20),
             name="finish",
         )(keep, move(send, late[-1], count))
         grad_router = grad_router.T

time: 161 us -> 159 us (0.988)
    unnamed x70 -> x68, local copies, waits for them, and re-layouts: 3.96 us -> 3.38 us
where the time goes in v6:
time: 159 us
  Pallas kernels  95.4 us (60%)
  starting transfers between devices  37.6 us (24%)
  waiting for transfers between devices  12.9 us (8%)
  local copies, waits for them, and re-layouts  7.41 us (5%)
  other arithmetic  3.82 us (2%)
  between operations  1.76 us (1%)
    pallas_call x7, Pallas kernels, call(): pl.pallas_call(kernel, grid=grid, in_specs=in_specs, out_specs=out_specs,...  63.1 us
    ppermute x30, starting transfers between devices, move(): return lax.ppermute(value, AXES, xor_pairs(count, mask))  37.6 us
    ppermute x30, waiting for transfers between devices, move(): return lax.ppermute(value, AXES, xor_pairs(count, mask))  12.9 us
    pallas_call x2, Pallas kernels, turn(): pl.pallas_call(functools.partial(turn_kernel, n, len(again) > 0), grid=(t...  11.7 us
    pallas_call x2, Pallas kernels, back(): pl.pallas_call(attend_back_kernel, grid=(per_row,), in_specs=[part(2), bo...  11.4 us
    pallas_call x2, Pallas kernels, results(): pl.pallas_call(functools.partial(result_kernel, n), grid=(tiles // 2,), i...  7 us
    unnamed x68, local copies, waits for them, and re-layouts  3.38 us
  transfers between devices with their start and end apart: 30, of which 15 were waited for; matrix products, arithmetic and copies ran while one was open for 5% of the time, Pallas kernels for 41%

profile of v6, /device:TPU:0, one launch (start us, length us, event | category | flops | bytes accessed | tf_op | source)
XLA Modules:
  0.0 158.9 jit_solution(17266143841714182943)
XLA Ops:
  0.7 1.5 pack.1
  2.1 4.1 %collective-permute-start = (bf16[16,1280]{1,0:T(8,128)(2,1)S(1)}, bf16[16,1280]{1,0:T(8,128)(2,1)S(1)}, u32[]{:S(2)}, u32[]{:S(2)}) collective-permute-start(bf16[16,1280]{1,0:T(8,128)(2,1)S(1)} %get-tuple-element.93), channel_id=1, source_target_pairs={{0,8},{1,9},{2,10},{3,11},{4,12},{5,13},{6,14},{7,15},{8,0},{9,1},... | collective-permute-start | bytes 122888 | tf_op jit(solution)/shard_map/ppermute | solution.py:550
  8.6 1.5 collective-permute-start.1
  10.2 2.9 %collective-permute-start.7 = (bf16[16,4096]{1,0:T(8,128)(2,1)S(1)}, bf16[16,4096]{1,0:T(8,128)(2,1)S(1)}, u32[]{:S(2)}, u32[]{:S(2)}) collective-permute-start(bf16[16,4096]{1,0:T(8,128)(2,1)S(1)} %get-tuple-element.96), channel_id=1, source_target_pairs={{0,8},{1,9},{2,10},{3,11},{4,12},{5,13},{6,14},{7,15},{8,0},{9,1},... | collective-permute-start | bytes 393224 | tf_op jit(solution)/shard_map/ppermute | solution.py:550
  13.9 1.7 %collective-permute-start.4 = (bf16[2,2,16,640]{3,2,1,0:T(8,128)(2,1)S(1)}, bf16[2,2,16,640]{3,2,1,0:T(8,128)(2,1)S(1)}, u32[]{:S(2)}, u32[]{:S(2)}) collective-permute-start(bf16[2,2,16,640]{3,2,1,0:T(8,128)(2,1)S(1)} %get-tuple-element.186), channel_id=1, source_target_pairs={{0,16},{1,17},{2,18},{3,19},{4,20},{5,21},{6,22},{7,23},{8,24},{9,... | collective-permute-start | bytes 245768 | tf_op jit(solution)/shard_map/ppermute | solution.py:550
  15.6 1.5 collective-permute-start.2
  18.5 1.6 %collective-permute-start.5 = (bf16[2,2,2,16,640]{4,3,2,1,0:T(8,128)(2,1)S(1)}, bf16[2,2,2,16,640]{4,3,2,1,0:T(8,128)(2,1)S(1)}, u32[]{:S(2)}, u32[]{:S(2)}) collective-permute-start(bf16[2,2,2,16,640]{4,3,2,1,0:T(8,128)(2,1)S(1)} %maximum_select_fusion.11), channel_id=1, source_target_pairs={{0,2},{1,3},{2,0},{3,1},{4,6},{5,7},{6,4},{7,5},{8,10},{9,11},{10,... | collective-permute-start | bytes 491528 | tf_op jit(solution)/shard_map/ppermute | solution.py:550
  20.3 1.5 collective-permute-start.3
  21.7 2.2 %collective-permute-start.8 = (bf16[2,16,4096]{2,1,0:T(8,128)(2,1)S(1)}, bf16[2,16,4096]{2,1,0:T(8,128)(2,1)S(1)}, u32[]{:S(2)}, u32[]{:S(2)}) collective-permute-start(bf16[2,16,4096]{2,1,0:T(8,128)(2,1)S(1)} %maximum_select_fusion.7), channel_id=1, source_target_pairs={{0,4},{1,5},{2,6},{3,7},{4,0},{5,1},{6,2},{7,3},{8,12},{9,13},{10,... | collective-permute-start | bytes 786440 | tf_op jit(solution)/shard_map/ppermute | solution.py:550
  24.0 1.6 %collective-permute-done.3 = bf16[2,2,2,16,640]{4,3,1,0,2:T(8,128)(2,1)S(1)} collective-permute-done((bf16[2,2,2,16,640]{4,3,1,0,2:T(8,128)(2,1)S(1)}, bf16[2,2,2,16,640]{4,3,1,0,2:T(8,128)(2,1)S(1)}, u32[]{:S(2)}, u32[]{:S(2)}) %collective-permute-start.3) | collective-permute-done | bytes 163872 | tf_op jit(solution)/shard_map/ppermute | solution.py:550
  25.9 2.3 %collective-permute-done.8 = bf16[2,16,4096]{2,1,0:T(8,128)(2,1)S(1)} collective-permute-done((bf16[2,16,4096]{2,1,0:T(8,128)(2,1)S(1)}, bf16[2,16,4096]{2,1,0:T(8,128)(2,1)S(1)}, u32[]{:S(2)}, u32[]{:S(2)}) %collective-permute-start.8) | collective-permute-done | bytes 262176 | tf_op jit(solution)/shard_map/ppermute | solution.py:550
  30.4 8.1 %project.1 = (bf16[2048,512]{1,0:T(8,128)(2,1)}, bf16[2,2048,128]{2,1,0:T(8,128)(2,1)S(1)}, bf16[2048,256]{1,0:T(8,128)(2,1)}, bf16[2048,256]{1,0:T(8,128)(2,1)}...) custom-call(s32[1]{0:T(128)} %bitcast.me, s32[2,4]{1,0:T(2,128)S(1)} %copy-done.13, bf16[2048,512]{1,0:T(8,128)(2,1)} %tok.5, ...), custom_call_target="tpu_custom_call" | custom-call | flops 8999999488 | bytes 1024 | tf_op jit(solution)/shard_map/project/pallas_call | solution.py:662
  40.9 10.2 %attend.1 = (f32[2048,128]{1,0:T(8,128)S(1)}, bf16[2048,512]{1,0:T(8,128)(2,1)S(1)}, bf16[2,2048,128]{2,1,0:T(8,128)(2,1)}) custom-call(s32[2,4]{1,0:T(2,128)S(1)} %copy-done.13, s32[2048,2]{1,0:T(8,128)S(1)} %copy.56.routes, bf16[2,2048,128]{2,1,0:T(8,128)(2,1)S(1)} %get-tuple-element.100.qa, bf16[2048,256]{1,0:T(8,128)(2,1)S(1)} %copy-done.19, ...), custom_call_target="tpu_custom_call" | custom-call | flops 12999999488 | bytes 1024 | tf_op jit(solution)/shard_map/attend/pallas_call | solution.py:662
  54.7 3.8 %mix.1 = (f32[2048,512]{1,0:T(8,128)}, bf16[2048,512]{1,0:T(8,128)(2,1)S(1)}) custom-call(s32[1]{0:T(128)} %bitcast.me, bf16[2048,512]{1,0:T(8,128)(2,1)S(1)} %copy-done.9, bf16[2048,512]{1,0:T(8,128)(2,1)S(1)} %get-tuple-element.107.u, f32[32,512]{1,0:T(8,128)S(1)} %get-tuple-element.108.vec, bf16[16,16,1280]{2,1,0:T(8,128)(2,1)S(1)} %pad_maximum_fusion.refs_0_, ...), custom_call_target="tpu_custom_call" | custom-call | flops 5000000000 | bytes 1024 | tf_op jit(solution)/shard_map/mix/pallas_call | solution.py:662
  58.5 27.3 %feed.1 = (bf16[2048,2048]{1,0:T(8,128)(2,1)}, bf16[2048,2048]{1,0:T(8,128)(2,1)}, f32[8,512]{1,0:T(8,128)S(1)}, bf16[16,16,2048]{2,1,0:T(8,128)(2,1)}, bf16[16,...) custom-call(s32[1]{0:T(128)} %bitcast.me, ...), custom_call_target="tpu_custom_call" | custom-call | flops 24999999488 | bytes 1024 | tf_op jit(solution)/shard_map/feed/pallas_call | solution.py:662
  87.6 5.9 %turn.2 = (f32[2048,512]{1,0:T(8,128)S(1)}, bf16[2048,512]{1,0:T(8,128)(2,1)S(1)}, f32[32,512]{1,0:T(8,128)S(1)}) custom-call(s32[1]{0:T(128)} %bitcast.me, bf16[2048,2048]{1,0:T(8,128)(2,1)} %get-tuple-element.117.dz, bf16[2048,512]{1,0:T(8,128)(2,1)} %dy.5, f32[2048,512]{1,0:T(8,128)} %get-tuple-element.149.x1, f32[32,512]{1,0:T(8,128)S(1)} %get-tuple-element.108.vec, ...), custom_call_target="tpu_custom_call" | custom-call | flops 6000000000 | bytes 1024 | tf_op jit(solution)/shard_map/turn/pallas_call | solution.py:747
  93.6 1.7 %add_convert_fusion = bf16[16,16,2048]{2,1,0:T(8,128)(2,1)S(1)} fusion(bf16[16,16,2048]{2,1,0:T(8,128)(2,1)} %collective-permute-done.16, bf16[16,16,2048]{2,1,0:T(8,128)(2,1)S(1)} %copy-done.29), kind=kLoop, calls=%fused_computation | loop fusion | flops 2097152 | bytes 3145728 | tf_op jit(solution)/shard_map/convert_element_type | solution.py:571
  96.4 1.4 collective-permute-start.17
  97.9 5.8 %turn.3 = (f32[2048,512]{1,0:T(8,128)S(1)}, bf16[2048,512]{1,0:T(8,128)(2,1)S(1)}, f32[32,512]{1,0:T(8,128)S(1)}) custom-call(s32[1]{0:T(128)} %bitcast.me, bf16[2048,2048]{1,0:T(8,128)(2,1)} %get-tuple-element.117.dz, bf16[2048,512]{1,0:T(8,128)(2,1)} %dy.5, f32[2048,512]{1,0:T(8,128)} %get-tuple-element.149.x1, ...), custom_call_target="tpu_custom_call", output_to_operand_aliasing={{0}: (6, {}), {1}: (7, {})} | custom-call | flops 6000000000 | bytes 1024 | tf_op jit(solution)/shard_map/turn/pallas_call | solution.py:747
  103.7 6.1 %gates.1 = (bf16[2,2048,128]{2,1,0:T(8,128)(2,1)S(1)}, bf16[2,2048,128]{2,1,0:T(8,128)(2,1)S(1)}, bf16[2048,128]{1,0:T(8,128)(2,1)S(1)}, f32[8,128]{1,0:T(8,128)S(1)}, bf16[512,512]{1,0:T(8,128)(2,1)S(1)}) custom-call(s32[1]{0:T(128)} %bitcast.me, bf16[2048,512]{1,0:T(8,128)(2,1)S(1)} %get-tuple-element.126.dx1, s32[2048,2]{1,0:T(8,128)S(1)} %copy-done.6, ...), custom_call_target="tpu_custom_call" | custom-call | flops 8999999488 | bytes 1024 | tf_op jit(solution)/shard_map/gates/pallas_call | solution.py:662
  111.0 1.5 collective-permute-start.19
  112.5 5.7 %attend_back.2 = (bf16[2048,512]{1,0:T(8,128)(2,1)S(1)}, bf16[2048,128]{1,0:T(8,128)(2,1)S(1)}) custom-call(s32[2048,2]{1,0:T(8,128)S(1)} %copy-done.6, bf16[2,2048,128]{2,1,0:T(8,128)(2,1)S(1)} %copy-done.18, bf16[2,2048,128]{2,1,0:T(8,128)(2,1)S(1)} %copy-done.23, bf16[2048,256]{1,0:T(8,128)(2,1)S(1)} %copy-done.20, bf16[2048,256]{1,0:T(8,128)(2,1)S(1)} %copy-done.22, ...), custom_call_target="tpu_custom_call" | custom-call | flops 8000000000 | bytes 1024 | tf_op jit(solution)/shard_map/attend_back/pallas_call | solution.py:797
  119.0 2.3 %collective-permute-start.21 = (bf16[2,16,4096]{2,1,0:T(8,128)(2,1)S(1)}, bf16[2,16,4096]{2,1,0:T(8,128)(2,1)S(1)}, u32[]{:S(2)}, u32[]{:S(2)}) collective-permute-start(bf16[2,16,4096]{2,1,0:T(8,128)(2,1)S(1)} %dynamic-slice_bitcast_fusion), channel_id=1, source_target_pairs={{0,4},{1,5},{2,6},{3,7},{4,0},{5,1},{6,2},{7,3},{8,12},{9,13},{10,... | collective-permute-start | bytes 786440 | tf_op jit(solution)/shard_map/ppermute | solution.py:550
  121.2 5.7 %attend_back.3 = (bf16[2048,512]{1,0:T(8,128)(2,1)S(1)}, bf16[2048,128]{1,0:T(8,128)(2,1)S(1)}) custom-call(s32[2048,2]{1,0:T(8,128)S(1)} %copy-done.6, bf16[2,2048,128]{2,1,0:T(8,128)(2,1)S(1)} %copy-done.18, bf16[2,2048,128]{2,1,0:T(8,128)(2,1)S(1)} %copy-done.23, bf16[2048,256]{1,0:T(8,128)(2,1)S(1)} %copy-done.20, ...), custom_call_target="tpu_custom_call", output_to_operand_aliasing={{0}: (7, {}), {1}: (8, {})} | custom-call | flops 8000000000 | bytes 1024 | tf_op jit(solution)/shard_map/attend_back/pallas_call | solution.py:797
  127.0 2.2 %collective-permute-start.25 = (bf16[16,4096]{1,0:T(8,128)(2,1)S(1)}, bf16[16,4096]{1,0:T(8,128)(2,1)S(1)}, u32[]{:S(2)}, u32[]{:S(2)}) collective-permute-start(bf16[16,4096]{1,0:T(8,128)(2,1)S(1)} %dynamic-slice_bitcast_fusion.3), channel_id=1, source_target_pairs={{0,8},{1,9},{2,10},{3,11},{4,12},{5,13},{6,14},{7,15},{8,0},{9,1},... | collective-permute-start | bytes 393224 | tf_op jit(solution)/shard_map/ppermute | solution.py:550
  129.3 3.6 %sums.1 = (bf16[16,16,1280]{2,1,0:T(8,128)(2,1)S(1)}, bf16[16,16,1280]{2,1,0:T(8,128)(2,1)S(1)}) custom-call(s32[1]{0:T(128)} %bitcast.me, bf16[2048,512]{1,0:T(8,128)(2,1)S(1)} %copy-done.16, bf16[2048,512]{1,0:T(8,128)(2,1)S(1)} %get-tuple-element.138.dq, bf16[2048,128]{1,0:T(8,128)(2,1)S(1)} %get-tuple-element.142.kv, ...), custom_call_target="tpu_custom_call" | custom-call | flops 6000000000 | bytes 1024 | tf_op jit(solution)/shard_map/sums/pallas_call | solution.py:662
  132.9 1.6 collective-permute-done.25
  137.2 4.1 %close.1 = bf16[2048,512]{1,0:T(8,128)(2,1)} custom-call(s32[1]{0:T(128)} %bitcast.me, f32[2048,512]{1,0:T(8,128)S(1)} %get-tuple-element.152.dx1, bf16[2048,512]{1,0:T(8,128)(2,1)S(1)} %get-tuple-element.138.dq, bf16[2048,128]{1,0:T(8,128)(2,1)S(1)} %get-tuple-element.142.kv, bf16[2048,128]{1,0:T(8,128)(2,1)S(1)} %get-tuple-element.133.ds, ...), custom_call_target="tpu_custom_call" | custom-call | flops 6000000000 | bytes 1024 | tf_op jit(solution)/shard_map/close/pallas_call | solution.py:662
  143.3 1.5 collective-permute-start.26
  144.8 3.5 %result.2.refs_4_ = bf16[2048,512]{1,0:T(8,128)(2,1)} custom-call(s32[1]{0:T(128)} %bitcast.me, bf16[2048,2048]{1,0:T(8,128)(2,1)S(1)} %bitcast.115, f32[2048,512]{1,0:T(8,128)S(1)} %copy-done, f32[32,512]{1,0:T(8,128)S(1)} %get-tuple-element.108.vec, bf16[16,16,2048]{2,1,0:T(8,128)(2,1)S(1)} %bitcast.120, ...), custom_call_target="tpu_custom_call" | custom-call | flops 3500000000 | bytes 1024 | tf_op jit(solution)/shard_map/result/pallas_call | solution.py:861
  149.5 3.5 %result.3 = bf16[2048,512]{1,0:T(8,128)(2,1)} custom-call(s32[1]{0:T(128)} %bitcast.me, bf16[2048,2048]{1,0:T(8,128)(2,1)S(1)} %bitcast.115, f32[2048,512]{1,0:T(8,128)S(1)} %copy-done, f32[32,512]{1,0:T(8,128)S(1)} %get-tuple-element.108.vec, bf16[16,16,2048]{2,1,0:T(8,128)(2,1)S(1)} %bitcast.121, ...), custom_call_target="tpu_custom_call", output_to_operand_aliasing={{}: (8, {})} | custom-call | flops 3500000000 | bytes 1024 | tf_op jit(solution)/shard_map/result/pallas_call | solution.py:861
  155.2 1.6 %reshape.281 = f32[16,2048]{1,0:T(8,128)} reshape(f32[16,32,4,16]{3,2,1,0:T(4,128)S(1)} %copy.68) | data formatting | bytes 262144 | tf_op jit(solution)/shard_map/reshape | solution.py:879
  (169 shorter events, 27.9 us)
Async XLA Ops:
  2.1 6.5 %collective-permute-start = (bf16[16,1280]{1,0:T(8,128)(2,1)S(1)}, bf16[16,1280]{1,0:T(8,128)(2,1)S(1)}, u32[]{:S(2)}, u32[]{:S(2)}) collective-permute-start(bf16[16,1280]{1,0:T(8,128)(2,1)S(1)} %get-tuple-element.93), channel_id=1, source_target_pairs={{0,8},{1,9},{2,10},{3,11},{4,12},{5,13},{6,14},{7,15},{8,0},{9,1},... | collective-permute-start | bytes 122888 | tf_op jit(solution)/shard_map/ppermute | solution.py:550
  7.3 33.6 %copy-start.5 = (s32[2048,2]{1,0:T(8,128)}, s32[2048,2]{1,0:T(8,128)S(1)}, u32[]{:S(2)}) copy-start(s32[2048,2]{1,0:T(8,128)S(1)} %copy.56.routes) | copy-start | bytes 49156
  8.6 5.2 %collective-permute-start.1 = (bf16[2,16,1280]{2,1,0:T(8,128)(2,1)S(1)}, bf16[2,16,1280]{2,1,0:T(8,128)(2,1)S(1)}, u32[]{:S(2)}, u32[]{:S(2)}) collective-permute-start(bf16[2,16,1280]{2,1,0:T(8,128)(2,1)S(1)} %maximum_select_fusion.13), channel_id=1, source_target_pairs={{0,4},{1,5},{2,6},{3,7},{4,0},{5,1},{6,2},{7,3},{8,12},{9,13},{10,... | collective-permute-start | bytes 245768 | tf_op jit(solution)/shard_map/ppermute | solution.py:550
  10.2 7.8 %collective-permute-start.7 = (bf16[16,4096]{1,0:T(8,128)(2,1)S(1)}, bf16[16,4096]{1,0:T(8,128)(2,1)S(1)}, u32[]{:S(2)}, u32[]{:S(2)}) collective-permute-start(bf16[16,4096]{1,0:T(8,128)(2,1)S(1)} %get-tuple-element.96), channel_id=1, source_target_pairs={{0,8},{1,9},{2,10},{3,11},{4,12},{5,13},{6,14},{7,15},{8,0},{9,1},... | collective-permute-start | bytes 393224 | tf_op jit(solution)/shard_map/ppermute | solution.py:550
  13.9 4.5 %collective-permute-start.4 = (bf16[2,2,16,640]{3,2,1,0:T(8,128)(2,1)S(1)}, bf16[2,2,16,640]{3,2,1,0:T(8,128)(2,1)S(1)}, u32[]{:S(2)}, u32[]{:S(2)}) collective-permute-start(bf16[2,2,16,640]{3,2,1,0:T(8,128)(2,1)S(1)} %get-tuple-element.186), channel_id=1, source_target_pairs={{0,16},{1,17},{2,18},{3,19},{4,20},{5,21},{6,22},{7,23},{8,24},{9,... | collective-permute-start | bytes 245768 | tf_op jit(solution)/shard_map/ppermute | solution.py:550
  15.6 4.6 %collective-permute-start.2 = (bf16[2,2,16,640]{3,2,1,0:T(8,128)(2,1)S(1)}, bf16[2,2,16,640]{3,2,1,0:T(8,128)(2,1)S(1)}, u32[]{:S(2)}, u32[]{:S(2)}) collective-permute-start(bf16[2,2,16,640]{3,2,1,0:T(8,128)(2,1)S(1)} %get-tuple-element.187), channel_id=1, source_target_pairs={{0,2},{1,3},{2,0},{3,1},{4,6},{5,7},{6,4},{7,5},{8,10},{9,11},{10,... | collective-permute-start | bytes 245768 | tf_op jit(solution)/shard_map/ppermute | solution.py:550
  18.5 5.5 %collective-permute-start.5 = (bf16[2,2,2,16,640]{4,3,2,1,0:T(8,128)(2,1)S(1)}, bf16[2,2,2,16,640]{4,3,2,1,0:T(8,128)(2,1)S(1)}, u32[]{:S(2)}, u32[]{:S(2)}) collective-permute-start(bf16[2,2,2,16,640]{4,3,2,1,0:T(8,128)(2,1)S(1)} %maximum_select_fusion.11), channel_id=1, source_target_pairs={{0,2},{1,3},{2,0},{3,1},{4,6},{5,7},{6,4},{7,5},{8,10},{9,11},{10,... | collective-permute-start | bytes 491528 | tf_op jit(solution)/shard_map/ppermute | solution.py:550
  20.3 5.4 %collective-permute-start.3 = (bf16[2,2,2,16,640]{4,3,1,0,2:T(8,128)(2,1)S(1)}, bf16[2,2,2,16,640]{4,3,1,0,2:T(8,128)(2,1)S(1)}, u32[]{:S(2)}, u32[]{:S(2)}) collective-permute-start(bf16[2,2,2,16,640]{4,3,1,0,2:T(8,128)(2,1)S(1)} %maximum_select_fusion.9), channel_id=1, source_target_pairs={{0,16},{1,17},{2,18},{3,19},{4,20},{5,21},{6,22},{7,23},{8,24},{9,... | collective-permute-start | bytes 491528 | tf_op jit(solution)/shard_map/ppermute | solution.py:550
  21.7 6.5 %collective-permute-start.8 = (bf16[2,16,4096]{2,1,0:T(8,128)(2,1)S(1)}, bf16[2,16,4096]{2,1,0:T(8,128)(2,1)S(1)}, u32[]{:S(2)}, u32[]{:S(2)}) collective-permute-start(bf16[2,16,4096]{2,1,0:T(8,128)(2,1)S(1)} %maximum_select_fusion.7), channel_id=1, source_target_pairs={{0,4},{1,5},{2,6},{3,7},{4,0},{5,1},{6,2},{7,3},{8,12},{9,13},{10,... | collective-permute-start | bytes 786440 | tf_op jit(solution)/shard_map/ppermute | solution.py:550
  25.8 28.1 %copy-start.7 = (bf16[16,16,1280]{2,1,0:T(8,128)(2,1)}, bf16[16,16,1280]{2,1,0:T(8,128)(2,1)S(1)}, u32[]{:S(2)}) copy-start(bf16[16,16,1280]{2,1,0:T(8,128)(2,1)S(1)} %pad_maximum_fusion.refs_0_) | copy-start | bytes 1966084
  25.8 2.5 %collective-permute-start.6 = (bf16[16,16,1280]{2,1,0:T(8,128)(2,1)S(1)}, bf16[16,16,1280]{2,1,0:T(8,128)(2,1)S(1)}, u32[]{:S(2)}, u32[]{:S(2)}) collective-permute-start(bf16[16,16,1280]{2,1,0:T(8,128)(2,1)S(1)} %pad_maximum_fusion.refs_0_), channel_id=1, source_target_pairs={{0,1},{1,0},{2,3},{3,2},{4,5},{5,4},{6,7},{7,6},{8,9},{9,8},{10,11... | collective-permute-start | bytes 1966088 | tf_op jit(solution)/shard_map/ppermute | solution.py:550
  28.4 10.2 %collective-permute-start.9 = (bf16[2,2,16,2048]{3,2,0,1:T(8,128)(2,1)S(1)}, bf16[2,2,16,2048]{3,2,0,1:T(8,128)(2,1)S(1)}, u32[]{:S(2)}, u32[]{:S(2)}) collective-permute-start(bf16[2,2,16,2048]{3,2,0,1:T(8,128)(2,1)S(1)} %get-tuple-element.98), channel_id=1, source_target_pairs={{0,2},{1,3},{2,0},{3,1},{4,6},{5,7},{6,4},{7,5},{8,10},{9,11},{10,... | collective-permute-start | bytes 786440 | tf_op jit(solution)/shard_map/ppermute | solution.py:550
  29.5 9.2 %collective-permute-start.10 = (bf16[2,2,16,2048]{3,2,0,1:T(8,128)(2,1)S(1)}, bf16[2,2,16,2048]{3,2,0,1:T(8,128)(2,1)S(1)}, u32[]{:S(2)}, u32[]{:S(2)}) collective-permute-start(bf16[2,2,16,2048]{3,2,0,1:T(8,128)(2,1)S(1)} %get-tuple-element.99), channel_id=1, source_target_pairs={{0,16},{1,17},{2,18},{3,19},{4,20},{5,21},{6,22},{7,23},{8,24},{9,... | collective-permute-start | bytes 786440 | tf_op jit(solution)/shard_map/ppermute | solution.py:550
  38.8 13.0 %collective-permute-start.11 = (bf16[2,2,2,16,2048]{4,3,0,1,2:T(8,128)(2,1)S(1)}, bf16[2,2,2,16,2048]{4,3,0,1,2:T(8,128)(2,1)S(1)}, u32[]{:S(2)}, u32[]{:S(2)}) collective-permute-start(bf16[2,2,2,16,2048]{4,3,0,1,2:T(8,128)(2,1)S(1)} %maximum_select_fusion.3), channel_id=1, source_target_pairs={{0,16},{1,17},{2,18},{3,19},{4,20},{5,21},{6,22},{7,23},{8,24},{9,... | collective-permute-start | bytes 1572872 | tf_op jit(solution)/shard_map/ppermute | solution.py:550
  39.9 13.1 %collective-permute-start.12 = (bf16[2,2,2,16,2048]{4,3,1,2,0:T(8,128)(2,1)S(1)}, bf16[2,2,2,16,2048]{4,3,1,2,0:T(8,128)(2,1)S(1)}, u32[]{:S(2)}, u32[]{:S(2)}) collective-permute-start(bf16[2,2,2,16,2048]{4,3,1,2,0:T(8,128)(2,1)S(1)} %maximum_select_fusion.4), channel_id=1, source_target_pairs={{0,2},{1,3},{2,0},{3,1},{4,6},{5,7},{6,4},{7,5},{8,10},{9,11},{10,... | collective-permute-start | bytes 1572872 | tf_op jit(solution)/shard_map/ppermute | solution.py:550
  53.3 5.1 %collective-permute-start.13 = (bf16[16,16,2048]{2,1,0:T(8,128)(2,1)S(1)}, bf16[16,16,2048]{2,1,0:T(8,128)(2,1)S(1)}, u32[]{:S(2)}, u32[]{:S(2)}) collective-permute-start(bf16[16,16,2048]{2,1,0:T(8,128)(2,1)S(1)} %bitcast.116), channel_id=1, source_target_pairs={{0,1},{1,0},{2,3},{3,2},{4,5},{5,4},{6,7},{7,6},{8,9},{9,8},{10,11... | collective-permute-start | bytes 3145736 | tf_op jit(solution)/shard_map/ppermute | solution.py:550
  53.4 5.1 %collective-permute-start.14 = (bf16[16,16,2048]{2,1,0:T(8,128)(2,1)S(1)}, bf16[16,16,2048]{2,1,0:T(8,128)(2,1)S(1)}, u32[]{:S(2)}, u32[]{:S(2)}) collective-permute-start(bf16[16,16,2048]{2,1,0:T(8,128)(2,1)S(1)} %bitcast.122), channel_id=1, source_target_pairs={{0,1},{1,0},{2,3},{3,2},{4,5},{5,4},{6,7},{7,6},{8,9},{9,8},{10,11... | collective-permute-start | bytes 3145736 | tf_op jit(solution)/shard_map/ppermute | solution.py:550
  85.8 7.7 %collective-permute-start.16 = (bf16[16,16,2048]{2,1,0:T(8,128)(2,1)}, bf16[16,16,2048]{2,1,0:T(8,128)(2,1)}, u32[]{:S(2)}, u32[]{:S(2)}) collective-permute-start(bf16[16,16,2048]{2,1,0:T(8,128)(2,1)} %get-tuple-element.122), channel_id=1, source_target_pairs={{0,1},{1,0},{2,3},{3,2},{4,5},{5,4},{6,7},{7,6},{8,9},{9,8},{10,11... | collective-permute-start | bytes 3145736 | tf_op jit(solution)/shard_map/ppermute | solution.py:550
  85.9 10.0 %collective-permute-start.15 = (bf16[16,16,2048]{2,1,0:T(8,128)(2,1)}, bf16[16,16,2048]{2,1,0:T(8,128)(2,1)S(1)}, u32[]{:S(2)}, u32[]{:S(2)}) collective-permute-start(bf16[16,16,2048]{2,1,0:T(8,128)(2,1)} %get-tuple-element.120), channel_id=1, source_target_pairs={{0,1},{1,0},{2,3},{3,2},{4,5},{5,4},{6,7},{7,6},{8,9},{9,8},{10,11... | collective-permute-start | bytes 3145736 | tf_op jit(solution)/shard_map/ppermute | solution.py:550
  95.3 14.5 %collective-permute-start.18 = (bf16[2,2,2,16,2048]{4,3,1,2,0:T(8,128)(2,1)S(1)}, bf16[2,2,2,16,2048]{4,3,1,2,0:T(8,128)(2,1)S(1)}, u32[]{:S(2)}, u32[]{:S(2)}) collective-permute-start(bf16[2,2,2,16,2048]{4,3,1,2,0:T(8,128)(2,1)S(1)} %copy_bitcast_fusion), channel_id=1, source_target_pairs={{0,2},{1,3},{2,0},{3,1},{4,6},{5,7},{6,4},{7,5},{8,10},{9,11},{10,... | collective-permute-start | bytes 1572872 | tf_op jit(solution)/shard_map/ppermute | solution.py:550
  96.4 14.4 %collective-permute-start.17 = (bf16[2,2,2,16,2048]{4,3,0,1,2:T(8,128)(2,1)S(1)}, bf16[2,2,2,16,2048]{4,3,0,1,2:T(8,128)(2,1)S(1)}, u32[]{:S(2)}, u32[]{:S(2)}) collective-permute-start(bf16[2,2,2,16,2048]{4,3,0,1,2:T(8,128)(2,1)S(1)} %copy_bitcast_fusion.1), channel_id=1, source_target_pairs={{0,16},{1,17},{2,18},{3,19},{4,20},{5,21},{6,22},{7,23},{8,24},{9,... | collective-permute-start | bytes 1572872 | tf_op jit(solution)/shard_map/ppermute | solution.py:550
  110.0 8.2 %collective-permute-start.20 = (bf16[2,2,16,2048]{3,2,0,1:T(8,128)(2,1)S(1)}, bf16[2,2,16,2048]{3,2,0,1:T(8,128)(2,1)S(1)}, u32[]{:S(2)}, u32[]{:S(2)}) collective-permute-start(bf16[2,2,16,2048]{3,2,0,1:T(8,128)(2,1)S(1)} %dynamic-slice_bitcast_fusion.1), channel_id=1, source_target_pairs={{0,16},{1,17},{2,18},{3,19},{4,20},{5,21},{6,22},{7,23},{8,24},{9,... | collective-permute-start | bytes 786440 | tf_op jit(solution)/shard_map/ppermute | solution.py:550
  111.0 7.8 %collective-permute-start.19 = (bf16[2,2,16,2048]{3,2,0,1:T(8,128)(2,1)S(1)}, bf16[2,2,16,2048]{3,2,0,1:T(8,128)(2,1)S(1)}, u32[]{:S(2)}, u32[]{:S(2)}) collective-permute-start(bf16[2,2,16,2048]{3,2,0,1:T(8,128)(2,1)S(1)} %dynamic-slice_bitcast_fusion.2), channel_id=1, source_target_pairs={{0,2},{1,3},{2,0},{3,1},{4,6},{5,7},{6,4},{7,5},{8,10},{9,11},{10,... | collective-permute-start | bytes 786440 | tf_op jit(solution)/shard_map/ppermute | solution.py:550
  119.0 7.9 %collective-permute-start.21 = (bf16[2,16,4096]{2,1,0:T(8,128)(2,1)S(1)}, bf16[2,16,4096]{2,1,0:T(8,128)(2,1)S(1)}, u32[]{:S(2)}, u32[]{:S(2)}) collective-permute-start(bf16[2,16,4096]{2,1,0:T(8,128)(2,1)S(1)} %dynamic-slice_bitcast_fusion), channel_id=1, source_target_pairs={{0,4},{1,5},{2,6},{3,7},{4,0},{5,1},{6,2},{7,3},{8,12},{9,13},{10,... | collective-permute-start | bytes 786440 | tf_op jit(solution)/shard_map/ppermute | solution.py:550
  127.0 7.4 %collective-permute-start.25 = (bf16[16,4096]{1,0:T(8,128)(2,1)S(1)}, bf16[16,4096]{1,0:T(8,128)(2,1)S(1)}, u32[]{:S(2)}, u32[]{:S(2)}) collective-permute-start(bf16[16,4096]{1,0:T(8,128)(2,1)S(1)} %dynamic-slice_bitcast_fusion.3), channel_id=1, source_target_pairs={{0,8},{1,9},{2,10},{3,11},{4,12},{5,13},{6,14},{7,15},{8,0},{9,1},... | collective-permute-start | bytes 393224 | tf_op jit(solution)/shard_map/ppermute | solution.py:550
  132.8 2.2 %collective-permute-start.22 = (bf16[16,16,1280]{2,1,0:T(8,128)(2,1)S(1)}, bf16[16,16,1280]{2,1,0:T(8,128)(2,1)S(1)}, u32[]{:S(2)}, u32[]{:S(2)}) collective-permute-start(bf16[16,16,1280]{2,1,0:T(8,128)(2,1)S(1)} %get-tuple-element.148), channel_id=1, source_target_pairs={{0,1},{1,0},{2,3},{3,2},{4,5},{5,4},{6,7},{7,6},{8,9},{9,8},{10,11... | collective-permute-start | bytes 1966088 | tf_op jit(solution)/shard_map/ppermute | solution.py:550
  135.3 6.3 %collective-permute-start.24 = (bf16[2,2,2,16,640]{4,3,1,2,0:T(8,128)(2,1)S(1)}, bf16[2,2,2,16,640]{4,3,1,2,0:T(8,128)(2,1)S(1)}, u32[]{:S(2)}, u32[]{:S(2)}) collective-permute-start(bf16[2,2,2,16,640]{4,3,1,2,0:T(8,128)(2,1)S(1)} %bitcast.156), channel_id=1, source_target_pairs={{0,2},{1,3},{2,0},{3,1},{4,6},{5,7},{6,4},{7,5},{8,10},{9,11},{10,... | collective-permute-start | bytes 491528 | tf_op jit(solution)/shard_map/ppermute | solution.py:550
  136.1 6.0 %collective-permute-start.23 = (bf16[2,2,2,16,640]{4,3,0,1,2:T(8,128)(2,1)S(1)}, bf16[2,2,2,16,640]{4,3,0,1,2:T(8,128)(2,1)S(1)}, u32[]{:S(2)}, u32[]{:S(2)}) collective-permute-start(bf16[2,2,2,16,640]{4,3,0,1,2:T(8,128)(2,1)S(1)} %bitcast.157), channel_id=1, source_target_pairs={{0,16},{1,17},{2,18},{3,19},{4,20},{5,21},{6,22},{7,23},{8,24},{9,... | collective-permute-start | bytes 491528 | tf_op jit(solution)/shard_map/ppermute | solution.py:550
  142.2 6.1 %collective-permute-start.27 = (bf16[2,2,16,640]{3,2,0,1:T(8,128)(2,1)S(1)}, bf16[2,2,16,640]{3,2,0,1:T(8,128)(2,1)S(1)}, u32[]{:S(2)}, u32[]{:S(2)}) collective-permute-start(bf16[2,2,16,640]{3,2,0,1:T(8,128)(2,1)S(1)} %dynamic-slice_bitcast_fusion.5), channel_id=1, source_target_pairs={{0,16},{1,17},{2,18},{3,19},{4,20},{5,21},{6,22},{7,23},{8,24},{9,... | collective-permute-start | bytes 245768 | tf_op jit(solution)/shard_map/ppermute | solution.py:550
  143.3 5.0 %collective-permute-start.26 = (bf16[2,2,16,640]{3,2,0,1:T(8,128)(2,1)S(1)}, bf16[2,2,16,640]{3,2,0,1:T(8,128)(2,1)S(1)}, u32[]{:S(2)}, u32[]{:S(2)}) collective-permute-start(bf16[2,2,16,640]{3,2,0,1:T(8,128)(2,1)S(1)} %dynamic-slice_bitcast_fusion.6), channel_id=1, source_target_pairs={{0,2},{1,3},{2,0},{3,1},{4,6},{5,7},{6,4},{7,5},{8,10},{9,11},{10,... | collective-permute-start | bytes 245768 | tf_op jit(solution)/shard_map/ppermute | solution.py:550
  148.4 4.5 %collective-permute-start.28 = (bf16[2,16,1280]{2,1,0:T(8,128)(2,1)S(1)}, bf16[2,16,1280]{2,1,0:T(8,128)(2,1)S(1)}, u32[]{:S(2)}, u32[]{:S(2)}) collective-permute-start(bf16[2,16,1280]{2,1,0:T(8,128)(2,1)S(1)} %dynamic-slice_bitcast_fusion.4), channel_id=1, source_target_pairs={{0,4},{1,5},{2,6},{3,7},{4,0},{5,1},{6,2},{7,3},{8,12},{9,13},{10,... | collective-permute-start | bytes 245768 | tf_op jit(solution)/shard_map/ppermute | solution.py:550
  153.0 5.0 %collective-permute-start.29 = (bf16[16,1280]{1,0:T(8,128)(2,1)S(1)}, bf16[16,1280]{1,0:T(8,128)(2,1)S(1)}, u32[]{:S(2)}, u32[]{:S(2)}) collective-permute-start(bf16[16,1280]{1,0:T(8,128)(2,1)S(1)} %get-tuple-element.188), channel_id=1, source_target_pairs={{0,8},{1,9},{2,10},{3,11},{4,12},{5,13},{6,14},{7,15},{8,0},{9,1},... | collective-permute-start | bytes 122888 | tf_op jit(solution)/shard_map/ppermute | solution.py:550
  (30 other events, 191.2 us)

commit v7 on v6

--- a/solution.py
+++ b/solution.py
@@ -839,7 +839,7 @@
     closing = dx1
     if fast:
         tail = joined(w_grads[0], move(w_grads[1], orders[0][-1], count)).reshape(*dims, block, first_width)
-        closing = after(dx1, tail, acc)
+        closing = after(dx1, tail)
         tails = [tail[..., : first_width // 2], tail[..., first_width // 2 :]]
         tails = [fall(part, order, 0) for part, order in zip(tails, back_orders)]
     grad_tokens = call(

time: 159 us -> 159 us (level)
  no operation moved by 1% of the time
where the time goes in v7:
time: 159 us
  Pallas kernels  95.4 us (60%)
  starting transfers between devices  37.6 us (24%)
  waiting for transfers between devices  12.9 us (8%)
  local copies, waits for them, and re-layouts  7.41 us (5%)
  other arithmetic  3.82 us (2%)
  between operations  1.76 us (1%)
    pallas_call x7, Pallas kernels, call(): pl.pallas_call(kernel, grid=grid, in_specs=in_specs, out_specs=out_specs,...  63.1 us
    ppermute x30, starting transfers between devices, move(): return lax.ppermute(value, AXES, xor_pairs(count, mask))  37.6 us
    ppermute x30, waiting for transfers between devices, move(): return lax.ppermute(value, AXES, xor_pairs(count, mask))  12.9 us
    pallas_call x2, Pallas kernels, turn(): pl.pallas_call(functools.partial(turn_kernel, n, len(again) > 0), grid=(t...  11.7 us
    pallas_call x2, Pallas kernels, back(): pl.pallas_call(attend_back_kernel, grid=(per_row,), in_specs=[part(2), bo...  11.4 us
    pallas_call x2, Pallas kernels, results(): pl.pallas_call(functools.partial(result_kernel, n), grid=(tiles // 2,), i...  7 us
    unnamed x68, local copies, waits for them, and re-layouts  3.38 us
  transfers between devices with their start and end apart: 30, of which 15 were waited for; matrix products, arithmetic and copies ran while one was open for 5% of the time, Pallas kernels for 41%

profile of v7, /device:TPU:0, one launch (start us, length us, event | category | flops | bytes accessed | tf_op | source)
XLA Modules:
  0.0 158.9 jit_solution(17266143841714182943)
XLA Ops:
  0.7 1.5 pack.1
  2.1 4.1 %collective-permute-start = (bf16[16,1280]{1,0:T(8,128)(2,1)S(1)}, bf16[16,1280]{1,0:T(8,128)(2,1)S(1)}, u32[]{:S(2)}, u32[]{:S(2)}) collective-permute-start(bf16[16,1280]{1,0:T(8,128)(2,1)S(1)} %get-tuple-element.93), channel_id=1, source_target_pairs={{0,8},{1,9},{2,10},{3,11},{4,12},{5,13},{6,14},{7,15},{8,0},{9,1},... | collective-permute-start | bytes 122888 | tf_op jit(solution)/shard_map/ppermute | solution.py:550
  8.6 1.5 collective-permute-start.1
  10.2 2.9 %collective-permute-start.7 = (bf16[16,4096]{1,0:T(8,128)(2,1)S(1)}, bf16[16,4096]{1,0:T(8,128)(2,1)S(1)}, u32[]{:S(2)}, u32[]{:S(2)}) collective-permute-start(bf16[16,4096]{1,0:T(8,128)(2,1)S(1)} %get-tuple-element.96), channel_id=1, source_target_pairs={{0,8},{1,9},{2,10},{3,11},{4,12},{5,13},{6,14},{7,15},{8,0},{9,1},... | collective-permute-start | bytes 393224 | tf_op jit(solution)/shard_map/ppermute | solution.py:550
  13.9 1.7 %collective-permute-start.4 = (bf16[2,2,16,640]{3,2,1,0:T(8,128)(2,1)S(1)}, bf16[2,2,16,640]{3,2,1,0:T(8,128)(2,1)S(1)}, u32[]{:S(2)}, u32[]{:S(2)}) collective-permute-start(bf16[2,2,16,640]{3,2,1,0:T(8,128)(2,1)S(1)} %get-tuple-element.186), channel_id=1, source_target_pairs={{0,16},{1,17},{2,18},{3,19},{4,20},{5,21},{6,22},{7,23},{8,24},{9,... | collective-permute-start | bytes 245768 | tf_op jit(solution)/shard_map/ppermute | solution.py:550
  15.6 1.5 collective-permute-start.2
  18.5 1.6 %collective-permute-start.5 = (bf16[2,2,2,16,640]{4,3,2,1,0:T(8,128)(2,1)S(1)}, bf16[2,2,2,16,640]{4,3,2,1,0:T(8,128)(2,1)S(1)}, u32[]{:S(2)}, u32[]{:S(2)}) collective-permute-start(bf16[2,2,2,16,640]{4,3,2,1,0:T(8,128)(2,1)S(1)} %maximum_select_fusion.11), channel_id=1, source_target_pairs={{0,2},{1,3},{2,0},{3,1},{4,6},{5,7},{6,4},{7,5},{8,10},{9,11},{10,... | collective-permute-start | bytes 491528 | tf_op jit(solution)/shard_map/ppermute | solution.py:550
  20.3 1.5 collective-permute-start.3
  21.7 2.2 %collective-permute-start.8 = (bf16[2,16,4096]{2,1,0:T(8,128)(2,1)S(1)}, bf16[2,16,4096]{2,1,0:T(8,128)(2,1)S(1)}, u32[]{:S(2)}, u32[]{:S(2)}) collective-permute-start(bf16[2,16,4096]{2,1,0:T(8,128)(2,1)S(1)} %maximum_select_fusion.7), channel_id=1, source_target_pairs={{0,4},{1,5},{2,6},{3,7},{4,0},{5,1},{6,2},{7,3},{8,12},{9,13},{10,... | collective-permute-start | bytes 786440 | tf_op jit(solution)/shard_map/ppermute | solution.py:550
  24.0 1.6 %collective-permute-done.3 = bf16[2,2,2,16,640]{4,3,1,0,2:T(8,128)(2,1)S(1)} collective-permute-done((bf16[2,2,2,16,640]{4,3,1,0,2:T(8,128)(2,1)S(1)}, bf16[2,2,2,16,640]{4,3,1,0,2:T(8,128)(2,1)S(1)}, u32[]{:S(2)}, u32[]{:S(2)}) %collective-permute-start.3) | collective-permute-done | bytes 163872 | tf_op jit(solution)/shard_map/ppermute | solution.py:550
  25.9 2.3 %collective-permute-done.8 = bf16[2,16,4096]{2,1,0:T(8,128)(2,1)S(1)} collective-permute-done((bf16[2,16,4096]{2,1,0:T(8,128)(2,1)S(1)}, bf16[2,16,4096]{2,1,0:T(8,128)(2,1)S(1)}, u32[]{:S(2)}, u32[]{:S(2)}) %collective-permute-start.8) | collective-permute-done | bytes 262176 | tf_op jit(solution)/shard_map/ppermute | solution.py:550
  30.4 8.1 %project.1 = (bf16[2048,512]{1,0:T(8,128)(2,1)}, bf16[2,2048,128]{2,1,0:T(8,128)(2,1)S(1)}, bf16[2048,256]{1,0:T(8,128)(2,1)}, bf16[2048,256]{1,0:T(8,128)(2,1)}...) custom-call(s32[1]{0:T(128)} %bitcast.me, s32[2,4]{1,0:T(2,128)S(1)} %copy-done.13, bf16[2048,512]{1,0:T(8,128)(2,1)} %tok.5, ...), custom_call_target="tpu_custom_call" | custom-call | flops 8999999488 | bytes 1024 | tf_op jit(solution)/shard_map/project/pallas_call | solution.py:662
  40.9 10.2 %attend.1 = (f32[2048,128]{1,0:T(8,128)S(1)}, bf16[2048,512]{1,0:T(8,128)(2,1)S(1)}, bf16[2,2048,128]{2,1,0:T(8,128)(2,1)}) custom-call(s32[2,4]{1,0:T(2,128)S(1)} %copy-done.13, s32[2048,2]{1,0:T(8,128)S(1)} %copy.56.routes, bf16[2,2048,128]{2,1,0:T(8,128)(2,1)S(1)} %get-tuple-element.100.qa, bf16[2048,256]{1,0:T(8,128)(2,1)S(1)} %copy-done.19, ...), custom_call_target="tpu_custom_call" | custom-call | flops 12999999488 | bytes 1024 | tf_op jit(solution)/shard_map/attend/pallas_call | solution.py:662
  54.7 3.8 %mix.1 = (f32[2048,512]{1,0:T(8,128)}, bf16[2048,512]{1,0:T(8,128)(2,1)S(1)}) custom-call(s32[1]{0:T(128)} %bitcast.me, bf16[2048,512]{1,0:T(8,128)(2,1)S(1)} %copy-done.9, bf16[2048,512]{1,0:T(8,128)(2,1)S(1)} %get-tuple-element.107.u, f32[32,512]{1,0:T(8,128)S(1)} %get-tuple-element.108.vec, bf16[16,16,1280]{2,1,0:T(8,128)(2,1)S(1)} %pad_maximum_fusion.refs_0_, ...), custom_call_target="tpu_custom_call" | custom-call | flops 5000000000 | bytes 1024 | tf_op jit(solution)/shard_map/mix/pallas_call | solution.py:662
  58.5 27.3 %feed.1 = (bf16[2048,2048]{1,0:T(8,128)(2,1)}, bf16[2048,2048]{1,0:T(8,128)(2,1)}, f32[8,512]{1,0:T(8,128)S(1)}, bf16[16,16,2048]{2,1,0:T(8,128)(2,1)}, bf16[16,...) custom-call(s32[1]{0:T(128)} %bitcast.me, ...), custom_call_target="tpu_custom_call" | custom-call | flops 24999999488 | bytes 1024 | tf_op jit(solution)/shard_map/feed/pallas_call | solution.py:662
  87.6 5.9 %turn.2 = (f32[2048,512]{1,0:T(8,128)S(1)}, bf16[2048,512]{1,0:T(8,128)(2,1)S(1)}, f32[32,512]{1,0:T(8,128)S(1)}) custom-call(s32[1]{0:T(128)} %bitcast.me, bf16[2048,2048]{1,0:T(8,128)(2,1)} %get-tuple-element.117.dz, bf16[2048,512]{1,0:T(8,128)(2,1)} %dy.5, f32[2048,512]{1,0:T(8,128)} %get-tuple-element.149.x1, f32[32,512]{1,0:T(8,128)S(1)} %get-tuple-element.108.vec, ...), custom_call_target="tpu_custom_call" | custom-call | flops 6000000000 | bytes 1024 | tf_op jit(solution)/shard_map/turn/pallas_call | solution.py:747
  93.6 1.7 %add_convert_fusion = bf16[16,16,2048]{2,1,0:T(8,128)(2,1)S(1)} fusion(bf16[16,16,2048]{2,1,0:T(8,128)(2,1)} %collective-permute-done.16, bf16[16,16,2048]{2,1,0:T(8,128)(2,1)S(1)} %copy-done.29), kind=kLoop, calls=%fused_computation | loop fusion | flops 2097152 | bytes 3145728 | tf_op jit(solution)/shard_map/convert_element_type | solution.py:571
  96.4 1.4 collective-permute-start.17
  97.9 5.8 %turn.3 = (f32[2048,512]{1,0:T(8,128)S(1)}, bf16[2048,512]{1,0:T(8,128)(2,1)S(1)}, f32[32,512]{1,0:T(8,128)S(1)}) custom-call(s32[1]{0:T(128)} %bitcast.me, bf16[2048,2048]{1,0:T(8,128)(2,1)} %get-tuple-element.117.dz, bf16[2048,512]{1,0:T(8,128)(2,1)} %dy.5, f32[2048,512]{1,0:T(8,128)} %get-tuple-element.149.x1, ...), custom_call_target="tpu_custom_call", output_to_operand_aliasing={{0}: (6, {}), {1}: (7, {})} | custom-call | flops 6000000000 | bytes 1024 | tf_op jit(solution)/shard_map/turn/pallas_call | solution.py:747
  103.7 6.1 %gates.1 = (bf16[2,2048,128]{2,1,0:T(8,128)(2,1)S(1)}, bf16[2,2048,128]{2,1,0:T(8,128)(2,1)S(1)}, bf16[2048,128]{1,0:T(8,128)(2,1)S(1)}, f32[8,128]{1,0:T(8,128)S(1)}, bf16[512,512]{1,0:T(8,128)(2,1)S(1)}) custom-call(s32[1]{0:T(128)} %bitcast.me, bf16[2048,512]{1,0:T(8,128)(2,1)S(1)} %get-tuple-element.126.dx1, s32[2048,2]{1,0:T(8,128)S(1)} %copy-done.6, ...), custom_call_target="tpu_custom_call" | custom-call | flops 8999999488 | bytes 1024 | tf_op jit(solution)/shard_map/gates/pallas_call | solution.py:662
  111.0 1.5 collective-permute-start.19
  112.5 5.7 %attend_back.2 = (bf16[2048,512]{1,0:T(8,128)(2,1)S(1)}, bf16[2048,128]{1,0:T(8,128)(2,1)S(1)}) custom-call(s32[2048,2]{1,0:T(8,128)S(1)} %copy-done.6, bf16[2,2048,128]{2,1,0:T(8,128)(2,1)S(1)} %copy-done.18, bf16[2,2048,128]{2,1,0:T(8,128)(2,1)S(1)} %copy-done.23, bf16[2048,256]{1,0:T(8,128)(2,1)S(1)} %copy-done.20, bf16[2048,256]{1,0:T(8,128)(2,1)S(1)} %copy-done.22, ...), custom_call_target="tpu_custom_call" | custom-call | flops 8000000000 | bytes 1024 | tf_op jit(solution)/shard_map/attend_back/pallas_call | solution.py:797
  119.0 2.3 %collective-permute-start.21 = (bf16[2,16,4096]{2,1,0:T(8,128)(2,1)S(1)}, bf16[2,16,4096]{2,1,0:T(8,128)(2,1)S(1)}, u32[]{:S(2)}, u32[]{:S(2)}) collective-permute-start(bf16[2,16,4096]{2,1,0:T(8,128)(2,1)S(1)} %dynamic-slice_bitcast_fusion), channel_id=1, source_target_pairs={{0,4},{1,5},{2,6},{3,7},{4,0},{5,1},{6,2},{7,3},{8,12},{9,13},{10,... | collective-permute-start | bytes 786440 | tf_op jit(solution)/shard_map/ppermute | solution.py:550
  121.2 5.7 %attend_back.3 = (bf16[2048,512]{1,0:T(8,128)(2,1)S(1)}, bf16[2048,128]{1,0:T(8,128)(2,1)S(1)}) custom-call(s32[2048,2]{1,0:T(8,128)S(1)} %copy-done.6, bf16[2,2048,128]{2,1,0:T(8,128)(2,1)S(1)} %copy-done.18, bf16[2,2048,128]{2,1,0:T(8,128)(2,1)S(1)} %copy-done.23, bf16[2048,256]{1,0:T(8,128)(2,1)S(1)} %copy-done.20, ...), custom_call_target="tpu_custom_call", output_to_operand_aliasing={{0}: (7, {}), {1}: (8, {})} | custom-call | flops 8000000000 | bytes 1024 | tf_op jit(solution)/shard_map/attend_back/pallas_call | solution.py:797
  127.0 2.2 %collective-permute-start.29 = (bf16[16,4096]{1,0:T(8,128)(2,1)S(1)}, bf16[16,4096]{1,0:T(8,128)(2,1)S(1)}, u32[]{:S(2)}, u32[]{:S(2)}) collective-permute-start(bf16[16,4096]{1,0:T(8,128)(2,1)S(1)} %dynamic-slice_bitcast_fusion.3), channel_id=1, source_target_pairs={{0,8},{1,9},{2,10},{3,11},{4,12},{5,13},{6,14},{7,15},{8,0},{9,1},... | collective-permute-start | bytes 393224 | tf_op jit(solution)/shard_map/ppermute | solution.py:550
  129.3 3.6 %sums.1 = (bf16[16,16,1280]{2,1,0:T(8,128)(2,1)S(1)}, bf16[16,16,1280]{2,1,0:T(8,128)(2,1)S(1)}) custom-call(s32[1]{0:T(128)} %bitcast.me, bf16[2048,512]{1,0:T(8,128)(2,1)S(1)} %copy-done.16, bf16[2048,512]{1,0:T(8,128)(2,1)S(1)} %get-tuple-element.138.dq, bf16[2048,128]{1,0:T(8,128)(2,1)S(1)} %get-tuple-element.142.kv, ...), custom_call_target="tpu_custom_call" | custom-call | flops 6000000000 | bytes 1024 | tf_op jit(solution)/shard_map/sums/pallas_call | solution.py:662
  132.9 1.6 collective-permute-done.29
  137.2 4.1 %close.1 = bf16[2048,512]{1,0:T(8,128)(2,1)} custom-call(s32[1]{0:T(128)} %bitcast.me, f32[2048,512]{1,0:T(8,128)S(1)} %get-tuple-element.151.dx1, bf16[2048,512]{1,0:T(8,128)(2,1)S(1)} %get-tuple-element.138.dq, bf16[2048,128]{1,0:T(8,128)(2,1)S(1)} %get-tuple-element.142.kv, bf16[2048,128]{1,0:T(8,128)(2,1)S(1)} %get-tuple-element.133.ds, ...), custom_call_target="tpu_custom_call" | custom-call | flops 6000000000 | bytes 1024 | tf_op jit(solution)/shard_map/close/pallas_call | solution.py:662
  143.3 1.5 collective-permute-start.25
  144.8 3.5 %result.2.refs_4_ = bf16[2048,512]{1,0:T(8,128)(2,1)} custom-call(s32[1]{0:T(128)} %bitcast.me, bf16[2048,2048]{1,0:T(8,128)(2,1)S(1)} %bitcast.115, f32[2048,512]{1,0:T(8,128)S(1)} %copy-done, f32[32,512]{1,0:T(8,128)S(1)} %get-tuple-element.108.vec, bf16[16,16,2048]{2,1,0:T(8,128)(2,1)S(1)} %bitcast.120, ...), custom_call_target="tpu_custom_call" | custom-call | flops 3500000000 | bytes 1024 | tf_op jit(solution)/shard_map/result/pallas_call | solution.py:861
  149.5 3.5 %result.3 = bf16[2048,512]{1,0:T(8,128)(2,1)} custom-call(s32[1]{0:T(128)} %bitcast.me, bf16[2048,2048]{1,0:T(8,128)(2,1)S(1)} %bitcast.115, f32[2048,512]{1,0:T(8,128)S(1)} %copy-done, f32[32,512]{1,0:T(8,128)S(1)} %get-tuple-element.108.vec, bf16[16,16,2048]{2,1,0:T(8,128)(2,1)S(1)} %bitcast.121, ...), custom_call_target="tpu_custom_call", output_to_operand_aliasing={{}: (8, {})} | custom-call | flops 3500000000 | bytes 1024 | tf_op jit(solution)/shard_map/result/pallas_call | solution.py:861
  155.2 1.6 %reshape.281 = f32[16,2048]{1,0:T(8,128)} reshape(f32[16,32,4,16]{3,2,1,0:T(4,128)S(1)} %copy.68) | data formatting | bytes 262144 | tf_op jit(solution)/shard_map/reshape | solution.py:879
  (169 shorter events, 27.9 us)
Async XLA Ops:
  2.1 6.5 %collective-permute-start = (bf16[16,1280]{1,0:T(8,128)(2,1)S(1)}, bf16[16,1280]{1,0:T(8,128)(2,1)S(1)}, u32[]{:S(2)}, u32[]{:S(2)}) collective-permute-start(bf16[16,1280]{1,0:T(8,128)(2,1)S(1)} %get-tuple-element.93), channel_id=1, source_target_pairs={{0,8},{1,9},{2,10},{3,11},{4,12},{5,13},{6,14},{7,15},{8,0},{9,1},... | collective-permute-start | bytes 122888 | tf_op jit(solution)/shard_map/ppermute | solution.py:550
  7.3 33.6 %copy-start.5 = (s32[2048,2]{1,0:T(8,128)}, s32[2048,2]{1,0:T(8,128)S(1)}, u32[]{:S(2)}) copy-start(s32[2048,2]{1,0:T(8,128)S(1)} %copy.56.routes) | copy-start | bytes 49156
  8.6 5.2 %collective-permute-start.1 = (bf16[2,16,1280]{2,1,0:T(8,128)(2,1)S(1)}, bf16[2,16,1280]{2,1,0:T(8,128)(2,1)S(1)}, u32[]{:S(2)}, u32[]{:S(2)}) collective-permute-start(bf16[2,16,1280]{2,1,0:T(8,128)(2,1)S(1)} %maximum_select_fusion.13), channel_id=1, source_target_pairs={{0,4},{1,5},{2,6},{3,7},{4,0},{5,1},{6,2},{7,3},{8,12},{9,13},{10,... | collective-permute-start | bytes 245768 | tf_op jit(solution)/shard_map/ppermute | solution.py:550
  10.2 7.8 %collective-permute-start.7 = (bf16[16,4096]{1,0:T(8,128)(2,1)S(1)}, bf16[16,4096]{1,0:T(8,128)(2,1)S(1)}, u32[]{:S(2)}, u32[]{:S(2)}) collective-permute-start(bf16[16,4096]{1,0:T(8,128)(2,1)S(1)} %get-tuple-element.96), channel_id=1, source_target_pairs={{0,8},{1,9},{2,10},{3,11},{4,12},{5,13},{6,14},{7,15},{8,0},{9,1},... | collective-permute-start | bytes 393224 | tf_op jit(solution)/shard_map/ppermute | solution.py:550
  13.9 4.5 %collective-permute-start.4 = (bf16[2,2,16,640]{3,2,1,0:T(8,128)(2,1)S(1)}, bf16[2,2,16,640]{3,2,1,0:T(8,128)(2,1)S(1)}, u32[]{:S(2)}, u32[]{:S(2)}) collective-permute-start(bf16[2,2,16,640]{3,2,1,0:T(8,128)(2,1)S(1)} %get-tuple-element.186), channel_id=1, source_target_pairs={{0,16},{1,17},{2,18},{3,19},{4,20},{5,21},{6,22},{7,23},{8,24},{9,... | collective-permute-start | bytes 245768 | tf_op jit(solution)/shard_map/ppermute | solution.py:550
  15.6 4.6 %collective-permute-start.2 = (bf16[2,2,16,640]{3,2,1,0:T(8,128)(2,1)S(1)}, bf16[2,2,16,640]{3,2,1,0:T(8,128)(2,1)S(1)}, u32[]{:S(2)}, u32[]{:S(2)}) collective-permute-start(bf16[2,2,16,640]{3,2,1,0:T(8,128)(2,1)S(1)} %get-tuple-element.187), channel_id=1, source_target_pairs={{0,2},{1,3},{2,0},{3,1},{4,6},{5,7},{6,4},{7,5},{8,10},{9,11},{10,... | collective-permute-start | bytes 245768 | tf_op jit(solution)/shard_map/ppermute | solution.py:550
  18.5 5.5 %collective-permute-start.5 = (bf16[2,2,2,16,640]{4,3,2,1,0:T(8,128)(2,1)S(1)}, bf16[2,2,2,16,640]{4,3,2,1,0:T(8,128)(2,1)S(1)}, u32[]{:S(2)}, u32[]{:S(2)}) collective-permute-start(bf16[2,2,2,16,640]{4,3,2,1,0:T(8,128)(2,1)S(1)} %maximum_select_fusion.11), channel_id=1, source_target_pairs={{0,2},{1,3},{2,0},{3,1},{4,6},{5,7},{6,4},{7,5},{8,10},{9,11},{10,... | collective-permute-start | bytes 491528 | tf_op jit(solution)/shard_map/ppermute | solution.py:550
  20.3 5.4 %collective-permute-start.3 = (bf16[2,2,2,16,640]{4,3,1,0,2:T(8,128)(2,1)S(1)}, bf16[2,2,2,16,640]{4,3,1,0,2:T(8,128)(2,1)S(1)}, u32[]{:S(2)}, u32[]{:S(2)}) collective-permute-start(bf16[2,2,2,16,640]{4,3,1,0,2:T(8,128)(2,1)S(1)} %maximum_select_fusion.9), channel_id=1, source_target_pairs={{0,16},{1,17},{2,18},{3,19},{4,20},{5,21},{6,22},{7,23},{8,24},{9,... | collective-permute-start | bytes 491528 | tf_op jit(solution)/shard_map/ppermute | solution.py:550
  21.7 6.5 %collective-permute-start.8 = (bf16[2,16,4096]{2,1,0:T(8,128)(2,1)S(1)}, bf16[2,16,4096]{2,1,0:T(8,128)(2,1)S(1)}, u32[]{:S(2)}, u32[]{:S(2)}) collective-permute-start(bf16[2,16,4096]{2,1,0:T(8,128)(2,1)S(1)} %maximum_select_fusion.7), channel_id=1, source_target_pairs={{0,4},{1,5},{2,6},{3,7},{4,0},{5,1},{6,2},{7,3},{8,12},{9,13},{10,... | collective-permute-start | bytes 786440 | tf_op jit(solution)/shard_map/ppermute | solution.py:550
  25.8 28.1 %copy-start.7 = (bf16[16,16,1280]{2,1,0:T(8,128)(2,1)}, bf16[16,16,1280]{2,1,0:T(8,128)(2,1)S(1)}, u32[]{:S(2)}) copy-start(bf16[16,16,1280]{2,1,0:T(8,128)(2,1)S(1)} %pad_maximum_fusion.refs_0_) | copy-start | bytes 1966084
  25.8 2.5 %collective-permute-start.6 = (bf16[16,16,1280]{2,1,0:T(8,128)(2,1)S(1)}, bf16[16,16,1280]{2,1,0:T(8,128)(2,1)S(1)}, u32[]{:S(2)}, u32[]{:S(2)}) collective-permute-start(bf16[16,16,1280]{2,1,0:T(8,128)(2,1)S(1)} %pad_maximum_fusion.refs_0_), channel_id=1, source_target_pairs={{0,1},{1,0},{2,3},{3,2},{4,5},{5,4},{6,7},{7,6},{8,9},{9,8},{10,11... | collective-permute-start | bytes 1966088 | tf_op jit(solution)/shard_map/ppermute | solution.py:550
  28.4 10.2 %collective-permute-start.9 = (bf16[2,2,16,2048]{3,2,0,1:T(8,128)(2,1)S(1)}, bf16[2,2,16,2048]{3,2,0,1:T(8,128)(2,1)S(1)}, u32[]{:S(2)}, u32[]{:S(2)}) collective-permute-start(bf16[2,2,16,2048]{3,2,0,1:T(8,128)(2,1)S(1)} %get-tuple-element.98), channel_id=1, source_target_pairs={{0,2},{1,3},{2,0},{3,1},{4,6},{5,7},{6,4},{7,5},{8,10},{9,11},{10,... | collective-permute-start | bytes 786440 | tf_op jit(solution)/shard_map/ppermute | solution.py:550
  29.5 9.2 %collective-permute-start.10 = (bf16[2,2,16,2048]{3,2,0,1:T(8,128)(2,1)S(1)}, bf16[2,2,16,2048]{3,2,0,1:T(8,128)(2,1)S(1)}, u32[]{:S(2)}, u32[]{:S(2)}) collective-permute-start(bf16[2,2,16,2048]{3,2,0,1:T(8,128)(2,1)S(1)} %get-tuple-element.99), channel_id=1, source_target_pairs={{0,16},{1,17},{2,18},{3,19},{4,20},{5,21},{6,22},{7,23},{8,24},{9,... | collective-permute-start | bytes 786440 | tf_op jit(solution)/shard_map/ppermute | solution.py:550
  38.8 13.0 %collective-permute-start.11 = (bf16[2,2,2,16,2048]{4,3,0,1,2:T(8,128)(2,1)S(1)}, bf16[2,2,2,16,2048]{4,3,0,1,2:T(8,128)(2,1)S(1)}, u32[]{:S(2)}, u32[]{:S(2)}) collective-permute-start(bf16[2,2,2,16,2048]{4,3,0,1,2:T(8,128)(2,1)S(1)} %maximum_select_fusion.3), channel_id=1, source_target_pairs={{0,16},{1,17},{2,18},{3,19},{4,20},{5,21},{6,22},{7,23},{8,24},{9,... | collective-permute-start | bytes 1572872 | tf_op jit(solution)/shard_map/ppermute | solution.py:550
  39.9 13.1 %collective-permute-start.12 = (bf16[2,2,2,16,2048]{4,3,1,2,0:T(8,128)(2,1)S(1)}, bf16[2,2,2,16,2048]{4,3,1,2,0:T(8,128)(2,1)S(1)}, u32[]{:S(2)}, u32[]{:S(2)}) collective-permute-start(bf16[2,2,2,16,2048]{4,3,1,2,0:T(8,128)(2,1)S(1)} %maximum_select_fusion.4), channel_id=1, source_target_pairs={{0,2},{1,3},{2,0},{3,1},{4,6},{5,7},{6,4},{7,5},{8,10},{9,11},{10,... | collective-permute-start | bytes 1572872 | tf_op jit(solution)/shard_map/ppermute | solution.py:550
  53.3 5.1 %collective-permute-start.13 = (bf16[16,16,2048]{2,1,0:T(8,128)(2,1)S(1)}, bf16[16,16,2048]{2,1,0:T(8,128)(2,1)S(1)}, u32[]{:S(2)}, u32[]{:S(2)}) collective-permute-start(bf16[16,16,2048]{2,1,0:T(8,128)(2,1)S(1)} %bitcast.116), channel_id=1, source_target_pairs={{0,1},{1,0},{2,3},{3,2},{4,5},{5,4},{6,7},{7,6},{8,9},{9,8},{10,11... | collective-permute-start | bytes 3145736 | tf_op jit(solution)/shard_map/ppermute | solution.py:550
  53.4 5.1 %collective-permute-start.14 = (bf16[16,16,2048]{2,1,0:T(8,128)(2,1)S(1)}, bf16[16,16,2048]{2,1,0:T(8,128)(2,1)S(1)}, u32[]{:S(2)}, u32[]{:S(2)}) collective-permute-start(bf16[16,16,2048]{2,1,0:T(8,128)(2,1)S(1)} %bitcast.122), channel_id=1, source_target_pairs={{0,1},{1,0},{2,3},{3,2},{4,5},{5,4},{6,7},{7,6},{8,9},{9,8},{10,11... | collective-permute-start | bytes 3145736 | tf_op jit(solution)/shard_map/ppermute | solution.py:550
  85.8 7.7 %collective-permute-start.16 = (bf16[16,16,2048]{2,1,0:T(8,128)(2,1)}, bf16[16,16,2048]{2,1,0:T(8,128)(2,1)}, u32[]{:S(2)}, u32[]{:S(2)}) collective-permute-start(bf16[16,16,2048]{2,1,0:T(8,128)(2,1)} %get-tuple-element.122), channel_id=1, source_target_pairs={{0,1},{1,0},{2,3},{3,2},{4,5},{5,4},{6,7},{7,6},{8,9},{9,8},{10,11... | collective-permute-start | bytes 3145736 | tf_op jit(solution)/shard_map/ppermute | solution.py:550
  85.9 10.0 %collective-permute-start.15 = (bf16[16,16,2048]{2,1,0:T(8,128)(2,1)}, bf16[16,16,2048]{2,1,0:T(8,128)(2,1)S(1)}, u32[]{:S(2)}, u32[]{:S(2)}) collective-permute-start(bf16[16,16,2048]{2,1,0:T(8,128)(2,1)} %get-tuple-element.120), channel_id=1, source_target_pairs={{0,1},{1,0},{2,3},{3,2},{4,5},{5,4},{6,7},{7,6},{8,9},{9,8},{10,11... | collective-permute-start | bytes 3145736 | tf_op jit(solution)/shard_map/ppermute | solution.py:550
  95.3 14.5 %collective-permute-start.18 = (bf16[2,2,2,16,2048]{4,3,1,2,0:T(8,128)(2,1)S(1)}, bf16[2,2,2,16,2048]{4,3,1,2,0:T(8,128)(2,1)S(1)}, u32[]{:S(2)}, u32[]{:S(2)}) collective-permute-start(bf16[2,2,2,16,2048]{4,3,1,2,0:T(8,128)(2,1)S(1)} %copy_bitcast_fusion), channel_id=1, source_target_pairs={{0,2},{1,3},{2,0},{3,1},{4,6},{5,7},{6,4},{7,5},{8,10},{9,11},{10,... | collective-permute-start | bytes 1572872 | tf_op jit(solution)/shard_map/ppermute | solution.py:550
  96.4 14.4 %collective-permute-start.17 = (bf16[2,2,2,16,2048]{4,3,0,1,2:T(8,128)(2,1)S(1)}, bf16[2,2,2,16,2048]{4,3,0,1,2:T(8,128)(2,1)S(1)}, u32[]{:S(2)}, u32[]{:S(2)}) collective-permute-start(bf16[2,2,2,16,2048]{4,3,0,1,2:T(8,128)(2,1)S(1)} %copy_bitcast_fusion.1), channel_id=1, source_target_pairs={{0,16},{1,17},{2,18},{3,19},{4,20},{5,21},{6,22},{7,23},{8,24},{9,... | collective-permute-start | bytes 1572872 | tf_op jit(solution)/shard_map/ppermute | solution.py:550
  110.0 8.2 %collective-permute-start.20 = (bf16[2,2,16,2048]{3,2,0,1:T(8,128)(2,1)S(1)}, bf16[2,2,16,2048]{3,2,0,1:T(8,128)(2,1)S(1)}, u32[]{:S(2)}, u32[]{:S(2)}) collective-permute-start(bf16[2,2,16,2048]{3,2,0,1:T(8,128)(2,1)S(1)} %dynamic-slice_bitcast_fusion.1), channel_id=1, source_target_pairs={{0,16},{1,17},{2,18},{3,19},{4,20},{5,21},{6,22},{7,23},{8,24},{9,... | collective-permute-start | bytes 786440 | tf_op jit(solution)/shard_map/ppermute | solution.py:550
  111.0 7.8 %collective-permute-start.19 = (bf16[2,2,16,2048]{3,2,0,1:T(8,128)(2,1)S(1)}, bf16[2,2,16,2048]{3,2,0,1:T(8,128)(2,1)S(1)}, u32[]{:S(2)}, u32[]{:S(2)}) collective-permute-start(bf16[2,2,16,2048]{3,2,0,1:T(8,128)(2,1)S(1)} %dynamic-slice_bitcast_fusion.2), channel_id=1, source_target_pairs={{0,2},{1,3},{2,0},{3,1},{4,6},{5,7},{6,4},{7,5},{8,10},{9,11},{10,... | collective-permute-start | bytes 786440 | tf_op jit(solution)/shard_map/ppermute | solution.py:550
  119.0 7.9 %collective-permute-start.21 = (bf16[2,16,4096]{2,1,0:T(8,128)(2,1)S(1)}, bf16[2,16,4096]{2,1,0:T(8,128)(2,1)S(1)}, u32[]{:S(2)}, u32[]{:S(2)}) collective-permute-start(bf16[2,16,4096]{2,1,0:T(8,128)(2,1)S(1)} %dynamic-slice_bitcast_fusion), channel_id=1, source_target_pairs={{0,4},{1,5},{2,6},{3,7},{4,0},{5,1},{6,2},{7,3},{8,12},{9,13},{10,... | collective-permute-start | bytes 786440 | tf_op jit(solution)/shard_map/ppermute | solution.py:550
  127.0 7.4 %collective-permute-start.29 = (bf16[16,4096]{1,0:T(8,128)(2,1)S(1)}, bf16[16,4096]{1,0:T(8,128)(2,1)S(1)}, u32[]{:S(2)}, u32[]{:S(2)}) collective-permute-start(bf16[16,4096]{1,0:T(8,128)(2,1)S(1)} %dynamic-slice_bitcast_fusion.3), channel_id=1, source_target_pairs={{0,8},{1,9},{2,10},{3,11},{4,12},{5,13},{6,14},{7,15},{8,0},{9,1},... | collective-permute-start | bytes 393224 | tf_op jit(solution)/shard_map/ppermute | solution.py:550
  132.8 2.2 %collective-permute-start.22 = (bf16[16,16,1280]{2,1,0:T(8,128)(2,1)S(1)}, bf16[16,16,1280]{2,1,0:T(8,128)(2,1)S(1)}, u32[]{:S(2)}, u32[]{:S(2)}) collective-permute-start(bf16[16,16,1280]{2,1,0:T(8,128)(2,1)S(1)} %get-tuple-element.148), channel_id=1, source_target_pairs={{0,1},{1,0},{2,3},{3,2},{4,5},{5,4},{6,7},{7,6},{8,9},{9,8},{10,11... | collective-permute-start | bytes 1966088 | tf_op jit(solution)/shard_map/ppermute | solution.py:550
  135.3 6.3 %collective-permute-start.24 = (bf16[2,2,2,16,640]{4,3,1,2,0:T(8,128)(2,1)S(1)}, bf16[2,2,2,16,640]{4,3,1,2,0:T(8,128)(2,1)S(1)}, u32[]{:S(2)}, u32[]{:S(2)}) collective-permute-start(bf16[2,2,2,16,640]{4,3,1,2,0:T(8,128)(2,1)S(1)} %bitcast.156), channel_id=1, source_target_pairs={{0,2},{1,3},{2,0},{3,1},{4,6},{5,7},{6,4},{7,5},{8,10},{9,11},{10,... | collective-permute-start | bytes 491528 | tf_op jit(solution)/shard_map/ppermute | solution.py:550
  136.1 6.0 %collective-permute-start.23 = (bf16[2,2,2,16,640]{4,3,0,1,2:T(8,128)(2,1)S(1)}, bf16[2,2,2,16,640]{4,3,0,1,2:T(8,128)(2,1)S(1)}, u32[]{:S(2)}, u32[]{:S(2)}) collective-permute-start(bf16[2,2,2,16,640]{4,3,0,1,2:T(8,128)(2,1)S(1)} %bitcast.157), channel_id=1, source_target_pairs={{0,16},{1,17},{2,18},{3,19},{4,20},{5,21},{6,22},{7,23},{8,24},{9,... | collective-permute-start | bytes 491528 | tf_op jit(solution)/shard_map/ppermute | solution.py:550
  142.2 6.1 %collective-permute-start.26 = (bf16[2,2,16,640]{3,2,0,1:T(8,128)(2,1)S(1)}, bf16[2,2,16,640]{3,2,0,1:T(8,128)(2,1)S(1)}, u32[]{:S(2)}, u32[]{:S(2)}) collective-permute-start(bf16[2,2,16,640]{3,2,0,1:T(8,128)(2,1)S(1)} %dynamic-slice_bitcast_fusion.5), channel_id=1, source_target_pairs={{0,16},{1,17},{2,18},{3,19},{4,20},{5,21},{6,22},{7,23},{8,24},{9,... | collective-permute-start | bytes 245768 | tf_op jit(solution)/shard_map/ppermute | solution.py:550
  143.3 5.0 %collective-permute-start.25 = (bf16[2,2,16,640]{3,2,0,1:T(8,128)(2,1)S(1)}, bf16[2,2,16,640]{3,2,0,1:T(8,128)(2,1)S(1)}, u32[]{:S(2)}, u32[]{:S(2)}) collective-permute-start(bf16[2,2,16,640]{3,2,0,1:T(8,128)(2,1)S(1)} %dynamic-slice_bitcast_fusion.6), channel_id=1, source_target_pairs={{0,2},{1,3},{2,0},{3,1},{4,6},{5,7},{6,4},{7,5},{8,10},{9,11},{10,... | collective-permute-start | bytes 245768 | tf_op jit(solution)/shard_map/ppermute | solution.py:550
  148.4 4.5 %collective-permute-start.27 = (bf16[2,16,1280]{2,1,0:T(8,128)(2,1)S(1)}, bf16[2,16,1280]{2,1,0:T(8,128)(2,1)S(1)}, u32[]{:S(2)}, u32[]{:S(2)}) collective-permute-start(bf16[2,16,1280]{2,1,0:T(8,128)(2,1)S(1)} %dynamic-slice_bitcast_fusion.4), channel_id=1, source_target_pairs={{0,4},{1,5},{2,6},{3,7},{4,0},{5,1},{6,2},{7,3},{8,12},{9,13},{10,... | collective-permute-start | bytes 245768 | tf_op jit(solution)/shard_map/ppermute | solution.py:550
  153.0 5.0 %collective-permute-start.28 = (bf16[16,1280]{1,0:T(8,128)(2,1)S(1)}, bf16[16,1280]{1,0:T(8,128)(2,1)S(1)}, u32[]{:S(2)}, u32[]{:S(2)}) collective-permute-start(bf16[16,1280]{1,0:T(8,128)(2,1)S(1)} %get-tuple-element.188), channel_id=1, source_target_pairs={{0,8},{1,9},{2,10},{3,11},{4,12},{5,13},{6,14},{7,15},{8,0},{9,1},... | collective-permute-start | bytes 122888 | tf_op jit(solution)/shard_map/ppermute | solution.py:550
  (30 other events, 191.2 us)
